TPU v7x, 32 devices: a whole 2x2x4 slice. The times are simulated.
32 devices in a mesh: expert: 4 (over x, core), split: 8 (over z, y).
Axes of the slice: x: 2, y: 2, z: 4, core: 2. Of those that a mesh axis runs over, the one named last changes fastest.
Arguments:
- tokens: bfloat16 [1024, 3072], P('expert', 'split'), may hold values from -6 to 6
- expert_ids: int32 [1024, 2], P('expert'), may hold values from 0 to 3, all different within a row; in each aligned block of 256 rows (0 to 255, 256 to 511, ...) at most 256 rows name the same one
- pair_logits: float32 [1024, 2], P('expert'), may hold values from -6 to 6
- gate_weight: bfloat16 [4, 3072, 8192], P('expert', None, 'split'), may hold values from -0.109375 to 0.109375
- up_weight: bfloat16 [4, 3072, 8192], P('expert', None, 'split'), may hold values from -0.109375 to 0.109375
- down_weight: bfloat16 [4, 8192, 3072], P('expert', 'split'), may hold values from -0.0625 to 0.0625
Outputs:
- mixed: bfloat16 [1024, 3072], P('expert', 'split')
Inputs may be any that keep to these rules, and one draw needn't show every extreme that they name: `expert_ids`: the two experts of a token differ. Within each aligned block of 256 tokens (the tokens of one index of expert) no expert is named by more than 256 pairs, a bound that some block reaches.
All inputs are finite; a program needn't handle non-finite values.
Results may differ from a plain program's by a relative error of at most 0.019.
Values may be sent and summed in bfloat16 or wider, within the bound.
No kernel may reach another device: no remote copies, remote signals or barrier semaphores. Data moves between devices by JAX's collectives and lax.ppermute only.
A program may use at most 64 MiB of HBM per device.

v0:
```python
import jax
import jax.numpy as jnp
from jax import lax
from jax.sharding import PartitionSpec as P


def body(tokens, expert_ids, pair_logits, gate_weight, up_weight, down_weight):
    experts = lax.axis_size("expert")
    tok_rows = tokens.shape[0]
    capacity = 4 * tok_rows // experts
    flat = expert_ids.reshape(-1)
    labels = jnp.arange(experts, dtype=jnp.int32)
    onehot = (flat[:, None] == labels[None, :]).astype(jnp.int32)
    before = jnp.cumsum(onehot, axis=0) - onehot
    slot = jnp.sum(before * onehot, axis=1)
    dest = flat * capacity + slot
    first = jax.nn.sigmoid(pair_logits[:, 0] - pair_logits[:, 1])
    mix = jnp.stack([first, 1.0 - first], axis=1).reshape(-1)
    w_gate = gate_weight[0]
    w_up = up_weight[0]
    w_down = down_weight[0]
    narrow = tokens.shape[1]
    select = (jnp.arange(experts * capacity, dtype=jnp.int32)[:, None] == dest[None, :]).astype(
        jnp.bfloat16
    )
    doubled = jnp.repeat(tokens, 2, axis=0)
    packed = jnp.dot(select, doubled, preferred_element_type=jnp.float32).astype(jnp.bfloat16)
    sending = packed.reshape(experts, capacity, narrow)
    arrived = lax.all_to_all(sending, "expert", split_axis=0, concat_axis=0, tiled=True).reshape(
        experts * capacity, narrow
    )
    piece = lax.all_gather(arrived, "split", axis=1, tiled=True)
    gate = jnp.dot(piece, w_gate, preferred_element_type=jnp.float32)
    up_part = jnp.dot(piece, w_up, preferred_element_type=jnp.float32)
    hidden = (jax.nn.silu(gate) * up_part).astype(jnp.bfloat16)
    terms = jnp.dot(hidden, w_down, preferred_element_type=jnp.float32)
    result = lax.psum_scatter(
        terms.astype(jnp.bfloat16), "split", scatter_dimension=1, tiled=True
    ).astype(jnp.float32)
    narrow = result.shape[1]
    returned = lax.all_to_all(
        result.reshape(experts, capacity, narrow).astype(jnp.bfloat16),
        "expert",
        split_axis=0,
        concat_axis=0,
        tiled=True,
    ).astype(jnp.float32)
    returned = returned.reshape(experts * capacity, narrow)
    picked = returned[dest] * mix[:, None]
    mixed = picked.reshape(tok_rows, 2, narrow).sum(axis=1)
    return mixed.astype(jnp.bfloat16)


def solution(mesh):
    in_specs = (
        P("expert", "split"),
        P("expert", None),
        P("expert", None),
        P("expert", None, "split"),
        P("expert", None, "split"),
        P("expert", "split", None),
    )
    out_specs = P("expert", "split")
    return jax.shard_map(body, mesh=mesh, in_specs=in_specs, out_specs=out_specs, check_vma=False)
```

profile of v0, /device:TPU:0, one launch (start us, length us, event | category | flops | bytes accessed | tf_op | source)
XLA Modules:
  0.0 314.7 jit_solution(1214880064522008676)
XLA Ops:
  6.5 0.0 all-gather.2.cloned.1.call-start
  6.5 0.8 copy.12
  7.4 0.1 eq.40
  7.5 0.1 reshape.81
  7.7 1.2 reduce-window.6
  8.9 0.2 slice_reduce_fusion
  9.1 0.2 reduce-window.9
  9.3 0.1 add_bitcast_fusion
  9.4 1.1 broadcast_in_dim.2
  10.5 0.1 reshape.83
  10.7 0.7 fusion.14
  11.4 15.8 %all_to_all.10 = bf16[4,256,384]{2,1,0:T(8,128)(2,1)} all-to-all(bf16[4,256,384]{2,1,0:T(8,128)(2,1)S(1)} %bitcast.50), channel_id=1, replica_groups=mesh['expert'=4,'split'=8] {'expert'}, dimensions={0} | all-to-all | bytes 1572864 | tf_op jit(solution)/shard_map/all_to_all | solution.py:29
  27.2 0.0 all-gather.2.cloned.1.call-update
  27.2 0.0 reduce-scatter.4.cloned.1.call-start
  27.3 100.8 %all-gather.2.cloned.1.call-done = bf16[1024,3072]{1,0:T(8,128)(2,1)} async-done(((bf16[1024,384]{1,0:T(8,128)(2,1)}), bf16[1024,3072]{1,0:T(8,128)(2,1)}) %all-gather.2.cloned.1.call-update) | async-done | bytes 6291472 | tf_op jit(solution)/shard_map/all_gather | solution.py:32
  128.1 11.9 %fusion.2 = f32[1024,1024]{1,0:T(8,128)} fusion(bf16[1024,3072]{1,0:T(8,128)(2,1)} %all-gather.2.cloned.1.call-done, bf16[1,3072,1024]{2,1,0:T(8,128)(2,1)} %param.10), kind=kOutput, calls=%fused_computation.3 | convolution fusion | flops 6442450944 | bytes 16777216 | tf_op jit(solution)/shard_map/dot_general | solution.py:34
  140.0 21.5 %fusion.6 = bf16[1024,3072]{1,0:T(8,128)(2,1)} fusion(bf16[1,1024,3072]{2,1,0:T(8,128)(2,1)} %param.11, f32[1024,1024]{1,0:T(8,128)} %fusion.2, bf16[1024,3072]{1,0:T(8,128)(2,1)} %all-gather.2.cloned.1.call-done, bf16[1,3072,1024]{2,1,0:T(8,128)(2,1)} %param.9), kind=kOutput, calls=%fused_computation.7 | convolution fusion | flops 12894339072 | bytes 29360128 | tf_op jit(solution)/shard_map/dot_general | solution.py:36
  161.5 8.7 %copy.16 = bf16[1024,3072]{0,1:T(8,128)(2,1)} copy(bf16[1024,3072]{1,0:T(8,128)(2,1)} %fusion.6) | data formatting | bytes 12582912
  170.2 0.0 reduce-scatter.4.cloned.1.call-update
  170.2 0.7 copy-done
  170.9 0.1 copy.14
  171.0 0.1 mul.50
  171.2 115.3 %reduce-scatter.4.cloned.1.call-done = bf16[384,1024]{1,0:T(8,128)(2,1)} async-done(((bf16[3072,1024]{1,0:T(8,128)(2,1)}), bf16[384,1024]{1,0:T(8,128)(2,1)}) %reduce-scatter.4.cloned.1.call-update) | async-done | bytes 786448
  286.5 2.3 copy.17
  288.8 3.7 %all-to-all-start.1 = ((bf16[4,256,384]{2,1,0:T(8,128)(2,1)}), bf16[4,256,384]{2,1,0:T(8,128)(2,1)S(1)}, u32[]{:S(2)}, u32[]{:S(2)}) async-start(bf16[4,256,384]{2,1,0:T(8,128)(2,1)} %bitcast.6), calls=%async_computation.1 | async-start | bytes 1572864 | tf_op jit(solution)/shard_map/all_to_all | solution.py:41
  292.5 0.0 copy-done.1
  292.5 0.1 copy.15
  292.7 11.2 %all-to-all-done.1 = bf16[4,256,384]{2,1,0:T(8,128)(2,1)S(1)} async-done(((bf16[4,256,384]{2,1,0:T(8,128)(2,1)}), bf16[4,256,384]{2,1,0:T(8,128)(2,1)S(1)}, u32[]{:S(2)}, u32[]{:S(2)}) %all-to-all-start.1) | async-done | bytes 786464 | tf_op jit(solution)/shard_map/all_to_all | solution.py:41
  303.9 0.2 bitcast_convert_fusion
  304.1 1.6 gather_fusion
  305.7 0.5 gather.6
  306.2 1.7 multiply_reduce_fusion
  (10 shorter events, 0.1 us)
Async XLA Ops:
  6.5 121.5 %all-gather.2.cloned.1.call-start = ((), (), s32[]{:S(2)}) async-start(), calls=%async_computation.3 | async-start | bytes 7077888 | tf_op jit(solution)/shard_map/all_gather | solution.py:32
  27.2 259.3 %reduce-scatter.4.cloned.1.call-start = ((), (), s32[]{:S(2)}) async-start(), calls=%async_computation.4 | async-start | bytes 7077888
  170.2 0.7 copy-start
  170.2 122.3 %copy-start.1 = (f32[256,2]{0,1:T(2,128)S(1)}, f32[256,2]{0,1:T(2,128)}, u32[]{:S(2)}) copy-start(f32[256,2]{0,1:T(2,128)} %param.8) | copy-start | bytes 6148
  288.8 15.1 %all-to-all-start.1 = ((bf16[4,256,384]{2,1,0:T(8,128)(2,1)}), bf16[4,256,384]{2,1,0:T(8,128)(2,1)S(1)}, u32[]{:S(2)}, u32[]{:S(2)}) async-start(bf16[4,256,384]{2,1,0:T(8,128)(2,1)} %bitcast.6), calls=%async_computation.1 | async-start | bytes 1572864 | tf_op jit(solution)/shard_map/all_to_all | solution.py:41
Sparse Core Ops, SparseCore 0:
  27.3 100.6 all-gather.1
  170.3 116.0 reduce-scatter.3
where the time goes:
time: 315 us
  waiting for transfers between devices  227 us (72%)
  matrix products  34.2 us (11%)
  local copies, waits for them, and re-layouts  16.7 us (5%)
  blocking collectives  15.8 us (5%)
  between operations  13.5 us (4%)
  starting transfers between devices  3.72 us (1%)
  other arithmetic  3.43 us (1%)
    unnamed x3, waiting for transfers between devices  115 us
    all_gather x1, waiting for transfers between devices, body(): piece = lax.all_gather(arrived, 'split', axis=1, tiled=True)  101 us
    dot_general x1, matrix products, body(): terms = jnp.dot(hidden, w_down, preferred_element_type=jnp.float32)  21.5 us
    all_to_all x1, blocking collectives, body(): lax.all_to_all(sending, 'expert', split_axis=0, concat_axis=0, tiled=True)  15.8 us
    unnamed x7, local copies, waits for them, and re-layouts  12.4 us
    dot_general x1, matrix products, body(): up_part = jnp.dot(piece, w_up, preferred_element_type=jnp.float32)  11.9 us
    all_to_all x1, waiting for transfers between devices, body(): lax.all_to_all(result.reshape(experts, capacity, narrow).astype(jnp.bfloa...  11.2 us
  transfers between devices with their start and end apart: 3, of which 3 were waited for; matrix products, arithmetic and copies ran while one was open for 0% of the time, Pallas kernels for 0%

commit v1 on v0

--- a/solution.py
+++ b/solution.py
@@ -1,25 +1,30 @@
 import jax
 import jax.numpy as jnp
 from jax import lax
+from jax.experimental import pallas as pl
+from jax.experimental.pallas import tpu as pltpu
 from jax.sharding import PartitionSpec as P
 
-
-def body(tokens, expert_ids, pair_logits, gate_weight, up_weight, down_weight):
+BOTH = ("expert", "split")
+HIDDEN_TILE = 512
+SCALE = 4
+
+
+def pair_mix(pair_logits):
+    first = jax.nn.sigmoid(pair_logits[:, 0] - pair_logits[:, 1])
+    return jnp.stack([first, 1.0 - first], axis=1)
+
+
+def dispatched(tokens, expert_ids, pair_logits, w_gate, w_up, w_down, capacity):
     experts = lax.axis_size("expert")
-    tok_rows = tokens.shape[0]
-    capacity = 4 * tok_rows // experts
+    tok_rows, narrow = tokens.shape
     flat = expert_ids.reshape(-1)
     labels = jnp.arange(experts, dtype=jnp.int32)
     onehot = (flat[:, None] == labels[None, :]).astype(jnp.int32)
     before = jnp.cumsum(onehot, axis=0) - onehot
     slot = jnp.sum(before * onehot, axis=1)
     dest = flat * capacity + slot
-    first = jax.nn.sigmoid(pair_logits[:, 0] - pair_logits[:, 1])
-    mix = jnp.stack([first, 1.0 - first], axis=1).reshape(-1)
-    w_gate = gate_weight[0]
-    w_up = up_weight[0]
-    w_down = down_weight[0]
-    narrow = tokens.shape[1]
+    mix = pair_mix(pair_logits).reshape(-1)
     select = (jnp.arange(experts * capacity, dtype=jnp.int32)[:, None] == dest[None, :]).astype(
         jnp.bfloat16
     )
@@ -51,6 +56,356 @@
     return mixed.astype(jnp.bfloat16)
 
 
+def send(value, x=0, c=0, z=0, y=0):
+    experts, splits = lax.axis_size("expert"), lax.axis_size("split")
+    flip_expert, flip_split = x * 2 + c, z * 2 + y
+    pairs = [
+        (e * splits + s, (e ^ flip_expert) * splits + (s ^ flip_split))
+        for e in range(experts)
+        for s in range(splits)
+    ]
+    return lax.ppermute(value, BOTH, pairs)
+
+
+def after(value, *earlier):
+    return lax.optimization_barrier((value, earlier))[0]
+
+
+def relayed(over_x, over_y):
+    half = over_y[0].shape[1] // 2
+    first = jnp.concatenate([v[:, :half] for v in over_y])
+    last = jnp.concatenate([v[:, half : 2 * half] for v in over_x])
+    return send(first, x=1), send(last, y=1)
+
+
+def swapped(*blocks):
+    return [(v, send(v, c=1)) for v in blocks]
+
+
+def summed(terms, y, x, rows=slice(None)):
+    return total(*[term[y, :, rows] for term in terms[x]])
+
+
+def diagonal(terms):
+    half = terms[0][0].shape[2] // 2
+    first = summed(terms, 1, 1, slice(0, half)).astype(jnp.bfloat16)
+    last = summed(terms, 1, 1, slice(half, 2 * half)).astype(jnp.bfloat16)
+    return send(first, x=1), send(last, y=1)
+
+
+def plane_sums(terms, first, last):
+    half = terms[0][0].shape[2] // 2
+    first, last = first.astype(jnp.float32), last.astype(jnp.float32)
+    to_x = summed(terms, 0, 1) + jnp.pad(last, ((0, 0), (half, 0), (0, 0)))
+    to_y = summed(terms, 1, 0) + jnp.pad(first, ((0, 0), (0, half), (0, 0)))
+    return to_x.astype(jnp.bfloat16), to_y.astype(jnp.bfloat16)
+
+
+def total(*terms):
+    result = terms[0].astype(jnp.float32)
+    for term in terms[1:]:
+        result = result + term.astype(jnp.float32)
+    return result
+
+
+def pieces(x, pair):
+    blocks, over_x, over_y, first, last = pair
+    size = blocks[1][0][0].shape[1]
+    arrays, found = [], []
+    for z in range(2):
+        for c in range(2):
+            parts = [(blocks[z], 0, 0), (over_y[z], 0, 1)]
+            if x:
+                parts = [(over_x[z], 0, 0), (first[z], 0, 1), (last[z], size // 2, 1)]
+            for (array, index), row, y in parts:
+                array = array[c]
+                if not any(array is v for v in arrays):
+                    arrays.append(array)
+                place = [i for i, v in enumerate(arrays) if v is array][0]
+                found.append((place, index, z, c * size + row, y, min(size, array.shape[1])))
+    return arrays, found
+
+
+def fill(place, arrays, found, z_places, rows, sems):
+    my_y = place[place.shape[0] - 1]
+    copies = []
+    for i, (which, index, z, row, y, count) in enumerate(found):
+        source = arrays[which].at[index, pl.ds(0, count)]
+        column = ((place[z_places[z]] & 1) * 2 + (my_y ^ y)) * source.shape[1]
+        columns = pl.ds(pl.multiple_of(column, 128), source.shape[1])
+        target = rows.at[pl.ds(row, count), columns]
+        copies.append(pltpu.make_async_copy(source, target, sems.at[i]))
+    return copies
+
+
+def all_of(copies):
+    for copy in copies:
+        copy.start()
+    for copy in copies:
+        copy.wait()
+
+
+def weights_kernel(place, *refs, z):
+    w_gate, w_up, gate, up, sems = refs[-5:]
+    depth = gate.shape[0]
+    quarter = depth // 4
+    base = pl.multiple_of((place[z] // 2) * depth, depth)
+    all_of(
+        [
+            pltpu.make_async_copy(
+                weight.at[pl.ds(base + q * quarter, quarter)],
+                result.at[pl.ds(q * quarter, quarter)],
+                sems.at[i, q],
+            )
+            for q in range(4)
+            for i, (weight, result) in enumerate(((w_gate, gate), (w_up, up)))
+        ]
+    )
+
+
+def first_kernel(place, *refs, found, z_places):
+    arrays, (w_gate, w_up, gate, up, rows, sems) = refs[:-6], refs[-6:]
+    all_of(fill(place, arrays, found, z_places, rows, sems))
+    for weight, result in ((w_gate, gate), (w_up, up)):
+        for t in range(result.shape[0]):
+            tile = slice(t * HIDDEN_TILE, (t + 1) * HIDDEN_TILE)
+            result[t] = jnp.dot(rows[...], weight[:, tile], preferred_element_type=jnp.float32)
+
+
+def share_column(place, blocks, tails, sems, size):
+    experts = place[place.shape[0] - 2]
+    expert = place[place.shape[0] - 3]
+    copies = []
+    for c, block in enumerate(blocks):
+        tail = pl.ds(size, tails.shape[1])
+        copies.append(pltpu.make_async_copy(block.at[0, tail], tails.at[c], sems.at[c]))
+    all_of(copies)
+    column = []
+    for c in range(2):
+        row = lax.broadcasted_iota(jnp.int32, tails.shape[1:], 0)
+        mine = (row == expert) | (row == expert + experts)
+        shares = jnp.where(mine, tails[c].astype(jnp.float32), 0.0)
+        shares = jnp.sum(shares, axis=0, keepdims=True)[:, :size]
+        column.append(jnp.broadcast_to(shares, (128, size)).T)
+    return jnp.concatenate(column)[:, :1]
+
+
+def second_kernel(place, *refs, found, z_places, pairs):
+    arrays, refs = refs[:-18], refs[-18:]
+    w_gate, w_up, gate, up, w_down = refs[:5]
+    results = refs[7:9], refs[9:11]
+    rows, downs, hidden, tails, sems, d_sems, t_sems = refs[11:]
+    my_y = place[place.shape[0] - 1]
+    size, span = results[0][0].shape[2], downs.shape[2]
+    copies = fill(place, arrays, found, z_places, rows, sems)
+    downs_in = []
+    for k, pair in enumerate(pairs):
+        columns = pl.ds(pl.multiple_of((place[pair[0]] // 2) * span, span), span)
+        downs_in.append(pltpu.make_async_copy(w_down.at[:, columns], downs.at[k], d_sems.at[k]))
+    for copy in copies + downs_in:
+        copy.start()
+    share = 0.5 * share_column(place, refs[5:7], tails, t_sems, size)
+    for copy in copies:
+        copy.wait()
+    for t in range(gate.shape[0]):
+        tile = slice(t * HIDDEN_TILE, (t + 1) * HIDDEN_TILE)
+        g = gate[t] + jnp.dot(rows[...], w_gate[:, tile], preferred_element_type=jnp.float32)
+        u = up[t] + jnp.dot(rows[...], w_up[:, tile], preferred_element_type=jnp.float32)
+        value = (g + g * jnp.tanh(0.5 * g)) * u * share
+        hidden[:, tile] = value.astype(jnp.bfloat16)
+    narrow = results[0][0].shape[3]
+    for k, pair in enumerate(pairs):
+        downs_in[k].wait()
+        terms = jnp.dot(hidden[...], downs[k], preferred_element_type=jnp.float32)
+        terms = terms.astype(jnp.bfloat16)
+        for r, result in enumerate(results[k]):
+            for z in range(2):
+                n = (place[pair[0]] & 1) ^ z
+                for y in range(2):
+                    start = (z * 2 + y) * narrow
+                    piece = terms[r * size : (r + 1) * size, start : start + narrow]
+                    result[my_y ^ y, n] = piece
+
+
+def cost(flops, bytes_accessed, transcendentals):
+    return pl.CostEstimate(
+        flops=flops // SCALE,
+        bytes_accessed=bytes_accessed // SCALE,
+        transcendentals=transcendentals // SCALE,
+    )
+
+
+def in_hbm(value):
+    return pltpu.with_memory_space_constraint(value, pltpu.HBM)
+
+
+def in_vmem(value):
+    return pltpu.with_memory_space_constraint(value, pltpu.VMEM)
+
+
+ANY = pl.BlockSpec(memory_space=pl.ANY)
+SCALARS = pl.BlockSpec(memory_space=pltpu.SMEM)
+VMEM = pl.BlockSpec(memory_space=pltpu.VMEM)
+SEMS = pltpu.SemaphoreType.DMA
+
+
+def params(mebibytes):
+    return pltpu.CompilerParams(vmem_limit_bytes=mebibytes * 1024 * 1024)
+
+
+def pair_weights(place, z, w_gate, w_up, narrow, *earlier):
+    width, depth = w_gate.shape[1], 4 * narrow
+    return pl.pallas_call(
+        lambda *refs: weights_kernel(*refs, z=z),
+        in_specs=[SCALARS] + [ANY] * (len(earlier) + 2),
+        out_specs=[VMEM] * 2,
+        scratch_shapes=[SEMS((2, 4))],
+        out_shape=[pltpu.VMEM((depth, width), jnp.bfloat16)] * 2,
+        compiler_params=params(2),
+        cost_estimate=cost(flops=0, bytes_accessed=8 * depth * width, transcendentals=0),
+        name="pair_weights",
+    )(place, *earlier, w_gate, w_up)
+
+
+def first_part(place, x, pair, z_places, weights):
+    arrays, found = pieces(x, pair)
+    size, narrow = pair[0][1][0][0].shape[1:]
+    depth, width = weights[0].shape
+    rows = 2 * size
+    sums = (width // HIDDEN_TILE, rows, HIDDEN_TILE)
+    return pl.pallas_call(
+        lambda *refs: first_kernel(*refs, found=found, z_places=z_places),
+        in_specs=[SCALARS] + [ANY] * len(arrays) + [VMEM, VMEM],
+        out_specs=[VMEM, VMEM],
+        scratch_shapes=[pltpu.VMEM((rows, depth), jnp.bfloat16), SEMS((len(found),))],
+        out_shape=[pltpu.VMEM(sums, jnp.float32)] * 2,
+        compiler_params=params(4),
+        cost_estimate=cost(
+            flops=4 * rows * depth * width,
+            bytes_accessed=4 * depth * width + 2 * rows * depth + 8 * rows * width,
+            transcendentals=0,
+        ),
+        name="first_part",
+    )(place, *arrays, *[in_vmem(v) for v in weights])
+
+
+def second_part(place, x, pair, z_places, weights, sums, shares, w_down, pairs):
+    arrays, found = pieces(x, pair)
+    size, narrow = pair[0][1][0][0].shape[1:]
+    depth, width = weights[0].shape
+    rows, tail = 2 * size, shares[0].shape[1] - size
+    return pl.pallas_call(
+        lambda *refs: second_kernel(*refs, found=found, z_places=z_places, pairs=pairs),
+        in_specs=[SCALARS] + [ANY] * len(arrays) + [VMEM] * 4 + [ANY] * 3,
+        out_specs=[VMEM] * 4,
+        scratch_shapes=[
+            pltpu.VMEM((rows, depth), jnp.bfloat16),
+            pltpu.VMEM((2, width, depth), jnp.bfloat16),
+            pltpu.VMEM((rows, width), jnp.bfloat16),
+            pltpu.VMEM((2, tail, narrow), jnp.bfloat16),
+            SEMS((len(found),)),
+            SEMS((2,)),
+            SEMS((2,)),
+        ],
+        out_shape=[pltpu.VMEM((2, 2, size, narrow), jnp.bfloat16)] * 4,
+        compiler_params=params(13),
+        cost_estimate=cost(
+            flops=4 * rows * depth * width + 4 * rows * width * depth,
+            bytes_accessed=8 * depth * width + 6 * rows * depth + 8 * rows * width,
+            transcendentals=rows * width,
+        ),
+        name="second_part",
+    )(place, *arrays, *[in_vmem(v) for v in (*weights, *sums)], w_down, *shares)
+
+
+def shares_of(expert_ids, pair_logits):
+    mix = pair_mix(pair_logits)
+    labels = jnp.arange(lax.axis_size("expert"), dtype=jnp.int32)
+    named = expert_ids[None, :, :] == labels[:, None, None]
+    return jnp.sum(jnp.where(named, mix[None], 0.0), axis=2)
+
+
+def share_rows(shares, narrow):
+    high = lax.reduce_precision(shares, 8, 7)
+    rows = jnp.concatenate([high, shares - high]).astype(jnp.bfloat16)
+    return jnp.pad(rows, ((0, -rows.shape[0] % 16), (0, narrow - rows.shape[1])))
+
+
+def every_row(tokens, expert_ids, pair_logits, w_gate, w_up, w_down):
+    expert, split = lax.axis_index("expert"), lax.axis_index("split")
+    size, narrow = tokens.shape
+    place = [(split // 2) ^ z for z in range(4)]
+    place = jnp.stack(place + [expert, lax.axis_size("expert"), split % 2]).astype(jnp.int32)
+    w_gate, w_up, w_down = in_hbm(w_gate), in_hbm(w_up), in_hbm(w_down)
+
+    w_gate, w_up, w_down = in_hbm(w_gate), in_hbm(w_up), in_hbm(w_down)
+    z0 = tokens[None]
+    z1 = send(z0, z=1)
+    own = shares_of(expert_ids, pair_logits)
+    block = jnp.concatenate([tokens, share_rows(own, narrow)])[None]
+    sent = after(z0, own)
+    x0, y0, z2 = send(block, x=1), send(sent, y=1), send(sent, z=2)
+    x1, y1 = send(z1, x=1), send(z1, y=1)
+    sz0, sz1, sx0, sx1, sy0, sy1 = swapped(block, z1, x0, x1, y0, y1)
+    near_weights = pair_weights(place, 0, w_gate, w_up, narrow, x0)
+    far_weights = pair_weights(place, 2, w_gate, w_up, narrow, x0)
+    (x1_, y1_), z2, near_weights, far_weights = after(
+        ((x1, y1), z2, near_weights, far_weights)
+    )
+    first, last = relayed([x0, x1_], [y0, y1_])
+    z3 = send(z2, z=1)
+    x2, y2 = send(z2, x=1), send(z2, y=1)
+    near = [[(sz0, 0), (sz1, 0)], [(sx0, 0), (sx1, 0)], [(sy0, 0), (sy1, 0)], None, None]
+    sums_0 = first_part(place, 0, near, (0, 1), near_weights)
+
+    z3, sums_0 = after((z3, sums_0))
+    (first, last, x2, y2), sums_0 = after(((first, last, x2, y2), sums_0))
+    x3, y3 = send(z3, x=1), send(z3, y=1)
+    both_of = lambda v: [(v, 0), (v, 1)]
+    near[3:] = [both_of(v) for v in swapped(first, last)]
+    sz2, sz3, sx2, sy2 = swapped(z2, z3, x2, y2)
+    sums_1 = first_part(place, 1, near, (0, 1), near_weights)
+    (x3, y3), sums_1 = after(((x3, y3), sums_1))
+    first, last = relayed([x2, x3], [y2, y3])
+    sx3, sy3 = swapped(x3, y3)
+    far = [[(sz2, 0), (sz3, 0)], [(sx2, 0), (sx3, 0)], [(sy2, 0), (sy3, 0)], None, None]
+    pairs = (3, 2), (1, 0)
+    parts_0 = second_part(place, 0, far, (2, 3), far_weights, sums_0, sz0, w_down, pairs)
+    (first, last), parts_0 = after(((first, last), parts_0))
+    far[3:] = [both_of(v) for v in swapped(first, last)]
+    far_0, near_0 = [(parts_0[i], send(parts_0[i + 1], c=1)) for i in (0, 2)]
+    to_z = total(*[v[:, :1] for v in near_0]).astype(jnp.bfloat16)
+    passed_0 = send(to_z, z=1)
+    sums_1 = after(sums_1, to_z)
+    parts_1 = second_part(place, 1, far, (2, 3), far_weights, sums_1, sx0, w_down, pairs)
+    passed_0, parts_1 = after((passed_0, parts_1))
+    far_1, near_1 = [(parts_1[i], send(parts_1[i + 1], c=1)) for i in (0, 2)]
+
+    far = far_0, far_1
+    to_x, to_y = plane_sums(far, *diagonal(far))
+    passed_1 = send(total(*[v[:, :1] for v in near_1]).astype(jnp.bfloat16), z=1)
+    from_3 = send(to_x[:1], x=1), send(to_y[:1], y=1)
+    to_x, to_y = after((to_x, to_y), *from_3)
+    from_2 = send(to_x[1:], x=1), send(to_y[1:], y=1)
+    here = summed(far, 0, 0)
+    to_2 = send(total(here[:1], *from_3).astype(jnp.bfloat16), z=1)
+    to_0 = send(total(here[1:], *from_2, to_2).astype(jnp.bfloat16), z=2)
+    last_block = lambda terms, passed: [v[:, 1:] for v in terms] + [passed]
+    near = last_block(near_0, passed_0), last_block(near_1, passed_1)
+    to_x, to_y = plane_sums(near, *diagonal(near))
+    from_0 = send(to_x, x=1), send(to_y, y=1)
+    return total(summed(near, 0, 0), *from_0, to_0)[0].astype(jnp.bfloat16)
+
+
+def body(tokens, expert_ids, pair_logits, gate_weight, up_weight, down_weight):
+    capacity = 4 * tokens.shape[0] // lax.axis_size("expert")
+    arrays = (tokens, expert_ids, pair_logits, gate_weight[0], up_weight[0], down_weight[0])
+    splits = lax.axis_size("split")
+    if capacity == tokens.shape[0] and splits == 8 and tokens.shape[0] <= tokens.shape[1]:
+        return every_row(*arrays)
+    return dispatched(*arrays, capacity)
+
+
 def solution(mesh):
     in_specs = (
         P("expert", "split"),

time: 315 us -> 108 us (0.34)
  waiting for transfers between devices: 227 us -> 23.6 us
  starting transfers between devices: 3.72 us -> 46 us
  matrix products: 34.2 us -> 0 us
  Pallas kernels: 0 us -> 32.8 us
  local copies, waits for them, and re-layouts: 16.7 us -> 0.26 us
  blocking collectives: 15.8 us -> 0 us
  between operations: 13.5 us -> 0.38 us
    unnamed x3 -> x0, waiting for transfers between devices: 115 us -> none
    all_gather x1 -> x0, waiting for transfers between devices: 101 us -> none  [body(): piece = lax.all_gather(arrived, 'split', axis=1, tiled=True)]
    ppermute x0 -> x49, starting transfers between devices: none -> 46 us  [send(): return lax.ppermute(value, BOTH, pairs)]
    dot_general x3 -> x0, matrix products: 34.2 us -> none  [the longest x1 21.5 us: body(): terms = jnp.dot(hidden, w_down, preferred_element_type=jnp.float32)]
    pallas_call x0 -> x6, Pallas kernels: none -> 32.8 us  [the longest x2 17.4 us: second_part(): pl.pallas_call(lambda *refs: second_kernel(*refs, found=found, z_places=z...]
    ppermute x0 -> x49, waiting for transfers between devices: none -> 23.6 us  [send(): return lax.ppermute(value, BOTH, pairs)]
    all_to_all x1 -> x0, blocking collectives: 15.8 us -> none  [body(): lax.all_to_all(sending, 'expert', split_axis=0, concat_axis=0, tiled=True)]
    unnamed x7 -> x0, local copies, waits for them, and re-layouts: 12.4 us -> none
  transfers between devices with their start and end apart: 3 -> 49, of which waited for: 3 -> 15; matrix products, arithmetic and copies ran while one was open for 0% -> 4% of each run, Pallas kernels for 0% -> 30%
where the time goes in v1:
time: 108 us; the launch traced here: 107 us
  starting transfers between devices  46 us (43%)
  Pallas kernels  32.8 us (30%)
  waiting for transfers between devices  23.6 us (22%)
  other arithmetic  4.47 us (4%)
    ppermute x49, starting transfers between devices, send(): return lax.ppermute(value, BOTH, pairs)  46 us
    ppermute x49, waiting for transfers between devices, send(): return lax.ppermute(value, BOTH, pairs)  23.6 us
    pallas_call x2, Pallas kernels, second_part(): pl.pallas_call(lambda *refs: second_kernel(*refs, found=found, z_places=z...  17.4 us
    pallas_call x2, Pallas kernels, first_part(): pl.pallas_call(lambda *refs: first_kernel(*refs, found=found, z_places=z_...  8.58 us
    pallas_call x2, Pallas kernels, pair_weights(): pl.pallas_call(lambda *refs: weights_kernel(*refs, z=z), in_specs=[SCALAR...  6.82 us
  transfers between devices with their start and end apart: 49, of which 15 were waited for; matrix products, arithmetic and copies ran while one was open for 4% of the time, Pallas kernels for 30%

profile of v1, /device:TPU:0, one launch (start us, length us, event | category | flops | bytes accessed | tf_op | source)
XLA Modules:
  0.0 107.5 jit_solution(6873599195081450222)
XLA Ops:
  0.0 3.0 %collective-permute-start.1 = (bf16[1,256,384]{2,1,0:T(8,128)(2,1)}, bf16[1,256,384]{2,1,0:T(8,128)(2,1)S(1)}, u32[]{:S(2)}, u32[]{:S(2)}) collective-permute-start(bf16[1,256,384]{2,1,0:T(8,128)(2,1)} %bitcast.72), channel_id=1, source_target_pairs={{0,2},{1,3},{2,0},{3,1},{4,6},{5,7},{6,4},{7,5},{8,10},{9,11},{10,... | collective-permute-start | bytes 589832 | tf_op jit(solution)/shard_map/ppermute | solution.py:67
  5.5 1.6 %collective-permute-start.5 = (bf16[1,272,384]{2,1,0:T(8,128)(2,1)S(1)}, bf16[1,272,384]{2,1,0:T(8,128)(2,1)S(1)}, u32[]{:S(2)}, u32[]{:S(2)}) collective-permute-start(bf16[1,272,384]{2,1,0:T(8,128)(2,1)S(1)} %maximum_bitcast_fusion.refs_1_.refs_14_), channel_id=1, source_target_pairs={{0,16},{1,17},{2,18},{3,19},{4,20},{5,21},{6,22},{7,23},{8,24},{9,... | collective-permute-start | bytes 626696 | tf_op jit(solution)/shard_map/ppermute | solution.py:67
  7.0 1.5 %collective-permute-start = (bf16[1,256,384]{2,1,0:T(8,128)(2,1)}, bf16[1,256,384]{2,1,0:T(8,128)(2,1)S(1)}, u32[]{:S(2)}, u32[]{:S(2)}) collective-permute-start(bf16[1,256,384]{2,1,0:T(8,128)(2,1)} %bitcast.73), channel_id=1, source_target_pairs={{0,1},{1,0},{2,3},{3,2},{4,5},{5,4},{6,7},{7,6},{8,9},{9,8},{10,11... | collective-permute-start | bytes 589832 | tf_op jit(solution)/shard_map/ppermute | solution.py:67
  8.6 2.6 %collective-permute-start.4 = (bf16[1,256,384]{2,1,0:T(8,128)(2,1)}, bf16[1,256,384]{2,1,0:T(8,128)(2,1)S(1)}, u32[]{:S(2)}, u32[]{:S(2)}) collective-permute-start(bf16[1,256,384]{2,1,0:T(8,128)(2,1)} %bitcast.74), channel_id=1, source_target_pairs={{0,4},{1,5},{2,6},{3,7},{4,0},{5,1},{6,2},{7,3},{8,12},{9,13},{10,... | collective-permute-start | bytes 589832 | tf_op jit(solution)/shard_map/ppermute | solution.py:67
  12.3 1.8 %collective-permute-done.refs_2_ = bf16[1,256,384]{2,1,0:T(8,128)(2,1)S(1)} collective-permute-done((bf16[1,256,384]{2,1,0:T(8,128)(2,1)}, bf16[1,256,384]{2,1,0:T(8,128)(2,1)S(1)}, u32[]{:S(2)}, u32[]{:S(2)}) %collective-permute-start) | collective-permute-done | bytes 196640 | tf_op jit(solution)/shard_map/ppermute | solution.py:67
  14.7 3.4 %pair_weights.2 = (bf16[1536,1024]{1,0:T(8,128)(2,1)S(1)}, bf16[1536,1024]{1,0:T(8,128)(2,1)S(1)}) custom-call(s32[7]{0:T(128)S(1)} %stack.33.refs_0_, bf16[1,272,384]{2,1,0:T(8,128)(2,1)S(1)} %collective-permute-done.5.refs_1_.refs_14_, bf16[3072,1024]{1,0:T(8,128)(2,1)} %bitcast.66, bf16[3072,1024]{1,0:T(8,128)(2,1)} %bitcast.68), custom_call_target="tpu_custom_call" | custom-call | bytes 3145728 | tf_op jit(solution)/shard_map/pair_weights/pallas_call | solution.py:258
  18.1 3.4 %pair_weights.3 = (bf16[1536,1024]{1,0:T(8,128)(2,1)S(1)}, bf16[1536,1024]{1,0:T(8,128)(2,1)S(1)}) custom-call(s32[7]{0:T(128)S(1)} %stack.33.refs_0_, bf16[1,272,384]{2,1,0:T(8,128)(2,1)S(1)} %collective-permute-done.5.refs_1_.refs_14_, bf16[3072,1024]{1,0:T(8,128)(2,1)} %bitcast.67, bf16[3072,1024]{1,0:T(8,128)(2,1)} %bitcast.69), custom_call_target="tpu_custom_call" | custom-call | bytes 3145728 | tf_op jit(solution)/shard_map/pair_weights/pallas_call | solution.py:258
  22.4 2.4 %collective-permute-start.7 = (bf16[2,128,384]{2,1,0:T(8,128)(2,1)S(1)}, bf16[2,128,384]{2,1,0:T(8,128)(2,1)S(1)}, u32[]{:S(2)}, u32[]{:S(2)}) collective-permute-start(bf16[2,128,384]{2,1,0:T(8,128)(2,1)S(1)} %pad_maximum_fusion.1), channel_id=1, source_target_pairs={{0,1},{1,0},{2,3},{3,2},{4,5},{5,4},{6,7},{7,6},{8,9},{9,8},{10,11... | collective-permute-start | bytes 589832 | tf_op jit(solution)/shard_map/ppermute | solution.py:67
  24.9 1.9 %collective-permute-start.6 = (bf16[2,128,384]{2,1,0:T(8,128)(2,1)S(1)}, bf16[2,128,384]{2,1,0:T(8,128)(2,1)S(1)}, u32[]{:S(2)}, u32[]{:S(2)}) collective-permute-start(bf16[2,128,384]{2,1,0:T(8,128)(2,1)S(1)} %pad_maximum_fusion), channel_id=1, source_target_pairs={{0,16},{1,17},{2,18},{3,19},{4,20},{5,21},{6,22},{7,23},{8,24},{9,... | collective-permute-start | bytes 589832 | tf_op jit(solution)/shard_map/ppermute | solution.py:67
  26.9 2.1 %collective-permute-done.10.refs_5_ = bf16[1,256,384]{2,1,0:T(8,128)(2,1)S(1)} collective-permute-done((bf16[1,256,384]{2,1,0:T(8,128)(2,1)S(1)}, bf16[1,256,384]{2,1,0:T(8,128)(2,1)S(1)}, u32[]{:S(2)}, u32[]{:S(2)}) %collective-permute-start.10) | collective-permute-done | bytes 196640 | tf_op jit(solution)/shard_map/ppermute | solution.py:67
  29.0 4.3 %first_part.2 = (f32[2,512,512]{2,1,0:T(8,128)S(1)}, f32[2,512,512]{2,1,0:T(8,128)S(1)}) custom-call(s32[7]{0:T(128)S(1)} %stack.33.refs_0_, bf16[1,272,384]{2,1,0:T(8,128)(2,1)S(1)} %maximum_bitcast_fusion.refs_1_.refs_14_, bf16[1,256,384]{2,1,0:T(8,128)(2,1)S(1)} %collective-permute-done.refs_2_, ...), custom_call_target="tpu_custom_call" | custom-call | flops 805306368 | bytes 3014656 | tf_op jit(solution)/shard_map/first_part/pallas_call | solution.py:276
  34.8 1.7 %collective-permute-start.15 = (bf16[1,256,384]{2,1,0:T(8,128)(2,1)S(1)}, bf16[1,256,384]{2,1,0:T(8,128)(2,1)S(1)}, u32[]{:S(2)}, u32[]{:S(2)}) collective-permute-start(bf16[1,256,384]{2,1,0:T(8,128)(2,1)S(1)} %collective-permute-done.10.refs_5_), channel_id=1, source_target_pairs={{0,16},{1,17},{2,18},{3,19},{4,20},{5,21},{6,22},{7,23},{8,24},{9,... | collective-permute-start | bytes 589832 | tf_op jit(solution)/shard_map/ppermute | solution.py:67
  36.4 1.7 %collective-permute-start.16 = (bf16[1,256,384]{2,1,0:T(8,128)(2,1)S(1)}, bf16[1,256,384]{2,1,0:T(8,128)(2,1)S(1)}, u32[]{:S(2)}, u32[]{:S(2)}) collective-permute-start(bf16[1,256,384]{2,1,0:T(8,128)(2,1)S(1)} %collective-permute-done.10.refs_5_), channel_id=1, source_target_pairs={{0,1},{1,0},{2,3},{3,2},{4,5},{5,4},{6,7},{7,6},{8,9},{9,8},{10,11... | collective-permute-start | bytes 589832 | tf_op jit(solution)/shard_map/ppermute | solution.py:67
  38.9 4.3 %first_part.3 = (f32[2,512,512]{2,1,0:T(8,128)S(1)}, f32[2,512,512]{2,1,0:T(8,128)S(1)}) custom-call(s32[7]{0:T(128)S(1)} %stack.33.refs_0_, bf16[1,272,384]{2,1,0:T(8,128)(2,1)S(1)} %collective-permute-done.5.refs_1_.refs_14_, bf16[2,128,384]{2,1,0:T(8,128)(2,1)S(1)} %collective-permute-done.6.refs_2_, ...), custom_call_target="tpu_custom_call" | custom-call | flops 805306368 | bytes 3014656 | tf_op jit(solution)/shard_map/first_part/pallas_call | solution.py:276
  45.7 8.6 %second_part.2 = (bf16[2,2,256,384]{3,2,1,0:T(8,128)(2,1)S(1)}, bf16[2,2,256,384]{3,2,1,0:T(8,128)(2,1)S(1)}, bf16[2,2,256,384]{3,2,1,0:T(8,128)(2,1)S(1)}, bf16[2,2,256,384]{3,2,1,0:T(8,128)(2,1)S(1)}) custom-call(s32[7]{0:T(128)S(1)} %stack.33.refs_0_, bf16[1,256,384]{2,1,0:T(8,128)(2,1)S(1)} %collective-permute-done.4.refs_1_, ...), custom_call_target="tpu_custom_call" | custom-call | flops 1610612736 | bytes 5373952 | tf_op jit(solution)/shard_map/second_part/pallas_call | solution.py:297
  54.9 1.8 %collective-permute-done.27 = bf16[2,2,256,384]{3,2,1,0:T(8,128)(2,1)S(1)} collective-permute-done((bf16[2,2,256,384]{3,2,1,0:T(8,128)(2,1)S(1)}, bf16[2,2,256,384]{3,2,1,0:T(8,128)(2,1)S(1)}, u32[]{:S(2)}, u32[]{:S(2)}) %collective-permute-start.27) | collective-permute-done | bytes 786464 | tf_op jit(solution)/shard_map/ppermute | solution.py:67
  56.8 1.7 %collective-permute-start.28 = (bf16[2,1,256,384]{3,2,1,0:T(8,128)(2,1)S(1)}, bf16[2,1,256,384]{3,2,1,0:T(8,128)(2,1)S(1)}, u32[]{:S(2)}, u32[]{:S(2)}) collective-permute-start(bf16[2,1,256,384]{3,2,1,0:T(8,128)(2,1)S(1)} %add_convert_fusion.1), channel_id=1, source_target_pairs={{0,2},{1,3},{2,0},{3,1},{4,6},{5,7},{6,4},{7,5},{8,10},{9,11},{10,... | collective-permute-start | bytes 1179656 | tf_op jit(solution)/shard_map/ppermute | solution.py:67
  60.5 8.8 %second_part.3 = (bf16[2,2,256,384]{3,2,1,0:T(8,128)(2,1)S(1)}, bf16[2,2,256,384]{3,2,1,0:T(8,128)(2,1)S(1)}, bf16[2,2,256,384]{3,2,1,0:T(8,128)(2,1)S(1)}, bf16[2,2,256,384]{3,2,1,0:T(8,128)(2,1)S(1)}) custom-call(s32[7]{0:T(128)S(1)} %stack.33.refs_0_, bf16[1,256,384]{2,1,0:T(8,128)(2,1)S(1)} %collective-permute-done.8.refs_1_, ...), custom_call_target="tpu_custom_call" | custom-call | flops 1610612736 | bytes 5373952 | tf_op jit(solution)/shard_map/second_part/pallas_call | solution.py:297
  70.0 1.7 %collective-permute-done.40 = bf16[2,2,256,384]{3,2,1,0:T(8,128)(2,1)S(1)} collective-permute-done((bf16[2,2,256,384]{3,2,1,0:T(8,128)(2,1)S(1)}, bf16[2,2,256,384]{3,2,1,0:T(8,128)(2,1)S(1)}, u32[]{:S(2)}, u32[]{:S(2)}) %collective-permute-start.40) | collective-permute-done | bytes 786464 | tf_op jit(solution)/shard_map/ppermute | solution.py:67
  71.7 1.1 %collective-permute-start.41 = (bf16[2,128,384]{2,1,0:T(8,128)(2,1)S(1)}, bf16[2,128,384]{2,1,0:T(8,128)(2,1)S(1)}, u32[]{:S(2)}, u32[]{:S(2)}) collective-permute-start(bf16[2,128,384]{2,1,0:T(8,128)(2,1)S(1)} %get-tuple-element.113), channel_id=1, source_target_pairs={{0,1},{1,0},{2,3},{3,2},{4,5},{5,4},{6,7},{7,6},{8,9},{9,8},{10,11... | collective-permute-start | bytes 589832 | tf_op jit(solution)/shard_map/ppermute | solution.py:67
  73.4 1.6 %collective-permute-start.42 = (bf16[2,128,384]{2,1,0:T(8,128)(2,1)S(1)}, bf16[2,128,384]{2,1,0:T(8,128)(2,1)S(1)}, u32[]{:S(2)}, u32[]{:S(2)}) collective-permute-start(bf16[2,128,384]{2,1,0:T(8,128)(2,1)S(1)} %get-tuple-element.114), channel_id=1, source_target_pairs={{0,16},{1,17},{2,18},{3,19},{4,20},{5,21},{6,22},{7,23},{8,24},{9,... | collective-permute-start | bytes 589832 | tf_op jit(solution)/shard_map/ppermute | solution.py:67
  74.9 3.9 %collective-permute-done.41 = bf16[2,128,384]{2,1,0:T(8,128)(2,1)S(1)} collective-permute-done((bf16[2,128,384]{2,1,0:T(8,128)(2,1)S(1)}, bf16[2,128,384]{2,1,0:T(8,128)(2,1)S(1)}, u32[]{:S(2)}, u32[]{:S(2)}) %collective-permute-start.41) | collective-permute-done | bytes 196640 | tf_op jit(solution)/shard_map/ppermute | solution.py:67
  79.0 1.7 %collective-permute-start.43 = (bf16[1,256,384]{2,1,0:T(8,128)(2,1)S(1)}, bf16[1,256,384]{2,1,0:T(8,128)(2,1)S(1)}, u32[]{:S(2)}, u32[]{:S(2)}) collective-permute-start(bf16[1,256,384]{2,1,0:T(8,128)(2,1)S(1)} %slice.220), channel_id=1, source_target_pairs={{0,16},{1,17},{2,18},{3,19},{4,20},{5,21},{6,22},{7,23},{8,24},{9,... | collective-permute-start | bytes 589832 | tf_op jit(solution)/shard_map/ppermute | solution.py:67
  80.9 1.1 %collective-permute-start.44 = (bf16[1,256,384]{2,1,0:T(8,128)(2,1)S(1)}, bf16[1,256,384]{2,1,0:T(8,128)(2,1)S(1)}, u32[]{:S(2)}, u32[]{:S(2)}) collective-permute-start(bf16[1,256,384]{2,1,0:T(8,128)(2,1)S(1)} %slice.221), channel_id=1, source_target_pairs={{0,1},{1,0},{2,3},{3,2},{4,5},{5,4},{6,7},{7,6},{8,9},{9,8},{10,11... | collective-permute-start | bytes 589832 | tf_op jit(solution)/shard_map/ppermute | solution.py:67
  82.0 2.2 %collective-permute-done.34 = bf16[2,1,256,384]{3,2,1,0:T(8,128)(2,1)S(1)} collective-permute-done((bf16[2,1,256,384]{3,2,1,0:T(8,128)(2,1)S(1)}, bf16[2,1,256,384]{3,2,1,0:T(8,128)(2,1)S(1)}, u32[]{:S(2)}, u32[]{:S(2)}) %collective-permute-start.34) | collective-permute-done | bytes 393248 | tf_op jit(solution)/shard_map/ppermute | solution.py:67
  84.3 1.1 %collective-permute-start.35 = (bf16[1,128,384]{2,1,0:T(8,128)(2,1)S(1)}, bf16[1,128,384]{2,1,0:T(8,128)(2,1)S(1)}, u32[]{:S(2)}, u32[]{:S(2)}) collective-permute-start(bf16[1,128,384]{2,1,0:T(8,128)(2,1)S(1)} %get-tuple-element.111), channel_id=1, source_target_pairs={{0,1},{1,0},{2,3},{3,2},{4,5},{5,4},{6,7},{7,6},{8,9},{9,8},{10,11... | collective-permute-start | bytes 294920 | tf_op jit(solution)/shard_map/ppermute | solution.py:67
  85.4 1.7 %collective-permute-start.37 = (bf16[1,128,384]{2,1,0:T(8,128)(2,1)S(1)}, bf16[1,128,384]{2,1,0:T(8,128)(2,1)S(1)}, u32[]{:S(2)}, u32[]{:S(2)}) collective-permute-start(bf16[1,128,384]{2,1,0:T(8,128)(2,1)S(1)} %get-tuple-element.112), channel_id=1, source_target_pairs={{0,16},{1,17},{2,18},{3,19},{4,20},{5,21},{6,22},{7,23},{8,24},{9,... | collective-permute-start | bytes 294920 | tf_op jit(solution)/shard_map/ppermute | solution.py:67
  88.0 1.2 %collective-permute-start.46 = (bf16[1,256,384]{2,1,0:T(8,128)(2,1)S(1)}, bf16[1,256,384]{2,1,0:T(8,128)(2,1)S(1)}, u32[]{:S(2)}, u32[]{:S(2)}) collective-permute-start(bf16[1,256,384]{2,1,0:T(8,128)(2,1)S(1)} %slice.199), channel_id=1, source_target_pairs={{0,1},{1,0},{2,3},{3,2},{4,5},{5,4},{6,7},{7,6},{8,9},{9,8},{10,11... | collective-permute-start | bytes 589832 | tf_op jit(solution)/shard_map/ppermute | solution.py:67
  89.2 3.2 %collective-permute-start.47 = (bf16[1,256,384]{2,1,0:T(8,128)(2,1)S(1)}, bf16[1,256,384]{2,1,0:T(8,128)(2,1)S(1)}, u32[]{:S(2)}, u32[]{:S(2)}) collective-permute-start(bf16[1,256,384]{2,1,0:T(8,128)(2,1)S(1)} %fusion.4), channel_id=1, source_target_pairs={{0,2},{1,3},{2,0},{3,1},{4,6},{5,7},{6,4},{7,5},{8,10},{9,11},{10,... | collective-permute-start | bytes 589832 | tf_op jit(solution)/shard_map/ppermute | solution.py:67
  93.7 1.8 %collective-permute-done.45 = bf16[1,256,384]{2,1,0:T(8,128)(2,1)S(1)} collective-permute-done((bf16[1,256,384]{2,1,0:T(8,128)(2,1)S(1)}, bf16[1,256,384]{2,1,0:T(8,128)(2,1)S(1)}, u32[]{:S(2)}, u32[]{:S(2)}) %collective-permute-start.45) | collective-permute-done | bytes 196640 | tf_op jit(solution)/shard_map/ppermute | solution.py:67
  96.2 4.7 %collective-permute-start.48 = (bf16[1,256,384]{2,1,0:T(8,128)(2,1)S(1)}, bf16[1,256,384]{2,1,0:T(8,128)(2,1)S(1)}, u32[]{:S(2)}, u32[]{:S(2)}) collective-permute-start(bf16[1,256,384]{2,1,0:T(8,128)(2,1)S(1)} %fusion.8), channel_id=1, source_target_pairs={{0,4},{1,5},{2,6},{3,7},{4,0},{5,1},{6,2},{7,3},{8,12},{9,13},{10,... | collective-permute-start | bytes 589832 | tf_op jit(solution)/shard_map/ppermute | solution.py:67
  100.9 5.8 %collective-permute-done.48 = bf16[1,256,384]{2,1,0:T(8,128)(2,1)S(1)} collective-permute-done((bf16[1,256,384]{2,1,0:T(8,128)(2,1)S(1)}, bf16[1,256,384]{2,1,0:T(8,128)(2,1)S(1)}, u32[]{:S(2)}, u32[]{:S(2)}) %collective-permute-start.48) | collective-permute-done | bytes 196640 | tf_op jit(solution)/shard_map/ppermute | solution.py:67
  (107 shorter events, 17.8 us)
Async XLA Ops:
  0.0 11.2 %collective-permute-start.1 = (bf16[1,256,384]{2,1,0:T(8,128)(2,1)}, bf16[1,256,384]{2,1,0:T(8,128)(2,1)S(1)}, u32[]{:S(2)}, u32[]{:S(2)}) collective-permute-start(bf16[1,256,384]{2,1,0:T(8,128)(2,1)} %bitcast.72), channel_id=1, source_target_pairs={{0,2},{1,3},{2,0},{3,1},{4,6},{5,7},{6,4},{7,5},{8,10},{9,11},{10,... | collective-permute-start | bytes 589832 | tf_op jit(solution)/shard_map/ppermute | solution.py:67
  5.5 8.7 %collective-permute-start.5 = (bf16[1,272,384]{2,1,0:T(8,128)(2,1)S(1)}, bf16[1,272,384]{2,1,0:T(8,128)(2,1)S(1)}, u32[]{:S(2)}, u32[]{:S(2)}) collective-permute-start(bf16[1,272,384]{2,1,0:T(8,128)(2,1)S(1)} %maximum_bitcast_fusion.refs_1_.refs_14_), channel_id=1, source_target_pairs={{0,16},{1,17},{2,18},{3,19},{4,20},{5,21},{6,22},{7,23},{8,24},{9,... | collective-permute-start | bytes 626696 | tf_op jit(solution)/shard_map/ppermute | solution.py:67
  7.0 7.1 %collective-permute-start = (bf16[1,256,384]{2,1,0:T(8,128)(2,1)}, bf16[1,256,384]{2,1,0:T(8,128)(2,1)S(1)}, u32[]{:S(2)}, u32[]{:S(2)}) collective-permute-start(bf16[1,256,384]{2,1,0:T(8,128)(2,1)} %bitcast.73), channel_id=1, source_target_pairs={{0,1},{1,0},{2,3},{3,2},{4,5},{5,4},{6,7},{7,6},{8,9},{9,8},{10,11... | collective-permute-start | bytes 589832 | tf_op jit(solution)/shard_map/ppermute | solution.py:67
  8.6 13.0 %collective-permute-start.4 = (bf16[1,256,384]{2,1,0:T(8,128)(2,1)}, bf16[1,256,384]{2,1,0:T(8,128)(2,1)S(1)}, u32[]{:S(2)}, u32[]{:S(2)}) collective-permute-start(bf16[1,256,384]{2,1,0:T(8,128)(2,1)} %bitcast.74), channel_id=1, source_target_pairs={{0,4},{1,5},{2,6},{3,7},{4,0},{5,1},{6,2},{7,3},{8,12},{9,13},{10,... | collective-permute-start | bytes 589832 | tf_op jit(solution)/shard_map/ppermute | solution.py:67
  11.2 10.5 %collective-permute-start.2 = (bf16[1,256,384]{2,1,0:T(8,128)(2,1)S(1)}, bf16[1,256,384]{2,1,0:T(8,128)(2,1)S(1)}, u32[]{:S(2)}, u32[]{:S(2)}) collective-permute-start(bf16[1,256,384]{2,1,0:T(8,128)(2,1)S(1)} %collective-permute-done.1.refs_5_), channel_id=1, source_target_pairs={{0,16},{1,17},{2,18},{3,19},{4,20},{5,21},{6,22},{7,23},{8,24},{9,... | collective-permute-start | bytes 589832 | tf_op jit(solution)/shard_map/ppermute | solution.py:67
  11.7 10.0 %collective-permute-start.3 = (bf16[1,256,384]{2,1,0:T(8,128)(2,1)S(1)}, bf16[1,256,384]{2,1,0:T(8,128)(2,1)S(1)}, u32[]{:S(2)}, u32[]{:S(2)}) collective-permute-start(bf16[1,256,384]{2,1,0:T(8,128)(2,1)S(1)} %collective-permute-done.1.refs_5_), channel_id=1, source_target_pairs={{0,1},{1,0},{2,3},{3,2},{4,5},{5,4},{6,7},{7,6},{8,9},{9,8},{10,11... | collective-permute-start | bytes 589832 | tf_op jit(solution)/shard_map/ppermute | solution.py:67
  14.1 8.2 %collective-permute-start.11 = (bf16[1,272,384]{2,1,0:T(8,128)(2,1)S(1)}, bf16[1,272,384]{2,1,0:T(8,128)(2,1)S(1)}, u32[]{:S(2)}, u32[]{:S(2)}) collective-permute-start(bf16[1,272,384]{2,1,0:T(8,128)(2,1)S(1)} %maximum_bitcast_fusion.refs_1_.refs_14_), channel_id=1, source_target_pairs={{0,8},{1,9},{2,10},{3,11},{4,12},{5,13},{6,14},{7,15},{8,0},{9,1},... | collective-permute-start | bytes 626696 | tf_op jit(solution)/shard_map/ppermute | solution.py:67
  14.1 8.3 %collective-permute-start.12 = (bf16[1,256,384]{2,1,0:T(8,128)(2,1)S(1)}, bf16[1,256,384]{2,1,0:T(8,128)(2,1)S(1)}, u32[]{:S(2)}, u32[]{:S(2)}) collective-permute-start(bf16[1,256,384]{2,1,0:T(8,128)(2,1)S(1)} %collective-permute-done.refs_2_), channel_id=1, source_target_pairs={{0,8},{1,9},{2,10},{3,11},{4,12},{5,13},{6,14},{7,15},{8,0},{9,1},... | collective-permute-start | bytes 589832 | tf_op jit(solution)/shard_map/ppermute | solution.py:67
  21.7 7.3 %collective-permute-start.10 = (bf16[1,256,384]{2,1,0:T(8,128)(2,1)S(1)}, bf16[1,256,384]{2,1,0:T(8,128)(2,1)S(1)}, u32[]{:S(2)}, u32[]{:S(2)}) collective-permute-start(bf16[1,256,384]{2,1,0:T(8,128)(2,1)S(1)} %collective-permute-done.4.refs_1_), channel_id=1, source_target_pairs={{0,2},{1,3},{2,0},{3,1},{4,6},{5,7},{6,4},{7,5},{8,10},{9,11},{10,... | collective-permute-start | bytes 589832 | tf_op jit(solution)/shard_map/ppermute | solution.py:67
  22.4 11.5 %collective-permute-start.8 = (bf16[1,256,384]{2,1,0:T(8,128)(2,1)S(1)}, bf16[1,256,384]{2,1,0:T(8,128)(2,1)S(1)}, u32[]{:S(2)}, u32[]{:S(2)}) collective-permute-start(bf16[1,256,384]{2,1,0:T(8,128)(2,1)S(1)} %collective-permute-done.4.refs_1_), channel_id=1, source_target_pairs={{0,16},{1,17},{2,18},{3,19},{4,20},{5,21},{6,22},{7,23},{8,24},{9,... | collective-permute-start | bytes 589832 | tf_op jit(solution)/shard_map/ppermute | solution.py:67
  22.4 10.8 %collective-permute-start.7 = (bf16[2,128,384]{2,1,0:T(8,128)(2,1)S(1)}, bf16[2,128,384]{2,1,0:T(8,128)(2,1)S(1)}, u32[]{:S(2)}, u32[]{:S(2)}) collective-permute-start(bf16[2,128,384]{2,1,0:T(8,128)(2,1)S(1)} %pad_maximum_fusion.1), channel_id=1, source_target_pairs={{0,1},{1,0},{2,3},{3,2},{4,5},{5,4},{6,7},{7,6},{8,9},{9,8},{10,11... | collective-permute-start | bytes 589832 | tf_op jit(solution)/shard_map/ppermute | solution.py:67
  24.9 9.0 %collective-permute-start.6 = (bf16[2,128,384]{2,1,0:T(8,128)(2,1)S(1)}, bf16[2,128,384]{2,1,0:T(8,128)(2,1)S(1)}, u32[]{:S(2)}, u32[]{:S(2)}) collective-permute-start(bf16[2,128,384]{2,1,0:T(8,128)(2,1)S(1)} %pad_maximum_fusion), channel_id=1, source_target_pairs={{0,16},{1,17},{2,18},{3,19},{4,20},{5,21},{6,22},{7,23},{8,24},{9,... | collective-permute-start | bytes 589832 | tf_op jit(solution)/shard_map/ppermute | solution.py:67
  26.8 7.4 %collective-permute-start.9 = (bf16[1,256,384]{2,1,0:T(8,128)(2,1)S(1)}, bf16[1,256,384]{2,1,0:T(8,128)(2,1)S(1)}, u32[]{:S(2)}, u32[]{:S(2)}) collective-permute-start(bf16[1,256,384]{2,1,0:T(8,128)(2,1)S(1)} %collective-permute-done.4.refs_1_), channel_id=1, source_target_pairs={{0,1},{1,0},{2,3},{3,2},{4,5},{5,4},{6,7},{7,6},{8,9},{9,8},{10,11... | collective-permute-start | bytes 589832 | tf_op jit(solution)/shard_map/ppermute | solution.py:67
  29.0 7.4 %collective-permute-start.17 = (bf16[1,272,384]{2,1,0:T(8,128)(2,1)S(1)}, bf16[1,272,384]{2,1,0:T(8,128)(2,1)S(1)}, u32[]{:S(2)}, u32[]{:S(2)}) collective-permute-start(bf16[1,272,384]{2,1,0:T(8,128)(2,1)S(1)} %collective-permute-done.5.refs_1_.refs_14_), channel_id=1, source_target_pairs={{0,8},{1,9},{2,10},{3,11},{4,12},{5,13},{6,14},{7,15},{8,0},{9,1},... | collective-permute-start | bytes 626696 | tf_op jit(solution)/shard_map/ppermute | solution.py:67
  34.8 8.4 %collective-permute-start.15 = (bf16[1,256,384]{2,1,0:T(8,128)(2,1)S(1)}, bf16[1,256,384]{2,1,0:T(8,128)(2,1)S(1)}, u32[]{:S(2)}, u32[]{:S(2)}) collective-permute-start(bf16[1,256,384]{2,1,0:T(8,128)(2,1)S(1)} %collective-permute-done.10.refs_5_), channel_id=1, source_target_pairs={{0,16},{1,17},{2,18},{3,19},{4,20},{5,21},{6,22},{7,23},{8,24},{9,... | collective-permute-start | bytes 589832 | tf_op jit(solution)/shard_map/ppermute | solution.py:67
  38.3 7.4 %collective-permute-start.24 = (bf16[1,256,384]{2,1,0:T(8,128)(2,1)S(1)}, bf16[1,256,384]{2,1,0:T(8,128)(2,1)S(1)}, u32[]{:S(2)}, u32[]{:S(2)}) collective-permute-start(bf16[1,256,384]{2,1,0:T(8,128)(2,1)S(1)} %collective-permute-done.9.refs_2_), channel_id=1, source_target_pairs={{0,8},{1,9},{2,10},{3,11},{4,12},{5,13},{6,14},{7,15},{8,0},{9,1},... | collective-permute-start | bytes 589832 | tf_op jit(solution)/shard_map/ppermute | solution.py:67
  38.8 6.9 %collective-permute-start.25 = (bf16[1,256,384]{2,1,0:T(8,128)(2,1)S(1)}, bf16[1,256,384]{2,1,0:T(8,128)(2,1)S(1)}, u32[]{:S(2)}, u32[]{:S(2)}) collective-permute-start(bf16[1,256,384]{2,1,0:T(8,128)(2,1)S(1)} %collective-permute-done.10.refs_5_), channel_id=1, source_target_pairs={{0,8},{1,9},{2,10},{3,11},{4,12},{5,13},{6,14},{7,15},{8,0},{9,1},... | collective-permute-start | bytes 589832 | tf_op jit(solution)/shard_map/ppermute | solution.py:67
  43.8 10.5 %collective-permute-start.22 = (bf16[2,128,384]{2,1,0:T(8,128)(2,1)S(1)}, bf16[2,128,384]{2,1,0:T(8,128)(2,1)S(1)}, u32[]{:S(2)}, u32[]{:S(2)}) collective-permute-start(bf16[2,128,384]{2,1,0:T(8,128)(2,1)S(1)} %pad_maximum_fusion.3), channel_id=1, source_target_pairs={{0,1},{1,0},{2,3},{3,2},{4,5},{5,4},{6,7},{7,6},{8,9},{9,8},{10,11... | collective-permute-start | bytes 589832 | tf_op jit(solution)/shard_map/ppermute | solution.py:67
  44.9 9.4 %collective-permute-start.21 = (bf16[2,128,384]{2,1,0:T(8,128)(2,1)S(1)}, bf16[2,128,384]{2,1,0:T(8,128)(2,1)S(1)}, u32[]{:S(2)}, u32[]{:S(2)}) collective-permute-start(bf16[2,128,384]{2,1,0:T(8,128)(2,1)S(1)} %pad_maximum_fusion.2), channel_id=1, source_target_pairs={{0,16},{1,17},{2,18},{3,19},{4,20},{5,21},{6,22},{7,23},{8,24},{9,... | collective-permute-start | bytes 589832 | tf_op jit(solution)/shard_map/ppermute | solution.py:67
  56.8 12.5 %collective-permute-start.28 = (bf16[2,1,256,384]{3,2,1,0:T(8,128)(2,1)S(1)}, bf16[2,1,256,384]{3,2,1,0:T(8,128)(2,1)S(1)}, u32[]{:S(2)}, u32[]{:S(2)}) collective-permute-start(bf16[2,1,256,384]{3,2,1,0:T(8,128)(2,1)S(1)} %add_convert_fusion.1), channel_id=1, source_target_pairs={{0,2},{1,3},{2,0},{3,1},{4,6},{5,7},{6,4},{7,5},{8,10},{9,11},{10,... | collective-permute-start | bytes 1179656 | tf_op jit(solution)/shard_map/ppermute | solution.py:67
  59.0 10.9 %collective-permute-start.39 = (bf16[2,2,256,384]{3,2,1,0:T(8,128)(2,1)S(1)}, bf16[2,2,256,384]{3,2,1,0:T(8,128)(2,1)S(1)}, u32[]{:S(2)}, u32[]{:S(2)}) collective-permute-start(bf16[2,2,256,384]{3,2,1,0:T(8,128)(2,1)S(1)} %get-tuple-element.104), channel_id=1, source_target_pairs={{0,8},{1,9},{2,10},{3,11},{4,12},{5,13},{6,14},{7,15},{8,0},{9,1},... | collective-permute-start | bytes 2359304 | tf_op jit(solution)/shard_map/ppermute | solution.py:67
  71.7 7.1 %collective-permute-start.41 = (bf16[2,128,384]{2,1,0:T(8,128)(2,1)S(1)}, bf16[2,128,384]{2,1,0:T(8,128)(2,1)S(1)}, u32[]{:S(2)}, u32[]{:S(2)}) collective-permute-start(bf16[2,128,384]{2,1,0:T(8,128)(2,1)S(1)} %get-tuple-element.113), channel_id=1, source_target_pairs={{0,1},{1,0},{2,3},{3,2},{4,5},{5,4},{6,7},{7,6},{8,9},{9,8},{10,11... | collective-permute-start | bytes 589832 | tf_op jit(solution)/shard_map/ppermute | solution.py:67
  73.0 11.2 %collective-permute-start.34 = (bf16[2,1,256,384]{3,2,1,0:T(8,128)(2,1)S(1)}, bf16[2,1,256,384]{3,2,1,0:T(8,128)(2,1)S(1)}, u32[]{:S(2)}, u32[]{:S(2)}) collective-permute-start(bf16[2,1,256,384]{3,2,1,0:T(8,128)(2,1)S(1)} %add_convert_fusion), channel_id=1, source_target_pairs={{0,2},{1,3},{2,0},{3,1},{4,6},{5,7},{6,4},{7,5},{8,10},{9,11},{10,... | collective-permute-start | bytes 1179656 | tf_op jit(solution)/shard_map/ppermute | solution.py:67
  73.4 7.4 %collective-permute-start.42 = (bf16[2,128,384]{2,1,0:T(8,128)(2,1)S(1)}, bf16[2,128,384]{2,1,0:T(8,128)(2,1)S(1)}, u32[]{:S(2)}, u32[]{:S(2)}) collective-permute-start(bf16[2,128,384]{2,1,0:T(8,128)(2,1)S(1)} %get-tuple-element.114), channel_id=1, source_target_pairs={{0,16},{1,17},{2,18},{3,19},{4,20},{5,21},{6,22},{7,23},{8,24},{9,... | collective-permute-start | bytes 589832 | tf_op jit(solution)/shard_map/ppermute | solution.py:67
  79.0 8.0 %collective-permute-start.43 = (bf16[1,256,384]{2,1,0:T(8,128)(2,1)S(1)}, bf16[1,256,384]{2,1,0:T(8,128)(2,1)S(1)}, u32[]{:S(2)}, u32[]{:S(2)}) collective-permute-start(bf16[1,256,384]{2,1,0:T(8,128)(2,1)S(1)} %slice.220), channel_id=1, source_target_pairs={{0,16},{1,17},{2,18},{3,19},{4,20},{5,21},{6,22},{7,23},{8,24},{9,... | collective-permute-start | bytes 589832 | tf_op jit(solution)/shard_map/ppermute | solution.py:67
  84.3 8.1 %collective-permute-start.35 = (bf16[1,128,384]{2,1,0:T(8,128)(2,1)S(1)}, bf16[1,128,384]{2,1,0:T(8,128)(2,1)S(1)}, u32[]{:S(2)}, u32[]{:S(2)}) collective-permute-start(bf16[1,128,384]{2,1,0:T(8,128)(2,1)S(1)} %get-tuple-element.111), channel_id=1, source_target_pairs={{0,1},{1,0},{2,3},{3,2},{4,5},{5,4},{6,7},{7,6},{8,9},{9,8},{10,11... | collective-permute-start | bytes 294920 | tf_op jit(solution)/shard_map/ppermute | solution.py:67
  85.4 7.2 %collective-permute-start.37 = (bf16[1,128,384]{2,1,0:T(8,128)(2,1)S(1)}, bf16[1,128,384]{2,1,0:T(8,128)(2,1)S(1)}, u32[]{:S(2)}, u32[]{:S(2)}) collective-permute-start(bf16[1,128,384]{2,1,0:T(8,128)(2,1)S(1)} %get-tuple-element.112), channel_id=1, source_target_pairs={{0,16},{1,17},{2,18},{3,19},{4,20},{5,21},{6,22},{7,23},{8,24},{9,... | collective-permute-start | bytes 294920 | tf_op jit(solution)/shard_map/ppermute | solution.py:67
  87.6 7.9 %collective-permute-start.45 = (bf16[1,256,384]{2,1,0:T(8,128)(2,1)S(1)}, bf16[1,256,384]{2,1,0:T(8,128)(2,1)S(1)}, u32[]{:S(2)}, u32[]{:S(2)}) collective-permute-start(bf16[1,256,384]{2,1,0:T(8,128)(2,1)S(1)} %slice.198), channel_id=1, source_target_pairs={{0,16},{1,17},{2,18},{3,19},{4,20},{5,21},{6,22},{7,23},{8,24},{9,... | collective-permute-start | bytes 589832 | tf_op jit(solution)/shard_map/ppermute | solution.py:67
  88.0 7.7 %collective-permute-start.46 = (bf16[1,256,384]{2,1,0:T(8,128)(2,1)S(1)}, bf16[1,256,384]{2,1,0:T(8,128)(2,1)S(1)}, u32[]{:S(2)}, u32[]{:S(2)}) collective-permute-start(bf16[1,256,384]{2,1,0:T(8,128)(2,1)S(1)} %slice.199), channel_id=1, source_target_pairs={{0,1},{1,0},{2,3},{3,2},{4,5},{5,4},{6,7},{7,6},{8,9},{9,8},{10,11... | collective-permute-start | bytes 589832 | tf_op jit(solution)/shard_map/ppermute | solution.py:67
  92.5 8.4 %collective-permute-start.36 = (bf16[1,256,384]{2,1,0:T(8,128)(2,1)S(1)}, bf16[1,256,384]{2,1,0:T(8,128)(2,1)S(1)}, u32[]{:S(2)}, u32[]{:S(2)}) collective-permute-start(bf16[1,256,384]{2,1,0:T(8,128)(2,1)S(1)} %fusion.10), channel_id=1, source_target_pairs={{0,16},{1,17},{2,18},{3,19},{4,20},{5,21},{6,22},{7,23},{8,24},{9,... | collective-permute-start | bytes 589832 | tf_op jit(solution)/shard_map/ppermute | solution.py:67
  92.7 8.2 %collective-permute-start.38 = (bf16[1,256,384]{2,1,0:T(8,128)(2,1)S(1)}, bf16[1,256,384]{2,1,0:T(8,128)(2,1)S(1)}, u32[]{:S(2)}, u32[]{:S(2)}) collective-permute-start(bf16[1,256,384]{2,1,0:T(8,128)(2,1)S(1)} %fusion.9), channel_id=1, source_target_pairs={{0,1},{1,0},{2,3},{3,2},{4,5},{5,4},{6,7},{7,6},{8,9},{9,8},{10,11... | collective-permute-start | bytes 589832 | tf_op jit(solution)/shard_map/ppermute | solution.py:67
  96.2 10.4 %collective-permute-start.48 = (bf16[1,256,384]{2,1,0:T(8,128)(2,1)S(1)}, bf16[1,256,384]{2,1,0:T(8,128)(2,1)S(1)}, u32[]{:S(2)}, u32[]{:S(2)}) collective-permute-start(bf16[1,256,384]{2,1,0:T(8,128)(2,1)S(1)} %fusion.8), channel_id=1, source_target_pairs={{0,4},{1,5},{2,6},{3,7},{4,0},{5,1},{6,2},{7,3},{8,12},{9,13},{10,... | collective-permute-start | bytes 589832 | tf_op jit(solution)/shard_map/ppermute | solution.py:67
  (17 other events, 68.3 us)

commit v2 on v1

--- a/solution.py
+++ b/solution.py
@@ -145,31 +145,43 @@
         copy.wait()
 
 
-def weights_kernel(place, *refs, z):
-    w_gate, w_up, gate, up, sems = refs[-5:]
-    depth = gate.shape[0]
+def weight_copies(place, z, weight, result, sems):
+    depth = result.shape[0]
     quarter = depth // 4
     base = pl.multiple_of((place[z] // 2) * depth, depth)
+    return [
+        pltpu.make_async_copy(
+            weight.at[pl.ds(base + q * quarter, quarter)],
+            result.at[pl.ds(q * quarter, quarter)],
+            sems.at[q],
+        )
+        for q in range(4)
+    ]
+
+
+def weights_kernel(place, *refs, z):
+    w_gate, w_up, gate, up, gate_sems, up_sems = refs[-6:]
     all_of(
-        [
-            pltpu.make_async_copy(
-                weight.at[pl.ds(base + q * quarter, quarter)],
-                result.at[pl.ds(q * quarter, quarter)],
-                sems.at[i, q],
-            )
-            for q in range(4)
-            for i, (weight, result) in enumerate(((w_gate, gate), (w_up, up)))
-        ]
-    )
-
-
-def first_kernel(place, *refs, found, z_places):
-    arrays, (w_gate, w_up, gate, up, rows, sems) = refs[:-6], refs[-6:]
-    all_of(fill(place, arrays, found, z_places, rows, sems))
+        weight_copies(place, z, w_gate, gate, gate_sems)
+        + weight_copies(place, z, w_up, up, up_sems)
+    )
+
+
+def first_kernel(place, *refs, found, z_places, following):
+    arrays, refs = refs[:-9], refs[-9:]
+    w_gate, w_up, later, gate, up, later_rows, rows, sems, later_sems = refs
+    later = weight_copies(place, following, later, later_rows, later_sems)
+    copies = fill(place, arrays, found, z_places, rows, sems)
+    for copy in copies + later:
+        copy.start()
+    for copy in copies:
+        copy.wait()
     for weight, result in ((w_gate, gate), (w_up, up)):
         for t in range(result.shape[0]):
             tile = slice(t * HIDDEN_TILE, (t + 1) * HIDDEN_TILE)
             result[t] = jnp.dot(rows[...], weight[:, tile], preferred_element_type=jnp.float32)
+    for copy in later:
+        copy.wait()
 
 
 def share_column(place, blocks, tails, sems, size):
@@ -190,21 +202,41 @@
     return jnp.concatenate(column)[:, :1]
 
 
-def second_kernel(place, *refs, found, z_places, pairs):
-    arrays, refs = refs[:-18], refs[-18:]
+def down_copy(place, pair, w_down, tile, sem):
+    span = tile.shape[1]
+    columns = pl.ds(pl.multiple_of((place[pair[0]] // 2) * span, span), span)
+    return pltpu.make_async_copy(w_down.at[:, columns], tile, sem)
+
+
+def down_products(place, pair, hidden, tile, results):
+    my_y = place[place.shape[0] - 1]
+    size, narrow = results[0].shape[2:]
+    terms = jnp.dot(hidden[...], tile[...], preferred_element_type=jnp.float32)
+    terms = terms.astype(jnp.bfloat16)
+    for r, result in enumerate(results):
+        for z in range(2):
+            n = (place[pair[0]] & 1) ^ z
+            for y in range(2):
+                start = (z * 2 + y) * narrow
+                piece = terms[r * size : (r + 1) * size, start : start + narrow]
+                result[my_y ^ y, n] = piece
+
+
+def second_kernel(place, *refs, x, found, z_places, pairs):
+    count = 17 if x else 19
+    arrays, refs = refs[:-count], refs[-count:]
     w_gate, w_up, gate, up, w_down = refs[:5]
-    results = refs[7:9], refs[9:11]
-    rows, downs, hidden, tails, sems, d_sems, t_sems = refs[11:]
-    my_y = place[place.shape[0] - 1]
-    size, span = results[0][0].shape[2], downs.shape[2]
+    shares, out = refs[5:7], refs[7:11]
+    rows, tails, sems, t_sems, d_sems, first_tile = refs[11:17]
+    hidden, second_tile = out[2:] if x else refs[17:]
     copies = fill(place, arrays, found, z_places, rows, sems)
-    downs_in = []
-    for k, pair in enumerate(pairs):
-        columns = pl.ds(pl.multiple_of((place[pair[0]] // 2) * span, span), span)
-        downs_in.append(pltpu.make_async_copy(w_down.at[:, columns], downs.at[k], d_sems.at[k]))
+    downs_in = [
+        down_copy(place, pair, w_down, tile, d_sems.at[k])
+        for k, (pair, tile) in enumerate(zip(pairs, (first_tile, second_tile)))
+    ]
     for copy in copies + downs_in:
         copy.start()
-    share = 0.5 * share_column(place, refs[5:7], tails, t_sems, size)
+    share = 0.5 * share_column(place, shares, tails, t_sems, out[0].shape[2])
     for copy in copies:
         copy.wait()
     for t in range(gate.shape[0]):
@@ -213,18 +245,15 @@
         u = up[t] + jnp.dot(rows[...], w_up[:, tile], preferred_element_type=jnp.float32)
         value = (g + g * jnp.tanh(0.5 * g)) * u * share
         hidden[:, tile] = value.astype(jnp.bfloat16)
-    narrow = results[0][0].shape[3]
-    for k, pair in enumerate(pairs):
-        downs_in[k].wait()
-        terms = jnp.dot(hidden[...], downs[k], preferred_element_type=jnp.float32)
-        terms = terms.astype(jnp.bfloat16)
-        for r, result in enumerate(results[k]):
-            for z in range(2):
-                n = (place[pair[0]] & 1) ^ z
-                for y in range(2):
-                    start = (z * 2 + y) * narrow
-                    piece = terms[r * size : (r + 1) * size, start : start + narrow]
-                    result[my_y ^ y, n] = piece
+    downs_in[0].wait()
+    down_products(place, pairs[0], hidden, first_tile, out[:2])
+    downs_in[1].wait()
+    if x == 0:
+        down_products(place, pairs[1], hidden, second_tile, out[2:])
+
+
+def third_kernel(place, hidden, tile, own, sibling, pair):
+    down_products(place, pair, hidden, tile, (own, sibling))
 
 
 def cost(flops, bytes_accessed, transcendentals):
@@ -259,7 +288,7 @@
         lambda *refs: weights_kernel(*refs, z=z),
         in_specs=[SCALARS] + [ANY] * (len(earlier) + 2),
         out_specs=[VMEM] * 2,
-        scratch_shapes=[SEMS((2, 4))],
+        scratch_shapes=[SEMS((4,)), SEMS((4,))],
         out_shape=[pltpu.VMEM((depth, width), jnp.bfloat16)] * 2,
         compiler_params=params(2),
         cost_estimate=cost(flops=0, bytes_accessed=8 * depth * width, transcendentals=0),
@@ -267,18 +296,22 @@
     )(place, *earlier, w_gate, w_up)
 
 
-def first_part(place, x, pair, z_places, weights):
+def first_part(place, x, pair, z_places, weights, following, later):
     arrays, found = pieces(x, pair)
     size, narrow = pair[0][1][0][0].shape[1:]
     depth, width = weights[0].shape
     rows = 2 * size
-    sums = (width // HIDDEN_TILE, rows, HIDDEN_TILE)
+    sums = pltpu.VMEM((width // HIDDEN_TILE, rows, HIDDEN_TILE), jnp.float32)
     return pl.pallas_call(
-        lambda *refs: first_kernel(*refs, found=found, z_places=z_places),
-        in_specs=[SCALARS] + [ANY] * len(arrays) + [VMEM, VMEM],
-        out_specs=[VMEM, VMEM],
-        scratch_shapes=[pltpu.VMEM((rows, depth), jnp.bfloat16), SEMS((len(found),))],
-        out_shape=[pltpu.VMEM(sums, jnp.float32)] * 2,
+        lambda *refs: first_kernel(*refs, found=found, z_places=z_places, following=following),
+        in_specs=[SCALARS] + [ANY] * len(arrays) + [VMEM, VMEM, ANY],
+        out_specs=[VMEM] * 3,
+        scratch_shapes=[
+            pltpu.VMEM((rows, depth), jnp.bfloat16),
+            SEMS((len(found),)),
+            SEMS((4,)),
+        ],
+        out_shape=[sums, sums, pltpu.VMEM((depth, width), jnp.bfloat16)],
         compiler_params=params(4),
         cost_estimate=cost(
             flops=4 * rows * depth * width,
@@ -286,7 +319,7 @@
             transcendentals=0,
         ),
         name="first_part",
-    )(place, *arrays, *[in_vmem(v) for v in weights])
+    )(place, *arrays, *[in_vmem(v) for v in weights], later)
 
 
 def second_part(place, x, pair, z_places, weights, sums, shares, w_down, pairs):
@@ -294,21 +327,25 @@
     size, narrow = pair[0][1][0][0].shape[1:]
     depth, width = weights[0].shape
     rows, tail = 2 * size, shares[0].shape[1] - size
+    part = pltpu.VMEM((2, 2, size, narrow), jnp.bfloat16)
+    hidden, tile = [pltpu.VMEM(v, jnp.bfloat16) for v in ((rows, width), (width, depth))]
     return pl.pallas_call(
-        lambda *refs: second_kernel(*refs, found=found, z_places=z_places, pairs=pairs),
+        lambda *refs: second_kernel(
+            *refs, x=x, found=found, z_places=z_places, pairs=pairs
+        ),
         in_specs=[SCALARS] + [ANY] * len(arrays) + [VMEM] * 4 + [ANY] * 3,
         out_specs=[VMEM] * 4,
         scratch_shapes=[
             pltpu.VMEM((rows, depth), jnp.bfloat16),
-            pltpu.VMEM((2, width, depth), jnp.bfloat16),
-            pltpu.VMEM((rows, width), jnp.bfloat16),
             pltpu.VMEM((2, tail, narrow), jnp.bfloat16),
             SEMS((len(found),)),
             SEMS((2,)),
             SEMS((2,)),
-        ],
-        out_shape=[pltpu.VMEM((2, 2, size, narrow), jnp.bfloat16)] * 4,
-        compiler_params=params(13),
+            tile,
+        ]
+        + ([] if x else [hidden, tile]),
+        out_shape=[part, part] + ([hidden, tile] if x else [part, part]),
+        compiler_params=params(9 if x else 13),
         cost_estimate=cost(
             flops=4 * rows * depth * width + 4 * rows * width * depth,
             bytes_accessed=8 * depth * width + 6 * rows * depth + 8 * rows * width,
@@ -316,6 +353,24 @@
         ),
         name="second_part",
     )(place, *arrays, *[in_vmem(v) for v in (*weights, *sums)], w_down, *shares)
+
+
+def third_part(place, hidden, tile, pair, size):
+    rows, width = hidden.shape
+    narrow = tile.shape[1] // 4
+    return pl.pallas_call(
+        lambda *refs: third_kernel(*refs, pair=pair),
+        in_specs=[SCALARS, VMEM, VMEM],
+        out_specs=[VMEM] * 2,
+        out_shape=[pltpu.VMEM((2, 2, size, narrow), jnp.bfloat16)] * 2,
+        compiler_params=params(8),
+        cost_estimate=cost(
+            flops=2 * rows * width * tile.shape[1],
+            bytes_accessed=2 * width * (rows + tile.shape[1]) + 2 * rows * tile.shape[1],
+            transcendentals=0,
+        ),
+        name="third_part",
+    )(place, in_vmem(hidden), in_vmem(tile))
 
 
 def shares_of(expert_ids, pair_logits):
@@ -348,15 +403,12 @@
     x1, y1 = send(z1, x=1), send(z1, y=1)
     sz0, sz1, sx0, sx1, sy0, sy1 = swapped(block, z1, x0, x1, y0, y1)
     near_weights = pair_weights(place, 0, w_gate, w_up, narrow, x0)
-    far_weights = pair_weights(place, 2, w_gate, w_up, narrow, x0)
-    (x1_, y1_), z2, near_weights, far_weights = after(
-        ((x1, y1), z2, near_weights, far_weights)
-    )
+    (x1_, y1_), z2, near_weights = after(((x1, y1), z2, near_weights))
     first, last = relayed([x0, x1_], [y0, y1_])
     z3 = send(z2, z=1)
     x2, y2 = send(z2, x=1), send(z2, y=1)
     near = [[(sz0, 0), (sz1, 0)], [(sx0, 0), (sx1, 0)], [(sy0, 0), (sy1, 0)], None, None]
-    sums_0 = first_part(place, 0, near, (0, 1), near_weights)
+    *sums_0, far_gate = first_part(place, 0, near, (0, 1), near_weights, 2, w_gate)
 
     z3, sums_0 = after((z3, sums_0))
     (first, last, x2, y2), sums_0 = after(((first, last, x2, y2), sums_0))
@@ -364,35 +416,49 @@
     both_of = lambda v: [(v, 0), (v, 1)]
     near[3:] = [both_of(v) for v in swapped(first, last)]
     sz2, sz3, sx2, sy2 = swapped(z2, z3, x2, y2)
-    sums_1 = first_part(place, 1, near, (0, 1), near_weights)
+    *sums_1, far_up = first_part(place, 1, near, (0, 1), near_weights, 2, w_up)
+    far_weights = far_gate, far_up
     (x3, y3), sums_1 = after(((x3, y3), sums_1))
     first, last = relayed([x2, x3], [y2, y3])
     sx3, sy3 = swapped(x3, y3)
     far = [[(sz2, 0), (sz3, 0)], [(sx2, 0), (sx3, 0)], [(sy2, 0), (sy3, 0)], None, None]
     pairs = (3, 2), (1, 0)
     parts_0 = second_part(place, 0, far, (2, 3), far_weights, sums_0, sz0, w_down, pairs)
-    (first, last), parts_0 = after(((first, last), parts_0))
+    (first, last, sx2, sx3), parts_0 = after(((first, last, sx2, sx3), parts_0))
+    far[1] = [(sx2, 0), (sx3, 0)]
     far[3:] = [both_of(v) for v in swapped(first, last)]
-    far_0, near_0 = [(parts_0[i], send(parts_0[i + 1], c=1)) for i in (0, 2)]
+    near_0 = parts_0[2], send(parts_0[3], c=1)
+    near_0, parts_0 = after((near_0, parts_0), far[3:])
+    far_0 = parts_0[0], send(parts_0[1], c=1)
     to_z = total(*[v[:, :1] for v in near_0]).astype(jnp.bfloat16)
     passed_0 = send(to_z, z=1)
     sums_1 = after(sums_1, to_z)
-    parts_1 = second_part(place, 1, far, (2, 3), far_weights, sums_1, sx0, w_down, pairs)
-    passed_0, parts_1 = after((passed_0, parts_1))
-    far_1, near_1 = [(parts_1[i], send(parts_1[i + 1], c=1)) for i in (0, 2)]
+    *parts_1, hidden, tile = second_part(
+        place, 1, far, (2, 3), far_weights, sums_1, sx0, w_down, pairs
+    )
+    passed_0, far_0, parts_1 = after((passed_0, far_0, parts_1))
+    other_1 = send(parts_1[1], c=1)
+    last_1 = third_part(place, after(hidden, far_0), tile, pairs[1], size)
+    other_1, last_1 = after((other_1, last_1))
+    far_1, near_1 = (parts_1[0], other_1), (last_1[0], send(last_1[1], c=1))
 
     far = far_0, far_1
-    to_x, to_y = plane_sums(far, *diagonal(far))
-    passed_1 = send(total(*[v[:, :1] for v in near_1]).astype(jnp.bfloat16), z=1)
+    corner = diagonal(far)
+    to_z = total(*[v[:, :1] for v in near_1]).astype(jnp.bfloat16)
+    passed_1 = send(to_z, z=1)
+    to_x, to_y = plane_sums(far, *after(corner, to_z))
     from_3 = send(to_x[:1], x=1), send(to_y[:1], y=1)
-    to_x, to_y = after((to_x, to_y), *from_3)
+    here = summed(far, 0, 0)
+    to_2 = total(here[:1], *from_3).astype(jnp.bfloat16)
+    to_x, to_y = after((to_x, to_y), to_2)
+    to_2 = send(to_2, z=1)
     from_2 = send(to_x[1:], x=1), send(to_y[1:], y=1)
-    here = summed(far, 0, 0)
-    to_2 = send(total(here[:1], *from_3).astype(jnp.bfloat16), z=1)
-    to_0 = send(total(here[1:], *from_2, to_2).astype(jnp.bfloat16), z=2)
     last_block = lambda terms, passed: [v[:, 1:] for v in terms] + [passed]
     near = last_block(near_0, passed_0), last_block(near_1, passed_1)
-    to_x, to_y = plane_sums(near, *diagonal(near))
+    corner = diagonal(near)
+    from_2, corner = after((from_2, corner))
+    to_0 = send(total(here[1:], *from_2, to_2).astype(jnp.bfloat16), z=2)
+    to_x, to_y = plane_sums(near, *after(corner, to_2))
     from_0 = send(to_x, x=1), send(to_y, y=1)
     return total(summed(near, 0, 0), *from_0, to_0)[0].astype(jnp.bfloat16)
 

time: 108 us -> 106 us (0.981)
  waiting for transfers between devices: 23.6 us -> 28.7 us
  starting transfers between devices: 46 us -> 42.1 us
  Pallas kernels: 32.8 us -> 30.1 us
    ppermute x49, waiting for transfers between devices: 23.6 us -> 28.7 us  [send(): return lax.ppermute(value, BOTH, pairs)]
    ppermute x49, starting transfers between devices: 46 us -> 42.1 us  [send(): return lax.ppermute(value, BOTH, pairs)]
    pallas_call x2 -> x1, Pallas kernels: 6.82 us -> 3.41 us  [pair_weights(): pl.pallas_call(lambda *refs: weights_kernel(*refs, z=z), in_specs=[SCALAR...]
    pallas_call x2 -> x3, Pallas kernels: 17.4 us -> 18 us  [the longest x2 15.6 us: second_part(): pl.pallas_call(lambda *refs: second_kernel(*refs, x=x, found=found, z_pla...]
  transfers between devices with their start and end apart: 49 -> 49, of which waited for: 15 -> 17; matrix products, arithmetic and copies ran while one was open for 4% -> 4% of each run, Pallas kernels for 30% -> 28%
where the time goes in v2:
time: 106 us
  starting transfers between devices  42.1 us (40%)
  Pallas kernels  30.1 us (28%)
  waiting for transfers between devices  28.7 us (27%)
  other arithmetic  4.45 us (4%)
    ppermute x49, starting transfers between devices, send(): return lax.ppermute(value, BOTH, pairs)  42.1 us
    ppermute x49, waiting for transfers between devices, send(): return lax.ppermute(value, BOTH, pairs)  28.7 us
    pallas_call x2, Pallas kernels, second_part(): pl.pallas_call(lambda *refs: second_kernel(*refs, x=x, found=found, z_pla...  15.6 us
    pallas_call x2, Pallas kernels, first_part(): pl.pallas_call(lambda *refs: first_kernel(*refs, found=found, z_places=z_...  8.7 us
    pallas_call x1, Pallas kernels, pair_weights(): pl.pallas_call(lambda *refs: weights_kernel(*refs, z=z), in_specs=[SCALAR...  3.41 us
    pallas_call x1, Pallas kernels, third_part(): pl.pallas_call(lambda *refs: third_kernel(*refs, pair=pair), in_specs=[SC...  2.37 us
  transfers between devices with their start and end apart: 49, of which 17 were waited for; matrix products, arithmetic and copies ran while one was open for 4% of the time, Pallas kernels for 28%

profile of v2, /device:TPU:0, one launch (start us, length us, event | category | flops | bytes accessed | tf_op | source)
XLA Modules:
  0.0 105.9 jit_solution(5024110821947440947)
XLA Ops:
  0.0 3.0 %collective-permute-start.1 = (bf16[1,256,384]{2,1,0:T(8,128)(2,1)}, bf16[1,256,384]{2,1,0:T(8,128)(2,1)S(1)}, u32[]{:S(2)}, u32[]{:S(2)}) collective-permute-start(bf16[1,256,384]{2,1,0:T(8,128)(2,1)} %bitcast.72), channel_id=1, source_target_pairs={{0,2},{1,3},{2,0},{3,1},{4,6},{5,7},{6,4},{7,5},{8,10},{9,11},{10,... | collective-permute-start | bytes 589832 | tf_op jit(solution)/shard_map/ppermute | solution.py:67
  5.5 1.6 %collective-permute-start.5 = (bf16[1,272,384]{2,1,0:T(8,128)(2,1)S(1)}, bf16[1,272,384]{2,1,0:T(8,128)(2,1)S(1)}, u32[]{:S(2)}, u32[]{:S(2)}) collective-permute-start(bf16[1,272,384]{2,1,0:T(8,128)(2,1)S(1)} %maximum_bitcast_fusion.refs_1_.refs_14_), channel_id=1, source_target_pairs={{0,16},{1,17},{2,18},{3,19},{4,20},{5,21},{6,22},{7,23},{8,24},{9,... | collective-permute-start | bytes 626696 | tf_op jit(solution)/shard_map/ppermute | solution.py:67
  7.0 1.5 %collective-permute-start = (bf16[1,256,384]{2,1,0:T(8,128)(2,1)}, bf16[1,256,384]{2,1,0:T(8,128)(2,1)S(1)}, u32[]{:S(2)}, u32[]{:S(2)}) collective-permute-start(bf16[1,256,384]{2,1,0:T(8,128)(2,1)} %bitcast.73), channel_id=1, source_target_pairs={{0,1},{1,0},{2,3},{3,2},{4,5},{5,4},{6,7},{7,6},{8,9},{9,8},{10,11... | collective-permute-start | bytes 589832 | tf_op jit(solution)/shard_map/ppermute | solution.py:67
  8.6 2.6 %collective-permute-start.4 = (bf16[1,256,384]{2,1,0:T(8,128)(2,1)}, bf16[1,256,384]{2,1,0:T(8,128)(2,1)S(1)}, u32[]{:S(2)}, u32[]{:S(2)}) collective-permute-start(bf16[1,256,384]{2,1,0:T(8,128)(2,1)} %bitcast.74), channel_id=1, source_target_pairs={{0,4},{1,5},{2,6},{3,7},{4,0},{5,1},{6,2},{7,3},{8,12},{9,13},{10,... | collective-permute-start | bytes 589832 | tf_op jit(solution)/shard_map/ppermute | solution.py:67
  12.3 1.8 %collective-permute-done.refs_2_ = bf16[1,256,384]{2,1,0:T(8,128)(2,1)S(1)} collective-permute-done((bf16[1,256,384]{2,1,0:T(8,128)(2,1)}, bf16[1,256,384]{2,1,0:T(8,128)(2,1)S(1)}, u32[]{:S(2)}, u32[]{:S(2)}) %collective-permute-start) | collective-permute-done | bytes 196640 | tf_op jit(solution)/shard_map/ppermute | solution.py:67
  14.7 3.4 %pair_weights.1 = (bf16[1536,1024]{1,0:T(8,128)(2,1)S(1)}, bf16[1536,1024]{1,0:T(8,128)(2,1)S(1)}) custom-call(s32[7]{0:T(128)S(1)} %stack.33.refs_0_, bf16[1,272,384]{2,1,0:T(8,128)(2,1)S(1)} %collective-permute-done.5.refs_1_.refs_14_, bf16[3072,1024]{1,0:T(8,128)(2,1)} %bitcast.66, bf16[3072,1024]{1,0:T(8,128)(2,1)} %bitcast.68), custom_call_target="tpu_custom_call" | custom-call | bytes 3145728 | tf_op jit(solution)/shard_map/pair_weights/pallas_call | solution.py:287
  18.2 1.4 %collective-permute-done.4.refs_1_ = bf16[1,256,384]{2,1,0:T(8,128)(2,1)S(1)} collective-permute-done((bf16[1,256,384]{2,1,0:T(8,128)(2,1)}, bf16[1,256,384]{2,1,0:T(8,128)(2,1)S(1)}, u32[]{:S(2)}, u32[]{:S(2)}) %collective-permute-start.4) | collective-permute-done | bytes 196640 | tf_op jit(solution)/shard_map/ppermute | solution.py:67
  21.5 1.9 %collective-permute-start.6 = (bf16[2,128,384]{2,1,0:T(8,128)(2,1)S(1)}, bf16[2,128,384]{2,1,0:T(8,128)(2,1)S(1)}, u32[]{:S(2)}, u32[]{:S(2)}) collective-permute-start(bf16[2,128,384]{2,1,0:T(8,128)(2,1)S(1)} %pad_maximum_fusion), channel_id=1, source_target_pairs={{0,16},{1,17},{2,18},{3,19},{4,20},{5,21},{6,22},{7,23},{8,24},{9,... | collective-permute-start | bytes 589832 | tf_op jit(solution)/shard_map/ppermute | solution.py:67
  24.4 2.5 %collective-permute-done.10.refs_5_ = bf16[1,256,384]{2,1,0:T(8,128)(2,1)S(1)} collective-permute-done((bf16[1,256,384]{2,1,0:T(8,128)(2,1)S(1)}, bf16[1,256,384]{2,1,0:T(8,128)(2,1)S(1)}, u32[]{:S(2)}, u32[]{:S(2)}) %collective-permute-start.10) | collective-permute-done | bytes 196640 | tf_op jit(solution)/shard_map/ppermute | solution.py:67
  26.9 4.3 %first_part.2 = (f32[2,512,512]{2,1,0:T(8,128)S(1)}, f32[2,512,512]{2,1,0:T(8,128)S(1)}, bf16[1536,1024]{1,0:T(8,128)(2,1)S(1)}) custom-call(s32[7]{0:T(128)S(1)} %stack.33.refs_0_, bf16[1,272,384]{2,1,0:T(8,128)(2,1)S(1)} %maximum_bitcast_fusion.refs_1_.refs_14_, bf16[1,256,384]{2,1,0:T(8,128)(2,1)S(1)} %collective-permute-done.refs_2_, ...), custom_call_target="tpu_custom_call" | custom-call | flops 805306368 | bytes 3014656 | tf_op jit(solution)/shard_map/first_part/pallas_call | solution.py:305
  32.4 1.3 %collective-permute-start.15 = (bf16[1,256,384]{2,1,0:T(8,128)(2,1)S(1)}, bf16[1,256,384]{2,1,0:T(8,128)(2,1)S(1)}, u32[]{:S(2)}, u32[]{:S(2)}) collective-permute-start(bf16[1,256,384]{2,1,0:T(8,128)(2,1)S(1)} %collective-permute-done.10.refs_5_), channel_id=1, source_target_pairs={{0,16},{1,17},{2,18},{3,19},{4,20},{5,21},{6,22},{7,23},{8,24},{9,... | collective-permute-start | bytes 589832 | tf_op jit(solution)/shard_map/ppermute | solution.py:67
  35.5 4.4 %first_part.3 = (f32[2,512,512]{2,1,0:T(8,128)S(1)}, f32[2,512,512]{2,1,0:T(8,128)S(1)}, bf16[1536,1024]{1,0:T(8,128)(2,1)S(1)}) custom-call(s32[7]{0:T(128)S(1)} %stack.33.refs_0_, bf16[1,272,384]{2,1,0:T(8,128)(2,1)S(1)} %collective-permute-done.5.refs_1_.refs_14_, bf16[2,128,384]{2,1,0:T(8,128)(2,1)S(1)} %collective-permute-done.6.refs_2_, ...), custom_call_target="tpu_custom_call" | custom-call | flops 805306368 | bytes 3014656 | tf_op jit(solution)/shard_map/first_part/pallas_call | solution.py:305
  42.4 8.6 %second_part.2 = (bf16[2,2,256,384]{3,2,1,0:T(8,128)(2,1)S(1)}, bf16[2,2,256,384]{3,2,1,0:T(8,128)(2,1)S(1)}, bf16[2,2,256,384]{3,2,1,0:T(8,128)(2,1)S(1)}, bf16[2,2,256,384]{3,2,1,0:T(8,128)(2,1)S(1)}) custom-call(s32[7]{0:T(128)S(1)} %stack.33.refs_0_, bf16[1,256,384]{2,1,0:T(8,128)(2,1)S(1)} %collective-permute-done.4.refs_1_, ...), custom_call_target="tpu_custom_call" | custom-call | flops 1610612736 | bytes 5373952 | tf_op jit(solution)/shard_map/second_part/pallas_call | solution.py:332
  52.0 1.7 %collective-permute-done.30.refs_5_ = bf16[2,128,384]{2,1,0:T(8,128)(2,1)S(1)} collective-permute-done((bf16[2,128,384]{2,1,0:T(8,128)(2,1)S(1)}, bf16[2,128,384]{2,1,0:T(8,128)(2,1)S(1)}, u32[]{:S(2)}, u32[]{:S(2)}) %collective-permute-start.30) | collective-permute-done | bytes 196640 | tf_op jit(solution)/shard_map/ppermute | solution.py:67
  54.5 2.0 %collective-permute-start.32 = (bf16[2,1,256,384]{3,2,1,0:T(8,128)(2,1)S(1)}, bf16[2,1,256,384]{3,2,1,0:T(8,128)(2,1)S(1)}, u32[]{:S(2)}, u32[]{:S(2)}) collective-permute-start(bf16[2,1,256,384]{3,2,1,0:T(8,128)(2,1)S(1)} %add_convert_fusion.1), channel_id=1, source_target_pairs={{0,2},{1,3},{2,0},{3,1},{4,6},{5,7},{6,4},{7,5},{8,10},{9,11},{10,... | collective-permute-start | bytes 1179656 | tf_op jit(solution)/shard_map/ppermute | solution.py:67
  56.5 7.0 %second_part.3 = (bf16[2,2,256,384]{3,2,1,0:T(8,128)(2,1)S(1)}, bf16[2,2,256,384]{3,2,1,0:T(8,128)(2,1)S(1)}, bf16[512,1024]{1,0:T(8,128)(2,1)S(1)}, bf16[1024,1536]{1,0:T(8,128)(2,1)S(1)}) custom-call(s32[7]{0:T(128)S(1)} %stack.33.refs_0_, bf16[1,256,384]{2,1,0:T(8,128)(2,1)S(1)} %collective-permute-done.8.refs_1_, ...), custom_call_target="tpu_custom_call" | custom-call | flops 1610612736 | bytes 5373952 | tf_op jit(solution)/shard_map/second_part/pallas_call | solution.py:332
  63.5 2.4 %collective-permute-done.32 = bf16[2,1,256,384]{3,2,1,0:T(8,128)(2,1)S(1)} collective-permute-done((bf16[2,1,256,384]{3,2,1,0:T(8,128)(2,1)S(1)}, bf16[2,1,256,384]{3,2,1,0:T(8,128)(2,1)S(1)}, u32[]{:S(2)}, u32[]{:S(2)}) %collective-permute-start.32) | collective-permute-done | bytes 393248 | tf_op jit(solution)/shard_map/ppermute | solution.py:67
  65.9 2.4 %third_part.1 = (bf16[2,2,256,384]{3,2,1,0:T(8,128)(2,1)S(1)}, bf16[2,2,256,384]{3,2,1,0:T(8,128)(2,1)S(1)}) custom-call(s32[7]{0:T(128)S(1)} %stack.33.refs_0_, bf16[512,1024]{1,0:T(8,128)(2,1)S(1)} %get-tuple-element.131.refs_1_, bf16[1024,1536]{1,0:T(8,128)(2,1)S(1)} %get-tuple-element.132.refs_2_), custom_call_target="tpu_custom_call" | custom-call | flops 402653184 | bytes 1441792 | tf_op jit(solution)/shard_map/third_part/pallas_call | solution.py:361
  69.0 1.5 %collective-permute-start.37 = (bf16[2,128,384]{2,1,0:T(8,128)(2,1)S(1)}, bf16[2,128,384]{2,1,0:T(8,128)(2,1)S(1)}, u32[]{:S(2)}, u32[]{:S(2)}) collective-permute-start(bf16[2,128,384]{2,1,0:T(8,128)(2,1)S(1)} %get-tuple-element.154), channel_id=1, source_target_pairs={{0,16},{1,17},{2,18},{3,19},{4,20},{5,21},{6,22},{7,23},{8,24},{9,... | collective-permute-start | bytes 589832 | tf_op jit(solution)/shard_map/ppermute | solution.py:67
  71.6 1.8 %collective-permute-start.36 = (bf16[2,1,256,384]{3,2,1,0:T(8,128)(2,1)S(1)}, bf16[2,1,256,384]{3,2,1,0:T(8,128)(2,1)S(1)}, u32[]{:S(2)}, u32[]{:S(2)}) collective-permute-start(bf16[2,1,256,384]{3,2,1,0:T(8,128)(2,1)S(1)} %add_convert_fusion), channel_id=1, source_target_pairs={{0,2},{1,3},{2,0},{3,1},{4,6},{5,7},{6,4},{7,5},{8,10},{9,11},{10,... | collective-permute-start | bytes 1179656 | tf_op jit(solution)/shard_map/ppermute | solution.py:67
  73.4 2.5 %collective-permute-done.37 = bf16[2,128,384]{2,1,0:T(8,128)(2,1)S(1)} collective-permute-done((bf16[2,128,384]{2,1,0:T(8,128)(2,1)S(1)}, bf16[2,128,384]{2,1,0:T(8,128)(2,1)S(1)}, u32[]{:S(2)}, u32[]{:S(2)}) %collective-permute-start.37) | collective-permute-done | bytes 196640 | tf_op jit(solution)/shard_map/ppermute | solution.py:67
  75.8 1.1 %collective-permute-done.38 = bf16[2,128,384]{2,1,0:T(8,128)(2,1)S(1)} collective-permute-done((bf16[2,128,384]{2,1,0:T(8,128)(2,1)S(1)}, bf16[2,128,384]{2,1,0:T(8,128)(2,1)S(1)}, u32[]{:S(2)}, u32[]{:S(2)}) %collective-permute-start.38) | collective-permute-done | bytes 196640 | tf_op jit(solution)/shard_map/ppermute | solution.py:67
  78.0 1.1 %collective-permute-start.40 = (bf16[1,256,384]{2,1,0:T(8,128)(2,1)S(1)}, bf16[1,256,384]{2,1,0:T(8,128)(2,1)S(1)}, u32[]{:S(2)}, u32[]{:S(2)}) collective-permute-start(bf16[1,256,384]{2,1,0:T(8,128)(2,1)S(1)} %slice.209), channel_id=1, source_target_pairs={{0,1},{1,0},{2,3},{3,2},{4,5},{5,4},{6,7},{7,6},{8,9},{9,8},{10,11... | collective-permute-start | bytes 589832 | tf_op jit(solution)/shard_map/ppermute | solution.py:67
  79.1 3.7 %collective-permute-done.39 = bf16[1,256,384]{2,1,0:T(8,128)(2,1)S(1)} collective-permute-done((bf16[1,256,384]{2,1,0:T(8,128)(2,1)S(1)}, bf16[1,256,384]{2,1,0:T(8,128)(2,1)S(1)}, u32[]{:S(2)}, u32[]{:S(2)}) %collective-permute-start.39) | collective-permute-done | bytes 196640 | tf_op jit(solution)/shard_map/ppermute | solution.py:67
  83.8 1.8 %collective-permute-start.45 = (bf16[1,256,384]{2,1,0:T(8,128)(2,1)S(1)}, bf16[1,256,384]{2,1,0:T(8,128)(2,1)S(1)}, u32[]{:S(2)}, u32[]{:S(2)}) collective-permute-start(bf16[1,256,384]{2,1,0:T(8,128)(2,1)S(1)} %fusion.8), channel_id=1, source_target_pairs={{0,2},{1,3},{2,0},{3,1},{4,6},{5,7},{6,4},{7,5},{8,10},{9,11},{10,... | collective-permute-start | bytes 589832 | tf_op jit(solution)/shard_map/ppermute | solution.py:67
  85.6 1.5 %collective-permute-start.41 = (bf16[1,256,384]{2,1,0:T(8,128)(2,1)S(1)}, bf16[1,256,384]{2,1,0:T(8,128)(2,1)S(1)}, u32[]{:S(2)}, u32[]{:S(2)}) collective-permute-start(bf16[1,256,384]{2,1,0:T(8,128)(2,1)S(1)} %slice.189), channel_id=1, source_target_pairs={{0,16},{1,17},{2,18},{3,19},{4,20},{5,21},{6,22},{7,23},{8,24},{9,... | collective-permute-start | bytes 589832 | tf_op jit(solution)/shard_map/ppermute | solution.py:67
  87.1 1.1 %collective-permute-start.42 = (bf16[1,256,384]{2,1,0:T(8,128)(2,1)S(1)}, bf16[1,256,384]{2,1,0:T(8,128)(2,1)S(1)}, u32[]{:S(2)}, u32[]{:S(2)}) collective-permute-start(bf16[1,256,384]{2,1,0:T(8,128)(2,1)S(1)} %slice.190), channel_id=1, source_target_pairs={{0,1},{1,0},{2,3},{3,2},{4,5},{5,4},{6,7},{7,6},{8,9},{9,8},{10,11... | collective-permute-start | bytes 589832 | tf_op jit(solution)/shard_map/ppermute | solution.py:67
  90.0 1.4 %collective-permute-done.41 = bf16[1,256,384]{2,1,0:T(8,128)(2,1)S(1)} collective-permute-done((bf16[1,256,384]{2,1,0:T(8,128)(2,1)S(1)}, bf16[1,256,384]{2,1,0:T(8,128)(2,1)S(1)}, u32[]{:S(2)}, u32[]{:S(2)}) %collective-permute-start.41) | collective-permute-done | bytes 196640 | tf_op jit(solution)/shard_map/ppermute | solution.py:67
  91.4 1.5 %collective-permute-done.42 = bf16[1,256,384]{2,1,0:T(8,128)(2,1)S(1)} collective-permute-done((bf16[1,256,384]{2,1,0:T(8,128)(2,1)S(1)}, bf16[1,256,384]{2,1,0:T(8,128)(2,1)S(1)}, u32[]{:S(2)}, u32[]{:S(2)}) %collective-permute-start.42) | collective-permute-done | bytes 196640 | tf_op jit(solution)/shard_map/ppermute | solution.py:67
  93.0 1.3 %collective-permute-done.44 = bf16[1,128,384]{2,1,0:T(8,128)(2,1)S(1)} collective-permute-done((bf16[1,128,384]{2,1,0:T(8,128)(2,1)S(1)}, bf16[1,128,384]{2,1,0:T(8,128)(2,1)S(1)}, u32[]{:S(2)}, u32[]{:S(2)}) %collective-permute-start.44) | collective-permute-done | bytes 98336 | tf_op jit(solution)/shard_map/ppermute | solution.py:67
  96.5 2.5 %collective-permute-start.48 = (bf16[1,256,384]{2,1,0:T(8,128)(2,1)S(1)}, bf16[1,256,384]{2,1,0:T(8,128)(2,1)S(1)}, u32[]{:S(2)}, u32[]{:S(2)}) collective-permute-start(bf16[1,256,384]{2,1,0:T(8,128)(2,1)S(1)} %fusion.5), channel_id=1, source_target_pairs={{0,4},{1,5},{2,6},{3,7},{4,0},{5,1},{6,2},{7,3},{8,12},{9,13},{10,... | collective-permute-start | bytes 589832 | tf_op jit(solution)/shard_map/ppermute | solution.py:67
  101.1 3.9 %collective-permute-done.48 = bf16[1,256,384]{2,1,0:T(8,128)(2,1)S(1)} collective-permute-done((bf16[1,256,384]{2,1,0:T(8,128)(2,1)S(1)}, bf16[1,256,384]{2,1,0:T(8,128)(2,1)S(1)}, u32[]{:S(2)}, u32[]{:S(2)}) %collective-permute-start.48) | collective-permute-done | bytes 196640 | tf_op jit(solution)/shard_map/ppermute | solution.py:67
  (107 shorter events, 25.1 us)
Async XLA Ops:
  0.0 11.2 %collective-permute-start.1 = (bf16[1,256,384]{2,1,0:T(8,128)(2,1)}, bf16[1,256,384]{2,1,0:T(8,128)(2,1)S(1)}, u32[]{:S(2)}, u32[]{:S(2)}) collective-permute-start(bf16[1,256,384]{2,1,0:T(8,128)(2,1)} %bitcast.72), channel_id=1, source_target_pairs={{0,2},{1,3},{2,0},{3,1},{4,6},{5,7},{6,4},{7,5},{8,10},{9,11},{10,... | collective-permute-start | bytes 589832 | tf_op jit(solution)/shard_map/ppermute | solution.py:67
  5.5 8.7 %collective-permute-start.5 = (bf16[1,272,384]{2,1,0:T(8,128)(2,1)S(1)}, bf16[1,272,384]{2,1,0:T(8,128)(2,1)S(1)}, u32[]{:S(2)}, u32[]{:S(2)}) collective-permute-start(bf16[1,272,384]{2,1,0:T(8,128)(2,1)S(1)} %maximum_bitcast_fusion.refs_1_.refs_14_), channel_id=1, source_target_pairs={{0,16},{1,17},{2,18},{3,19},{4,20},{5,21},{6,22},{7,23},{8,24},{9,... | collective-permute-start | bytes 626696 | tf_op jit(solution)/shard_map/ppermute | solution.py:67
  7.0 7.1 %collective-permute-start = (bf16[1,256,384]{2,1,0:T(8,128)(2,1)}, bf16[1,256,384]{2,1,0:T(8,128)(2,1)S(1)}, u32[]{:S(2)}, u32[]{:S(2)}) collective-permute-start(bf16[1,256,384]{2,1,0:T(8,128)(2,1)} %bitcast.73), channel_id=1, source_target_pairs={{0,1},{1,0},{2,3},{3,2},{4,5},{5,4},{6,7},{7,6},{8,9},{9,8},{10,11... | collective-permute-start | bytes 589832 | tf_op jit(solution)/shard_map/ppermute | solution.py:67
  8.6 11.0 %collective-permute-start.4 = (bf16[1,256,384]{2,1,0:T(8,128)(2,1)}, bf16[1,256,384]{2,1,0:T(8,128)(2,1)S(1)}, u32[]{:S(2)}, u32[]{:S(2)}) collective-permute-start(bf16[1,256,384]{2,1,0:T(8,128)(2,1)} %bitcast.74), channel_id=1, source_target_pairs={{0,4},{1,5},{2,6},{3,7},{4,0},{5,1},{6,2},{7,3},{8,12},{9,13},{10,... | collective-permute-start | bytes 589832 | tf_op jit(solution)/shard_map/ppermute | solution.py:67
  11.2 8.5 %collective-permute-start.2 = (bf16[1,256,384]{2,1,0:T(8,128)(2,1)S(1)}, bf16[1,256,384]{2,1,0:T(8,128)(2,1)S(1)}, u32[]{:S(2)}, u32[]{:S(2)}) collective-permute-start(bf16[1,256,384]{2,1,0:T(8,128)(2,1)S(1)} %collective-permute-done.1.refs_5_), channel_id=1, source_target_pairs={{0,16},{1,17},{2,18},{3,19},{4,20},{5,21},{6,22},{7,23},{8,24},{9,... | collective-permute-start | bytes 589832 | tf_op jit(solution)/shard_map/ppermute | solution.py:67
  11.7 7.9 %collective-permute-start.3 = (bf16[1,256,384]{2,1,0:T(8,128)(2,1)S(1)}, bf16[1,256,384]{2,1,0:T(8,128)(2,1)S(1)}, u32[]{:S(2)}, u32[]{:S(2)}) collective-permute-start(bf16[1,256,384]{2,1,0:T(8,128)(2,1)S(1)} %collective-permute-done.1.refs_5_), channel_id=1, source_target_pairs={{0,1},{1,0},{2,3},{3,2},{4,5},{5,4},{6,7},{7,6},{8,9},{9,8},{10,11... | collective-permute-start | bytes 589832 | tf_op jit(solution)/shard_map/ppermute | solution.py:67
  14.1 6.2 %collective-permute-start.11 = (bf16[1,272,384]{2,1,0:T(8,128)(2,1)S(1)}, bf16[1,272,384]{2,1,0:T(8,128)(2,1)S(1)}, u32[]{:S(2)}, u32[]{:S(2)}) collective-permute-start(bf16[1,272,384]{2,1,0:T(8,128)(2,1)S(1)} %maximum_bitcast_fusion.refs_1_.refs_14_), channel_id=1, source_target_pairs={{0,8},{1,9},{2,10},{3,11},{4,12},{5,13},{6,14},{7,15},{8,0},{9,1},... | collective-permute-start | bytes 626696 | tf_op jit(solution)/shard_map/ppermute | solution.py:67
  14.1 6.8 %collective-permute-start.12 = (bf16[1,256,384]{2,1,0:T(8,128)(2,1)S(1)}, bf16[1,256,384]{2,1,0:T(8,128)(2,1)S(1)}, u32[]{:S(2)}, u32[]{:S(2)}) collective-permute-start(bf16[1,256,384]{2,1,0:T(8,128)(2,1)S(1)} %collective-permute-done.refs_2_), channel_id=1, source_target_pairs={{0,8},{1,9},{2,10},{3,11},{4,12},{5,13},{6,14},{7,15},{8,0},{9,1},... | collective-permute-start | bytes 589832 | tf_op jit(solution)/shard_map/ppermute | solution.py:67
  19.6 7.3 %collective-permute-start.10 = (bf16[1,256,384]{2,1,0:T(8,128)(2,1)S(1)}, bf16[1,256,384]{2,1,0:T(8,128)(2,1)S(1)}, u32[]{:S(2)}, u32[]{:S(2)}) collective-permute-start(bf16[1,256,384]{2,1,0:T(8,128)(2,1)S(1)} %collective-permute-done.4.refs_1_), channel_id=1, source_target_pairs={{0,2},{1,3},{2,0},{3,1},{4,6},{5,7},{6,4},{7,5},{8,10},{9,11},{10,... | collective-permute-start | bytes 589832 | tf_op jit(solution)/shard_map/ppermute | solution.py:67
  20.3 11.5 %collective-permute-start.8 = (bf16[1,256,384]{2,1,0:T(8,128)(2,1)S(1)}, bf16[1,256,384]{2,1,0:T(8,128)(2,1)S(1)}, u32[]{:S(2)}, u32[]{:S(2)}) collective-permute-start(bf16[1,256,384]{2,1,0:T(8,128)(2,1)S(1)} %collective-permute-done.4.refs_1_), channel_id=1, source_target_pairs={{0,16},{1,17},{2,18},{3,19},{4,20},{5,21},{6,22},{7,23},{8,24},{9,... | collective-permute-start | bytes 589832 | tf_op jit(solution)/shard_map/ppermute | solution.py:67
  21.0 10.3 %collective-permute-start.7 = (bf16[2,128,384]{2,1,0:T(8,128)(2,1)S(1)}, bf16[2,128,384]{2,1,0:T(8,128)(2,1)S(1)}, u32[]{:S(2)}, u32[]{:S(2)}) collective-permute-start(bf16[2,128,384]{2,1,0:T(8,128)(2,1)S(1)} %pad_maximum_fusion.1), channel_id=1, source_target_pairs={{0,1},{1,0},{2,3},{3,2},{4,5},{5,4},{6,7},{7,6},{8,9},{9,8},{10,11... | collective-permute-start | bytes 589832 | tf_op jit(solution)/shard_map/ppermute | solution.py:67
  21.5 10.4 %collective-permute-start.6 = (bf16[2,128,384]{2,1,0:T(8,128)(2,1)S(1)}, bf16[2,128,384]{2,1,0:T(8,128)(2,1)S(1)}, u32[]{:S(2)}, u32[]{:S(2)}) collective-permute-start(bf16[2,128,384]{2,1,0:T(8,128)(2,1)S(1)} %pad_maximum_fusion), channel_id=1, source_target_pairs={{0,16},{1,17},{2,18},{3,19},{4,20},{5,21},{6,22},{7,23},{8,24},{9,... | collective-permute-start | bytes 589832 | tf_op jit(solution)/shard_map/ppermute | solution.py:67
  23.4 8.4 %collective-permute-start.9 = (bf16[1,256,384]{2,1,0:T(8,128)(2,1)S(1)}, bf16[1,256,384]{2,1,0:T(8,128)(2,1)S(1)}, u32[]{:S(2)}, u32[]{:S(2)}) collective-permute-start(bf16[1,256,384]{2,1,0:T(8,128)(2,1)S(1)} %collective-permute-done.4.refs_1_), channel_id=1, source_target_pairs={{0,1},{1,0},{2,3},{3,2},{4,5},{5,4},{6,7},{7,6},{8,9},{9,8},{10,11... | collective-permute-start | bytes 589832 | tf_op jit(solution)/shard_map/ppermute | solution.py:67
  26.9 6.8 %collective-permute-start.17 = (bf16[1,272,384]{2,1,0:T(8,128)(2,1)S(1)}, bf16[1,272,384]{2,1,0:T(8,128)(2,1)S(1)}, u32[]{:S(2)}, u32[]{:S(2)}) collective-permute-start(bf16[1,272,384]{2,1,0:T(8,128)(2,1)S(1)} %collective-permute-done.5.refs_1_.refs_14_), channel_id=1, source_target_pairs={{0,8},{1,9},{2,10},{3,11},{4,12},{5,13},{6,14},{7,15},{8,0},{9,1},... | collective-permute-start | bytes 626696 | tf_op jit(solution)/shard_map/ppermute | solution.py:67
  32.4 7.4 %collective-permute-start.15 = (bf16[1,256,384]{2,1,0:T(8,128)(2,1)S(1)}, bf16[1,256,384]{2,1,0:T(8,128)(2,1)S(1)}, u32[]{:S(2)}, u32[]{:S(2)}) collective-permute-start(bf16[1,256,384]{2,1,0:T(8,128)(2,1)S(1)} %collective-permute-done.10.refs_5_), channel_id=1, source_target_pairs={{0,16},{1,17},{2,18},{3,19},{4,20},{5,21},{6,22},{7,23},{8,24},{9,... | collective-permute-start | bytes 589832 | tf_op jit(solution)/shard_map/ppermute | solution.py:67
  33.7 6.6 %collective-permute-start.16 = (bf16[1,256,384]{2,1,0:T(8,128)(2,1)S(1)}, bf16[1,256,384]{2,1,0:T(8,128)(2,1)S(1)}, u32[]{:S(2)}, u32[]{:S(2)}) collective-permute-start(bf16[1,256,384]{2,1,0:T(8,128)(2,1)S(1)} %collective-permute-done.10.refs_5_), channel_id=1, source_target_pairs={{0,1},{1,0},{2,3},{3,2},{4,5},{5,4},{6,7},{7,6},{8,9},{9,8},{10,11... | collective-permute-start | bytes 589832 | tf_op jit(solution)/shard_map/ppermute | solution.py:67
  34.8 5.7 %collective-permute-start.25 = (bf16[1,256,384]{2,1,0:T(8,128)(2,1)S(1)}, bf16[1,256,384]{2,1,0:T(8,128)(2,1)S(1)}, u32[]{:S(2)}, u32[]{:S(2)}) collective-permute-start(bf16[1,256,384]{2,1,0:T(8,128)(2,1)S(1)} %collective-permute-done.4.refs_1_), channel_id=1, source_target_pairs={{0,8},{1,9},{2,10},{3,11},{4,12},{5,13},{6,14},{7,15},{8,0},{9,1},... | collective-permute-start | bytes 589832 | tf_op jit(solution)/shard_map/ppermute | solution.py:67
  34.9 6.7 %collective-permute-start.26 = (bf16[1,256,384]{2,1,0:T(8,128)(2,1)S(1)}, bf16[1,256,384]{2,1,0:T(8,128)(2,1)S(1)}, u32[]{:S(2)}, u32[]{:S(2)}) collective-permute-start(bf16[1,256,384]{2,1,0:T(8,128)(2,1)S(1)} %collective-permute-done.9.refs_2_), channel_id=1, source_target_pairs={{0,8},{1,9},{2,10},{3,11},{4,12},{5,13},{6,14},{7,15},{8,0},{9,1},... | collective-permute-start | bytes 589832 | tf_op jit(solution)/shard_map/ppermute | solution.py:67
  35.4 7.0 %collective-permute-start.27 = (bf16[1,256,384]{2,1,0:T(8,128)(2,1)S(1)}, bf16[1,256,384]{2,1,0:T(8,128)(2,1)S(1)}, u32[]{:S(2)}, u32[]{:S(2)}) collective-permute-start(bf16[1,256,384]{2,1,0:T(8,128)(2,1)S(1)} %collective-permute-done.10.refs_5_), channel_id=1, source_target_pairs={{0,8},{1,9},{2,10},{3,11},{4,12},{5,13},{6,14},{7,15},{8,0},{9,1},... | collective-permute-start | bytes 589832 | tf_op jit(solution)/shard_map/ppermute | solution.py:67
  39.9 11.1 %collective-permute-start.23 = (bf16[1,256,384]{2,1,0:T(8,128)(2,1)S(1)}, bf16[1,256,384]{2,1,0:T(8,128)(2,1)S(1)}, u32[]{:S(2)}, u32[]{:S(2)}) collective-permute-start(bf16[1,256,384]{2,1,0:T(8,128)(2,1)S(1)} %collective-permute-done.8.refs_1_), channel_id=1, source_target_pairs={{0,8},{1,9},{2,10},{3,11},{4,12},{5,13},{6,14},{7,15},{8,0},{9,1},... | collective-permute-start | bytes 589832 | tf_op jit(solution)/shard_map/ppermute | solution.py:67
  40.6 10.4 %collective-permute-start.22 = (bf16[2,128,384]{2,1,0:T(8,128)(2,1)S(1)}, bf16[2,128,384]{2,1,0:T(8,128)(2,1)S(1)}, u32[]{:S(2)}, u32[]{:S(2)}) collective-permute-start(bf16[2,128,384]{2,1,0:T(8,128)(2,1)S(1)} %pad_maximum_fusion.3), channel_id=1, source_target_pairs={{0,1},{1,0},{2,3},{3,2},{4,5},{5,4},{6,7},{7,6},{8,9},{9,8},{10,11... | collective-permute-start | bytes 589832 | tf_op jit(solution)/shard_map/ppermute | solution.py:67
  41.6 9.3 %collective-permute-start.21 = (bf16[2,128,384]{2,1,0:T(8,128)(2,1)S(1)}, bf16[2,128,384]{2,1,0:T(8,128)(2,1)S(1)}, u32[]{:S(2)}, u32[]{:S(2)}) collective-permute-start(bf16[2,128,384]{2,1,0:T(8,128)(2,1)S(1)} %pad_maximum_fusion.2), channel_id=1, source_target_pairs={{0,16},{1,17},{2,18},{3,19},{4,20},{5,21},{6,22},{7,23},{8,24},{9,... | collective-permute-start | bytes 589832 | tf_op jit(solution)/shard_map/ppermute | solution.py:67
  42.3 8.6 %collective-permute-start.24 = (bf16[1,256,384]{2,1,0:T(8,128)(2,1)S(1)}, bf16[1,256,384]{2,1,0:T(8,128)(2,1)S(1)}, u32[]{:S(2)}, u32[]{:S(2)}) collective-permute-start(bf16[1,256,384]{2,1,0:T(8,128)(2,1)S(1)} %collective-permute-done.15.refs_7_), channel_id=1, source_target_pairs={{0,8},{1,9},{2,10},{3,11},{4,12},{5,13},{6,14},{7,15},{8,0},{9,1},... | collective-permute-start | bytes 589832 | tf_op jit(solution)/shard_map/ppermute | solution.py:67
  54.0 11.9 %collective-permute-start.33 = (bf16[2,2,256,384]{3,2,1,0:T(8,128)(2,1)S(1)}, bf16[2,2,256,384]{3,2,1,0:T(8,128)(2,1)S(1)}, u32[]{:S(2)}, u32[]{:S(2)}) collective-permute-start(bf16[2,2,256,384]{3,2,1,0:T(8,128)(2,1)S(1)} %get-tuple-element.115), channel_id=1, source_target_pairs={{0,8},{1,9},{2,10},{3,11},{4,12},{5,13},{6,14},{7,15},{8,0},{9,1},... | collective-permute-start | bytes 2359304 | tf_op jit(solution)/shard_map/ppermute | solution.py:67
  54.5 11.4 %collective-permute-start.32 = (bf16[2,1,256,384]{3,2,1,0:T(8,128)(2,1)S(1)}, bf16[2,1,256,384]{3,2,1,0:T(8,128)(2,1)S(1)}, u32[]{:S(2)}, u32[]{:S(2)}) collective-permute-start(bf16[2,1,256,384]{3,2,1,0:T(8,128)(2,1)S(1)} %add_convert_fusion.1), channel_id=1, source_target_pairs={{0,2},{1,3},{2,0},{3,1},{4,6},{5,7},{6,4},{7,5},{8,10},{9,11},{10,... | collective-permute-start | bytes 1179656 | tf_op jit(solution)/shard_map/ppermute | solution.py:67
  69.0 6.9 %collective-permute-start.37 = (bf16[2,128,384]{2,1,0:T(8,128)(2,1)S(1)}, bf16[2,128,384]{2,1,0:T(8,128)(2,1)S(1)}, u32[]{:S(2)}, u32[]{:S(2)}) collective-permute-start(bf16[2,128,384]{2,1,0:T(8,128)(2,1)S(1)} %get-tuple-element.154), channel_id=1, source_target_pairs={{0,16},{1,17},{2,18},{3,19},{4,20},{5,21},{6,22},{7,23},{8,24},{9,... | collective-permute-start | bytes 589832 | tf_op jit(solution)/shard_map/ppermute | solution.py:67
  70.4 6.5 %collective-permute-start.38 = (bf16[2,128,384]{2,1,0:T(8,128)(2,1)S(1)}, bf16[2,128,384]{2,1,0:T(8,128)(2,1)S(1)}, u32[]{:S(2)}, u32[]{:S(2)}) collective-permute-start(bf16[2,128,384]{2,1,0:T(8,128)(2,1)S(1)} %get-tuple-element.153), channel_id=1, source_target_pairs={{0,1},{1,0},{2,3},{3,2},{4,5},{5,4},{6,7},{7,6},{8,9},{9,8},{10,11... | collective-permute-start | bytes 589832 | tf_op jit(solution)/shard_map/ppermute | solution.py:67
  71.6 16.6 %collective-permute-start.36 = (bf16[2,1,256,384]{3,2,1,0:T(8,128)(2,1)S(1)}, bf16[2,1,256,384]{3,2,1,0:T(8,128)(2,1)S(1)}, u32[]{:S(2)}, u32[]{:S(2)}) collective-permute-start(bf16[2,1,256,384]{3,2,1,0:T(8,128)(2,1)S(1)} %add_convert_fusion), channel_id=1, source_target_pairs={{0,2},{1,3},{2,0},{3,1},{4,6},{5,7},{6,4},{7,5},{8,10},{9,11},{10,... | collective-permute-start | bytes 1179656 | tf_op jit(solution)/shard_map/ppermute | solution.py:67
  77.1 5.7 %collective-permute-start.39 = (bf16[1,256,384]{2,1,0:T(8,128)(2,1)S(1)}, bf16[1,256,384]{2,1,0:T(8,128)(2,1)S(1)}, u32[]{:S(2)}, u32[]{:S(2)}) collective-permute-start(bf16[1,256,384]{2,1,0:T(8,128)(2,1)S(1)} %slice.208), channel_id=1, source_target_pairs={{0,16},{1,17},{2,18},{3,19},{4,20},{5,21},{6,22},{7,23},{8,24},{9,... | collective-permute-start | bytes 589832 | tf_op jit(solution)/shard_map/ppermute | solution.py:67
  78.0 5.7 %collective-permute-start.40 = (bf16[1,256,384]{2,1,0:T(8,128)(2,1)S(1)}, bf16[1,256,384]{2,1,0:T(8,128)(2,1)S(1)}, u32[]{:S(2)}, u32[]{:S(2)}) collective-permute-start(bf16[1,256,384]{2,1,0:T(8,128)(2,1)S(1)} %slice.209), channel_id=1, source_target_pairs={{0,1},{1,0},{2,3},{3,2},{4,5},{5,4},{6,7},{7,6},{8,9},{9,8},{10,11... | collective-permute-start | bytes 589832 | tf_op jit(solution)/shard_map/ppermute | solution.py:67
  83.8 10.5 %collective-permute-start.45 = (bf16[1,256,384]{2,1,0:T(8,128)(2,1)S(1)}, bf16[1,256,384]{2,1,0:T(8,128)(2,1)S(1)}, u32[]{:S(2)}, u32[]{:S(2)}) collective-permute-start(bf16[1,256,384]{2,1,0:T(8,128)(2,1)S(1)} %fusion.8), channel_id=1, source_target_pairs={{0,2},{1,3},{2,0},{3,1},{4,6},{5,7},{6,4},{7,5},{8,10},{9,11},{10,... | collective-permute-start | bytes 589832 | tf_op jit(solution)/shard_map/ppermute | solution.py:67
  96.5 8.5 %collective-permute-start.48 = (bf16[1,256,384]{2,1,0:T(8,128)(2,1)S(1)}, bf16[1,256,384]{2,1,0:T(8,128)(2,1)S(1)}, u32[]{:S(2)}, u32[]{:S(2)}) collective-permute-start(bf16[1,256,384]{2,1,0:T(8,128)(2,1)S(1)} %fusion.5), channel_id=1, source_target_pairs={{0,4},{1,5},{2,6},{3,7},{4,0},{5,1},{6,2},{7,3},{8,12},{9,13},{10,... | collective-permute-start | bytes 589832 | tf_op jit(solution)/shard_map/ppermute | solution.py:67
  (17 other events, 63.7 us)

commit v3 on v2

--- a/solution.py
+++ b/solution.py
@@ -399,7 +399,7 @@
     own = shares_of(expert_ids, pair_logits)
     block = jnp.concatenate([tokens, share_rows(own, narrow)])[None]
     sent = after(z0, own)
-    x0, y0, z2 = send(block, x=1), send(sent, y=1), send(sent, z=2)
+    x0, y0, z2 = send(block, x=1), send(sent, y=1), send(z0, z=2)
     x1, y1 = send(z1, x=1), send(z1, y=1)
     sz0, sz1, sx0, sx1, sy0, sy1 = swapped(block, z1, x0, x1, y0, y1)
     near_weights = pair_weights(place, 0, w_gate, w_up, narrow, x0)
@@ -432,11 +432,10 @@
     far_0 = parts_0[0], send(parts_0[1], c=1)
     to_z = total(*[v[:, :1] for v in near_0]).astype(jnp.bfloat16)
     passed_0 = send(to_z, z=1)
-    sums_1 = after(sums_1, to_z)
     *parts_1, hidden, tile = second_part(
         place, 1, far, (2, 3), far_weights, sums_1, sx0, w_down, pairs
     )
-    passed_0, far_0, parts_1 = after((passed_0, far_0, parts_1))
+    far_0, parts_1 = after((far_0, parts_1))
     other_1 = send(parts_1[1], c=1)
     last_1 = third_part(place, after(hidden, far_0), tile, pairs[1], size)
     other_1, last_1 = after((other_1, last_1))
@@ -456,9 +455,9 @@
     last_block = lambda terms, passed: [v[:, 1:] for v in terms] + [passed]
     near = last_block(near_0, passed_0), last_block(near_1, passed_1)
     corner = diagonal(near)
-    from_2, corner = after((from_2, corner))
-    to_0 = send(total(here[1:], *from_2, to_2).astype(jnp.bfloat16), z=2)
-    to_x, to_y = plane_sums(near, *after(corner, to_2))
+    to_0 = total(here[1:], *from_2, to_2).astype(jnp.bfloat16)
+    to_x, to_y = plane_sums(near, *after(corner, to_0))
+    to_0 = send(to_0, z=2)
     from_0 = send(to_x, x=1), send(to_y, y=1)
     return total(summed(near, 0, 0), *from_0, to_0)[0].astype(jnp.bfloat16)
 

time: 106 us -> 101 us (0.953)
  waiting for transfers between devices: 28.7 us -> 25.5 us
  starting transfers between devices: 42.1 us -> 40.4 us
    ppermute x49, waiting for transfers between devices: 28.7 us -> 25.5 us  [send(): return lax.ppermute(value, BOTH, pairs)]
    ppermute x49, starting transfers between devices: 42.1 us -> 40.4 us  [send(): return lax.ppermute(value, BOTH, pairs)]
  transfers between devices with their start and end apart: 49 -> 49, of which waited for: 17 -> 13; matrix products, arithmetic and copies ran while one was open for 4% -> 4% of each run, Pallas kernels for 28% -> 30%
where the time goes in v3:
time: 101 us
  starting transfers between devices  40.4 us (40%)
  Pallas kernels  30.1 us (30%)
  waiting for transfers between devices  25.5 us (25%)
  other arithmetic  4.46 us (4%)
    ppermute x49, starting transfers between devices, send(): return lax.ppermute(value, BOTH, pairs)  40.4 us
    ppermute x49, waiting for transfers between devices, send(): return lax.ppermute(value, BOTH, pairs)  25.5 us
    pallas_call x2, Pallas kernels, second_part(): pl.pallas_call(lambda *refs: second_kernel(*refs, x=x, found=found, z_pla...  15.6 us
    pallas_call x2, Pallas kernels, first_part(): pl.pallas_call(lambda *refs: first_kernel(*refs, found=found, z_places=z_...  8.7 us
    pallas_call x1, Pallas kernels, pair_weights(): pl.pallas_call(lambda *refs: weights_kernel(*refs, z=z), in_specs=[SCALAR...  3.41 us
    pallas_call x1, Pallas kernels, third_part(): pl.pallas_call(lambda *refs: third_kernel(*refs, pair=pair), in_specs=[SC...  2.37 us
  transfers between devices with their start and end apart: 49, of which 13 were waited for; matrix products, arithmetic and copies ran while one was open for 4% of the time, Pallas kernels for 30%

profile of v3, /device:TPU:0, one launch (start us, length us, event | category | flops | bytes accessed | tf_op | source)
XLA Modules:
  0.0 101.0 jit_solution(4290891856536757085)
XLA Ops:
  0.0 3.0 %collective-permute-start.1 = (bf16[1,256,384]{2,1,0:T(8,128)(2,1)}, bf16[1,256,384]{2,1,0:T(8,128)(2,1)S(1)}, u32[]{:S(2)}, u32[]{:S(2)}) collective-permute-start(bf16[1,256,384]{2,1,0:T(8,128)(2,1)} %bitcast.72), channel_id=1, source_target_pairs={{0,2},{1,3},{2,0},{3,1},{4,6},{5,7},{6,4},{7,5},{8,10},{9,11},{10,... | collective-permute-start | bytes 589832 | tf_op jit(solution)/shard_map/ppermute | solution.py:67
  5.5 1.6 %collective-permute-start.5 = (bf16[1,272,384]{2,1,0:T(8,128)(2,1)S(1)}, bf16[1,272,384]{2,1,0:T(8,128)(2,1)S(1)}, u32[]{:S(2)}, u32[]{:S(2)}) collective-permute-start(bf16[1,272,384]{2,1,0:T(8,128)(2,1)S(1)} %maximum_bitcast_fusion.refs_1_.refs_14_), channel_id=1, source_target_pairs={{0,16},{1,17},{2,18},{3,19},{4,20},{5,21},{6,22},{7,23},{8,24},{9,... | collective-permute-start | bytes 626696 | tf_op jit(solution)/shard_map/ppermute | solution.py:67
  7.0 1.5 %collective-permute-start = (bf16[1,256,384]{2,1,0:T(8,128)(2,1)}, bf16[1,256,384]{2,1,0:T(8,128)(2,1)S(1)}, u32[]{:S(2)}, u32[]{:S(2)}) collective-permute-start(bf16[1,256,384]{2,1,0:T(8,128)(2,1)} %bitcast.73), channel_id=1, source_target_pairs={{0,1},{1,0},{2,3},{3,2},{4,5},{5,4},{6,7},{7,6},{8,9},{9,8},{10,11... | collective-permute-start | bytes 589832 | tf_op jit(solution)/shard_map/ppermute | solution.py:67
  8.6 2.6 %collective-permute-start.4 = (bf16[1,256,384]{2,1,0:T(8,128)(2,1)}, bf16[1,256,384]{2,1,0:T(8,128)(2,1)S(1)}, u32[]{:S(2)}, u32[]{:S(2)}) collective-permute-start(bf16[1,256,384]{2,1,0:T(8,128)(2,1)} %bitcast.74), channel_id=1, source_target_pairs={{0,4},{1,5},{2,6},{3,7},{4,0},{5,1},{6,2},{7,3},{8,12},{9,13},{10,... | collective-permute-start | bytes 589832 | tf_op jit(solution)/shard_map/ppermute | solution.py:67
  12.3 1.8 %collective-permute-done.refs_2_ = bf16[1,256,384]{2,1,0:T(8,128)(2,1)S(1)} collective-permute-done((bf16[1,256,384]{2,1,0:T(8,128)(2,1)}, bf16[1,256,384]{2,1,0:T(8,128)(2,1)S(1)}, u32[]{:S(2)}, u32[]{:S(2)}) %collective-permute-start) | collective-permute-done | bytes 196640 | tf_op jit(solution)/shard_map/ppermute | solution.py:67
  14.7 3.4 %pair_weights.1 = (bf16[1536,1024]{1,0:T(8,128)(2,1)S(1)}, bf16[1536,1024]{1,0:T(8,128)(2,1)S(1)}) custom-call(s32[7]{0:T(128)S(1)} %stack.33.refs_0_, bf16[1,272,384]{2,1,0:T(8,128)(2,1)S(1)} %collective-permute-done.5.refs_1_.refs_14_, bf16[3072,1024]{1,0:T(8,128)(2,1)} %bitcast.66, bf16[3072,1024]{1,0:T(8,128)(2,1)} %bitcast.68), custom_call_target="tpu_custom_call" | custom-call | bytes 3145728 | tf_op jit(solution)/shard_map/pair_weights/pallas_call | solution.py:287
  18.2 1.4 %collective-permute-done.4.refs_1_ = bf16[1,256,384]{2,1,0:T(8,128)(2,1)S(1)} collective-permute-done((bf16[1,256,384]{2,1,0:T(8,128)(2,1)}, bf16[1,256,384]{2,1,0:T(8,128)(2,1)S(1)}, u32[]{:S(2)}, u32[]{:S(2)}) %collective-permute-start.4) | collective-permute-done | bytes 196640 | tf_op jit(solution)/shard_map/ppermute | solution.py:67
  21.5 1.9 %collective-permute-start.6 = (bf16[2,128,384]{2,1,0:T(8,128)(2,1)S(1)}, bf16[2,128,384]{2,1,0:T(8,128)(2,1)S(1)}, u32[]{:S(2)}, u32[]{:S(2)}) collective-permute-start(bf16[2,128,384]{2,1,0:T(8,128)(2,1)S(1)} %pad_maximum_fusion), channel_id=1, source_target_pairs={{0,16},{1,17},{2,18},{3,19},{4,20},{5,21},{6,22},{7,23},{8,24},{9,... | collective-permute-start | bytes 589832 | tf_op jit(solution)/shard_map/ppermute | solution.py:67
  24.4 2.5 %collective-permute-done.10.refs_5_ = bf16[1,256,384]{2,1,0:T(8,128)(2,1)S(1)} collective-permute-done((bf16[1,256,384]{2,1,0:T(8,128)(2,1)S(1)}, bf16[1,256,384]{2,1,0:T(8,128)(2,1)S(1)}, u32[]{:S(2)}, u32[]{:S(2)}) %collective-permute-start.10) | collective-permute-done | bytes 196640 | tf_op jit(solution)/shard_map/ppermute | solution.py:67
  26.9 4.3 %first_part.2 = (f32[2,512,512]{2,1,0:T(8,128)S(1)}, f32[2,512,512]{2,1,0:T(8,128)S(1)}, bf16[1536,1024]{1,0:T(8,128)(2,1)S(1)}) custom-call(s32[7]{0:T(128)S(1)} %stack.33.refs_0_, bf16[1,272,384]{2,1,0:T(8,128)(2,1)S(1)} %maximum_bitcast_fusion.refs_1_.refs_14_, bf16[1,256,384]{2,1,0:T(8,128)(2,1)S(1)} %collective-permute-done.refs_2_, ...), custom_call_target="tpu_custom_call" | custom-call | flops 805306368 | bytes 3014656 | tf_op jit(solution)/shard_map/first_part/pallas_call | solution.py:305
  32.4 1.3 %collective-permute-start.15 = (bf16[1,256,384]{2,1,0:T(8,128)(2,1)S(1)}, bf16[1,256,384]{2,1,0:T(8,128)(2,1)S(1)}, u32[]{:S(2)}, u32[]{:S(2)}) collective-permute-start(bf16[1,256,384]{2,1,0:T(8,128)(2,1)S(1)} %collective-permute-done.10.refs_5_), channel_id=1, source_target_pairs={{0,16},{1,17},{2,18},{3,19},{4,20},{5,21},{6,22},{7,23},{8,24},{9,... | collective-permute-start | bytes 589832 | tf_op jit(solution)/shard_map/ppermute | solution.py:67
  35.5 4.4 %first_part.3 = (f32[2,512,512]{2,1,0:T(8,128)S(1)}, f32[2,512,512]{2,1,0:T(8,128)S(1)}, bf16[1536,1024]{1,0:T(8,128)(2,1)S(1)}) custom-call(s32[7]{0:T(128)S(1)} %stack.33.refs_0_, bf16[1,272,384]{2,1,0:T(8,128)(2,1)S(1)} %collective-permute-done.5.refs_1_.refs_14_, bf16[2,128,384]{2,1,0:T(8,128)(2,1)S(1)} %collective-permute-done.6.refs_2_, ...), custom_call_target="tpu_custom_call" | custom-call | flops 805306368 | bytes 3014656 | tf_op jit(solution)/shard_map/first_part/pallas_call | solution.py:305
  40.6 1.1 %collective-permute-start.22 = (bf16[2,128,384]{2,1,0:T(8,128)(2,1)S(1)}, bf16[2,128,384]{2,1,0:T(8,128)(2,1)S(1)}, u32[]{:S(2)}, u32[]{:S(2)}) collective-permute-start(bf16[2,128,384]{2,1,0:T(8,128)(2,1)S(1)} %pad_maximum_fusion.3), channel_id=1, source_target_pairs={{0,1},{1,0},{2,3},{3,2},{4,5},{5,4},{6,7},{7,6},{8,9},{9,8},{10,11... | collective-permute-start | bytes 589832 | tf_op jit(solution)/shard_map/ppermute | solution.py:67
  42.4 8.6 %second_part.2 = (bf16[2,2,256,384]{3,2,1,0:T(8,128)(2,1)S(1)}, bf16[2,2,256,384]{3,2,1,0:T(8,128)(2,1)S(1)}, bf16[2,2,256,384]{3,2,1,0:T(8,128)(2,1)S(1)}, bf16[2,2,256,384]{3,2,1,0:T(8,128)(2,1)S(1)}) custom-call(s32[7]{0:T(128)S(1)} %stack.33.refs_0_, bf16[1,256,384]{2,1,0:T(8,128)(2,1)S(1)} %collective-permute-done.4.refs_1_, ...), custom_call_target="tpu_custom_call" | custom-call | flops 1610612736 | bytes 5373952 | tf_op jit(solution)/shard_map/second_part/pallas_call | solution.py:332
  52.0 1.7 %collective-permute-done.30.refs_5_ = bf16[2,128,384]{2,1,0:T(8,128)(2,1)S(1)} collective-permute-done((bf16[2,128,384]{2,1,0:T(8,128)(2,1)S(1)}, bf16[2,128,384]{2,1,0:T(8,128)(2,1)S(1)}, u32[]{:S(2)}, u32[]{:S(2)}) %collective-permute-start.30) | collective-permute-done | bytes 196640 | tf_op jit(solution)/shard_map/ppermute | solution.py:67
  54.4 7.0 %second_part.3 = (bf16[2,2,256,384]{3,2,1,0:T(8,128)(2,1)S(1)}, bf16[2,2,256,384]{3,2,1,0:T(8,128)(2,1)S(1)}, bf16[512,1024]{1,0:T(8,128)(2,1)S(1)}, bf16[1024,1536]{1,0:T(8,128)(2,1)S(1)}) custom-call(s32[7]{0:T(128)S(1)} %stack.33.refs_0_, bf16[1,256,384]{2,1,0:T(8,128)(2,1)S(1)} %collective-permute-done.8.refs_1_, ...), custom_call_target="tpu_custom_call" | custom-call | flops 1610612736 | bytes 5373952 | tf_op jit(solution)/shard_map/second_part/pallas_call | solution.py:332
  61.6 2.4 %third_part.1 = (bf16[2,2,256,384]{3,2,1,0:T(8,128)(2,1)S(1)}, bf16[2,2,256,384]{3,2,1,0:T(8,128)(2,1)S(1)}) custom-call(s32[7]{0:T(128)S(1)} %stack.33.refs_0_, bf16[512,1024]{1,0:T(8,128)(2,1)S(1)} %get-tuple-element.121.refs_1_, bf16[1024,1536]{1,0:T(8,128)(2,1)S(1)} %get-tuple-element.122.refs_2_), custom_call_target="tpu_custom_call" | custom-call | flops 402653184 | bytes 1441792 | tf_op jit(solution)/shard_map/third_part/pallas_call | solution.py:361
  64.6 2.0 %collective-permute-start.32 = (bf16[2,1,256,384]{3,2,1,0:T(8,128)(2,1)S(1)}, bf16[2,1,256,384]{3,2,1,0:T(8,128)(2,1)S(1)}, u32[]{:S(2)}, u32[]{:S(2)}) collective-permute-start(bf16[2,1,256,384]{3,2,1,0:T(8,128)(2,1)S(1)} %add_convert_fusion.1), channel_id=1, source_target_pairs={{0,2},{1,3},{2,0},{3,1},{4,6},{5,7},{6,4},{7,5},{8,10},{9,11},{10,... | collective-permute-start | bytes 1179656 | tf_op jit(solution)/shard_map/ppermute | solution.py:67
  66.7 1.5 %collective-permute-start.39 = (bf16[2,128,384]{2,1,0:T(8,128)(2,1)S(1)}, bf16[2,128,384]{2,1,0:T(8,128)(2,1)S(1)}, u32[]{:S(2)}, u32[]{:S(2)}) collective-permute-start(bf16[2,128,384]{2,1,0:T(8,128)(2,1)S(1)} %get-tuple-element.140), channel_id=1, source_target_pairs={{0,16},{1,17},{2,18},{3,19},{4,20},{5,21},{6,22},{7,23},{8,24},{9,... | collective-permute-start | bytes 589832 | tf_op jit(solution)/shard_map/ppermute | solution.py:67
  69.3 4.0 %collective-permute-done.39 = bf16[2,128,384]{2,1,0:T(8,128)(2,1)S(1)} collective-permute-done((bf16[2,128,384]{2,1,0:T(8,128)(2,1)S(1)}, bf16[2,128,384]{2,1,0:T(8,128)(2,1)S(1)}, u32[]{:S(2)}, u32[]{:S(2)}) %collective-permute-start.39) | collective-permute-done | bytes 196640 | tf_op jit(solution)/shard_map/ppermute | solution.py:67
  73.4 1.1 %collective-permute-done.40 = bf16[2,128,384]{2,1,0:T(8,128)(2,1)S(1)} collective-permute-done((bf16[2,128,384]{2,1,0:T(8,128)(2,1)S(1)}, bf16[2,128,384]{2,1,0:T(8,128)(2,1)S(1)}, u32[]{:S(2)}, u32[]{:S(2)}) %collective-permute-start.40) | collective-permute-done | bytes 196640 | tf_op jit(solution)/shard_map/ppermute | solution.py:67
  75.5 1.1 %collective-permute-start.42 = (bf16[1,256,384]{2,1,0:T(8,128)(2,1)S(1)}, bf16[1,256,384]{2,1,0:T(8,128)(2,1)S(1)}, u32[]{:S(2)}, u32[]{:S(2)}) collective-permute-start(bf16[1,256,384]{2,1,0:T(8,128)(2,1)S(1)} %slice.215), channel_id=1, source_target_pairs={{0,1},{1,0},{2,3},{3,2},{4,5},{5,4},{6,7},{7,6},{8,9},{9,8},{10,11... | collective-permute-start | bytes 589832 | tf_op jit(solution)/shard_map/ppermute | solution.py:67
  76.7 3.7 %collective-permute-done.41 = bf16[1,256,384]{2,1,0:T(8,128)(2,1)S(1)} collective-permute-done((bf16[1,256,384]{2,1,0:T(8,128)(2,1)S(1)}, bf16[1,256,384]{2,1,0:T(8,128)(2,1)S(1)}, u32[]{:S(2)}, u32[]{:S(2)}) %collective-permute-start.41) | collective-permute-done | bytes 196640 | tf_op jit(solution)/shard_map/ppermute | solution.py:67
  81.7 1.5 %collective-permute-start.43 = (bf16[1,256,384]{2,1,0:T(8,128)(2,1)S(1)}, bf16[1,256,384]{2,1,0:T(8,128)(2,1)S(1)}, u32[]{:S(2)}, u32[]{:S(2)}) collective-permute-start(bf16[1,256,384]{2,1,0:T(8,128)(2,1)S(1)} %slice.197), channel_id=1, source_target_pairs={{0,16},{1,17},{2,18},{3,19},{4,20},{5,21},{6,22},{7,23},{8,24},{9,... | collective-permute-start | bytes 589832 | tf_op jit(solution)/shard_map/ppermute | solution.py:67
  83.2 1.1 %collective-permute-start.44 = (bf16[1,256,384]{2,1,0:T(8,128)(2,1)S(1)}, bf16[1,256,384]{2,1,0:T(8,128)(2,1)S(1)}, u32[]{:S(2)}, u32[]{:S(2)}) collective-permute-start(bf16[1,256,384]{2,1,0:T(8,128)(2,1)S(1)} %slice.198), channel_id=1, source_target_pairs={{0,1},{1,0},{2,3},{3,2},{4,5},{5,4},{6,7},{7,6},{8,9},{9,8},{10,11... | collective-permute-start | bytes 589832 | tf_op jit(solution)/shard_map/ppermute | solution.py:67
  85.1 1.4 %collective-permute-start.37 = (bf16[1,128,384]{2,1,0:T(8,128)(2,1)S(1)}, bf16[1,128,384]{2,1,0:T(8,128)(2,1)S(1)}, u32[]{:S(2)}, u32[]{:S(2)}) collective-permute-start(bf16[1,128,384]{2,1,0:T(8,128)(2,1)S(1)} %get-tuple-element.138), channel_id=1, source_target_pairs={{0,16},{1,17},{2,18},{3,19},{4,20},{5,21},{6,22},{7,23},{8,24},{9,... | collective-permute-start | bytes 294920 | tf_op jit(solution)/shard_map/ppermute | solution.py:67
  86.5 1.8 %collective-permute-done.43 = bf16[1,256,384]{2,1,0:T(8,128)(2,1)S(1)} collective-permute-done((bf16[1,256,384]{2,1,0:T(8,128)(2,1)S(1)}, bf16[1,256,384]{2,1,0:T(8,128)(2,1)S(1)}, u32[]{:S(2)}, u32[]{:S(2)}) %collective-permute-start.43) | collective-permute-done | bytes 196640 | tf_op jit(solution)/shard_map/ppermute | solution.py:67
  88.2 1.1 %collective-permute-start.38 = (bf16[1,128,384]{2,1,0:T(8,128)(2,1)S(1)}, bf16[1,128,384]{2,1,0:T(8,128)(2,1)S(1)}, u32[]{:S(2)}, u32[]{:S(2)}) collective-permute-start(bf16[1,128,384]{2,1,0:T(8,128)(2,1)S(1)} %get-tuple-element.137), channel_id=1, source_target_pairs={{0,1},{1,0},{2,3},{3,2},{4,5},{5,4},{6,7},{7,6},{8,9},{9,8},{10,11... | collective-permute-start | bytes 294920 | tf_op jit(solution)/shard_map/ppermute | solution.py:67
  90.1 2.9 %collective-permute-start.48 = (bf16[1,256,384]{2,1,0:T(8,128)(2,1)S(1)}, bf16[1,256,384]{2,1,0:T(8,128)(2,1)S(1)}, u32[]{:S(2)}, u32[]{:S(2)}) collective-permute-start(bf16[1,256,384]{2,1,0:T(8,128)(2,1)S(1)} %fusion.8), channel_id=1, source_target_pairs={{0,4},{1,5},{2,6},{3,7},{4,0},{5,1},{6,2},{7,3},{8,12},{9,13},{10,... | collective-permute-start | bytes 589832 | tf_op jit(solution)/shard_map/ppermute | solution.py:67
  93.1 1.2 %collective-permute-start.46 = (bf16[1,256,384]{2,1,0:T(8,128)(2,1)S(1)}, bf16[1,256,384]{2,1,0:T(8,128)(2,1)S(1)}, u32[]{:S(2)}, u32[]{:S(2)}) collective-permute-start(bf16[1,256,384]{2,1,0:T(8,128)(2,1)S(1)} %fusion.10), channel_id=1, source_target_pairs={{0,16},{1,17},{2,18},{3,19},{4,20},{5,21},{6,22},{7,23},{8,24},{9,... | collective-permute-start | bytes 589832 | tf_op jit(solution)/shard_map/ppermute | solution.py:67
  94.4 1.1 %collective-permute-start.47 = (bf16[1,256,384]{2,1,0:T(8,128)(2,1)S(1)}, bf16[1,256,384]{2,1,0:T(8,128)(2,1)S(1)}, u32[]{:S(2)}, u32[]{:S(2)}) collective-permute-start(bf16[1,256,384]{2,1,0:T(8,128)(2,1)S(1)} %fusion.9), channel_id=1, source_target_pairs={{0,1},{1,0},{2,3},{3,2},{4,5},{5,4},{6,7},{7,6},{8,9},{9,8},{10,11... | collective-permute-start | bytes 589832 | tf_op jit(solution)/shard_map/ppermute | solution.py:67
  95.5 4.7 %collective-permute-done.48 = bf16[1,256,384]{2,1,0:T(8,128)(2,1)S(1)} collective-permute-done((bf16[1,256,384]{2,1,0:T(8,128)(2,1)S(1)}, bf16[1,256,384]{2,1,0:T(8,128)(2,1)S(1)}, u32[]{:S(2)}, u32[]{:S(2)}) %collective-permute-start.48) | collective-permute-done | bytes 196640 | tf_op jit(solution)/shard_map/ppermute | solution.py:67
  (107 shorter events, 20.1 us)
Async XLA Ops:
  0.0 11.2 %collective-permute-start.1 = (bf16[1,256,384]{2,1,0:T(8,128)(2,1)}, bf16[1,256,384]{2,1,0:T(8,128)(2,1)S(1)}, u32[]{:S(2)}, u32[]{:S(2)}) collective-permute-start(bf16[1,256,384]{2,1,0:T(8,128)(2,1)} %bitcast.72), channel_id=1, source_target_pairs={{0,2},{1,3},{2,0},{3,1},{4,6},{5,7},{6,4},{7,5},{8,10},{9,11},{10,... | collective-permute-start | bytes 589832 | tf_op jit(solution)/shard_map/ppermute | solution.py:67
  5.5 8.7 %collective-permute-start.5 = (bf16[1,272,384]{2,1,0:T(8,128)(2,1)S(1)}, bf16[1,272,384]{2,1,0:T(8,128)(2,1)S(1)}, u32[]{:S(2)}, u32[]{:S(2)}) collective-permute-start(bf16[1,272,384]{2,1,0:T(8,128)(2,1)S(1)} %maximum_bitcast_fusion.refs_1_.refs_14_), channel_id=1, source_target_pairs={{0,16},{1,17},{2,18},{3,19},{4,20},{5,21},{6,22},{7,23},{8,24},{9,... | collective-permute-start | bytes 626696 | tf_op jit(solution)/shard_map/ppermute | solution.py:67
  7.0 7.1 %collective-permute-start = (bf16[1,256,384]{2,1,0:T(8,128)(2,1)}, bf16[1,256,384]{2,1,0:T(8,128)(2,1)S(1)}, u32[]{:S(2)}, u32[]{:S(2)}) collective-permute-start(bf16[1,256,384]{2,1,0:T(8,128)(2,1)} %bitcast.73), channel_id=1, source_target_pairs={{0,1},{1,0},{2,3},{3,2},{4,5},{5,4},{6,7},{7,6},{8,9},{9,8},{10,11... | collective-permute-start | bytes 589832 | tf_op jit(solution)/shard_map/ppermute | solution.py:67
  8.6 11.0 %collective-permute-start.4 = (bf16[1,256,384]{2,1,0:T(8,128)(2,1)}, bf16[1,256,384]{2,1,0:T(8,128)(2,1)S(1)}, u32[]{:S(2)}, u32[]{:S(2)}) collective-permute-start(bf16[1,256,384]{2,1,0:T(8,128)(2,1)} %bitcast.74), channel_id=1, source_target_pairs={{0,4},{1,5},{2,6},{3,7},{4,0},{5,1},{6,2},{7,3},{8,12},{9,13},{10,... | collective-permute-start | bytes 589832 | tf_op jit(solution)/shard_map/ppermute | solution.py:67
  11.2 8.5 %collective-permute-start.2 = (bf16[1,256,384]{2,1,0:T(8,128)(2,1)S(1)}, bf16[1,256,384]{2,1,0:T(8,128)(2,1)S(1)}, u32[]{:S(2)}, u32[]{:S(2)}) collective-permute-start(bf16[1,256,384]{2,1,0:T(8,128)(2,1)S(1)} %collective-permute-done.1.refs_5_), channel_id=1, source_target_pairs={{0,16},{1,17},{2,18},{3,19},{4,20},{5,21},{6,22},{7,23},{8,24},{9,... | collective-permute-start | bytes 589832 | tf_op jit(solution)/shard_map/ppermute | solution.py:67
  11.7 7.9 %collective-permute-start.3 = (bf16[1,256,384]{2,1,0:T(8,128)(2,1)S(1)}, bf16[1,256,384]{2,1,0:T(8,128)(2,1)S(1)}, u32[]{:S(2)}, u32[]{:S(2)}) collective-permute-start(bf16[1,256,384]{2,1,0:T(8,128)(2,1)S(1)} %collective-permute-done.1.refs_5_), channel_id=1, source_target_pairs={{0,1},{1,0},{2,3},{3,2},{4,5},{5,4},{6,7},{7,6},{8,9},{9,8},{10,11... | collective-permute-start | bytes 589832 | tf_op jit(solution)/shard_map/ppermute | solution.py:67
  14.1 6.8 %collective-permute-start.12 = (bf16[1,256,384]{2,1,0:T(8,128)(2,1)S(1)}, bf16[1,256,384]{2,1,0:T(8,128)(2,1)S(1)}, u32[]{:S(2)}, u32[]{:S(2)}) collective-permute-start(bf16[1,256,384]{2,1,0:T(8,128)(2,1)S(1)} %collective-permute-done.refs_2_), channel_id=1, source_target_pairs={{0,8},{1,9},{2,10},{3,11},{4,12},{5,13},{6,14},{7,15},{8,0},{9,1},... | collective-permute-start | bytes 589832 | tf_op jit(solution)/shard_map/ppermute | solution.py:67
  19.6 7.3 %collective-permute-start.10 = (bf16[1,256,384]{2,1,0:T(8,128)(2,1)S(1)}, bf16[1,256,384]{2,1,0:T(8,128)(2,1)S(1)}, u32[]{:S(2)}, u32[]{:S(2)}) collective-permute-start(bf16[1,256,384]{2,1,0:T(8,128)(2,1)S(1)} %collective-permute-done.4.refs_1_), channel_id=1, source_target_pairs={{0,2},{1,3},{2,0},{3,1},{4,6},{5,7},{6,4},{7,5},{8,10},{9,11},{10,... | collective-permute-start | bytes 589832 | tf_op jit(solution)/shard_map/ppermute | solution.py:67
  20.3 11.5 %collective-permute-start.8 = (bf16[1,256,384]{2,1,0:T(8,128)(2,1)S(1)}, bf16[1,256,384]{2,1,0:T(8,128)(2,1)S(1)}, u32[]{:S(2)}, u32[]{:S(2)}) collective-permute-start(bf16[1,256,384]{2,1,0:T(8,128)(2,1)S(1)} %collective-permute-done.4.refs_1_), channel_id=1, source_target_pairs={{0,16},{1,17},{2,18},{3,19},{4,20},{5,21},{6,22},{7,23},{8,24},{9,... | collective-permute-start | bytes 589832 | tf_op jit(solution)/shard_map/ppermute | solution.py:67
  21.0 10.3 %collective-permute-start.7 = (bf16[2,128,384]{2,1,0:T(8,128)(2,1)S(1)}, bf16[2,128,384]{2,1,0:T(8,128)(2,1)S(1)}, u32[]{:S(2)}, u32[]{:S(2)}) collective-permute-start(bf16[2,128,384]{2,1,0:T(8,128)(2,1)S(1)} %pad_maximum_fusion.1), channel_id=1, source_target_pairs={{0,1},{1,0},{2,3},{3,2},{4,5},{5,4},{6,7},{7,6},{8,9},{9,8},{10,11... | collective-permute-start | bytes 589832 | tf_op jit(solution)/shard_map/ppermute | solution.py:67
  21.5 10.4 %collective-permute-start.6 = (bf16[2,128,384]{2,1,0:T(8,128)(2,1)S(1)}, bf16[2,128,384]{2,1,0:T(8,128)(2,1)S(1)}, u32[]{:S(2)}, u32[]{:S(2)}) collective-permute-start(bf16[2,128,384]{2,1,0:T(8,128)(2,1)S(1)} %pad_maximum_fusion), channel_id=1, source_target_pairs={{0,16},{1,17},{2,18},{3,19},{4,20},{5,21},{6,22},{7,23},{8,24},{9,... | collective-permute-start | bytes 589832 | tf_op jit(solution)/shard_map/ppermute | solution.py:67
  23.4 8.4 %collective-permute-start.9 = (bf16[1,256,384]{2,1,0:T(8,128)(2,1)S(1)}, bf16[1,256,384]{2,1,0:T(8,128)(2,1)S(1)}, u32[]{:S(2)}, u32[]{:S(2)}) collective-permute-start(bf16[1,256,384]{2,1,0:T(8,128)(2,1)S(1)} %collective-permute-done.4.refs_1_), channel_id=1, source_target_pairs={{0,1},{1,0},{2,3},{3,2},{4,5},{5,4},{6,7},{7,6},{8,9},{9,8},{10,11... | collective-permute-start | bytes 589832 | tf_op jit(solution)/shard_map/ppermute | solution.py:67
  26.9 6.8 %collective-permute-start.17 = (bf16[1,272,384]{2,1,0:T(8,128)(2,1)S(1)}, bf16[1,272,384]{2,1,0:T(8,128)(2,1)S(1)}, u32[]{:S(2)}, u32[]{:S(2)}) collective-permute-start(bf16[1,272,384]{2,1,0:T(8,128)(2,1)S(1)} %collective-permute-done.5.refs_1_.refs_14_), channel_id=1, source_target_pairs={{0,8},{1,9},{2,10},{3,11},{4,12},{5,13},{6,14},{7,15},{8,0},{9,1},... | collective-permute-start | bytes 626696 | tf_op jit(solution)/shard_map/ppermute | solution.py:67
  32.4 7.4 %collective-permute-start.15 = (bf16[1,256,384]{2,1,0:T(8,128)(2,1)S(1)}, bf16[1,256,384]{2,1,0:T(8,128)(2,1)S(1)}, u32[]{:S(2)}, u32[]{:S(2)}) collective-permute-start(bf16[1,256,384]{2,1,0:T(8,128)(2,1)S(1)} %collective-permute-done.10.refs_5_), channel_id=1, source_target_pairs={{0,16},{1,17},{2,18},{3,19},{4,20},{5,21},{6,22},{7,23},{8,24},{9,... | collective-permute-start | bytes 589832 | tf_op jit(solution)/shard_map/ppermute | solution.py:67
  33.7 6.6 %collective-permute-start.16 = (bf16[1,256,384]{2,1,0:T(8,128)(2,1)S(1)}, bf16[1,256,384]{2,1,0:T(8,128)(2,1)S(1)}, u32[]{:S(2)}, u32[]{:S(2)}) collective-permute-start(bf16[1,256,384]{2,1,0:T(8,128)(2,1)S(1)} %collective-permute-done.10.refs_5_), channel_id=1, source_target_pairs={{0,1},{1,0},{2,3},{3,2},{4,5},{5,4},{6,7},{7,6},{8,9},{9,8},{10,11... | collective-permute-start | bytes 589832 | tf_op jit(solution)/shard_map/ppermute | solution.py:67
  34.9 6.7 %collective-permute-start.26 = (bf16[1,256,384]{2,1,0:T(8,128)(2,1)S(1)}, bf16[1,256,384]{2,1,0:T(8,128)(2,1)S(1)}, u32[]{:S(2)}, u32[]{:S(2)}) collective-permute-start(bf16[1,256,384]{2,1,0:T(8,128)(2,1)S(1)} %collective-permute-done.9.refs_2_), channel_id=1, source_target_pairs={{0,8},{1,9},{2,10},{3,11},{4,12},{5,13},{6,14},{7,15},{8,0},{9,1},... | collective-permute-start | bytes 589832 | tf_op jit(solution)/shard_map/ppermute | solution.py:67
  35.4 7.0 %collective-permute-start.27 = (bf16[1,256,384]{2,1,0:T(8,128)(2,1)S(1)}, bf16[1,256,384]{2,1,0:T(8,128)(2,1)S(1)}, u32[]{:S(2)}, u32[]{:S(2)}) collective-permute-start(bf16[1,256,384]{2,1,0:T(8,128)(2,1)S(1)} %collective-permute-done.10.refs_5_), channel_id=1, source_target_pairs={{0,8},{1,9},{2,10},{3,11},{4,12},{5,13},{6,14},{7,15},{8,0},{9,1},... | collective-permute-start | bytes 589832 | tf_op jit(solution)/shard_map/ppermute | solution.py:67
  39.9 11.1 %collective-permute-start.23 = (bf16[1,256,384]{2,1,0:T(8,128)(2,1)S(1)}, bf16[1,256,384]{2,1,0:T(8,128)(2,1)S(1)}, u32[]{:S(2)}, u32[]{:S(2)}) collective-permute-start(bf16[1,256,384]{2,1,0:T(8,128)(2,1)S(1)} %collective-permute-done.8.refs_1_), channel_id=1, source_target_pairs={{0,8},{1,9},{2,10},{3,11},{4,12},{5,13},{6,14},{7,15},{8,0},{9,1},... | collective-permute-start | bytes 589832 | tf_op jit(solution)/shard_map/ppermute | solution.py:67
  40.6 10.4 %collective-permute-start.22 = (bf16[2,128,384]{2,1,0:T(8,128)(2,1)S(1)}, bf16[2,128,384]{2,1,0:T(8,128)(2,1)S(1)}, u32[]{:S(2)}, u32[]{:S(2)}) collective-permute-start(bf16[2,128,384]{2,1,0:T(8,128)(2,1)S(1)} %pad_maximum_fusion.3), channel_id=1, source_target_pairs={{0,1},{1,0},{2,3},{3,2},{4,5},{5,4},{6,7},{7,6},{8,9},{9,8},{10,11... | collective-permute-start | bytes 589832 | tf_op jit(solution)/shard_map/ppermute | solution.py:67
  41.6 9.3 %collective-permute-start.21 = (bf16[2,128,384]{2,1,0:T(8,128)(2,1)S(1)}, bf16[2,128,384]{2,1,0:T(8,128)(2,1)S(1)}, u32[]{:S(2)}, u32[]{:S(2)}) collective-permute-start(bf16[2,128,384]{2,1,0:T(8,128)(2,1)S(1)} %pad_maximum_fusion.2), channel_id=1, source_target_pairs={{0,16},{1,17},{2,18},{3,19},{4,20},{5,21},{6,22},{7,23},{8,24},{9,... | collective-permute-start | bytes 589832 | tf_op jit(solution)/shard_map/ppermute | solution.py:67
  42.3 8.6 %collective-permute-start.24 = (bf16[1,256,384]{2,1,0:T(8,128)(2,1)S(1)}, bf16[1,256,384]{2,1,0:T(8,128)(2,1)S(1)}, u32[]{:S(2)}, u32[]{:S(2)}) collective-permute-start(bf16[1,256,384]{2,1,0:T(8,128)(2,1)S(1)} %collective-permute-done.15.refs_7_), channel_id=1, source_target_pairs={{0,8},{1,9},{2,10},{3,11},{4,12},{5,13},{6,14},{7,15},{8,0},{9,1},... | collective-permute-start | bytes 589832 | tf_op jit(solution)/shard_map/ppermute | solution.py:67
  54.0 7.4 %collective-permute-start.33 = (bf16[2,2,256,384]{3,2,1,0:T(8,128)(2,1)S(1)}, bf16[2,2,256,384]{3,2,1,0:T(8,128)(2,1)S(1)}, u32[]{:S(2)}, u32[]{:S(2)}) collective-permute-start(bf16[2,2,256,384]{3,2,1,0:T(8,128)(2,1)S(1)} %get-tuple-element.108), channel_id=1, source_target_pairs={{0,8},{1,9},{2,10},{3,11},{4,12},{5,13},{6,14},{7,15},{8,0},{9,1},... | collective-permute-start | bytes 2359304 | tf_op jit(solution)/shard_map/ppermute | solution.py:67
  64.6 29.7 %collective-permute-start.32 = (bf16[2,1,256,384]{3,2,1,0:T(8,128)(2,1)S(1)}, bf16[2,1,256,384]{3,2,1,0:T(8,128)(2,1)S(1)}, u32[]{:S(2)}, u32[]{:S(2)}) collective-permute-start(bf16[2,1,256,384]{3,2,1,0:T(8,128)(2,1)S(1)} %add_convert_fusion.1), channel_id=1, source_target_pairs={{0,2},{1,3},{2,0},{3,1},{4,6},{5,7},{6,4},{7,5},{8,10},{9,11},{10,... | collective-permute-start | bytes 1179656 | tf_op jit(solution)/shard_map/ppermute | solution.py:67
  66.7 6.7 %collective-permute-start.39 = (bf16[2,128,384]{2,1,0:T(8,128)(2,1)S(1)}, bf16[2,128,384]{2,1,0:T(8,128)(2,1)S(1)}, u32[]{:S(2)}, u32[]{:S(2)}) collective-permute-start(bf16[2,128,384]{2,1,0:T(8,128)(2,1)S(1)} %get-tuple-element.140), channel_id=1, source_target_pairs={{0,16},{1,17},{2,18},{3,19},{4,20},{5,21},{6,22},{7,23},{8,24},{9,... | collective-permute-start | bytes 589832 | tf_op jit(solution)/shard_map/ppermute | solution.py:67
  68.1 6.4 %collective-permute-start.40 = (bf16[2,128,384]{2,1,0:T(8,128)(2,1)S(1)}, bf16[2,128,384]{2,1,0:T(8,128)(2,1)S(1)}, u32[]{:S(2)}, u32[]{:S(2)}) collective-permute-start(bf16[2,128,384]{2,1,0:T(8,128)(2,1)S(1)} %get-tuple-element.139), channel_id=1, source_target_pairs={{0,1},{1,0},{2,3},{3,2},{4,5},{5,4},{6,7},{7,6},{8,9},{9,8},{10,11... | collective-permute-start | bytes 589832 | tf_op jit(solution)/shard_map/ppermute | solution.py:67
  69.3 15.7 %collective-permute-start.36 = (bf16[2,1,256,384]{3,2,1,0:T(8,128)(2,1)S(1)}, bf16[2,1,256,384]{3,2,1,0:T(8,128)(2,1)S(1)}, u32[]{:S(2)}, u32[]{:S(2)}) collective-permute-start(bf16[2,1,256,384]{3,2,1,0:T(8,128)(2,1)S(1)} %add_convert_fusion), channel_id=1, source_target_pairs={{0,2},{1,3},{2,0},{3,1},{4,6},{5,7},{6,4},{7,5},{8,10},{9,11},{10,... | collective-permute-start | bytes 1179656 | tf_op jit(solution)/shard_map/ppermute | solution.py:67
  81.3 8.7 %collective-permute-start.45 = (bf16[1,256,384]{2,1,0:T(8,128)(2,1)S(1)}, bf16[1,256,384]{2,1,0:T(8,128)(2,1)S(1)}, u32[]{:S(2)}, u32[]{:S(2)}) collective-permute-start(bf16[1,256,384]{2,1,0:T(8,128)(2,1)S(1)} %fusion.4), channel_id=1, source_target_pairs={{0,2},{1,3},{2,0},{3,1},{4,6},{5,7},{6,4},{7,5},{8,10},{9,11},{10,... | collective-permute-start | bytes 589832 | tf_op jit(solution)/shard_map/ppermute | solution.py:67
  81.7 6.5 %collective-permute-start.43 = (bf16[1,256,384]{2,1,0:T(8,128)(2,1)S(1)}, bf16[1,256,384]{2,1,0:T(8,128)(2,1)S(1)}, u32[]{:S(2)}, u32[]{:S(2)}) collective-permute-start(bf16[1,256,384]{2,1,0:T(8,128)(2,1)S(1)} %slice.197), channel_id=1, source_target_pairs={{0,16},{1,17},{2,18},{3,19},{4,20},{5,21},{6,22},{7,23},{8,24},{9,... | collective-permute-start | bytes 589832 | tf_op jit(solution)/shard_map/ppermute | solution.py:67
  83.2 6.8 %collective-permute-start.44 = (bf16[1,256,384]{2,1,0:T(8,128)(2,1)S(1)}, bf16[1,256,384]{2,1,0:T(8,128)(2,1)S(1)}, u32[]{:S(2)}, u32[]{:S(2)}) collective-permute-start(bf16[1,256,384]{2,1,0:T(8,128)(2,1)S(1)} %slice.198), channel_id=1, source_target_pairs={{0,1},{1,0},{2,3},{3,2},{4,5},{5,4},{6,7},{7,6},{8,9},{9,8},{10,11... | collective-permute-start | bytes 589832 | tf_op jit(solution)/shard_map/ppermute | solution.py:67
  85.1 7.9 %collective-permute-start.37 = (bf16[1,128,384]{2,1,0:T(8,128)(2,1)S(1)}, bf16[1,128,384]{2,1,0:T(8,128)(2,1)S(1)}, u32[]{:S(2)}, u32[]{:S(2)}) collective-permute-start(bf16[1,128,384]{2,1,0:T(8,128)(2,1)S(1)} %get-tuple-element.138), channel_id=1, source_target_pairs={{0,16},{1,17},{2,18},{3,19},{4,20},{5,21},{6,22},{7,23},{8,24},{9,... | collective-permute-start | bytes 294920 | tf_op jit(solution)/shard_map/ppermute | solution.py:67
  90.1 10.1 %collective-permute-start.48 = (bf16[1,256,384]{2,1,0:T(8,128)(2,1)S(1)}, bf16[1,256,384]{2,1,0:T(8,128)(2,1)S(1)}, u32[]{:S(2)}, u32[]{:S(2)}) collective-permute-start(bf16[1,256,384]{2,1,0:T(8,128)(2,1)S(1)} %fusion.8), channel_id=1, source_target_pairs={{0,4},{1,5},{2,6},{3,7},{4,0},{5,1},{6,2},{7,3},{8,12},{9,13},{10,... | collective-permute-start | bytes 589832 | tf_op jit(solution)/shard_map/ppermute | solution.py:67
  93.1 7.1 %collective-permute-start.46 = (bf16[1,256,384]{2,1,0:T(8,128)(2,1)S(1)}, bf16[1,256,384]{2,1,0:T(8,128)(2,1)S(1)}, u32[]{:S(2)}, u32[]{:S(2)}) collective-permute-start(bf16[1,256,384]{2,1,0:T(8,128)(2,1)S(1)} %fusion.10), channel_id=1, source_target_pairs={{0,16},{1,17},{2,18},{3,19},{4,20},{5,21},{6,22},{7,23},{8,24},{9,... | collective-permute-start | bytes 589832 | tf_op jit(solution)/shard_map/ppermute | solution.py:67
  (17 other events, 66.9 us)

commit v4 on v3

--- a/solution.py
+++ b/solution.py
@@ -90,7 +90,11 @@
     half = terms[0][0].shape[2] // 2
     first = summed(terms, 1, 1, slice(0, half)).astype(jnp.bfloat16)
     last = summed(terms, 1, 1, slice(half, 2 * half)).astype(jnp.bfloat16)
-    return send(first, x=1), send(last, y=1)
+    return first, last
+
+
+def across(halves):
+    return send(halves[0], x=1), send(halves[1], y=1)
 
 
 def plane_sums(terms, first, last):
@@ -110,7 +114,7 @@
 
 def pieces(x, pair):
     blocks, over_x, over_y, first, last = pair
-    size = blocks[1][0][0].shape[1]
+    size = blocks[0][0][0].shape[1]
     arrays, found = [], []
     for z in range(2):
         for c in range(2):
@@ -298,7 +302,7 @@
 
 def first_part(place, x, pair, z_places, weights, following, later):
     arrays, found = pieces(x, pair)
-    size, narrow = pair[0][1][0][0].shape[1:]
+    size, narrow = pair[0][0][0][0].shape[1:]
     depth, width = weights[0].shape
     rows = 2 * size
     sums = pltpu.VMEM((width // HIDDEN_TILE, rows, HIDDEN_TILE), jnp.float32)
@@ -324,7 +328,7 @@
 
 def second_part(place, x, pair, z_places, weights, sums, shares, w_down, pairs):
     arrays, found = pieces(x, pair)
-    size, narrow = pair[0][1][0][0].shape[1:]
+    size, narrow = pair[0][0][0][0].shape[1:]
     depth, width = weights[0].shape
     rows, tail = 2 * size, shares[0].shape[1] - size
     part = pltpu.VMEM((2, 2, size, narrow), jnp.bfloat16)
@@ -396,14 +400,12 @@
     w_gate, w_up, w_down = in_hbm(w_gate), in_hbm(w_up), in_hbm(w_down)
     z0 = tokens[None]
     z1 = send(z0, z=1)
-    own = shares_of(expert_ids, pair_logits)
-    block = jnp.concatenate([tokens, share_rows(own, narrow)])[None]
-    sent = after(z0, own)
-    x0, y0, z2 = send(block, x=1), send(sent, y=1), send(z0, z=2)
+    x0, y0, z2 = send(z0, x=1), send(z0, y=1), send(z0, z=2)
     x1, y1 = send(z1, x=1), send(z1, y=1)
-    sz0, sz1, sx0, sx1, sy0, sy1 = swapped(block, z1, x0, x1, y0, y1)
+    sz0, sz1, sx0, sx1, sy0, sy1 = swapped(z0, z1, x0, x1, y0, y1)
     near_weights = pair_weights(place, 0, w_gate, w_up, narrow, x0)
-    (x1_, y1_), z2, near_weights = after(((x1, y1), z2, near_weights))
+    tail = share_rows(shares_of(expert_ids, after(pair_logits, x0)), narrow)[None]
+    (x1_, y1_), z2, near_weights, tail = after(((x1, y1), z2, near_weights, tail))
     first, last = relayed([x0, x1_], [y0, y1_])
     z3 = send(z2, z=1)
     x2, y2 = send(z2, x=1), send(z2, y=1)
@@ -412,10 +414,11 @@
 
     z3, sums_0 = after((z3, sums_0))
     (first, last, x2, y2), sums_0 = after(((first, last, x2, y2), sums_0))
-    x3, y3 = send(z3, x=1), send(z3, y=1)
+    block = jnp.concatenate([z3, tail], axis=1)
+    x3, y3 = send(block, x=1), send(z3, y=1)
     both_of = lambda v: [(v, 0), (v, 1)]
     near[3:] = [both_of(v) for v in swapped(first, last)]
-    sz2, sz3, sx2, sy2 = swapped(z2, z3, x2, y2)
+    sz2, sz3, sx2, sy2 = swapped(z2, block, x2, y2)
     *sums_1, far_up = first_part(place, 1, near, (0, 1), near_weights, 2, w_up)
     far_weights = far_gate, far_up
     (x3, y3), sums_1 = after(((x3, y3), sums_1))
@@ -423,7 +426,7 @@
     sx3, sy3 = swapped(x3, y3)
     far = [[(sz2, 0), (sz3, 0)], [(sx2, 0), (sx3, 0)], [(sy2, 0), (sy3, 0)], None, None]
     pairs = (3, 2), (1, 0)
-    parts_0 = second_part(place, 0, far, (2, 3), far_weights, sums_0, sz0, w_down, pairs)
+    parts_0 = second_part(place, 0, far, (2, 3), far_weights, sums_0, sz3, w_down, pairs)
     (first, last, sx2, sx3), parts_0 = after(((first, last, sx2, sx3), parts_0))
     far[1] = [(sx2, 0), (sx3, 0)]
     far[3:] = [both_of(v) for v in swapped(first, last)]
@@ -431,31 +434,36 @@
     near_0, parts_0 = after((near_0, parts_0), far[3:])
     far_0 = parts_0[0], send(parts_0[1], c=1)
     to_z = total(*[v[:, :1] for v in near_0]).astype(jnp.bfloat16)
-    passed_0 = send(to_z, z=1)
     *parts_1, hidden, tile = second_part(
-        place, 1, far, (2, 3), far_weights, sums_1, sx0, w_down, pairs
-    )
+        place, 1, far, (2, 3), far_weights, sums_1, sx3, w_down, pairs
+    )
+    far_0, parts_1 = after((far_0, parts_1))
     far_0, parts_1 = after((far_0, parts_1))
     other_1 = send(parts_1[1], c=1)
     last_1 = third_part(place, after(hidden, far_0), tile, pairs[1], size)
     other_1, last_1 = after((other_1, last_1))
-    far_1, near_1 = (parts_1[0], other_1), (last_1[0], send(last_1[1], c=1))
-
-    far = far_0, far_1
-    corner = diagonal(far)
+    far = far_0, (parts_1[0], other_1)
+    near_1 = last_1[0], send(last_1[1], c=1)
+
+    passed_0 = send(to_z, z=1)
     to_z = total(*[v[:, :1] for v in near_1]).astype(jnp.bfloat16)
     passed_1 = send(to_z, z=1)
-    to_x, to_y = plane_sums(far, *after(corner, to_z))
-    from_3 = send(to_x[:1], x=1), send(to_y[:1], y=1)
-    here = summed(far, 0, 0)
-    to_2 = total(here[:1], *from_3).astype(jnp.bfloat16)
-    to_x, to_y = after((to_x, to_y), to_2)
+    block_3, block_2 = [[[v[:, i : i + 1] for v in terms] for terms in far] for i in range(2)]
+    corner_3 = across(diagonal(block_3))
+    halves = after(diagonal(block_2), to_z)
+    to_x, to_y = plane_sums(block_3, *after(corner_3, halves))
+    corner_2 = across(halves)
+    from_3 = send(to_x, x=1), send(to_y, y=1)
+    from_3, passed_0 = after((from_3, passed_0))
+    to_2 = total(summed(block_3, 0, 0), *from_3).astype(jnp.bfloat16)
+    to_x, to_y = plane_sums(block_2, *after(corner_2, to_2))
     to_2 = send(to_2, z=1)
-    from_2 = send(to_x[1:], x=1), send(to_y[1:], y=1)
+    from_2 = send(to_x, x=1), send(to_y, y=1)
     last_block = lambda terms, passed: [v[:, 1:] for v in terms] + [passed]
     near = last_block(near_0, passed_0), last_block(near_1, passed_1)
-    corner = diagonal(near)
-    to_0 = total(here[1:], *from_2, to_2).astype(jnp.bfloat16)
+    corner = across(diagonal(near))
+    from_2, passed_1 = after((from_2, passed_1))
+    to_0 = total(summed(block_2, 0, 0), *from_2, to_2).astype(jnp.bfloat16)
     to_x, to_y = plane_sums(near, *after(corner, to_0))
     to_0 = send(to_0, z=2)
     from_0 = send(to_x, x=1), send(to_y, y=1)

time: 101 us -> 104 us (1.030)
  starting transfers between devices: 40.4 us -> 42.9 us
    ppermute x49 -> x51, starting transfers between devices: 40.4 us -> 42.9 us  [send(): return lax.ppermute(value, BOTH, pairs)]
    ppermute x49 -> x51, waiting for transfers between devices: 25.5 us -> 26.4 us  [send(): return lax.ppermute(value, BOTH, pairs)]
  transfers between devices with their start and end apart: 49 -> 51, of which waited for: 13 -> 14; matrix products, arithmetic and copies ran while one was open for 4% -> 3% of each run, Pallas kernels for 30% -> 29%
where the time goes in v4:
time: 104 us; the launch traced here: 103 us
  starting transfers between devices  42.9 us (41%)
  Pallas kernels  30.1 us (29%)
  waiting for transfers between devices  26.4 us (25%)
  other arithmetic  3.49 us (3%)
    ppermute x51, starting transfers between devices, send(): return lax.ppermute(value, BOTH, pairs)  42.9 us
    ppermute x51, waiting for transfers between devices, send(): return lax.ppermute(value, BOTH, pairs)  26.4 us
    pallas_call x2, Pallas kernels, second_part(): pl.pallas_call(lambda *refs: second_kernel(*refs, x=x, found=found, z_pla...  15.6 us
    pallas_call x2, Pallas kernels, first_part(): pl.pallas_call(lambda *refs: first_kernel(*refs, found=found, z_places=z_...  8.7 us
    pallas_call x1, Pallas kernels, pair_weights(): pl.pallas_call(lambda *refs: weights_kernel(*refs, z=z), in_specs=[SCALAR...  3.41 us
    pallas_call x1, Pallas kernels, third_part(): pl.pallas_call(lambda *refs: third_kernel(*refs, pair=pair), in_specs=[SC...  2.37 us
  transfers between devices with their start and end apart: 51, of which 14 were waited for; matrix products, arithmetic and copies ran while one was open for 3% of the time, Pallas kernels for 29%

profile of v4, /device:TPU:0, one launch (start us, length us, event | category | flops | bytes accessed | tf_op | source)
XLA Modules:
  0.0 103.5 jit_solution(17076230524750243718)
XLA Ops:
  0.0 2.9 %collective-permute-start.5 = (bf16[1,256,384]{2,1,0:T(8,128)(2,1)}, bf16[1,256,384]{2,1,0:T(8,128)(2,1)S(1)}, u32[]{:S(2)}, u32[]{:S(2)}) collective-permute-start(bf16[1,256,384]{2,1,0:T(8,128)(2,1)} %bitcast.74), channel_id=1, source_target_pairs={{0,16},{1,17},{2,18},{3,19},{4,20},{5,21},{6,22},{7,23},{8,24},{9,... | collective-permute-start | bytes 589832 | tf_op jit(solution)/shard_map/ppermute | solution.py:67
  2.9 1.6 %collective-permute-start.1 = (bf16[1,256,384]{2,1,0:T(8,128)(2,1)}, bf16[1,256,384]{2,1,0:T(8,128)(2,1)S(1)}, u32[]{:S(2)}, u32[]{:S(2)}) collective-permute-start(bf16[1,256,384]{2,1,0:T(8,128)(2,1)} %bitcast.75), channel_id=1, source_target_pairs={{0,2},{1,3},{2,0},{3,1},{4,6},{5,7},{6,4},{7,5},{8,10},{9,11},{10,... | collective-permute-start | bytes 589832 | tf_op jit(solution)/shard_map/ppermute | solution.py:67
  4.5 2.6 %collective-permute-start.4 = (bf16[1,256,384]{2,1,0:T(8,128)(2,1)}, bf16[1,256,384]{2,1,0:T(8,128)(2,1)S(1)}, u32[]{:S(2)}, u32[]{:S(2)}) collective-permute-start(bf16[1,256,384]{2,1,0:T(8,128)(2,1)} %bitcast.76), channel_id=1, source_target_pairs={{0,4},{1,5},{2,6},{3,7},{4,0},{5,1},{6,2},{7,3},{8,12},{9,13},{10,... | collective-permute-start | bytes 589832 | tf_op jit(solution)/shard_map/ppermute | solution.py:67
  7.1 1.5 %collective-permute-start = (bf16[1,256,384]{2,1,0:T(8,128)(2,1)}, bf16[1,256,384]{2,1,0:T(8,128)(2,1)S(1)}, u32[]{:S(2)}, u32[]{:S(2)}) collective-permute-start(bf16[1,256,384]{2,1,0:T(8,128)(2,1)} %bitcast.77), channel_id=1, source_target_pairs={{0,1},{1,0},{2,3},{3,2},{4,5},{5,4},{6,7},{7,6},{8,9},{9,8},{10,11... | collective-permute-start | bytes 589832 | tf_op jit(solution)/shard_map/ppermute | solution.py:67
  10.2 3.4 %collective-permute-done.1.refs_5_ = bf16[1,256,384]{2,1,0:T(8,128)(2,1)S(1)} collective-permute-done((bf16[1,256,384]{2,1,0:T(8,128)(2,1)}, bf16[1,256,384]{2,1,0:T(8,128)(2,1)S(1)}, u32[]{:S(2)}, u32[]{:S(2)}) %collective-permute-start.1) | collective-permute-done | bytes 196640 | tf_op jit(solution)/shard_map/ppermute | solution.py:67
  14.0 1.7 %collective-permute-start.3 = (bf16[1,256,384]{2,1,0:T(8,128)(2,1)S(1)}, bf16[1,256,384]{2,1,0:T(8,128)(2,1)S(1)}, u32[]{:S(2)}, u32[]{:S(2)}) collective-permute-start(bf16[1,256,384]{2,1,0:T(8,128)(2,1)S(1)} %collective-permute-done.1.refs_5_), channel_id=1, source_target_pairs={{0,1},{1,0},{2,3},{3,2},{4,5},{5,4},{6,7},{7,6},{8,9},{9,8},{10,11... | collective-permute-start | bytes 589832 | tf_op jit(solution)/shard_map/ppermute | solution.py:67
  15.8 3.4 %pair_weights.1 = (bf16[1536,1024]{1,0:T(8,128)(2,1)S(1)}, bf16[1536,1024]{1,0:T(8,128)(2,1)S(1)}) custom-call(s32[7]{0:T(128)S(1)} %stack.32.refs_0_, bf16[1,256,384]{2,1,0:T(8,128)(2,1)S(1)} %collective-permute-done.5.refs_1_, bf16[3072,1024]{1,0:T(8,128)(2,1)} %bitcast.80, bf16[3072,1024]{1,0:T(8,128)(2,1)} %bitcast.82), custom_call_target="tpu_custom_call" | custom-call | bytes 3145728 | tf_op jit(solution)/shard_map/pair_weights/pallas_call | solution.py:291
  20.1 1.6 %collective-permute-start.8 = (bf16[1,256,384]{2,1,0:T(8,128)(2,1)S(1)}, bf16[1,256,384]{2,1,0:T(8,128)(2,1)S(1)}, u32[]{:S(2)}, u32[]{:S(2)}) collective-permute-start(bf16[1,256,384]{2,1,0:T(8,128)(2,1)S(1)} %collective-permute-done.4.refs_1_), channel_id=1, source_target_pairs={{0,16},{1,17},{2,18},{3,19},{4,20},{5,21},{6,22},{7,23},{8,24},{9,... | collective-permute-start | bytes 589832 | tf_op jit(solution)/shard_map/ppermute | solution.py:67
  22.2 1.4 %collective-permute-start.7 = (bf16[2,128,384]{2,1,0:T(8,128)(2,1)S(1)}, bf16[2,128,384]{2,1,0:T(8,128)(2,1)S(1)}, u32[]{:S(2)}, u32[]{:S(2)}) collective-permute-start(bf16[2,128,384]{2,1,0:T(8,128)(2,1)S(1)} %pad_maximum_fusion.1), channel_id=1, source_target_pairs={{0,1},{1,0},{2,3},{3,2},{4,5},{5,4},{6,7},{7,6},{8,9},{9,8},{10,11... | collective-permute-start | bytes 589832 | tf_op jit(solution)/shard_map/ppermute | solution.py:67
  24.2 4.3 %first_part.2 = (f32[2,512,512]{2,1,0:T(8,128)S(1)}, f32[2,512,512]{2,1,0:T(8,128)S(1)}, bf16[1536,1024]{1,0:T(8,128)(2,1)S(1)}) custom-call(s32[7]{0:T(128)S(1)} %stack.32.refs_0_, bf16[1,256,384]{2,1,0:T(8,128)(2,1)S(1)} %bitcast.79, bf16[1,256,384]{2,1,0:T(8,128)(2,1)S(1)} %collective-permute-done.refs_2_, ...), custom_call_target="tpu_custom_call" | custom-call | flops 805306368 | bytes 3014656 | tf_op jit(solution)/shard_map/first_part/pallas_call | solution.py:309
  28.6 3.0 %collective-permute-done.6.refs_2_ = bf16[2,128,384]{2,1,0:T(8,128)(2,1)S(1)} collective-permute-done((bf16[2,128,384]{2,1,0:T(8,128)(2,1)S(1)}, bf16[2,128,384]{2,1,0:T(8,128)(2,1)S(1)}, u32[]{:S(2)}, u32[]{:S(2)}) %collective-permute-start.6) | collective-permute-done | bytes 196640 | tf_op jit(solution)/shard_map/ppermute | solution.py:67
  31.6 1.5 %collective-permute-done.9.refs_2_ = bf16[1,256,384]{2,1,0:T(8,128)(2,1)S(1)} collective-permute-done((bf16[1,256,384]{2,1,0:T(8,128)(2,1)S(1)}, bf16[1,256,384]{2,1,0:T(8,128)(2,1)S(1)}, u32[]{:S(2)}, u32[]{:S(2)}) %collective-permute-start.9) | collective-permute-done | bytes 196640 | tf_op jit(solution)/shard_map/ppermute | solution.py:67
  33.6 1.6 %collective-permute-start.15 = (bf16[1,272,384]{2,1,0:T(8,128)(2,1)S(1)}, bf16[1,272,384]{2,1,0:T(8,128)(2,1)S(1)}, u32[]{:S(2)}, u32[]{:S(2)}) collective-permute-start(bf16[1,272,384]{2,1,0:T(8,128)(2,1)S(1)} %constant_dynamic-update-slice_fusion.refs_5_.refs_14_), channel_id=1, source_target_pairs={{0,16},{1,17},{2,18},{3,19},{4,20},{5,21},{6,22},{7,23},{8,24},{9,... | collective-permute-start | bytes 626696 | tf_op jit(solution)/shard_map/ppermute | solution.py:67
  35.2 1.5 %collective-permute-start.16 = (bf16[1,256,384]{2,1,0:T(8,128)(2,1)S(1)}, bf16[1,256,384]{2,1,0:T(8,128)(2,1)S(1)}, u32[]{:S(2)}, u32[]{:S(2)}) collective-permute-start(bf16[1,256,384]{2,1,0:T(8,128)(2,1)S(1)} %collective-permute-done.10), channel_id=1, source_target_pairs={{0,1},{1,0},{2,3},{3,2},{4,5},{5,4},{6,7},{7,6},{8,9},{9,8},{10,11... | collective-permute-start | bytes 589832 | tf_op jit(solution)/shard_map/ppermute | solution.py:67
  37.4 4.4 %first_part.3 = (f32[2,512,512]{2,1,0:T(8,128)S(1)}, f32[2,512,512]{2,1,0:T(8,128)S(1)}, bf16[1536,1024]{1,0:T(8,128)(2,1)S(1)}) custom-call(s32[7]{0:T(128)S(1)} %stack.32.refs_0_, bf16[1,256,384]{2,1,0:T(8,128)(2,1)S(1)} %collective-permute-done.5.refs_1_, bf16[2,128,384]{2,1,0:T(8,128)(2,1)S(1)} %collective-permute-done.6.refs_2_, ...), custom_call_target="tpu_custom_call" | custom-call | flops 805306368 | bytes 3014656 | tf_op jit(solution)/shard_map/first_part/pallas_call | solution.py:309
  44.6 8.6 %second_part.2 = (bf16[2,2,256,384]{3,2,1,0:T(8,128)(2,1)S(1)}, bf16[2,2,256,384]{3,2,1,0:T(8,128)(2,1)S(1)}, bf16[2,2,256,384]{3,2,1,0:T(8,128)(2,1)S(1)}, bf16[2,2,256,384]{3,2,1,0:T(8,128)(2,1)S(1)}) custom-call(s32[7]{0:T(128)S(1)} %stack.32.refs_0_, bf16[1,256,384]{2,1,0:T(8,128)(2,1)S(1)} %collective-permute-done.4.refs_1_, ...), custom_call_target="tpu_custom_call" | custom-call | flops 1610612736 | bytes 5373952 | tf_op jit(solution)/shard_map/second_part/pallas_call | solution.py:336
  53.9 2.0 %collective-permute-done.30.refs_5_ = bf16[2,128,384]{2,1,0:T(8,128)(2,1)S(1)} collective-permute-done((bf16[2,128,384]{2,1,0:T(8,128)(2,1)S(1)}, bf16[2,128,384]{2,1,0:T(8,128)(2,1)S(1)}, u32[]{:S(2)}, u32[]{:S(2)}) %collective-permute-start.30) | collective-permute-done | bytes 196640 | tf_op jit(solution)/shard_map/ppermute | solution.py:67
  56.3 7.0 %second_part.3 = (bf16[2,2,256,384]{3,2,1,0:T(8,128)(2,1)S(1)}, bf16[2,2,256,384]{3,2,1,0:T(8,128)(2,1)S(1)}, bf16[512,1024]{1,0:T(8,128)(2,1)S(1)}, bf16[1024,1536]{1,0:T(8,128)(2,1)S(1)}) custom-call(s32[7]{0:T(128)S(1)} %stack.32.refs_0_, bf16[1,256,384]{2,1,0:T(8,128)(2,1)S(1)} %collective-permute-done.8.refs_1_, ...), custom_call_target="tpu_custom_call" | custom-call | flops 1610612736 | bytes 5373952 | tf_op jit(solution)/shard_map/second_part/pallas_call | solution.py:336
  63.8 2.4 %third_part.1 = (bf16[2,2,256,384]{3,2,1,0:T(8,128)(2,1)S(1)}, bf16[2,2,256,384]{3,2,1,0:T(8,128)(2,1)S(1)}) custom-call(s32[7]{0:T(128)S(1)} %stack.32.refs_0_, bf16[512,1024]{1,0:T(8,128)(2,1)S(1)} %get-tuple-element.131.refs_1_, bf16[1024,1536]{1,0:T(8,128)(2,1)S(1)} %get-tuple-element.132.refs_2_), custom_call_target="tpu_custom_call" | custom-call | flops 402653184 | bytes 1441792 | tf_op jit(solution)/shard_map/third_part/pallas_call | solution.py:365
  66.4 2.1 %collective-permute-start.39 = (bf16[2,1,256,384]{3,2,1,0:T(8,128)(2,1)S(1)}, bf16[2,1,256,384]{3,2,1,0:T(8,128)(2,1)S(1)}, u32[]{:S(2)}, u32[]{:S(2)}) collective-permute-start(bf16[2,1,256,384]{3,2,1,0:T(8,128)(2,1)S(1)} %add_convert_fusion), channel_id=1, source_target_pairs={{0,2},{1,3},{2,0},{3,1},{4,6},{5,7},{6,4},{7,5},{8,10},{9,11},{10,... | collective-permute-start | bytes 1179656 | tf_op jit(solution)/shard_map/ppermute | solution.py:67
  68.6 1.6 %collective-permute-start.34 = (bf16[1,128,384]{2,1,0:T(8,128)(2,1)S(1)}, bf16[1,128,384]{2,1,0:T(8,128)(2,1)S(1)}, u32[]{:S(2)}, u32[]{:S(2)}) collective-permute-start(bf16[1,128,384]{2,1,0:T(8,128)(2,1)S(1)} %get-tuple-element.158), channel_id=1, source_target_pairs={{0,16},{1,17},{2,18},{3,19},{4,20},{5,21},{6,22},{7,23},{8,24},{9,... | collective-permute-start | bytes 294920 | tf_op jit(solution)/shard_map/ppermute | solution.py:67
  71.3 2.2 %collective-permute-done.34 = bf16[1,128,384]{2,1,0:T(8,128)(2,1)S(1)} collective-permute-done((bf16[1,128,384]{2,1,0:T(8,128)(2,1)S(1)}, bf16[1,128,384]{2,1,0:T(8,128)(2,1)S(1)}, u32[]{:S(2)}, u32[]{:S(2)}) %collective-permute-start.34) | collective-permute-done | bytes 98336 | tf_op jit(solution)/shard_map/ppermute | solution.py:67
  73.5 1.3 %collective-permute-done.35 = bf16[1,128,384]{2,1,0:T(8,128)(2,1)S(1)} collective-permute-done((bf16[1,128,384]{2,1,0:T(8,128)(2,1)S(1)}, bf16[1,128,384]{2,1,0:T(8,128)(2,1)S(1)}, u32[]{:S(2)}, u32[]{:S(2)}) %collective-permute-start.35) | collective-permute-done | bytes 98336 | tf_op jit(solution)/shard_map/ppermute | solution.py:67
  76.8 1.5 %collective-permute-start.43 = (bf16[1,128,384]{2,1,0:T(8,128)(2,1)S(1)}, bf16[1,128,384]{2,1,0:T(8,128)(2,1)S(1)}, u32[]{:S(2)}, u32[]{:S(2)}) collective-permute-start(bf16[1,128,384]{2,1,0:T(8,128)(2,1)S(1)} %get-tuple-element.138), channel_id=1, source_target_pairs={{0,16},{1,17},{2,18},{3,19},{4,20},{5,21},{6,22},{7,23},{8,24},{9,... | collective-permute-start | bytes 294920 | tf_op jit(solution)/shard_map/ppermute | solution.py:67
  79.5 1.3 %collective-permute-done.38 = bf16[1,256,384]{2,1,0:T(8,128)(2,1)S(1)} collective-permute-done((bf16[1,256,384]{2,1,0:T(8,128)(2,1)S(1)}, bf16[1,256,384]{2,1,0:T(8,128)(2,1)S(1)}, u32[]{:S(2)}, u32[]{:S(2)}) %collective-permute-start.38) | collective-permute-done | bytes 196640 | tf_op jit(solution)/shard_map/ppermute | solution.py:67
  80.8 1.8 %collective-permute-done.37 = bf16[1,256,384]{2,1,0:T(8,128)(2,1)S(1)} collective-permute-done((bf16[1,256,384]{2,1,0:T(8,128)(2,1)S(1)}, bf16[1,256,384]{2,1,0:T(8,128)(2,1)S(1)}, u32[]{:S(2)}, u32[]{:S(2)}) %collective-permute-start.37) | collective-permute-done | bytes 196640 | tf_op jit(solution)/shard_map/ppermute | solution.py:67
  83.7 1.1 %collective-permute-start.46 = (bf16[1,256,384]{2,1,0:T(8,128)(2,1)S(1)}, bf16[1,256,384]{2,1,0:T(8,128)(2,1)S(1)}, u32[]{:S(2)}, u32[]{:S(2)}) collective-permute-start(bf16[1,256,384]{2,1,0:T(8,128)(2,1)S(1)} %fusion.1), channel_id=1, source_target_pairs={{0,1},{1,0},{2,3},{3,2},{4,5},{5,4},{6,7},{7,6},{8,9},{9,8},{10,11... | collective-permute-start | bytes 589832 | tf_op jit(solution)/shard_map/ppermute | solution.py:67
  85.8 2.8 %collective-permute-done.40 = bf16[2,1,256,384]{3,2,1,0:T(8,128)(2,1)S(1)} collective-permute-done((bf16[2,1,256,384]{3,2,1,0:T(8,128)(2,1)S(1)}, bf16[2,1,256,384]{3,2,1,0:T(8,128)(2,1)S(1)}, u32[]{:S(2)}, u32[]{:S(2)}) %collective-permute-start.40) | collective-permute-done | bytes 393248 | tf_op jit(solution)/shard_map/ppermute | solution.py:67
  88.7 1.6 %collective-permute-start.41 = (bf16[1,128,384]{2,1,0:T(8,128)(2,1)S(1)}, bf16[1,128,384]{2,1,0:T(8,128)(2,1)S(1)}, u32[]{:S(2)}, u32[]{:S(2)}) collective-permute-start(bf16[1,128,384]{2,1,0:T(8,128)(2,1)S(1)} %get-tuple-element.154), channel_id=1, source_target_pairs={{0,16},{1,17},{2,18},{3,19},{4,20},{5,21},{6,22},{7,23},{8,24},{9,... | collective-permute-start | bytes 294920 | tf_op jit(solution)/shard_map/ppermute | solution.py:67
  91.5 2.8 %collective-permute-start.50 = (bf16[1,256,384]{2,1,0:T(8,128)(2,1)S(1)}, bf16[1,256,384]{2,1,0:T(8,128)(2,1)S(1)}, u32[]{:S(2)}, u32[]{:S(2)}) collective-permute-start(bf16[1,256,384]{2,1,0:T(8,128)(2,1)S(1)} %fusion.7), channel_id=1, source_target_pairs={{0,4},{1,5},{2,6},{3,7},{4,0},{5,1},{6,2},{7,3},{8,12},{9,13},{10,... | collective-permute-start | bytes 589832 | tf_op jit(solution)/shard_map/ppermute | solution.py:67
  96.0 1.1 %collective-permute-start.49 = (bf16[1,256,384]{2,1,0:T(8,128)(2,1)S(1)}, bf16[1,256,384]{2,1,0:T(8,128)(2,1)S(1)}, u32[]{:S(2)}, u32[]{:S(2)}) collective-permute-start(bf16[1,256,384]{2,1,0:T(8,128)(2,1)S(1)} %fusion), channel_id=1, source_target_pairs={{0,1},{1,0},{2,3},{3,2},{4,5},{5,4},{6,7},{7,6},{8,9},{9,8},{10,11... | collective-permute-start | bytes 589832 | tf_op jit(solution)/shard_map/ppermute | solution.py:67
  97.2 5.5 %collective-permute-done.50 = bf16[1,256,384]{2,1,0:T(8,128)(2,1)S(1)} collective-permute-done((bf16[1,256,384]{2,1,0:T(8,128)(2,1)S(1)}, bf16[1,256,384]{2,1,0:T(8,128)(2,1)S(1)}, u32[]{:S(2)}, u32[]{:S(2)}) %collective-permute-start.50) | collective-permute-done | bytes 196640 | tf_op jit(solution)/shard_map/ppermute | solution.py:67
  (111 shorter events, 20.2 us)
Async XLA Ops:
  0.0 8.7 %collective-permute-start.5 = (bf16[1,256,384]{2,1,0:T(8,128)(2,1)}, bf16[1,256,384]{2,1,0:T(8,128)(2,1)S(1)}, u32[]{:S(2)}, u32[]{:S(2)}) collective-permute-start(bf16[1,256,384]{2,1,0:T(8,128)(2,1)} %bitcast.74), channel_id=1, source_target_pairs={{0,16},{1,17},{2,18},{3,19},{4,20},{5,21},{6,22},{7,23},{8,24},{9,... | collective-permute-start | bytes 589832 | tf_op jit(solution)/shard_map/ppermute | solution.py:67
  2.9 10.7 %collective-permute-start.1 = (bf16[1,256,384]{2,1,0:T(8,128)(2,1)}, bf16[1,256,384]{2,1,0:T(8,128)(2,1)S(1)}, u32[]{:S(2)}, u32[]{:S(2)}) collective-permute-start(bf16[1,256,384]{2,1,0:T(8,128)(2,1)} %bitcast.75), channel_id=1, source_target_pairs={{0,2},{1,3},{2,0},{3,1},{4,6},{5,7},{6,4},{7,5},{8,10},{9,11},{10,... | collective-permute-start | bytes 589832 | tf_op jit(solution)/shard_map/ppermute | solution.py:67
  4.5 14.7 %collective-permute-start.4 = (bf16[1,256,384]{2,1,0:T(8,128)(2,1)}, bf16[1,256,384]{2,1,0:T(8,128)(2,1)S(1)}, u32[]{:S(2)}, u32[]{:S(2)}) collective-permute-start(bf16[1,256,384]{2,1,0:T(8,128)(2,1)} %bitcast.76), channel_id=1, source_target_pairs={{0,4},{1,5},{2,6},{3,7},{4,0},{5,1},{6,2},{7,3},{8,12},{9,13},{10,... | collective-permute-start | bytes 589832 | tf_op jit(solution)/shard_map/ppermute | solution.py:67
  7.1 8.6 %collective-permute-start = (bf16[1,256,384]{2,1,0:T(8,128)(2,1)}, bf16[1,256,384]{2,1,0:T(8,128)(2,1)S(1)}, u32[]{:S(2)}, u32[]{:S(2)}) collective-permute-start(bf16[1,256,384]{2,1,0:T(8,128)(2,1)} %bitcast.77), channel_id=1, source_target_pairs={{0,1},{1,0},{2,3},{3,2},{4,5},{5,4},{6,7},{7,6},{8,9},{9,8},{10,11... | collective-permute-start | bytes 589832 | tf_op jit(solution)/shard_map/ppermute | solution.py:67
  8.6 11.5 %collective-permute-start.11 = (bf16[1,256,384]{2,1,0:T(8,128)(2,1)}, bf16[1,256,384]{2,1,0:T(8,128)(2,1)S(1)}, u32[]{:S(2)}, u32[]{:S(2)}) collective-permute-start(bf16[1,256,384]{2,1,0:T(8,128)(2,1)} %bitcast.78), channel_id=1, source_target_pairs={{0,8},{1,9},{2,10},{3,11},{4,12},{5,13},{6,14},{7,15},{8,0},{9,1},... | collective-permute-start | bytes 589832 | tf_op jit(solution)/shard_map/ppermute | solution.py:67
  13.6 6.2 %collective-permute-start.2 = (bf16[1,256,384]{2,1,0:T(8,128)(2,1)S(1)}, bf16[1,256,384]{2,1,0:T(8,128)(2,1)S(1)}, u32[]{:S(2)}, u32[]{:S(2)}) collective-permute-start(bf16[1,256,384]{2,1,0:T(8,128)(2,1)S(1)} %collective-permute-done.1.refs_5_), channel_id=1, source_target_pairs={{0,16},{1,17},{2,18},{3,19},{4,20},{5,21},{6,22},{7,23},{8,24},{9,... | collective-permute-start | bytes 589832 | tf_op jit(solution)/shard_map/ppermute | solution.py:67
  15.7 6.0 %collective-permute-start.13 = (bf16[1,256,384]{2,1,0:T(8,128)(2,1)S(1)}, bf16[1,256,384]{2,1,0:T(8,128)(2,1)S(1)}, u32[]{:S(2)}, u32[]{:S(2)}) collective-permute-start(bf16[1,256,384]{2,1,0:T(8,128)(2,1)S(1)} %collective-permute-done.1.refs_5_), channel_id=1, source_target_pairs={{0,8},{1,9},{2,10},{3,11},{4,12},{5,13},{6,14},{7,15},{8,0},{9,1},... | collective-permute-start | bytes 589832 | tf_op jit(solution)/shard_map/ppermute | solution.py:67
  19.8 8.8 %collective-permute-start.10 = (bf16[1,256,384]{2,1,0:T(8,128)(2,1)S(1)}, bf16[1,256,384]{2,1,0:T(8,128)(2,1)S(1)}, u32[]{:S(2)}, u32[]{:S(2)}) collective-permute-start(bf16[1,256,384]{2,1,0:T(8,128)(2,1)S(1)} %collective-permute-done.4.refs_1_), channel_id=1, source_target_pairs={{0,2},{1,3},{2,0},{3,1},{4,6},{5,7},{6,4},{7,5},{8,10},{9,11},{10,... | collective-permute-start | bytes 589832 | tf_op jit(solution)/shard_map/ppermute | solution.py:67
  20.1 11.5 %collective-permute-start.8 = (bf16[1,256,384]{2,1,0:T(8,128)(2,1)S(1)}, bf16[1,256,384]{2,1,0:T(8,128)(2,1)S(1)}, u32[]{:S(2)}, u32[]{:S(2)}) collective-permute-start(bf16[1,256,384]{2,1,0:T(8,128)(2,1)S(1)} %collective-permute-done.4.refs_1_), channel_id=1, source_target_pairs={{0,16},{1,17},{2,18},{3,19},{4,20},{5,21},{6,22},{7,23},{8,24},{9,... | collective-permute-start | bytes 589832 | tf_op jit(solution)/shard_map/ppermute | solution.py:67
  21.6 10.0 %collective-permute-start.6 = (bf16[2,128,384]{2,1,0:T(8,128)(2,1)S(1)}, bf16[2,128,384]{2,1,0:T(8,128)(2,1)S(1)}, u32[]{:S(2)}, u32[]{:S(2)}) collective-permute-start(bf16[2,128,384]{2,1,0:T(8,128)(2,1)S(1)} %pad_maximum_fusion), channel_id=1, source_target_pairs={{0,16},{1,17},{2,18},{3,19},{4,20},{5,21},{6,22},{7,23},{8,24},{9,... | collective-permute-start | bytes 589832 | tf_op jit(solution)/shard_map/ppermute | solution.py:67
  22.2 9.4 %collective-permute-start.7 = (bf16[2,128,384]{2,1,0:T(8,128)(2,1)S(1)}, bf16[2,128,384]{2,1,0:T(8,128)(2,1)S(1)}, u32[]{:S(2)}, u32[]{:S(2)}) collective-permute-start(bf16[2,128,384]{2,1,0:T(8,128)(2,1)S(1)} %pad_maximum_fusion.1), channel_id=1, source_target_pairs={{0,1},{1,0},{2,3},{3,2},{4,5},{5,4},{6,7},{7,6},{8,9},{9,8},{10,11... | collective-permute-start | bytes 589832 | tf_op jit(solution)/shard_map/ppermute | solution.py:67
  23.6 9.5 %collective-permute-start.9 = (bf16[1,256,384]{2,1,0:T(8,128)(2,1)S(1)}, bf16[1,256,384]{2,1,0:T(8,128)(2,1)S(1)}, u32[]{:S(2)}, u32[]{:S(2)}) collective-permute-start(bf16[1,256,384]{2,1,0:T(8,128)(2,1)S(1)} %collective-permute-done.4.refs_1_), channel_id=1, source_target_pairs={{0,1},{1,0},{2,3},{3,2},{4,5},{5,4},{6,7},{7,6},{8,9},{9,8},{10,11... | collective-permute-start | bytes 589832 | tf_op jit(solution)/shard_map/ppermute | solution.py:67
  28.6 6.6 %collective-permute-start.17 = (bf16[1,256,384]{2,1,0:T(8,128)(2,1)S(1)}, bf16[1,256,384]{2,1,0:T(8,128)(2,1)S(1)}, u32[]{:S(2)}, u32[]{:S(2)}) collective-permute-start(bf16[1,256,384]{2,1,0:T(8,128)(2,1)S(1)} %collective-permute-done.5.refs_1_), channel_id=1, source_target_pairs={{0,8},{1,9},{2,10},{3,11},{4,12},{5,13},{6,14},{7,15},{8,0},{9,1},... | collective-permute-start | bytes 589832 | tf_op jit(solution)/shard_map/ppermute | solution.py:67
  33.6 8.2 %collective-permute-start.15 = (bf16[1,272,384]{2,1,0:T(8,128)(2,1)S(1)}, bf16[1,272,384]{2,1,0:T(8,128)(2,1)S(1)}, u32[]{:S(2)}, u32[]{:S(2)}) collective-permute-start(bf16[1,272,384]{2,1,0:T(8,128)(2,1)S(1)} %constant_dynamic-update-slice_fusion.refs_5_.refs_14_), channel_id=1, source_target_pairs={{0,16},{1,17},{2,18},{3,19},{4,20},{5,21},{6,22},{7,23},{8,24},{9,... | collective-permute-start | bytes 626696 | tf_op jit(solution)/shard_map/ppermute | solution.py:67
  35.2 6.6 %collective-permute-start.16 = (bf16[1,256,384]{2,1,0:T(8,128)(2,1)S(1)}, bf16[1,256,384]{2,1,0:T(8,128)(2,1)S(1)}, u32[]{:S(2)}, u32[]{:S(2)}) collective-permute-start(bf16[1,256,384]{2,1,0:T(8,128)(2,1)S(1)} %collective-permute-done.10), channel_id=1, source_target_pairs={{0,1},{1,0},{2,3},{3,2},{4,5},{5,4},{6,7},{7,6},{8,9},{9,8},{10,11... | collective-permute-start | bytes 589832 | tf_op jit(solution)/shard_map/ppermute | solution.py:67
  36.8 6.2 %collective-permute-start.26 = (bf16[1,256,384]{2,1,0:T(8,128)(2,1)S(1)}, bf16[1,256,384]{2,1,0:T(8,128)(2,1)S(1)}, u32[]{:S(2)}, u32[]{:S(2)}) collective-permute-start(bf16[1,256,384]{2,1,0:T(8,128)(2,1)S(1)} %collective-permute-done.9.refs_2_), channel_id=1, source_target_pairs={{0,8},{1,9},{2,10},{3,11},{4,12},{5,13},{6,14},{7,15},{8,0},{9,1},... | collective-permute-start | bytes 589832 | tf_op jit(solution)/shard_map/ppermute | solution.py:67
  37.3 6.7 %collective-permute-start.27 = (bf16[1,272,384]{2,1,0:T(8,128)(2,1)S(1)}, bf16[1,272,384]{2,1,0:T(8,128)(2,1)S(1)}, u32[]{:S(2)}, u32[]{:S(2)}) collective-permute-start(bf16[1,272,384]{2,1,0:T(8,128)(2,1)S(1)} %constant_dynamic-update-slice_fusion.refs_5_.refs_14_), channel_id=1, source_target_pairs={{0,8},{1,9},{2,10},{3,11},{4,12},{5,13},{6,14},{7,15},{8,0},{9,1},... | collective-permute-start | bytes 626696 | tf_op jit(solution)/shard_map/ppermute | solution.py:67
  41.8 11.4 %collective-permute-start.24 = (bf16[1,272,384]{2,1,0:T(8,128)(2,1)S(1)}, bf16[1,272,384]{2,1,0:T(8,128)(2,1)S(1)}, u32[]{:S(2)}, u32[]{:S(2)}) collective-permute-start(bf16[1,272,384]{2,1,0:T(8,128)(2,1)S(1)} %collective-permute-done.15.refs_7_.refs_14_), channel_id=1, source_target_pairs={{0,8},{1,9},{2,10},{3,11},{4,12},{5,13},{6,14},{7,15},{8,0},{9,1},... | collective-permute-start | bytes 626696 | tf_op jit(solution)/shard_map/ppermute | solution.py:67
  42.5 10.7 %collective-permute-start.23 = (bf16[1,256,384]{2,1,0:T(8,128)(2,1)S(1)}, bf16[1,256,384]{2,1,0:T(8,128)(2,1)S(1)}, u32[]{:S(2)}, u32[]{:S(2)}) collective-permute-start(bf16[1,256,384]{2,1,0:T(8,128)(2,1)S(1)} %collective-permute-done.8.refs_1_), channel_id=1, source_target_pairs={{0,8},{1,9},{2,10},{3,11},{4,12},{5,13},{6,14},{7,15},{8,0},{9,1},... | collective-permute-start | bytes 589832 | tf_op jit(solution)/shard_map/ppermute | solution.py:67
  43.0 10.2 %collective-permute-start.22 = (bf16[2,128,384]{2,1,0:T(8,128)(2,1)S(1)}, bf16[2,128,384]{2,1,0:T(8,128)(2,1)S(1)}, u32[]{:S(2)}, u32[]{:S(2)}) collective-permute-start(bf16[2,128,384]{2,1,0:T(8,128)(2,1)S(1)} %pad_maximum_fusion.3), channel_id=1, source_target_pairs={{0,1},{1,0},{2,3},{3,2},{4,5},{5,4},{6,7},{7,6},{8,9},{9,8},{10,11... | collective-permute-start | bytes 589832 | tf_op jit(solution)/shard_map/ppermute | solution.py:67
  44.0 9.1 %collective-permute-start.21 = (bf16[2,128,384]{2,1,0:T(8,128)(2,1)S(1)}, bf16[2,128,384]{2,1,0:T(8,128)(2,1)S(1)}, u32[]{:S(2)}, u32[]{:S(2)}) collective-permute-start(bf16[2,128,384]{2,1,0:T(8,128)(2,1)S(1)} %pad_maximum_fusion.2), channel_id=1, source_target_pairs={{0,16},{1,17},{2,18},{3,19},{4,20},{5,21},{6,22},{7,23},{8,24},{9,... | collective-permute-start | bytes 589832 | tf_op jit(solution)/shard_map/ppermute | solution.py:67
  56.1 7.2 %collective-permute-start.32 = (bf16[2,2,256,384]{3,2,1,0:T(8,128)(2,1)S(1)}, bf16[2,2,256,384]{3,2,1,0:T(8,128)(2,1)S(1)}, u32[]{:S(2)}, u32[]{:S(2)}) collective-permute-start(bf16[2,2,256,384]{3,2,1,0:T(8,128)(2,1)S(1)} %get-tuple-element.117), channel_id=1, source_target_pairs={{0,8},{1,9},{2,10},{3,11},{4,12},{5,13},{6,14},{7,15},{8,0},{9,1},... | collective-permute-start | bytes 2359304 | tf_op jit(solution)/shard_map/ppermute | solution.py:67
  66.4 12.1 %collective-permute-start.39 = (bf16[2,1,256,384]{3,2,1,0:T(8,128)(2,1)S(1)}, bf16[2,1,256,384]{3,2,1,0:T(8,128)(2,1)S(1)}, u32[]{:S(2)}, u32[]{:S(2)}) collective-permute-start(bf16[2,1,256,384]{3,2,1,0:T(8,128)(2,1)S(1)} %add_convert_fusion), channel_id=1, source_target_pairs={{0,2},{1,3},{2,0},{3,1},{4,6},{5,7},{6,4},{7,5},{8,10},{9,11},{10,... | collective-permute-start | bytes 1179656 | tf_op jit(solution)/shard_map/ppermute | solution.py:67
  76.0 6.6 %collective-permute-start.37 = (bf16[1,256,384]{2,1,0:T(8,128)(2,1)S(1)}, bf16[1,256,384]{2,1,0:T(8,128)(2,1)S(1)}, u32[]{:S(2)}, u32[]{:S(2)}) collective-permute-start(bf16[1,256,384]{2,1,0:T(8,128)(2,1)S(1)} %fusion.13), channel_id=1, source_target_pairs={{0,16},{1,17},{2,18},{3,19},{4,20},{5,21},{6,22},{7,23},{8,24},{9,... | collective-permute-start | bytes 589832 | tf_op jit(solution)/shard_map/ppermute | solution.py:67
  76.6 12.1 %collective-permute-start.40 = (bf16[2,1,256,384]{3,2,1,0:T(8,128)(2,1)S(1)}, bf16[2,1,256,384]{3,2,1,0:T(8,128)(2,1)S(1)}, u32[]{:S(2)}, u32[]{:S(2)}) collective-permute-start(bf16[2,1,256,384]{3,2,1,0:T(8,128)(2,1)S(1)} %add_convert_fusion.1), channel_id=1, source_target_pairs={{0,2},{1,3},{2,0},{3,1},{4,6},{5,7},{6,4},{7,5},{8,10},{9,11},{10,... | collective-permute-start | bytes 1179656 | tf_op jit(solution)/shard_map/ppermute | solution.py:67
  76.8 6.9 %collective-permute-start.43 = (bf16[1,128,384]{2,1,0:T(8,128)(2,1)S(1)}, bf16[1,128,384]{2,1,0:T(8,128)(2,1)S(1)}, u32[]{:S(2)}, u32[]{:S(2)}) collective-permute-start(bf16[1,128,384]{2,1,0:T(8,128)(2,1)S(1)} %get-tuple-element.138), channel_id=1, source_target_pairs={{0,16},{1,17},{2,18},{3,19},{4,20},{5,21},{6,22},{7,23},{8,24},{9,... | collective-permute-start | bytes 294920 | tf_op jit(solution)/shard_map/ppermute | solution.py:67
  82.7 8.7 %collective-permute-start.47 = (bf16[1,256,384]{2,1,0:T(8,128)(2,1)S(1)}, bf16[1,256,384]{2,1,0:T(8,128)(2,1)S(1)}, u32[]{:S(2)}, u32[]{:S(2)}) collective-permute-start(bf16[1,256,384]{2,1,0:T(8,128)(2,1)S(1)} %fusion.3), channel_id=1, source_target_pairs={{0,2},{1,3},{2,0},{3,1},{4,6},{5,7},{6,4},{7,5},{8,10},{9,11},{10,... | collective-permute-start | bytes 589832 | tf_op jit(solution)/shard_map/ppermute | solution.py:67
  83.7 7.6 %collective-permute-start.46 = (bf16[1,256,384]{2,1,0:T(8,128)(2,1)S(1)}, bf16[1,256,384]{2,1,0:T(8,128)(2,1)S(1)}, u32[]{:S(2)}, u32[]{:S(2)}) collective-permute-start(bf16[1,256,384]{2,1,0:T(8,128)(2,1)S(1)} %fusion.1), channel_id=1, source_target_pairs={{0,1},{1,0},{2,3},{3,2},{4,5},{5,4},{6,7},{7,6},{8,9},{9,8},{10,11... | collective-permute-start | bytes 589832 | tf_op jit(solution)/shard_map/ppermute | solution.py:67
  84.9 6.4 %collective-permute-start.45 = (bf16[1,256,384]{2,1,0:T(8,128)(2,1)S(1)}, bf16[1,256,384]{2,1,0:T(8,128)(2,1)S(1)}, u32[]{:S(2)}, u32[]{:S(2)}) collective-permute-start(bf16[1,256,384]{2,1,0:T(8,128)(2,1)S(1)} %fusion.4), channel_id=1, source_target_pairs={{0,16},{1,17},{2,18},{3,19},{4,20},{5,21},{6,22},{7,23},{8,24},{9,... | collective-permute-start | bytes 589832 | tf_op jit(solution)/shard_map/ppermute | solution.py:67
  91.5 11.2 %collective-permute-start.50 = (bf16[1,256,384]{2,1,0:T(8,128)(2,1)S(1)}, bf16[1,256,384]{2,1,0:T(8,128)(2,1)S(1)}, u32[]{:S(2)}, u32[]{:S(2)}) collective-permute-start(bf16[1,256,384]{2,1,0:T(8,128)(2,1)S(1)} %fusion.7), channel_id=1, source_target_pairs={{0,4},{1,5},{2,6},{3,7},{4,0},{5,1},{6,2},{7,3},{8,12},{9,13},{10,... | collective-permute-start | bytes 589832 | tf_op jit(solution)/shard_map/ppermute | solution.py:67
  95.0 7.7 %collective-permute-start.48 = (bf16[1,256,384]{2,1,0:T(8,128)(2,1)S(1)}, bf16[1,256,384]{2,1,0:T(8,128)(2,1)S(1)}, u32[]{:S(2)}, u32[]{:S(2)}) collective-permute-start(bf16[1,256,384]{2,1,0:T(8,128)(2,1)S(1)} %fusion.8), channel_id=1, source_target_pairs={{0,16},{1,17},{2,18},{3,19},{4,20},{5,21},{6,22},{7,23},{8,24},{9,... | collective-permute-start | bytes 589832 | tf_op jit(solution)/shard_map/ppermute | solution.py:67
  96.0 6.6 %collective-permute-start.49 = (bf16[1,256,384]{2,1,0:T(8,128)(2,1)S(1)}, bf16[1,256,384]{2,1,0:T(8,128)(2,1)S(1)}, u32[]{:S(2)}, u32[]{:S(2)}) collective-permute-start(bf16[1,256,384]{2,1,0:T(8,128)(2,1)S(1)} %fusion), channel_id=1, source_target_pairs={{0,1},{1,0},{2,3},{3,2},{4,5},{5,4},{6,7},{7,6},{8,9},{9,8},{10,11... | collective-permute-start | bytes 589832 | tf_op jit(solution)/shard_map/ppermute | solution.py:67
  (20 other events, 88.4 us)

commit v5 on v3

--- a/solution.py
+++ b/solution.py
@@ -126,16 +126,13 @@
     return arrays, found
 
 
-def fill(place, arrays, found, z_places, rows, sems):
+def fill(place, arrays, found, z_places, rows):
     my_y = place[place.shape[0] - 1]
-    copies = []
-    for i, (which, index, z, row, y, count) in enumerate(found):
-        source = arrays[which].at[index, pl.ds(0, count)]
-        column = ((place[z_places[z]] & 1) * 2 + (my_y ^ y)) * source.shape[1]
-        columns = pl.ds(pl.multiple_of(column, 128), source.shape[1])
-        target = rows.at[pl.ds(row, count), columns]
-        copies.append(pltpu.make_async_copy(source, target, sems.at[i]))
-    return copies
+    for which, index, z, row, y, count in found:
+        narrow = arrays[which].shape[2]
+        column = ((place[z_places[z]] & 1) * 2 + (my_y ^ y)) * narrow
+        columns = pl.ds(pl.multiple_of(column, 128), narrow)
+        rows[row : row + count, columns] = arrays[which][index, :count]
 
 
 def all_of(copies):
@@ -168,14 +165,12 @@
 
 
 def first_kernel(place, *refs, found, z_places, following):
-    arrays, refs = refs[:-9], refs[-9:]
-    w_gate, w_up, later, gate, up, later_rows, rows, sems, later_sems = refs
+    arrays, refs = refs[:-8], refs[-8:]
+    w_gate, w_up, later, gate, up, later_rows, rows, later_sems = refs
     later = weight_copies(place, following, later, later_rows, later_sems)
-    copies = fill(place, arrays, found, z_places, rows, sems)
-    for copy in copies + later:
+    for copy in later:
         copy.start()
-    for copy in copies:
-        copy.wait()
+    fill(place, arrays, found, z_places, rows)
     for weight, result in ((w_gate, gate), (w_up, up)):
         for t in range(result.shape[0]):
             tile = slice(t * HIDDEN_TILE, (t + 1) * HIDDEN_TILE)
@@ -223,22 +218,20 @@
 
 
 def second_kernel(place, *refs, x, found, z_places, pairs):
-    count = 17 if x else 19
+    count = 16 if x else 18
     arrays, refs = refs[:-count], refs[-count:]
     w_gate, w_up, gate, up, w_down = refs[:5]
     shares, out = refs[5:7], refs[7:11]
-    rows, tails, sems, t_sems, d_sems, first_tile = refs[11:17]
-    hidden, second_tile = out[2:] if x else refs[17:]
-    copies = fill(place, arrays, found, z_places, rows, sems)
+    rows, tails, t_sems, d_sems, first_tile = refs[11:16]
+    hidden, second_tile = out[2:] if x else refs[16:]
     downs_in = [
         down_copy(place, pair, w_down, tile, d_sems.at[k])
         for k, (pair, tile) in enumerate(zip(pairs, (first_tile, second_tile)))
     ]
-    for copy in copies + downs_in:
+    for copy in downs_in:
         copy.start()
+    fill(place, arrays, found, z_places, rows)
     share = 0.5 * share_column(place, shares, tails, t_sems, out[0].shape[2])
-    for copy in copies:
-        copy.wait()
     for t in range(gate.shape[0]):
         tile = slice(t * HIDDEN_TILE, (t + 1) * HIDDEN_TILE)
         g = gate[t] + jnp.dot(rows[...], w_gate[:, tile], preferred_element_type=jnp.float32)
@@ -304,11 +297,10 @@
     sums = pltpu.VMEM((width // HIDDEN_TILE, rows, HIDDEN_TILE), jnp.float32)
     return pl.pallas_call(
         lambda *refs: first_kernel(*refs, found=found, z_places=z_places, following=following),
-        in_specs=[SCALARS] + [ANY] * len(arrays) + [VMEM, VMEM, ANY],
+        in_specs=[SCALARS] + [VMEM] * (len(arrays) + 2) + [ANY],
         out_specs=[VMEM] * 3,
         scratch_shapes=[
             pltpu.VMEM((rows, depth), jnp.bfloat16),
-            SEMS((len(found),)),
             SEMS((4,)),
         ],
         out_shape=[sums, sums, pltpu.VMEM((depth, width), jnp.bfloat16)],
@@ -319,7 +311,7 @@
             transcendentals=0,
         ),
         name="first_part",
-    )(place, *arrays, *[in_vmem(v) for v in weights], later)
+    )(place, *[in_vmem(v) for v in (*arrays, *weights)], later)
 
 
 def second_part(place, x, pair, z_places, weights, sums, shares, w_down, pairs):
@@ -333,12 +325,11 @@
         lambda *refs: second_kernel(
             *refs, x=x, found=found, z_places=z_places, pairs=pairs
         ),
-        in_specs=[SCALARS] + [ANY] * len(arrays) + [VMEM] * 4 + [ANY] * 3,
+        in_specs=[SCALARS] + [VMEM] * (len(arrays) + 4) + [ANY] * 3,
         out_specs=[VMEM] * 4,
         scratch_shapes=[
             pltpu.VMEM((rows, depth), jnp.bfloat16),
             pltpu.VMEM((2, tail, narrow), jnp.bfloat16),
-            SEMS((len(found),)),
             SEMS((2,)),
             SEMS((2,)),
             tile,
@@ -352,7 +343,7 @@
             transcendentals=rows * width,
         ),
         name="second_part",
-    )(place, *arrays, *[in_vmem(v) for v in (*weights, *sums)], w_down, *shares)
+    )(place, *[in_vmem(v) for v in (*arrays, *weights, *sums)], w_down, *shares)
 
 
 def third_part(place, hidden, tile, pair, size):

time: 101 us -> 102 us (level)
  starting transfers between devices: 40.4 us -> 37.8 us
  waiting for transfers between devices: 25.5 us -> 27.7 us
  Pallas kernels: 30.1 us -> 31.3 us
    ppermute x49, starting transfers between devices: 40.4 us -> 37.8 us  [send(): return lax.ppermute(value, BOTH, pairs)]
    ppermute x49, waiting for transfers between devices: 25.5 us -> 27.7 us  [send(): return lax.ppermute(value, BOTH, pairs)]
    pallas_call x2, Pallas kernels: 8.7 us -> 10.3 us  [first_part(): pl.pallas_call(lambda *refs: first_kernel(*refs, found=found, z_places=z_...]
  transfers between devices with their start and end apart: 49 -> 49, of which waited for: 13 -> 13; matrix products, arithmetic and copies ran while one was open for 4% -> 4% of each run, Pallas kernels for 30% -> 31%
where the time goes in v5:
time: 102 us
  starting transfers between devices  37.8 us (37%)
  Pallas kernels  31.3 us (31%)
  waiting for transfers between devices  27.7 us (27%)
  other arithmetic  4.46 us (4%)
    ppermute x49, starting transfers between devices, send(): return lax.ppermute(value, BOTH, pairs)  37.8 us
    ppermute x49, waiting for transfers between devices, send(): return lax.ppermute(value, BOTH, pairs)  27.7 us
    pallas_call x2, Pallas kernels, second_part(): pl.pallas_call(lambda *refs: second_kernel(*refs, x=x, found=found, z_pla...  15.2 us
    pallas_call x2, Pallas kernels, first_part(): pl.pallas_call(lambda *refs: first_kernel(*refs, found=found, z_places=z_...  10.3 us
    pallas_call x1, Pallas kernels, pair_weights(): pl.pallas_call(lambda *refs: weights_kernel(*refs, z=z), in_specs=[SCALAR...  3.41 us
    pallas_call x1, Pallas kernels, third_part(): pl.pallas_call(lambda *refs: third_kernel(*refs, pair=pair), in_specs=[SC...  2.37 us
  transfers between devices with their start and end apart: 49, of which 13 were waited for; matrix products, arithmetic and copies ran while one was open for 4% of the time, Pallas kernels for 31%

profile of v5, /device:TPU:0, one launch (start us, length us, event | category | flops | bytes accessed | tf_op | source)
XLA Modules:
  0.0 101.8 jit_solution(13543696430523485976)
XLA Ops:
  0.0 3.0 %collective-permute-start.1 = (bf16[1,256,384]{2,1,0:T(8,128)(2,1)}, bf16[1,256,384]{2,1,0:T(8,128)(2,1)S(1)}, u32[]{:S(2)}, u32[]{:S(2)}) collective-permute-start(bf16[1,256,384]{2,1,0:T(8,128)(2,1)} %bitcast.72), channel_id=1, source_target_pairs={{0,2},{1,3},{2,0},{3,1},{4,6},{5,7},{6,4},{7,5},{8,10},{9,11},{10,... | collective-permute-start | bytes 589832 | tf_op jit(solution)/shard_map/ppermute | solution.py:67
  4.5 1.0 maximum_bitcast_fusion.refs_1_.refs_14_
  5.5 1.6 %collective-permute-start.5 = (bf16[1,272,384]{2,1,0:T(8,128)(2,1)S(1)}, bf16[1,272,384]{2,1,0:T(8,128)(2,1)S(1)}, u32[]{:S(2)}, u32[]{:S(2)}) collective-permute-start(bf16[1,272,384]{2,1,0:T(8,128)(2,1)S(1)} %maximum_bitcast_fusion.refs_1_.refs_14_), channel_id=1, source_target_pairs={{0,16},{1,17},{2,18},{3,19},{4,20},{5,21},{6,22},{7,23},{8,24},{9,... | collective-permute-start | bytes 626696 | tf_op jit(solution)/shard_map/ppermute | solution.py:67
  7.0 1.5 %collective-permute-start = (bf16[1,256,384]{2,1,0:T(8,128)(2,1)}, bf16[1,256,384]{2,1,0:T(8,128)(2,1)S(1)}, u32[]{:S(2)}, u32[]{:S(2)}) collective-permute-start(bf16[1,256,384]{2,1,0:T(8,128)(2,1)} %bitcast.73), channel_id=1, source_target_pairs={{0,1},{1,0},{2,3},{3,2},{4,5},{5,4},{6,7},{7,6},{8,9},{9,8},{10,11... | collective-permute-start | bytes 589832 | tf_op jit(solution)/shard_map/ppermute | solution.py:67
  8.6 2.6 %collective-permute-start.4 = (bf16[1,256,384]{2,1,0:T(8,128)(2,1)}, bf16[1,256,384]{2,1,0:T(8,128)(2,1)S(1)}, u32[]{:S(2)}, u32[]{:S(2)}) collective-permute-start(bf16[1,256,384]{2,1,0:T(8,128)(2,1)} %bitcast.74), channel_id=1, source_target_pairs={{0,4},{1,5},{2,6},{3,7},{4,0},{5,1},{6,2},{7,3},{8,12},{9,13},{10,... | collective-permute-start | bytes 589832 | tf_op jit(solution)/shard_map/ppermute | solution.py:67
  12.3 1.8 %collective-permute-done.refs_2_ = bf16[1,256,384]{2,1,0:T(8,128)(2,1)S(1)} collective-permute-done((bf16[1,256,384]{2,1,0:T(8,128)(2,1)}, bf16[1,256,384]{2,1,0:T(8,128)(2,1)S(1)}, u32[]{:S(2)}, u32[]{:S(2)}) %collective-permute-start) | collective-permute-done | bytes 196640 | tf_op jit(solution)/shard_map/ppermute | solution.py:67
  14.7 3.4 %pair_weights.1 = (bf16[1536,1024]{1,0:T(8,128)(2,1)S(1)}, bf16[1536,1024]{1,0:T(8,128)(2,1)S(1)}) custom-call(s32[7]{0:T(128)S(1)} %stack.33.refs_0_, bf16[1,272,384]{2,1,0:T(8,128)(2,1)S(1)} %collective-permute-done.5.refs_1_.refs_14_, bf16[3072,1024]{1,0:T(8,128)(2,1)} %bitcast.66, bf16[3072,1024]{1,0:T(8,128)(2,1)} %bitcast.68), custom_call_target="tpu_custom_call" | custom-call | bytes 3145728 | tf_op jit(solution)/shard_map/pair_weights/pallas_call | solution.py:280
  18.2 1.4 %collective-permute-done.4.refs_1_ = bf16[1,256,384]{2,1,0:T(8,128)(2,1)S(1)} collective-permute-done((bf16[1,256,384]{2,1,0:T(8,128)(2,1)}, bf16[1,256,384]{2,1,0:T(8,128)(2,1)S(1)}, u32[]{:S(2)}, u32[]{:S(2)}) %collective-permute-start.4) | collective-permute-done | bytes 196640 | tf_op jit(solution)/shard_map/ppermute | solution.py:67
  21.5 1.9 %collective-permute-start.6 = (bf16[2,128,384]{2,1,0:T(8,128)(2,1)S(1)}, bf16[2,128,384]{2,1,0:T(8,128)(2,1)S(1)}, u32[]{:S(2)}, u32[]{:S(2)}) collective-permute-start(bf16[2,128,384]{2,1,0:T(8,128)(2,1)S(1)} %pad_maximum_fusion), channel_id=1, source_target_pairs={{0,16},{1,17},{2,18},{3,19},{4,20},{5,21},{6,22},{7,23},{8,24},{9,... | collective-permute-start | bytes 589832 | tf_op jit(solution)/shard_map/ppermute | solution.py:67
  23.4 1.0 collective-permute-start.9
  24.4 2.5 %collective-permute-done.10.refs_5_ = bf16[1,256,384]{2,1,0:T(8,128)(2,1)S(1)} collective-permute-done((bf16[1,256,384]{2,1,0:T(8,128)(2,1)S(1)}, bf16[1,256,384]{2,1,0:T(8,128)(2,1)S(1)}, u32[]{:S(2)}, u32[]{:S(2)}) %collective-permute-start.10) | collective-permute-done | bytes 196640 | tf_op jit(solution)/shard_map/ppermute | solution.py:67
  26.9 5.2 %first_part.2 = (f32[2,512,512]{2,1,0:T(8,128)S(1)}, f32[2,512,512]{2,1,0:T(8,128)S(1)}, bf16[1536,1024]{1,0:T(8,128)(2,1)S(1)}) custom-call(s32[7]{0:T(128)S(1)} %stack.33.refs_0_, bf16[1,272,384]{2,1,0:T(8,128)(2,1)S(1)} %maximum_bitcast_fusion.refs_1_.refs_14_, bf16[1,256,384]{2,1,0:T(8,128)(2,1)S(1)} %collective-permute-done.refs_2_, ...), custom_call_target="tpu_custom_call" | custom-call | flops 805306368 | bytes 3014656 | tf_op jit(solution)/shard_map/first_part/pallas_call | solution.py:298
  35.5 5.2 %first_part.3 = (f32[2,512,512]{2,1,0:T(8,128)S(1)}, f32[2,512,512]{2,1,0:T(8,128)S(1)}, bf16[1536,1024]{1,0:T(8,128)(2,1)S(1)}) custom-call(s32[7]{0:T(128)S(1)} %stack.33.refs_0_, bf16[1,272,384]{2,1,0:T(8,128)(2,1)S(1)} %collective-permute-done.5.refs_1_.refs_14_, bf16[2,128,384]{2,1,0:T(8,128)(2,1)S(1)} %collective-permute-done.6.refs_2_, ...), custom_call_target="tpu_custom_call" | custom-call | flops 805306368 | bytes 3014656 | tf_op jit(solution)/shard_map/first_part/pallas_call | solution.py:298
  41.3 1.2 %collective-permute-start.22 = (bf16[2,128,384]{2,1,0:T(8,128)(2,1)S(1)}, bf16[2,128,384]{2,1,0:T(8,128)(2,1)S(1)}, u32[]{:S(2)}, u32[]{:S(2)}) collective-permute-start(bf16[2,128,384]{2,1,0:T(8,128)(2,1)S(1)} %pad_maximum_fusion.3), channel_id=1, source_target_pairs={{0,1},{1,0},{2,3},{3,2},{4,5},{5,4},{6,7},{7,6},{8,9},{9,8},{10,11... | collective-permute-start | bytes 589832 | tf_op jit(solution)/shard_map/ppermute | solution.py:67
  42.6 1.4 %collective-permute-start.21 = (bf16[2,128,384]{2,1,0:T(8,128)(2,1)S(1)}, bf16[2,128,384]{2,1,0:T(8,128)(2,1)S(1)}, u32[]{:S(2)}, u32[]{:S(2)}) collective-permute-start(bf16[2,128,384]{2,1,0:T(8,128)(2,1)S(1)} %pad_maximum_fusion.2), channel_id=1, source_target_pairs={{0,16},{1,17},{2,18},{3,19},{4,20},{5,21},{6,22},{7,23},{8,24},{9,... | collective-permute-start | bytes 589832 | tf_op jit(solution)/shard_map/ppermute | solution.py:67
  44.0 8.4 %second_part.2 = (bf16[2,2,256,384]{3,2,1,0:T(8,128)(2,1)S(1)}, bf16[2,2,256,384]{3,2,1,0:T(8,128)(2,1)S(1)}, bf16[2,2,256,384]{3,2,1,0:T(8,128)(2,1)S(1)}, bf16[2,2,256,384]{3,2,1,0:T(8,128)(2,1)S(1)}) custom-call(s32[7]{0:T(128)S(1)} %stack.33.refs_0_, bf16[1,256,384]{2,1,0:T(8,128)(2,1)S(1)} %collective-permute-done.4.refs_1_, ...), custom_call_target="tpu_custom_call" | custom-call | flops 1610612736 | bytes 5373952 | tf_op jit(solution)/shard_map/second_part/pallas_call | solution.py:324
  53.5 1.7 %collective-permute-done.30.refs_5_ = bf16[2,128,384]{2,1,0:T(8,128)(2,1)S(1)} collective-permute-done((bf16[2,128,384]{2,1,0:T(8,128)(2,1)S(1)}, bf16[2,128,384]{2,1,0:T(8,128)(2,1)S(1)}, u32[]{:S(2)}, u32[]{:S(2)}) %collective-permute-start.30) | collective-permute-done | bytes 196640 | tf_op jit(solution)/shard_map/ppermute | solution.py:67
  55.9 6.7 %second_part.3 = (bf16[2,2,256,384]{3,2,1,0:T(8,128)(2,1)S(1)}, bf16[2,2,256,384]{3,2,1,0:T(8,128)(2,1)S(1)}, bf16[512,1024]{1,0:T(8,128)(2,1)S(1)}, bf16[1024,1536]{1,0:T(8,128)(2,1)S(1)}) custom-call(s32[7]{0:T(128)S(1)} %stack.33.refs_0_, bf16[1,256,384]{2,1,0:T(8,128)(2,1)S(1)} %collective-permute-done.8.refs_1_, ...), custom_call_target="tpu_custom_call" | custom-call | flops 1610612736 | bytes 5373952 | tf_op jit(solution)/shard_map/second_part/pallas_call | solution.py:324
  62.8 2.4 %third_part.1 = (bf16[2,2,256,384]{3,2,1,0:T(8,128)(2,1)S(1)}, bf16[2,2,256,384]{3,2,1,0:T(8,128)(2,1)S(1)}) custom-call(s32[7]{0:T(128)S(1)} %stack.33.refs_0_, bf16[512,1024]{1,0:T(8,128)(2,1)S(1)} %get-tuple-element.121.refs_1_, bf16[1024,1536]{1,0:T(8,128)(2,1)S(1)} %get-tuple-element.122.refs_2_), custom_call_target="tpu_custom_call" | custom-call | flops 402653184 | bytes 1441792 | tf_op jit(solution)/shard_map/third_part/pallas_call | solution.py:352
  65.7 1.1 %collective-permute-start.32 = (bf16[2,1,256,384]{3,2,1,0:T(8,128)(2,1)S(1)}, bf16[2,1,256,384]{3,2,1,0:T(8,128)(2,1)S(1)}, u32[]{:S(2)}, u32[]{:S(2)}) collective-permute-start(bf16[2,1,256,384]{3,2,1,0:T(8,128)(2,1)S(1)} %add_convert_fusion.1), channel_id=1, source_target_pairs={{0,2},{1,3},{2,0},{3,1},{4,6},{5,7},{6,4},{7,5},{8,10},{9,11},{10,... | collective-permute-start | bytes 1179656 | tf_op jit(solution)/shard_map/ppermute | solution.py:67
  67.0 1.5 %collective-permute-start.39 = (bf16[2,128,384]{2,1,0:T(8,128)(2,1)S(1)}, bf16[2,128,384]{2,1,0:T(8,128)(2,1)S(1)}, u32[]{:S(2)}, u32[]{:S(2)}) collective-permute-start(bf16[2,128,384]{2,1,0:T(8,128)(2,1)S(1)} %get-tuple-element.140), channel_id=1, source_target_pairs={{0,16},{1,17},{2,18},{3,19},{4,20},{5,21},{6,22},{7,23},{8,24},{9,... | collective-permute-start | bytes 589832 | tf_op jit(solution)/shard_map/ppermute | solution.py:67
  68.4 1.1 %collective-permute-start.40 = (bf16[2,128,384]{2,1,0:T(8,128)(2,1)S(1)}, bf16[2,128,384]{2,1,0:T(8,128)(2,1)S(1)}, u32[]{:S(2)}, u32[]{:S(2)}) collective-permute-start(bf16[2,128,384]{2,1,0:T(8,128)(2,1)S(1)} %get-tuple-element.139), channel_id=1, source_target_pairs={{0,1},{1,0},{2,3},{3,2},{4,5},{5,4},{6,7},{7,6},{8,9},{9,8},{10,11... | collective-permute-start | bytes 589832 | tf_op jit(solution)/shard_map/ppermute | solution.py:67
  69.7 4.0 %collective-permute-done.39 = bf16[2,128,384]{2,1,0:T(8,128)(2,1)S(1)} collective-permute-done((bf16[2,128,384]{2,1,0:T(8,128)(2,1)S(1)}, bf16[2,128,384]{2,1,0:T(8,128)(2,1)S(1)}, u32[]{:S(2)}, u32[]{:S(2)}) %collective-permute-start.39) | collective-permute-done | bytes 196640 | tf_op jit(solution)/shard_map/ppermute | solution.py:67
  73.7 1.1 %collective-permute-done.40 = bf16[2,128,384]{2,1,0:T(8,128)(2,1)S(1)} collective-permute-done((bf16[2,128,384]{2,1,0:T(8,128)(2,1)S(1)}, bf16[2,128,384]{2,1,0:T(8,128)(2,1)S(1)}, u32[]{:S(2)}, u32[]{:S(2)}) %collective-permute-start.40) | collective-permute-done | bytes 196640 | tf_op jit(solution)/shard_map/ppermute | solution.py:67
  76.8 4.0 %collective-permute-done.41 = bf16[1,256,384]{2,1,0:T(8,128)(2,1)S(1)} collective-permute-done((bf16[1,256,384]{2,1,0:T(8,128)(2,1)S(1)}, bf16[1,256,384]{2,1,0:T(8,128)(2,1)S(1)}, u32[]{:S(2)}, u32[]{:S(2)}) %collective-permute-start.41) | collective-permute-done | bytes 196640 | tf_op jit(solution)/shard_map/ppermute | solution.py:67
  81.7 1.0 %collective-permute-start.45 = (bf16[1,256,384]{2,1,0:T(8,128)(2,1)S(1)}, bf16[1,256,384]{2,1,0:T(8,128)(2,1)S(1)}, u32[]{:S(2)}, u32[]{:S(2)}) collective-permute-start(bf16[1,256,384]{2,1,0:T(8,128)(2,1)S(1)} %fusion.4), channel_id=1, source_target_pairs={{0,2},{1,3},{2,0},{3,1},{4,6},{5,7},{6,4},{7,5},{8,10},{9,11},{10,... | collective-permute-start | bytes 589832 | tf_op jit(solution)/shard_map/ppermute | solution.py:67
  83.5 1.1 %collective-permute-start.44 = (bf16[1,256,384]{2,1,0:T(8,128)(2,1)S(1)}, bf16[1,256,384]{2,1,0:T(8,128)(2,1)S(1)}, u32[]{:S(2)}, u32[]{:S(2)}) collective-permute-start(bf16[1,256,384]{2,1,0:T(8,128)(2,1)S(1)} %slice.198), channel_id=1, source_target_pairs={{0,1},{1,0},{2,3},{3,2},{4,5},{5,4},{6,7},{7,6},{8,9},{9,8},{10,11... | collective-permute-start | bytes 589832 | tf_op jit(solution)/shard_map/ppermute | solution.py:67
  84.6 1.6 %collective-permute-done.36 = bf16[2,1,256,384]{3,2,1,0:T(8,128)(2,1)S(1)} collective-permute-done((bf16[2,1,256,384]{3,2,1,0:T(8,128)(2,1)S(1)}, bf16[2,1,256,384]{3,2,1,0:T(8,128)(2,1)S(1)}, u32[]{:S(2)}, u32[]{:S(2)}) %collective-permute-start.36) | collective-permute-done | bytes 393248 | tf_op jit(solution)/shard_map/ppermute | solution.py:67
  86.9 2.5 %collective-permute-done.43 = bf16[1,256,384]{2,1,0:T(8,128)(2,1)S(1)} collective-permute-done((bf16[1,256,384]{2,1,0:T(8,128)(2,1)S(1)}, bf16[1,256,384]{2,1,0:T(8,128)(2,1)S(1)}, u32[]{:S(2)}, u32[]{:S(2)}) %collective-permute-start.43) | collective-permute-done | bytes 196640 | tf_op jit(solution)/shard_map/ppermute | solution.py:67
  89.4 1.0 collective-permute-start.38
  90.5 2.8 %collective-permute-start.48 = (bf16[1,256,384]{2,1,0:T(8,128)(2,1)S(1)}, bf16[1,256,384]{2,1,0:T(8,128)(2,1)S(1)}, u32[]{:S(2)}, u32[]{:S(2)}) collective-permute-start(bf16[1,256,384]{2,1,0:T(8,128)(2,1)S(1)} %fusion.8), channel_id=1, source_target_pairs={{0,4},{1,5},{2,6},{3,7},{4,0},{5,1},{6,2},{7,3},{8,12},{9,13},{10,... | collective-permute-start | bytes 589832 | tf_op jit(solution)/shard_map/ppermute | solution.py:67
  95.8 5.1 %collective-permute-done.48 = bf16[1,256,384]{2,1,0:T(8,128)(2,1)S(1)} collective-permute-done((bf16[1,256,384]{2,1,0:T(8,128)(2,1)S(1)}, bf16[1,256,384]{2,1,0:T(8,128)(2,1)S(1)}, u32[]{:S(2)}, u32[]{:S(2)}) %collective-permute-start.48) | collective-permute-done | bytes 196640 | tf_op jit(solution)/shard_map/ppermute | solution.py:67
  (107 shorter events, 19.7 us)
Async XLA Ops:
  0.0 11.2 %collective-permute-start.1 = (bf16[1,256,384]{2,1,0:T(8,128)(2,1)}, bf16[1,256,384]{2,1,0:T(8,128)(2,1)S(1)}, u32[]{:S(2)}, u32[]{:S(2)}) collective-permute-start(bf16[1,256,384]{2,1,0:T(8,128)(2,1)} %bitcast.72), channel_id=1, source_target_pairs={{0,2},{1,3},{2,0},{3,1},{4,6},{5,7},{6,4},{7,5},{8,10},{9,11},{10,... | collective-permute-start | bytes 589832 | tf_op jit(solution)/shard_map/ppermute | solution.py:67
  5.5 8.7 %collective-permute-start.5 = (bf16[1,272,384]{2,1,0:T(8,128)(2,1)S(1)}, bf16[1,272,384]{2,1,0:T(8,128)(2,1)S(1)}, u32[]{:S(2)}, u32[]{:S(2)}) collective-permute-start(bf16[1,272,384]{2,1,0:T(8,128)(2,1)S(1)} %maximum_bitcast_fusion.refs_1_.refs_14_), channel_id=1, source_target_pairs={{0,16},{1,17},{2,18},{3,19},{4,20},{5,21},{6,22},{7,23},{8,24},{9,... | collective-permute-start | bytes 626696 | tf_op jit(solution)/shard_map/ppermute | solution.py:67
  7.0 7.1 %collective-permute-start = (bf16[1,256,384]{2,1,0:T(8,128)(2,1)}, bf16[1,256,384]{2,1,0:T(8,128)(2,1)S(1)}, u32[]{:S(2)}, u32[]{:S(2)}) collective-permute-start(bf16[1,256,384]{2,1,0:T(8,128)(2,1)} %bitcast.73), channel_id=1, source_target_pairs={{0,1},{1,0},{2,3},{3,2},{4,5},{5,4},{6,7},{7,6},{8,9},{9,8},{10,11... | collective-permute-start | bytes 589832 | tf_op jit(solution)/shard_map/ppermute | solution.py:67
  8.6 11.0 %collective-permute-start.4 = (bf16[1,256,384]{2,1,0:T(8,128)(2,1)}, bf16[1,256,384]{2,1,0:T(8,128)(2,1)S(1)}, u32[]{:S(2)}, u32[]{:S(2)}) collective-permute-start(bf16[1,256,384]{2,1,0:T(8,128)(2,1)} %bitcast.74), channel_id=1, source_target_pairs={{0,4},{1,5},{2,6},{3,7},{4,0},{5,1},{6,2},{7,3},{8,12},{9,13},{10,... | collective-permute-start | bytes 589832 | tf_op jit(solution)/shard_map/ppermute | solution.py:67
  11.2 8.5 %collective-permute-start.2 = (bf16[1,256,384]{2,1,0:T(8,128)(2,1)S(1)}, bf16[1,256,384]{2,1,0:T(8,128)(2,1)S(1)}, u32[]{:S(2)}, u32[]{:S(2)}) collective-permute-start(bf16[1,256,384]{2,1,0:T(8,128)(2,1)S(1)} %collective-permute-done.1.refs_5_), channel_id=1, source_target_pairs={{0,16},{1,17},{2,18},{3,19},{4,20},{5,21},{6,22},{7,23},{8,24},{9,... | collective-permute-start | bytes 589832 | tf_op jit(solution)/shard_map/ppermute | solution.py:67
  11.7 7.9 %collective-permute-start.3 = (bf16[1,256,384]{2,1,0:T(8,128)(2,1)S(1)}, bf16[1,256,384]{2,1,0:T(8,128)(2,1)S(1)}, u32[]{:S(2)}, u32[]{:S(2)}) collective-permute-start(bf16[1,256,384]{2,1,0:T(8,128)(2,1)S(1)} %collective-permute-done.1.refs_5_), channel_id=1, source_target_pairs={{0,1},{1,0},{2,3},{3,2},{4,5},{5,4},{6,7},{7,6},{8,9},{9,8},{10,11... | collective-permute-start | bytes 589832 | tf_op jit(solution)/shard_map/ppermute | solution.py:67
  14.1 6.8 %collective-permute-start.12 = (bf16[1,256,384]{2,1,0:T(8,128)(2,1)S(1)}, bf16[1,256,384]{2,1,0:T(8,128)(2,1)S(1)}, u32[]{:S(2)}, u32[]{:S(2)}) collective-permute-start(bf16[1,256,384]{2,1,0:T(8,128)(2,1)S(1)} %collective-permute-done.refs_2_), channel_id=1, source_target_pairs={{0,8},{1,9},{2,10},{3,11},{4,12},{5,13},{6,14},{7,15},{8,0},{9,1},... | collective-permute-start | bytes 589832 | tf_op jit(solution)/shard_map/ppermute | solution.py:67
  19.6 7.3 %collective-permute-start.10 = (bf16[1,256,384]{2,1,0:T(8,128)(2,1)S(1)}, bf16[1,256,384]{2,1,0:T(8,128)(2,1)S(1)}, u32[]{:S(2)}, u32[]{:S(2)}) collective-permute-start(bf16[1,256,384]{2,1,0:T(8,128)(2,1)S(1)} %collective-permute-done.4.refs_1_), channel_id=1, source_target_pairs={{0,2},{1,3},{2,0},{3,1},{4,6},{5,7},{6,4},{7,5},{8,10},{9,11},{10,... | collective-permute-start | bytes 589832 | tf_op jit(solution)/shard_map/ppermute | solution.py:67
  20.3 12.4 %collective-permute-start.8 = (bf16[1,256,384]{2,1,0:T(8,128)(2,1)S(1)}, bf16[1,256,384]{2,1,0:T(8,128)(2,1)S(1)}, u32[]{:S(2)}, u32[]{:S(2)}) collective-permute-start(bf16[1,256,384]{2,1,0:T(8,128)(2,1)S(1)} %collective-permute-done.4.refs_1_), channel_id=1, source_target_pairs={{0,16},{1,17},{2,18},{3,19},{4,20},{5,21},{6,22},{7,23},{8,24},{9,... | collective-permute-start | bytes 589832 | tf_op jit(solution)/shard_map/ppermute | solution.py:67
  21.0 11.1 %collective-permute-start.7 = (bf16[2,128,384]{2,1,0:T(8,128)(2,1)S(1)}, bf16[2,128,384]{2,1,0:T(8,128)(2,1)S(1)}, u32[]{:S(2)}, u32[]{:S(2)}) collective-permute-start(bf16[2,128,384]{2,1,0:T(8,128)(2,1)S(1)} %pad_maximum_fusion.1), channel_id=1, source_target_pairs={{0,1},{1,0},{2,3},{3,2},{4,5},{5,4},{6,7},{7,6},{8,9},{9,8},{10,11... | collective-permute-start | bytes 589832 | tf_op jit(solution)/shard_map/ppermute | solution.py:67
  21.5 11.2 %collective-permute-start.6 = (bf16[2,128,384]{2,1,0:T(8,128)(2,1)S(1)}, bf16[2,128,384]{2,1,0:T(8,128)(2,1)S(1)}, u32[]{:S(2)}, u32[]{:S(2)}) collective-permute-start(bf16[2,128,384]{2,1,0:T(8,128)(2,1)S(1)} %pad_maximum_fusion), channel_id=1, source_target_pairs={{0,16},{1,17},{2,18},{3,19},{4,20},{5,21},{6,22},{7,23},{8,24},{9,... | collective-permute-start | bytes 589832 | tf_op jit(solution)/shard_map/ppermute | solution.py:67
  23.4 9.3 %collective-permute-start.9 = (bf16[1,256,384]{2,1,0:T(8,128)(2,1)S(1)}, bf16[1,256,384]{2,1,0:T(8,128)(2,1)S(1)}, u32[]{:S(2)}, u32[]{:S(2)}) collective-permute-start(bf16[1,256,384]{2,1,0:T(8,128)(2,1)S(1)} %collective-permute-done.4.refs_1_), channel_id=1, source_target_pairs={{0,1},{1,0},{2,3},{3,2},{4,5},{5,4},{6,7},{7,6},{8,9},{9,8},{10,11... | collective-permute-start | bytes 589832 | tf_op jit(solution)/shard_map/ppermute | solution.py:67
  26.9 7.0 %collective-permute-start.17 = (bf16[1,272,384]{2,1,0:T(8,128)(2,1)S(1)}, bf16[1,272,384]{2,1,0:T(8,128)(2,1)S(1)}, u32[]{:S(2)}, u32[]{:S(2)}) collective-permute-start(bf16[1,272,384]{2,1,0:T(8,128)(2,1)S(1)} %collective-permute-done.5.refs_1_.refs_14_), channel_id=1, source_target_pairs={{0,8},{1,9},{2,10},{3,11},{4,12},{5,13},{6,14},{7,15},{8,0},{9,1},... | collective-permute-start | bytes 626696 | tf_op jit(solution)/shard_map/ppermute | solution.py:67
  33.3 7.4 %collective-permute-start.15 = (bf16[1,256,384]{2,1,0:T(8,128)(2,1)S(1)}, bf16[1,256,384]{2,1,0:T(8,128)(2,1)S(1)}, u32[]{:S(2)}, u32[]{:S(2)}) collective-permute-start(bf16[1,256,384]{2,1,0:T(8,128)(2,1)S(1)} %collective-permute-done.10.refs_5_), channel_id=1, source_target_pairs={{0,16},{1,17},{2,18},{3,19},{4,20},{5,21},{6,22},{7,23},{8,24},{9,... | collective-permute-start | bytes 589832 | tf_op jit(solution)/shard_map/ppermute | solution.py:67
  33.9 7.3 %collective-permute-start.16 = (bf16[1,256,384]{2,1,0:T(8,128)(2,1)S(1)}, bf16[1,256,384]{2,1,0:T(8,128)(2,1)S(1)}, u32[]{:S(2)}, u32[]{:S(2)}) collective-permute-start(bf16[1,256,384]{2,1,0:T(8,128)(2,1)S(1)} %collective-permute-done.10.refs_5_), channel_id=1, source_target_pairs={{0,1},{1,0},{2,3},{3,2},{4,5},{5,4},{6,7},{7,6},{8,9},{9,8},{10,11... | collective-permute-start | bytes 589832 | tf_op jit(solution)/shard_map/ppermute | solution.py:67
  34.8 6.5 %collective-permute-start.25 = (bf16[1,256,384]{2,1,0:T(8,128)(2,1)S(1)}, bf16[1,256,384]{2,1,0:T(8,128)(2,1)S(1)}, u32[]{:S(2)}, u32[]{:S(2)}) collective-permute-start(bf16[1,256,384]{2,1,0:T(8,128)(2,1)S(1)} %collective-permute-done.4.refs_1_), channel_id=1, source_target_pairs={{0,8},{1,9},{2,10},{3,11},{4,12},{5,13},{6,14},{7,15},{8,0},{9,1},... | collective-permute-start | bytes 589832 | tf_op jit(solution)/shard_map/ppermute | solution.py:67
  34.9 7.7 %collective-permute-start.26 = (bf16[1,256,384]{2,1,0:T(8,128)(2,1)S(1)}, bf16[1,256,384]{2,1,0:T(8,128)(2,1)S(1)}, u32[]{:S(2)}, u32[]{:S(2)}) collective-permute-start(bf16[1,256,384]{2,1,0:T(8,128)(2,1)S(1)} %collective-permute-done.9.refs_2_), channel_id=1, source_target_pairs={{0,8},{1,9},{2,10},{3,11},{4,12},{5,13},{6,14},{7,15},{8,0},{9,1},... | collective-permute-start | bytes 589832 | tf_op jit(solution)/shard_map/ppermute | solution.py:67
  35.4 8.6 %collective-permute-start.27 = (bf16[1,256,384]{2,1,0:T(8,128)(2,1)S(1)}, bf16[1,256,384]{2,1,0:T(8,128)(2,1)S(1)}, u32[]{:S(2)}, u32[]{:S(2)}) collective-permute-start(bf16[1,256,384]{2,1,0:T(8,128)(2,1)S(1)} %collective-permute-done.10.refs_5_), channel_id=1, source_target_pairs={{0,8},{1,9},{2,10},{3,11},{4,12},{5,13},{6,14},{7,15},{8,0},{9,1},... | collective-permute-start | bytes 589832 | tf_op jit(solution)/shard_map/ppermute | solution.py:67
  40.6 11.8 %collective-permute-start.23 = (bf16[1,256,384]{2,1,0:T(8,128)(2,1)S(1)}, bf16[1,256,384]{2,1,0:T(8,128)(2,1)S(1)}, u32[]{:S(2)}, u32[]{:S(2)}) collective-permute-start(bf16[1,256,384]{2,1,0:T(8,128)(2,1)S(1)} %collective-permute-done.8.refs_1_), channel_id=1, source_target_pairs={{0,8},{1,9},{2,10},{3,11},{4,12},{5,13},{6,14},{7,15},{8,0},{9,1},... | collective-permute-start | bytes 589832 | tf_op jit(solution)/shard_map/ppermute | solution.py:67
  41.3 11.1 %collective-permute-start.22 = (bf16[2,128,384]{2,1,0:T(8,128)(2,1)S(1)}, bf16[2,128,384]{2,1,0:T(8,128)(2,1)S(1)}, u32[]{:S(2)}, u32[]{:S(2)}) collective-permute-start(bf16[2,128,384]{2,1,0:T(8,128)(2,1)S(1)} %pad_maximum_fusion.3), channel_id=1, source_target_pairs={{0,1},{1,0},{2,3},{3,2},{4,5},{5,4},{6,7},{7,6},{8,9},{9,8},{10,11... | collective-permute-start | bytes 589832 | tf_op jit(solution)/shard_map/ppermute | solution.py:67
  42.6 9.9 %collective-permute-start.21 = (bf16[2,128,384]{2,1,0:T(8,128)(2,1)S(1)}, bf16[2,128,384]{2,1,0:T(8,128)(2,1)S(1)}, u32[]{:S(2)}, u32[]{:S(2)}) collective-permute-start(bf16[2,128,384]{2,1,0:T(8,128)(2,1)S(1)} %pad_maximum_fusion.2), channel_id=1, source_target_pairs={{0,16},{1,17},{2,18},{3,19},{4,20},{5,21},{6,22},{7,23},{8,24},{9,... | collective-permute-start | bytes 589832 | tf_op jit(solution)/shard_map/ppermute | solution.py:67
  44.0 8.5 %collective-permute-start.24 = (bf16[1,256,384]{2,1,0:T(8,128)(2,1)S(1)}, bf16[1,256,384]{2,1,0:T(8,128)(2,1)S(1)}, u32[]{:S(2)}, u32[]{:S(2)}) collective-permute-start(bf16[1,256,384]{2,1,0:T(8,128)(2,1)S(1)} %collective-permute-done.15.refs_7_), channel_id=1, source_target_pairs={{0,8},{1,9},{2,10},{3,11},{4,12},{5,13},{6,14},{7,15},{8,0},{9,1},... | collective-permute-start | bytes 589832 | tf_op jit(solution)/shard_map/ppermute | solution.py:67
  55.5 7.1 %collective-permute-start.33 = (bf16[2,2,256,384]{3,2,1,0:T(8,128)(2,1)S(1)}, bf16[2,2,256,384]{3,2,1,0:T(8,128)(2,1)S(1)}, u32[]{:S(2)}, u32[]{:S(2)}) collective-permute-start(bf16[2,2,256,384]{3,2,1,0:T(8,128)(2,1)S(1)} %get-tuple-element.108), channel_id=1, source_target_pairs={{0,8},{1,9},{2,10},{3,11},{4,12},{5,13},{6,14},{7,15},{8,0},{9,1},... | collective-permute-start | bytes 2359304 | tf_op jit(solution)/shard_map/ppermute | solution.py:67
  65.7 29.1 %collective-permute-start.32 = (bf16[2,1,256,384]{3,2,1,0:T(8,128)(2,1)S(1)}, bf16[2,1,256,384]{3,2,1,0:T(8,128)(2,1)S(1)}, u32[]{:S(2)}, u32[]{:S(2)}) collective-permute-start(bf16[2,1,256,384]{3,2,1,0:T(8,128)(2,1)S(1)} %add_convert_fusion.1), channel_id=1, source_target_pairs={{0,2},{1,3},{2,0},{3,1},{4,6},{5,7},{6,4},{7,5},{8,10},{9,11},{10,... | collective-permute-start | bytes 1179656 | tf_op jit(solution)/shard_map/ppermute | solution.py:67
  67.0 6.7 %collective-permute-start.39 = (bf16[2,128,384]{2,1,0:T(8,128)(2,1)S(1)}, bf16[2,128,384]{2,1,0:T(8,128)(2,1)S(1)}, u32[]{:S(2)}, u32[]{:S(2)}) collective-permute-start(bf16[2,128,384]{2,1,0:T(8,128)(2,1)S(1)} %get-tuple-element.140), channel_id=1, source_target_pairs={{0,16},{1,17},{2,18},{3,19},{4,20},{5,21},{6,22},{7,23},{8,24},{9,... | collective-permute-start | bytes 589832 | tf_op jit(solution)/shard_map/ppermute | solution.py:67
  69.6 16.6 %collective-permute-start.36 = (bf16[2,1,256,384]{3,2,1,0:T(8,128)(2,1)S(1)}, bf16[2,1,256,384]{3,2,1,0:T(8,128)(2,1)S(1)}, u32[]{:S(2)}, u32[]{:S(2)}) collective-permute-start(bf16[2,1,256,384]{3,2,1,0:T(8,128)(2,1)S(1)} %add_convert_fusion), channel_id=1, source_target_pairs={{0,2},{1,3},{2,0},{3,1},{4,6},{5,7},{6,4},{7,5},{8,10},{9,11},{10,... | collective-permute-start | bytes 1179656 | tf_op jit(solution)/shard_map/ppermute | solution.py:67
  81.7 8.8 %collective-permute-start.45 = (bf16[1,256,384]{2,1,0:T(8,128)(2,1)S(1)}, bf16[1,256,384]{2,1,0:T(8,128)(2,1)S(1)}, u32[]{:S(2)}, u32[]{:S(2)}) collective-permute-start(bf16[1,256,384]{2,1,0:T(8,128)(2,1)S(1)} %fusion.4), channel_id=1, source_target_pairs={{0,2},{1,3},{2,0},{3,1},{4,6},{5,7},{6,4},{7,5},{8,10},{9,11},{10,... | collective-permute-start | bytes 589832 | tf_op jit(solution)/shard_map/ppermute | solution.py:67
  82.7 6.7 %collective-permute-start.43 = (bf16[1,256,384]{2,1,0:T(8,128)(2,1)S(1)}, bf16[1,256,384]{2,1,0:T(8,128)(2,1)S(1)}, u32[]{:S(2)}, u32[]{:S(2)}) collective-permute-start(bf16[1,256,384]{2,1,0:T(8,128)(2,1)S(1)} %slice.197), channel_id=1, source_target_pairs={{0,16},{1,17},{2,18},{3,19},{4,20},{5,21},{6,22},{7,23},{8,24},{9,... | collective-permute-start | bytes 589832 | tf_op jit(solution)/shard_map/ppermute | solution.py:67
  83.5 6.9 %collective-permute-start.44 = (bf16[1,256,384]{2,1,0:T(8,128)(2,1)S(1)}, bf16[1,256,384]{2,1,0:T(8,128)(2,1)S(1)}, u32[]{:S(2)}, u32[]{:S(2)}) collective-permute-start(bf16[1,256,384]{2,1,0:T(8,128)(2,1)S(1)} %slice.198), channel_id=1, source_target_pairs={{0,1},{1,0},{2,3},{3,2},{4,5},{5,4},{6,7},{7,6},{8,9},{9,8},{10,11... | collective-permute-start | bytes 589832 | tf_op jit(solution)/shard_map/ppermute | solution.py:67
  86.3 7.1 %collective-permute-start.37 = (bf16[1,128,384]{2,1,0:T(8,128)(2,1)S(1)}, bf16[1,128,384]{2,1,0:T(8,128)(2,1)S(1)}, u32[]{:S(2)}, u32[]{:S(2)}) collective-permute-start(bf16[1,128,384]{2,1,0:T(8,128)(2,1)S(1)} %get-tuple-element.138), channel_id=1, source_target_pairs={{0,16},{1,17},{2,18},{3,19},{4,20},{5,21},{6,22},{7,23},{8,24},{9,... | collective-permute-start | bytes 294920 | tf_op jit(solution)/shard_map/ppermute | solution.py:67
  90.5 10.4 %collective-permute-start.48 = (bf16[1,256,384]{2,1,0:T(8,128)(2,1)S(1)}, bf16[1,256,384]{2,1,0:T(8,128)(2,1)S(1)}, u32[]{:S(2)}, u32[]{:S(2)}) collective-permute-start(bf16[1,256,384]{2,1,0:T(8,128)(2,1)S(1)} %fusion.8), channel_id=1, source_target_pairs={{0,4},{1,5},{2,6},{3,7},{4,0},{5,1},{6,2},{7,3},{8,12},{9,13},{10,... | collective-permute-start | bytes 589832 | tf_op jit(solution)/shard_map/ppermute | solution.py:67
  94.1 6.8 %collective-permute-start.46 = (bf16[1,256,384]{2,1,0:T(8,128)(2,1)S(1)}, bf16[1,256,384]{2,1,0:T(8,128)(2,1)S(1)}, u32[]{:S(2)}, u32[]{:S(2)}) collective-permute-start(bf16[1,256,384]{2,1,0:T(8,128)(2,1)S(1)} %fusion.10), channel_id=1, source_target_pairs={{0,16},{1,17},{2,18},{3,19},{4,20},{5,21},{6,22},{7,23},{8,24},{9,... | collective-permute-start | bytes 589832 | tf_op jit(solution)/shard_map/ppermute | solution.py:67
  (17 other events, 65.1 us)

commit v6 on v3

--- a/solution.py
+++ b/solution.py
@@ -110,7 +110,7 @@
 
 def pieces(x, pair):
     blocks, over_x, over_y, first, last = pair
-    size = blocks[1][0][0].shape[1]
+    size = blocks[0][0][0].shape[1]
     arrays, found = [], []
     for z in range(2):
         for c in range(2):
@@ -223,33 +223,30 @@
 
 
 def second_kernel(place, *refs, x, found, z_places, pairs):
-    count = 17 if x else 19
+    count = 16 if x else 17
     arrays, refs = refs[:-count], refs[-count:]
     w_gate, w_up, gate, up, w_down = refs[:5]
-    shares, out = refs[5:7], refs[7:11]
-    rows, tails, sems, t_sems, d_sems, first_tile = refs[11:17]
-    hidden, second_tile = out[2:] if x else refs[17:]
+    shares, results, hidden = refs[5:7], refs[7:9], refs[9]
+    rows, tails, sems, t_sems, d_sems, tile = refs[-6:]
     copies = fill(place, arrays, found, z_places, rows, sems)
-    downs_in = [
-        down_copy(place, pair, w_down, tile, d_sems.at[k])
-        for k, (pair, tile) in enumerate(zip(pairs, (first_tile, second_tile)))
-    ]
+    downs_in = [down_copy(place, pairs[0], w_down, tile, d_sems.at[0])]
+    if x == 0:
+        downs_in.append(down_copy(place, pairs[1], w_down, refs[10], d_sems.at[1]))
     for copy in copies + downs_in:
         copy.start()
-    share = 0.5 * share_column(place, shares, tails, t_sems, out[0].shape[2])
+    share = 0.5 * share_column(place, shares, tails, t_sems, results[0].shape[2])
     for copy in copies:
         copy.wait()
     for t in range(gate.shape[0]):
-        tile = slice(t * HIDDEN_TILE, (t + 1) * HIDDEN_TILE)
-        g = gate[t] + jnp.dot(rows[...], w_gate[:, tile], preferred_element_type=jnp.float32)
-        u = up[t] + jnp.dot(rows[...], w_up[:, tile], preferred_element_type=jnp.float32)
+        span = slice(t * HIDDEN_TILE, (t + 1) * HIDDEN_TILE)
+        g = gate[t] + jnp.dot(rows[...], w_gate[:, span], preferred_element_type=jnp.float32)
+        u = up[t] + jnp.dot(rows[...], w_up[:, span], preferred_element_type=jnp.float32)
         value = (g + g * jnp.tanh(0.5 * g)) * u * share
-        hidden[:, tile] = value.astype(jnp.bfloat16)
+        hidden[:, span] = value.astype(jnp.bfloat16)
     downs_in[0].wait()
-    down_products(place, pairs[0], hidden, first_tile, out[:2])
-    downs_in[1].wait()
-    if x == 0:
-        down_products(place, pairs[1], hidden, second_tile, out[2:])
+    down_products(place, pairs[0], hidden, tile, results)
+    for copy in downs_in[1:]:
+        copy.wait()
 
 
 def third_kernel(place, hidden, tile, own, sibling, pair):
@@ -298,7 +295,7 @@
 
 def first_part(place, x, pair, z_places, weights, following, later):
     arrays, found = pieces(x, pair)
-    size, narrow = pair[0][1][0][0].shape[1:]
+    size, narrow = pair[0][0][0][0].shape[1:]
     depth, width = weights[0].shape
     rows = 2 * size
     sums = pltpu.VMEM((width // HIDDEN_TILE, rows, HIDDEN_TILE), jnp.float32)
@@ -324,7 +321,7 @@
 
 def second_part(place, x, pair, z_places, weights, sums, shares, w_down, pairs):
     arrays, found = pieces(x, pair)
-    size, narrow = pair[0][1][0][0].shape[1:]
+    size, narrow = pair[0][0][0][0].shape[1:]
     depth, width = weights[0].shape
     rows, tail = 2 * size, shares[0].shape[1] - size
     part = pltpu.VMEM((2, 2, size, narrow), jnp.bfloat16)
@@ -334,7 +331,7 @@
             *refs, x=x, found=found, z_places=z_places, pairs=pairs
         ),
         in_specs=[SCALARS] + [ANY] * len(arrays) + [VMEM] * 4 + [ANY] * 3,
-        out_specs=[VMEM] * 4,
+        out_specs=[VMEM] * (3 if x else 4),
         scratch_shapes=[
             pltpu.VMEM((rows, depth), jnp.bfloat16),
             pltpu.VMEM((2, tail, narrow), jnp.bfloat16),
@@ -342,10 +339,9 @@
             SEMS((2,)),
             SEMS((2,)),
             tile,
-        ]
-        + ([] if x else [hidden, tile]),
-        out_shape=[part, part] + ([hidden, tile] if x else [part, part]),
-        compiler_params=params(9 if x else 13),
+        ],
+        out_shape=[part, part, hidden] + ([] if x else [tile]),
+        compiler_params=params(9),
         cost_estimate=cost(
             flops=4 * rows * depth * width + 4 * rows * width * depth,
             bytes_accessed=8 * depth * width + 6 * rows * depth + 8 * rows * width,
@@ -397,13 +393,13 @@
     z0 = tokens[None]
     z1 = send(z0, z=1)
     own = shares_of(expert_ids, pair_logits)
-    block = jnp.concatenate([tokens, share_rows(own, narrow)])[None]
     sent = after(z0, own)
-    x0, y0, z2 = send(block, x=1), send(sent, y=1), send(z0, z=2)
+    x0, y0, z2 = send(sent, x=1), send(sent, y=1), send(sent, z=2)
+    tail = share_rows(own, narrow)[None]
     x1, y1 = send(z1, x=1), send(z1, y=1)
-    sz0, sz1, sx0, sx1, sy0, sy1 = swapped(block, z1, x0, x1, y0, y1)
+    sz0, sz1, sx0, sx1, sy0, sy1 = swapped(z0, z1, x0, x1, y0, y1)
     near_weights = pair_weights(place, 0, w_gate, w_up, narrow, x0)
-    (x1_, y1_), z2, near_weights = after(((x1, y1), z2, near_weights))
+    (x1_, y1_), z2, near_weights, tail = after(((x1, y1), z2, near_weights, tail))
     first, last = relayed([x0, x1_], [y0, y1_])
     z3 = send(z2, z=1)
     x2, y2 = send(z2, x=1), send(z2, y=1)
@@ -412,10 +408,11 @@
 
     z3, sums_0 = after((z3, sums_0))
     (first, last, x2, y2), sums_0 = after(((first, last, x2, y2), sums_0))
-    x3, y3 = send(z3, x=1), send(z3, y=1)
+    block = jnp.concatenate([z3, tail], axis=1)
+    x3, y3 = send(block, x=1), send(z3, y=1)
     both_of = lambda v: [(v, 0), (v, 1)]
     near[3:] = [both_of(v) for v in swapped(first, last)]
-    sz2, sz3, sx2, sy2 = swapped(z2, z3, x2, y2)
+    sz2, sz3, sx2, sy2 = swapped(z2, block, x2, y2)
     *sums_1, far_up = first_part(place, 1, near, (0, 1), near_weights, 2, w_up)
     far_weights = far_gate, far_up
     (x3, y3), sums_1 = after(((x3, y3), sums_1))
@@ -423,19 +420,23 @@
     sx3, sy3 = swapped(x3, y3)
     far = [[(sz2, 0), (sz3, 0)], [(sx2, 0), (sx3, 0)], [(sy2, 0), (sy3, 0)], None, None]
     pairs = (3, 2), (1, 0)
-    parts_0 = second_part(place, 0, far, (2, 3), far_weights, sums_0, sz0, w_down, pairs)
+    *parts_0, hidden, tile = second_part(
+        place, 0, far, (2, 3), far_weights, sums_0, sz3, w_down, pairs
+    )
     (first, last, sx2, sx3), parts_0 = after(((first, last, sx2, sx3), parts_0))
     far[1] = [(sx2, 0), (sx3, 0)]
-    far[3:] = [both_of(v) for v in swapped(first, last)]
-    near_0 = parts_0[2], send(parts_0[3], c=1)
-    near_0, parts_0 = after((near_0, parts_0), far[3:])
+    corners = swapped(first, last)
+    last_0 = third_part(place, hidden, tile, pairs[1], size)
+    corners, last_0 = after((corners, last_0))
+    far[3:] = [both_of(v) for v in corners]
     far_0 = parts_0[0], send(parts_0[1], c=1)
+    near_0 = last_0[0], send(last_0[1], c=1)
+    *parts_1, hidden = second_part(
+        place, 1, far, (2, 3), far_weights, sums_1, sx3, w_down, pairs
+    )
+    far_0, near_0, parts_1 = after((far_0, near_0, parts_1))
     to_z = total(*[v[:, :1] for v in near_0]).astype(jnp.bfloat16)
     passed_0 = send(to_z, z=1)
-    *parts_1, hidden, tile = second_part(
-        place, 1, far, (2, 3), far_weights, sums_1, sx0, w_down, pairs
-    )
-    far_0, parts_1 = after((far_0, parts_1))
     other_1 = send(parts_1[1], c=1)
     last_1 = third_part(place, after(hidden, far_0), tile, pairs[1], size)
     other_1, last_1 = after((other_1, last_1))

time: 101 us -> 103 us (1.020)
  waiting for transfers between devices: 25.5 us -> 30.9 us
  starting transfers between devices: 40.4 us -> 37 us
    ppermute x49, waiting for transfers between devices: 25.5 us -> 30.9 us  [send(): return lax.ppermute(value, BOTH, pairs)]
    ppermute x49, starting transfers between devices: 40.4 us -> 37 us  [send(): return lax.ppermute(value, BOTH, pairs)]
    pallas_call x1 -> x2, Pallas kernels: 2.37 us -> 4.73 us  [third_part(): pl.pallas_call(lambda *refs: third_kernel(*refs, pair=pair), in_specs=[SC...]
    pallas_call x2, Pallas kernels: 15.6 us -> 13.8 us  [second_part(): pl.pallas_call(lambda *refs: second_kernel(*refs, x=x, found=found, z_pla...]
  transfers between devices with their start and end apart: 49 -> 49, of which waited for: 13 -> 12; matrix products, arithmetic and copies ran while one was open for 4% -> 3% of each run, Pallas kernels for 30% -> 30%
where the time goes in v6:
time: 103 us
  starting transfers between devices  37 us (36%)
  waiting for transfers between devices  30.9 us (30%)
  Pallas kernels  30.7 us (30%)
  other arithmetic  3.51 us (3%)
    ppermute x49, starting transfers between devices, send(): return lax.ppermute(value, BOTH, pairs)  37 us
    ppermute x49, waiting for transfers between devices, send(): return lax.ppermute(value, BOTH, pairs)  30.9 us
    pallas_call x2, Pallas kernels, second_part(): pl.pallas_call(lambda *refs: second_kernel(*refs, x=x, found=found, z_pla...  13.8 us
    pallas_call x2, Pallas kernels, first_part(): pl.pallas_call(lambda *refs: first_kernel(*refs, found=found, z_places=z_...  8.71 us
    pallas_call x2, Pallas kernels, third_part(): pl.pallas_call(lambda *refs: third_kernel(*refs, pair=pair), in_specs=[SC...  4.73 us
    pallas_call x1, Pallas kernels, pair_weights(): pl.pallas_call(lambda *refs: weights_kernel(*refs, z=z), in_specs=[SCALAR...  3.41 us
  transfers between devices with their start and end apart: 49, of which 12 were waited for; matrix products, arithmetic and copies ran while one was open for 3% of the time, Pallas kernels for 30%

profile of v6, /device:TPU:0, one launch (start us, length us, event | category | flops | bytes accessed | tf_op | source)
XLA Modules:
  0.0 102.8 jit_solution(5055594089687420853)
XLA Ops:
  0.0 3.0 %collective-permute-start.1 = (bf16[1,256,384]{2,1,0:T(8,128)(2,1)}, bf16[1,256,384]{2,1,0:T(8,128)(2,1)S(1)}, u32[]{:S(2)}, u32[]{:S(2)}) collective-permute-start(bf16[1,256,384]{2,1,0:T(8,128)(2,1)} %bitcast.66), channel_id=1, source_target_pairs={{0,2},{1,3},{2,0},{3,1},{4,6},{5,7},{6,4},{7,5},{8,10},{9,11},{10,... | collective-permute-start | bytes 589832 | tf_op jit(solution)/shard_map/ppermute | solution.py:67
  4.5 1.5 %collective-permute-start.5 = (bf16[1,256,384]{2,1,0:T(8,128)(2,1)}, bf16[1,256,384]{2,1,0:T(8,128)(2,1)S(1)}, u32[]{:S(2)}, u32[]{:S(2)}) collective-permute-start(bf16[1,256,384]{2,1,0:T(8,128)(2,1)} %bitcast.67), channel_id=1, source_target_pairs={{0,16},{1,17},{2,18},{3,19},{4,20},{5,21},{6,22},{7,23},{8,24},{9,... | collective-permute-start | bytes 589832 | tf_op jit(solution)/shard_map/ppermute | solution.py:67
  6.1 2.6 %collective-permute-start.4 = (bf16[1,256,384]{2,1,0:T(8,128)(2,1)}, bf16[1,256,384]{2,1,0:T(8,128)(2,1)S(1)}, u32[]{:S(2)}, u32[]{:S(2)}) collective-permute-start(bf16[1,256,384]{2,1,0:T(8,128)(2,1)} %bitcast.68), channel_id=1, source_target_pairs={{0,4},{1,5},{2,6},{3,7},{4,0},{5,1},{6,2},{7,3},{8,12},{9,13},{10,... | collective-permute-start | bytes 589832 | tf_op jit(solution)/shard_map/ppermute | solution.py:67
  8.6 1.5 %collective-permute-start = (bf16[1,256,384]{2,1,0:T(8,128)(2,1)}, bf16[1,256,384]{2,1,0:T(8,128)(2,1)S(1)}, u32[]{:S(2)}, u32[]{:S(2)}) collective-permute-start(bf16[1,256,384]{2,1,0:T(8,128)(2,1)} %bitcast.69), channel_id=1, source_target_pairs={{0,1},{1,0},{2,3},{3,2},{4,5},{5,4},{6,7},{7,6},{8,9},{9,8},{10,11... | collective-permute-start | bytes 589832 | tf_op jit(solution)/shard_map/ppermute | solution.py:67
  11.0 1.5 %collective-permute-start.3 = (bf16[1,256,384]{2,1,0:T(8,128)(2,1)S(1)}, bf16[1,256,384]{2,1,0:T(8,128)(2,1)S(1)}, u32[]{:S(2)}, u32[]{:S(2)}) collective-permute-start(bf16[1,256,384]{2,1,0:T(8,128)(2,1)S(1)} %collective-permute-done.1.refs_5_), channel_id=1, source_target_pairs={{0,1},{1,0},{2,3},{3,2},{4,5},{5,4},{6,7},{7,6},{8,9},{9,8},{10,11... | collective-permute-start | bytes 589832 | tf_op jit(solution)/shard_map/ppermute | solution.py:67
  12.6 4.1 %collective-permute-done.refs_2_ = bf16[1,256,384]{2,1,0:T(8,128)(2,1)S(1)} collective-permute-done((bf16[1,256,384]{2,1,0:T(8,128)(2,1)}, bf16[1,256,384]{2,1,0:T(8,128)(2,1)S(1)}, u32[]{:S(2)}, u32[]{:S(2)}) %collective-permute-start) | collective-permute-done | bytes 196640 | tf_op jit(solution)/shard_map/ppermute | solution.py:67
  17.3 3.4 %pair_weights.1 = (bf16[1536,1024]{1,0:T(8,128)(2,1)S(1)}, bf16[1536,1024]{1,0:T(8,128)(2,1)S(1)}) custom-call(s32[7]{0:T(128)S(1)} %stack.33.refs_0_, bf16[1,256,384]{2,1,0:T(8,128)(2,1)S(1)} %collective-permute-done.5.refs_1_, bf16[3072,1024]{1,0:T(8,128)(2,1)} %bitcast.72, bf16[3072,1024]{1,0:T(8,128)(2,1)} %bitcast.74), custom_call_target="tpu_custom_call" | custom-call | bytes 3145728 | tf_op jit(solution)/shard_map/pair_weights/pallas_call | solution.py:284
  22.2 1.6 %collective-permute-start.6 = (bf16[2,128,384]{2,1,0:T(8,128)(2,1)S(1)}, bf16[2,128,384]{2,1,0:T(8,128)(2,1)S(1)}, u32[]{:S(2)}, u32[]{:S(2)}) collective-permute-start(bf16[2,128,384]{2,1,0:T(8,128)(2,1)S(1)} %pad_maximum_fusion), channel_id=1, source_target_pairs={{0,16},{1,17},{2,18},{3,19},{4,20},{5,21},{6,22},{7,23},{8,24},{9,... | collective-permute-start | bytes 589832 | tf_op jit(solution)/shard_map/ppermute | solution.py:67
  23.8 1.5 %collective-permute-start.7 = (bf16[2,128,384]{2,1,0:T(8,128)(2,1)S(1)}, bf16[2,128,384]{2,1,0:T(8,128)(2,1)S(1)}, u32[]{:S(2)}, u32[]{:S(2)}) collective-permute-start(bf16[2,128,384]{2,1,0:T(8,128)(2,1)S(1)} %pad_maximum_fusion.1), channel_id=1, source_target_pairs={{0,1},{1,0},{2,3},{3,2},{4,5},{5,4},{6,7},{7,6},{8,9},{9,8},{10,11... | collective-permute-start | bytes 589832 | tf_op jit(solution)/shard_map/ppermute | solution.py:67
  25.8 4.3 %first_part.2 = (f32[2,512,512]{2,1,0:T(8,128)S(1)}, f32[2,512,512]{2,1,0:T(8,128)S(1)}, bf16[1536,1024]{1,0:T(8,128)(2,1)S(1)}) custom-call(s32[7]{0:T(128)S(1)} %stack.33.refs_0_, bf16[1,256,384]{2,1,0:T(8,128)(2,1)S(1)} %bitcast.71, bf16[1,256,384]{2,1,0:T(8,128)(2,1)S(1)} %collective-permute-done.refs_2_, ...), custom_call_target="tpu_custom_call" | custom-call | flops 805306368 | bytes 3014656 | tf_op jit(solution)/shard_map/first_part/pallas_call | solution.py:302
  30.3 2.9 %collective-permute-done.6.refs_2_ = bf16[2,128,384]{2,1,0:T(8,128)(2,1)S(1)} collective-permute-done((bf16[2,128,384]{2,1,0:T(8,128)(2,1)S(1)}, bf16[2,128,384]{2,1,0:T(8,128)(2,1)S(1)}, u32[]{:S(2)}, u32[]{:S(2)}) %collective-permute-start.6) | collective-permute-done | bytes 196640 | tf_op jit(solution)/shard_map/ppermute | solution.py:67
  33.2 1.5 %collective-permute-done.9.refs_2_ = bf16[1,256,384]{2,1,0:T(8,128)(2,1)S(1)} collective-permute-done((bf16[1,256,384]{2,1,0:T(8,128)(2,1)S(1)}, bf16[1,256,384]{2,1,0:T(8,128)(2,1)S(1)}, u32[]{:S(2)}, u32[]{:S(2)}) %collective-permute-start.9) | collective-permute-done | bytes 196640 | tf_op jit(solution)/shard_map/ppermute | solution.py:67
  35.7 1.6 %collective-permute-start.16 = (bf16[1,256,384]{2,1,0:T(8,128)(2,1)S(1)}, bf16[1,256,384]{2,1,0:T(8,128)(2,1)S(1)}, u32[]{:S(2)}, u32[]{:S(2)}) collective-permute-start(bf16[1,256,384]{2,1,0:T(8,128)(2,1)S(1)} %collective-permute-done.10), channel_id=1, source_target_pairs={{0,1},{1,0},{2,3},{3,2},{4,5},{5,4},{6,7},{7,6},{8,9},{9,8},{10,11... | collective-permute-start | bytes 589832 | tf_op jit(solution)/shard_map/ppermute | solution.py:67
  38.0 4.4 %first_part.3 = (f32[2,512,512]{2,1,0:T(8,128)S(1)}, f32[2,512,512]{2,1,0:T(8,128)S(1)}, bf16[1536,1024]{1,0:T(8,128)(2,1)S(1)}) custom-call(s32[7]{0:T(128)S(1)} %stack.33.refs_0_, bf16[1,256,384]{2,1,0:T(8,128)(2,1)S(1)} %collective-permute-done.5.refs_1_, bf16[2,128,384]{2,1,0:T(8,128)(2,1)S(1)} %collective-permute-done.6.refs_2_, ...), custom_call_target="tpu_custom_call" | custom-call | flops 805306368 | bytes 3014656 | tf_op jit(solution)/shard_map/first_part/pallas_call | solution.py:302
  43.6 1.1 %collective-permute-start.22 = (bf16[2,128,384]{2,1,0:T(8,128)(2,1)S(1)}, bf16[2,128,384]{2,1,0:T(8,128)(2,1)S(1)}, u32[]{:S(2)}, u32[]{:S(2)}) collective-permute-start(bf16[2,128,384]{2,1,0:T(8,128)(2,1)S(1)} %pad_maximum_fusion.3), channel_id=1, source_target_pairs={{0,1},{1,0},{2,3},{3,2},{4,5},{5,4},{6,7},{7,6},{8,9},{9,8},{10,11... | collective-permute-start | bytes 589832 | tf_op jit(solution)/shard_map/ppermute | solution.py:67
  44.7 1.5 %collective-permute-start.21 = (bf16[2,128,384]{2,1,0:T(8,128)(2,1)S(1)}, bf16[2,128,384]{2,1,0:T(8,128)(2,1)S(1)}, u32[]{:S(2)}, u32[]{:S(2)}) collective-permute-start(bf16[2,128,384]{2,1,0:T(8,128)(2,1)S(1)} %pad_maximum_fusion.2), channel_id=1, source_target_pairs={{0,16},{1,17},{2,18},{3,19},{4,20},{5,21},{6,22},{7,23},{8,24},{9,... | collective-permute-start | bytes 589832 | tf_op jit(solution)/shard_map/ppermute | solution.py:67
  46.2 6.8 %second_part.2 = (bf16[2,2,256,384]{3,2,1,0:T(8,128)(2,1)S(1)}, bf16[2,2,256,384]{3,2,1,0:T(8,128)(2,1)S(1)}, bf16[512,1024]{1,0:T(8,128)(2,1)S(1)}, bf16[1024,1536]{1,0:T(8,128)(2,1)S(1)}) custom-call(s32[7]{0:T(128)S(1)} %stack.33.refs_0_, bf16[1,256,384]{2,1,0:T(8,128)(2,1)S(1)} %collective-permute-done.4.refs_1_, ...), custom_call_target="tpu_custom_call" | custom-call | flops 1610612736 | bytes 5373952 | tf_op jit(solution)/shard_map/second_part/pallas_call | solution.py:329
  53.6 2.4 %third_part.2 = (bf16[2,2,256,384]{3,2,1,0:T(8,128)(2,1)S(1)}, bf16[2,2,256,384]{3,2,1,0:T(8,128)(2,1)S(1)}) custom-call(s32[7]{0:T(128)S(1)} %stack.33.refs_0_, bf16[512,1024]{1,0:T(8,128)(2,1)S(1)} %get-tuple-element.106.refs_1_, bf16[1024,1536]{1,0:T(8,128)(2,1)S(1)} %get-tuple-element.107.refs_2_), custom_call_target="tpu_custom_call" | custom-call | flops 402653184 | bytes 1441792 | tf_op jit(solution)/shard_map/third_part/pallas_call | solution.py:357
  56.5 7.0 %second_part.3 = (bf16[2,2,256,384]{3,2,1,0:T(8,128)(2,1)S(1)}, bf16[2,2,256,384]{3,2,1,0:T(8,128)(2,1)S(1)}, bf16[512,1024]{1,0:T(8,128)(2,1)S(1)}) custom-call(s32[7]{0:T(128)S(1)} %stack.33.refs_0_, bf16[1,256,384]{2,1,0:T(8,128)(2,1)S(1)} %collective-permute-done.8.refs_1_, bf16[2,128,384]{2,1,0:T(8,128)(2,1)S(1)} %collective-permute-done.21.refs_2_, ...), custom_call_target="tpu_custom_call" | custom-call | flops 1610612736 | bytes 5373952 | tf_op jit(solution)/shard_map/second_part/pallas_call | solution.py:329
  63.8 2.4 %third_part.3 = (bf16[2,2,256,384]{3,2,1,0:T(8,128)(2,1)S(1)}, bf16[2,2,256,384]{3,2,1,0:T(8,128)(2,1)S(1)}) custom-call(s32[7]{0:T(128)S(1)} %stack.33.refs_0_, bf16[512,1024]{1,0:T(8,128)(2,1)S(1)} %get-tuple-element.130.refs_1_, bf16[1024,1536]{1,0:T(8,128)(2,1)S(1)} %get-tuple-element.107.refs_2_), custom_call_target="tpu_custom_call" | custom-call | flops 402653184 | bytes 1441792 | tf_op jit(solution)/shard_map/third_part/pallas_call | solution.py:357
  66.7 1.6 %collective-permute-start.33 = (bf16[2,1,256,384]{3,2,1,0:T(8,128)(2,1)S(1)}, bf16[2,1,256,384]{3,2,1,0:T(8,128)(2,1)S(1)}, u32[]{:S(2)}, u32[]{:S(2)}) collective-permute-start(bf16[2,1,256,384]{3,2,1,0:T(8,128)(2,1)S(1)} %add_convert_fusion.1), channel_id=1, source_target_pairs={{0,2},{1,3},{2,0},{3,1},{4,6},{5,7},{6,4},{7,5},{8,10},{9,11},{10,... | collective-permute-start | bytes 1179656 | tf_op jit(solution)/shard_map/ppermute | solution.py:67
  70.7 4.5 %collective-permute-done.39 = bf16[2,128,384]{2,1,0:T(8,128)(2,1)S(1)} collective-permute-done((bf16[2,128,384]{2,1,0:T(8,128)(2,1)S(1)}, bf16[2,128,384]{2,1,0:T(8,128)(2,1)S(1)}, u32[]{:S(2)}, u32[]{:S(2)}) %collective-permute-start.39) | collective-permute-done | bytes 196640 | tf_op jit(solution)/shard_map/ppermute | solution.py:67
  75.6 1.6 %collective-permute-start.41 = (bf16[1,256,384]{2,1,0:T(8,128)(2,1)S(1)}, bf16[1,256,384]{2,1,0:T(8,128)(2,1)S(1)}, u32[]{:S(2)}, u32[]{:S(2)}) collective-permute-start(bf16[1,256,384]{2,1,0:T(8,128)(2,1)S(1)} %slice.214), channel_id=1, source_target_pairs={{0,16},{1,17},{2,18},{3,19},{4,20},{5,21},{6,22},{7,23},{8,24},{9,... | collective-permute-start | bytes 589832 | tf_op jit(solution)/shard_map/ppermute | solution.py:67
  77.3 1.0 collective-permute-start.42
  78.4 2.9 %collective-permute-done.41 = bf16[1,256,384]{2,1,0:T(8,128)(2,1)S(1)} collective-permute-done((bf16[1,256,384]{2,1,0:T(8,128)(2,1)S(1)}, bf16[1,256,384]{2,1,0:T(8,128)(2,1)S(1)}, u32[]{:S(2)}, u32[]{:S(2)}) %collective-permute-start.41) | collective-permute-done | bytes 196640 | tf_op jit(solution)/shard_map/ppermute | solution.py:67
  81.3 1.7 %collective-permute-done.42 = bf16[1,256,384]{2,1,0:T(8,128)(2,1)S(1)} collective-permute-done((bf16[1,256,384]{2,1,0:T(8,128)(2,1)S(1)}, bf16[1,256,384]{2,1,0:T(8,128)(2,1)S(1)}, u32[]{:S(2)}, u32[]{:S(2)}) %collective-permute-start.42) | collective-permute-done | bytes 196640 | tf_op jit(solution)/shard_map/ppermute | solution.py:67
  84.3 1.0 collective-permute-start.44
  85.3 1.9 %collective-permute-done.36 = bf16[2,1,256,384]{3,2,1,0:T(8,128)(2,1)S(1)} collective-permute-done((bf16[2,1,256,384]{3,2,1,0:T(8,128)(2,1)S(1)}, bf16[2,1,256,384]{3,2,1,0:T(8,128)(2,1)S(1)}, u32[]{:S(2)}, u32[]{:S(2)}) %collective-permute-start.36) | collective-permute-done | bytes 393248 | tf_op jit(solution)/shard_map/ppermute | solution.py:67
  87.9 2.6 %collective-permute-done.43 = bf16[1,256,384]{2,1,0:T(8,128)(2,1)S(1)} collective-permute-done((bf16[1,256,384]{2,1,0:T(8,128)(2,1)S(1)}, bf16[1,256,384]{2,1,0:T(8,128)(2,1)S(1)}, u32[]{:S(2)}, u32[]{:S(2)}) %collective-permute-start.43) | collective-permute-done | bytes 196640 | tf_op jit(solution)/shard_map/ppermute | solution.py:67
  92.0 3.2 %collective-permute-done.38 = bf16[1,128,384]{2,1,0:T(8,128)(2,1)S(1)} collective-permute-done((bf16[1,128,384]{2,1,0:T(8,128)(2,1)S(1)}, bf16[1,128,384]{2,1,0:T(8,128)(2,1)S(1)}, u32[]{:S(2)}, u32[]{:S(2)}) %collective-permute-start.38) | collective-permute-done | bytes 98336 | tf_op jit(solution)/shard_map/ppermute | solution.py:67
  96.0 1.0 collective-permute-start.47
  97.0 4.9 %collective-permute-done.48 = bf16[1,256,384]{2,1,0:T(8,128)(2,1)S(1)} collective-permute-done((bf16[1,256,384]{2,1,0:T(8,128)(2,1)S(1)}, bf16[1,256,384]{2,1,0:T(8,128)(2,1)S(1)}, u32[]{:S(2)}, u32[]{:S(2)}) %collective-permute-start.48) | collective-permute-done | bytes 196640 | tf_op jit(solution)/shard_map/ppermute | solution.py:67
  (111 shorter events, 17.8 us)
Async XLA Ops:
  0.0 10.2 %collective-permute-start.1 = (bf16[1,256,384]{2,1,0:T(8,128)(2,1)}, bf16[1,256,384]{2,1,0:T(8,128)(2,1)S(1)}, u32[]{:S(2)}, u32[]{:S(2)}) collective-permute-start(bf16[1,256,384]{2,1,0:T(8,128)(2,1)} %bitcast.66), channel_id=1, source_target_pairs={{0,2},{1,3},{2,0},{3,1},{4,6},{5,7},{6,4},{7,5},{8,10},{9,11},{10,... | collective-permute-start | bytes 589832 | tf_op jit(solution)/shard_map/ppermute | solution.py:67
  4.5 12.2 %collective-permute-start.5 = (bf16[1,256,384]{2,1,0:T(8,128)(2,1)}, bf16[1,256,384]{2,1,0:T(8,128)(2,1)S(1)}, u32[]{:S(2)}, u32[]{:S(2)}) collective-permute-start(bf16[1,256,384]{2,1,0:T(8,128)(2,1)} %bitcast.67), channel_id=1, source_target_pairs={{0,16},{1,17},{2,18},{3,19},{4,20},{5,21},{6,22},{7,23},{8,24},{9,... | collective-permute-start | bytes 589832 | tf_op jit(solution)/shard_map/ppermute | solution.py:67
  6.1 14.7 %collective-permute-start.4 = (bf16[1,256,384]{2,1,0:T(8,128)(2,1)}, bf16[1,256,384]{2,1,0:T(8,128)(2,1)S(1)}, u32[]{:S(2)}, u32[]{:S(2)}) collective-permute-start(bf16[1,256,384]{2,1,0:T(8,128)(2,1)} %bitcast.68), channel_id=1, source_target_pairs={{0,4},{1,5},{2,6},{3,7},{4,0},{5,1},{6,2},{7,3},{8,12},{9,13},{10,... | collective-permute-start | bytes 589832 | tf_op jit(solution)/shard_map/ppermute | solution.py:67
  8.6 8.1 %collective-permute-start = (bf16[1,256,384]{2,1,0:T(8,128)(2,1)}, bf16[1,256,384]{2,1,0:T(8,128)(2,1)S(1)}, u32[]{:S(2)}, u32[]{:S(2)}) collective-permute-start(bf16[1,256,384]{2,1,0:T(8,128)(2,1)} %bitcast.69), channel_id=1, source_target_pairs={{0,1},{1,0},{2,3},{3,2},{4,5},{5,4},{6,7},{7,6},{8,9},{9,8},{10,11... | collective-permute-start | bytes 589832 | tf_op jit(solution)/shard_map/ppermute | solution.py:67
  10.2 10.7 %collective-permute-start.2 = (bf16[1,256,384]{2,1,0:T(8,128)(2,1)S(1)}, bf16[1,256,384]{2,1,0:T(8,128)(2,1)S(1)}, u32[]{:S(2)}, u32[]{:S(2)}) collective-permute-start(bf16[1,256,384]{2,1,0:T(8,128)(2,1)S(1)} %collective-permute-done.1.refs_5_), channel_id=1, source_target_pairs={{0,16},{1,17},{2,18},{3,19},{4,20},{5,21},{6,22},{7,23},{8,24},{9,... | collective-permute-start | bytes 589832 | tf_op jit(solution)/shard_map/ppermute | solution.py:67
  11.0 9.9 %collective-permute-start.3 = (bf16[1,256,384]{2,1,0:T(8,128)(2,1)S(1)}, bf16[1,256,384]{2,1,0:T(8,128)(2,1)S(1)}, u32[]{:S(2)}, u32[]{:S(2)}) collective-permute-start(bf16[1,256,384]{2,1,0:T(8,128)(2,1)S(1)} %collective-permute-done.1.refs_5_), channel_id=1, source_target_pairs={{0,1},{1,0},{2,3},{3,2},{4,5},{5,4},{6,7},{7,6},{8,9},{9,8},{10,11... | collective-permute-start | bytes 589832 | tf_op jit(solution)/shard_map/ppermute | solution.py:67
  20.9 9.3 %collective-permute-start.10 = (bf16[1,256,384]{2,1,0:T(8,128)(2,1)S(1)}, bf16[1,256,384]{2,1,0:T(8,128)(2,1)S(1)}, u32[]{:S(2)}, u32[]{:S(2)}) collective-permute-start(bf16[1,256,384]{2,1,0:T(8,128)(2,1)S(1)} %collective-permute-done.4.refs_1_), channel_id=1, source_target_pairs={{0,2},{1,3},{2,0},{3,1},{4,6},{5,7},{6,4},{7,5},{8,10},{9,11},{10,... | collective-permute-start | bytes 589832 | tf_op jit(solution)/shard_map/ppermute | solution.py:67
  21.7 11.5 %collective-permute-start.8 = (bf16[1,256,384]{2,1,0:T(8,128)(2,1)S(1)}, bf16[1,256,384]{2,1,0:T(8,128)(2,1)S(1)}, u32[]{:S(2)}, u32[]{:S(2)}) collective-permute-start(bf16[1,256,384]{2,1,0:T(8,128)(2,1)S(1)} %collective-permute-done.4.refs_1_), channel_id=1, source_target_pairs={{0,16},{1,17},{2,18},{3,19},{4,20},{5,21},{6,22},{7,23},{8,24},{9,... | collective-permute-start | bytes 589832 | tf_op jit(solution)/shard_map/ppermute | solution.py:67
  22.2 10.9 %collective-permute-start.6 = (bf16[2,128,384]{2,1,0:T(8,128)(2,1)S(1)}, bf16[2,128,384]{2,1,0:T(8,128)(2,1)S(1)}, u32[]{:S(2)}, u32[]{:S(2)}) collective-permute-start(bf16[2,128,384]{2,1,0:T(8,128)(2,1)S(1)} %pad_maximum_fusion), channel_id=1, source_target_pairs={{0,16},{1,17},{2,18},{3,19},{4,20},{5,21},{6,22},{7,23},{8,24},{9,... | collective-permute-start | bytes 589832 | tf_op jit(solution)/shard_map/ppermute | solution.py:67
  23.8 9.3 %collective-permute-start.7 = (bf16[2,128,384]{2,1,0:T(8,128)(2,1)S(1)}, bf16[2,128,384]{2,1,0:T(8,128)(2,1)S(1)}, u32[]{:S(2)}, u32[]{:S(2)}) collective-permute-start(bf16[2,128,384]{2,1,0:T(8,128)(2,1)S(1)} %pad_maximum_fusion.1), channel_id=1, source_target_pairs={{0,1},{1,0},{2,3},{3,2},{4,5},{5,4},{6,7},{7,6},{8,9},{9,8},{10,11... | collective-permute-start | bytes 589832 | tf_op jit(solution)/shard_map/ppermute | solution.py:67
  25.3 9.3 %collective-permute-start.9 = (bf16[1,256,384]{2,1,0:T(8,128)(2,1)S(1)}, bf16[1,256,384]{2,1,0:T(8,128)(2,1)S(1)}, u32[]{:S(2)}, u32[]{:S(2)}) collective-permute-start(bf16[1,256,384]{2,1,0:T(8,128)(2,1)S(1)} %collective-permute-done.4.refs_1_), channel_id=1, source_target_pairs={{0,1},{1,0},{2,3},{3,2},{4,5},{5,4},{6,7},{7,6},{8,9},{9,8},{10,11... | collective-permute-start | bytes 589832 | tf_op jit(solution)/shard_map/ppermute | solution.py:67
  35.2 7.2 %collective-permute-start.15 = (bf16[1,272,384]{2,1,0:T(8,128)(2,1)S(1)}, bf16[1,272,384]{2,1,0:T(8,128)(2,1)S(1)}, u32[]{:S(2)}, u32[]{:S(2)}) collective-permute-start(bf16[1,272,384]{2,1,0:T(8,128)(2,1)S(1)} %constant_dynamic-update-slice_fusion.refs_5_.refs_14_), channel_id=1, source_target_pairs={{0,16},{1,17},{2,18},{3,19},{4,20},{5,21},{6,22},{7,23},{8,24},{9,... | collective-permute-start | bytes 626696 | tf_op jit(solution)/shard_map/ppermute | solution.py:67
  35.7 6.7 %collective-permute-start.16 = (bf16[1,256,384]{2,1,0:T(8,128)(2,1)S(1)}, bf16[1,256,384]{2,1,0:T(8,128)(2,1)S(1)}, u32[]{:S(2)}, u32[]{:S(2)}) collective-permute-start(bf16[1,256,384]{2,1,0:T(8,128)(2,1)S(1)} %collective-permute-done.10), channel_id=1, source_target_pairs={{0,1},{1,0},{2,3},{3,2},{4,5},{5,4},{6,7},{7,6},{8,9},{9,8},{10,11... | collective-permute-start | bytes 589832 | tf_op jit(solution)/shard_map/ppermute | solution.py:67
  37.3 5.8 %collective-permute-start.25 = (bf16[1,256,384]{2,1,0:T(8,128)(2,1)S(1)}, bf16[1,256,384]{2,1,0:T(8,128)(2,1)S(1)}, u32[]{:S(2)}, u32[]{:S(2)}) collective-permute-start(bf16[1,256,384]{2,1,0:T(8,128)(2,1)S(1)} %collective-permute-done.4.refs_1_), channel_id=1, source_target_pairs={{0,8},{1,9},{2,10},{3,11},{4,12},{5,13},{6,14},{7,15},{8,0},{9,1},... | collective-permute-start | bytes 589832 | tf_op jit(solution)/shard_map/ppermute | solution.py:67
  37.4 6.2 %collective-permute-start.26 = (bf16[1,256,384]{2,1,0:T(8,128)(2,1)S(1)}, bf16[1,256,384]{2,1,0:T(8,128)(2,1)S(1)}, u32[]{:S(2)}, u32[]{:S(2)}) collective-permute-start(bf16[1,256,384]{2,1,0:T(8,128)(2,1)S(1)} %collective-permute-done.9.refs_2_), channel_id=1, source_target_pairs={{0,8},{1,9},{2,10},{3,11},{4,12},{5,13},{6,14},{7,15},{8,0},{9,1},... | collective-permute-start | bytes 589832 | tf_op jit(solution)/shard_map/ppermute | solution.py:67
  37.9 6.7 %collective-permute-start.27 = (bf16[1,272,384]{2,1,0:T(8,128)(2,1)S(1)}, bf16[1,272,384]{2,1,0:T(8,128)(2,1)S(1)}, u32[]{:S(2)}, u32[]{:S(2)}) collective-permute-start(bf16[1,272,384]{2,1,0:T(8,128)(2,1)S(1)} %constant_dynamic-update-slice_fusion.refs_5_.refs_14_), channel_id=1, source_target_pairs={{0,8},{1,9},{2,10},{3,11},{4,12},{5,13},{6,14},{7,15},{8,0},{9,1},... | collective-permute-start | bytes 626696 | tf_op jit(solution)/shard_map/ppermute | solution.py:67
  42.4 10.6 %collective-permute-start.24 = (bf16[1,272,384]{2,1,0:T(8,128)(2,1)S(1)}, bf16[1,272,384]{2,1,0:T(8,128)(2,1)S(1)}, u32[]{:S(2)}, u32[]{:S(2)}) collective-permute-start(bf16[1,272,384]{2,1,0:T(8,128)(2,1)S(1)} %collective-permute-done.15.refs_7_.refs_14_), channel_id=1, source_target_pairs={{0,8},{1,9},{2,10},{3,11},{4,12},{5,13},{6,14},{7,15},{8,0},{9,1},... | collective-permute-start | bytes 626696 | tf_op jit(solution)/shard_map/ppermute | solution.py:67
  43.1 9.9 %collective-permute-start.23 = (bf16[1,256,384]{2,1,0:T(8,128)(2,1)S(1)}, bf16[1,256,384]{2,1,0:T(8,128)(2,1)S(1)}, u32[]{:S(2)}, u32[]{:S(2)}) collective-permute-start(bf16[1,256,384]{2,1,0:T(8,128)(2,1)S(1)} %collective-permute-done.8.refs_1_), channel_id=1, source_target_pairs={{0,8},{1,9},{2,10},{3,11},{4,12},{5,13},{6,14},{7,15},{8,0},{9,1},... | collective-permute-start | bytes 589832 | tf_op jit(solution)/shard_map/ppermute | solution.py:67
  43.6 9.4 %collective-permute-start.22 = (bf16[2,128,384]{2,1,0:T(8,128)(2,1)S(1)}, bf16[2,128,384]{2,1,0:T(8,128)(2,1)S(1)}, u32[]{:S(2)}, u32[]{:S(2)}) collective-permute-start(bf16[2,128,384]{2,1,0:T(8,128)(2,1)S(1)} %pad_maximum_fusion.3), channel_id=1, source_target_pairs={{0,1},{1,0},{2,3},{3,2},{4,5},{5,4},{6,7},{7,6},{8,9},{9,8},{10,11... | collective-permute-start | bytes 589832 | tf_op jit(solution)/shard_map/ppermute | solution.py:67
  44.7 8.3 %collective-permute-start.21 = (bf16[2,128,384]{2,1,0:T(8,128)(2,1)S(1)}, bf16[2,128,384]{2,1,0:T(8,128)(2,1)S(1)}, u32[]{:S(2)}, u32[]{:S(2)}) collective-permute-start(bf16[2,128,384]{2,1,0:T(8,128)(2,1)S(1)} %pad_maximum_fusion.2), channel_id=1, source_target_pairs={{0,16},{1,17},{2,18},{3,19},{4,20},{5,21},{6,22},{7,23},{8,24},{9,... | collective-permute-start | bytes 589832 | tf_op jit(solution)/shard_map/ppermute | solution.py:67
  56.0 7.6 %collective-permute-start.29 = (bf16[2,2,256,384]{3,2,1,0:T(8,128)(2,1)S(1)}, bf16[2,2,256,384]{3,2,1,0:T(8,128)(2,1)S(1)}, u32[]{:S(2)}, u32[]{:S(2)}) collective-permute-start(bf16[2,2,256,384]{3,2,1,0:T(8,128)(2,1)S(1)} %get-tuple-element.103), channel_id=1, source_target_pairs={{0,8},{1,9},{2,10},{3,11},{4,12},{5,13},{6,14},{7,15},{8,0},{9,1},... | collective-permute-start | bytes 2359304 | tf_op jit(solution)/shard_map/ppermute | solution.py:67
  56.1 7.5 %collective-permute-start.32 = (bf16[2,2,256,384]{3,2,1,0:T(8,128)(2,1)S(1)}, bf16[2,2,256,384]{3,2,1,0:T(8,128)(2,1)S(1)}, u32[]{:S(2)}, u32[]{:S(2)}) collective-permute-start(bf16[2,2,256,384]{3,2,1,0:T(8,128)(2,1)S(1)} %get-tuple-element.111), channel_id=1, source_target_pairs={{0,8},{1,9},{2,10},{3,11},{4,12},{5,13},{6,14},{7,15},{8,0},{9,1},... | collective-permute-start | bytes 2359304 | tf_op jit(solution)/shard_map/ppermute | solution.py:67
  66.7 29.2 %collective-permute-start.33 = (bf16[2,1,256,384]{3,2,1,0:T(8,128)(2,1)S(1)}, bf16[2,1,256,384]{3,2,1,0:T(8,128)(2,1)S(1)}, u32[]{:S(2)}, u32[]{:S(2)}) collective-permute-start(bf16[2,1,256,384]{3,2,1,0:T(8,128)(2,1)S(1)} %add_convert_fusion.1), channel_id=1, source_target_pairs={{0,2},{1,3},{2,0},{3,1},{4,6},{5,7},{6,4},{7,5},{8,10},{9,11},{10,... | collective-permute-start | bytes 1179656 | tf_op jit(solution)/shard_map/ppermute | solution.py:67
  68.5 6.7 %collective-permute-start.39 = (bf16[2,128,384]{2,1,0:T(8,128)(2,1)S(1)}, bf16[2,128,384]{2,1,0:T(8,128)(2,1)S(1)}, u32[]{:S(2)}, u32[]{:S(2)}) collective-permute-start(bf16[2,128,384]{2,1,0:T(8,128)(2,1)S(1)} %get-tuple-element.148), channel_id=1, source_target_pairs={{0,16},{1,17},{2,18},{3,19},{4,20},{5,21},{6,22},{7,23},{8,24},{9,... | collective-permute-start | bytes 589832 | tf_op jit(solution)/shard_map/ppermute | solution.py:67
  69.1 6.4 %collective-permute-start.40 = (bf16[2,128,384]{2,1,0:T(8,128)(2,1)S(1)}, bf16[2,128,384]{2,1,0:T(8,128)(2,1)S(1)}, u32[]{:S(2)}, u32[]{:S(2)}) collective-permute-start(bf16[2,128,384]{2,1,0:T(8,128)(2,1)S(1)} %get-tuple-element.147), channel_id=1, source_target_pairs={{0,1},{1,0},{2,3},{3,2},{4,5},{5,4},{6,7},{7,6},{8,9},{9,8},{10,11... | collective-permute-start | bytes 589832 | tf_op jit(solution)/shard_map/ppermute | solution.py:67
  70.1 17.1 %collective-permute-start.36 = (bf16[2,1,256,384]{3,2,1,0:T(8,128)(2,1)S(1)}, bf16[2,1,256,384]{3,2,1,0:T(8,128)(2,1)S(1)}, u32[]{:S(2)}, u32[]{:S(2)}) collective-permute-start(bf16[2,1,256,384]{3,2,1,0:T(8,128)(2,1)S(1)} %add_convert_fusion), channel_id=1, source_target_pairs={{0,2},{1,3},{2,0},{3,1},{4,6},{5,7},{6,4},{7,5},{8,10},{9,11},{10,... | collective-permute-start | bytes 1179656 | tf_op jit(solution)/shard_map/ppermute | solution.py:67
  83.1 8.2 %collective-permute-start.45 = (bf16[1,256,384]{2,1,0:T(8,128)(2,1)S(1)}, bf16[1,256,384]{2,1,0:T(8,128)(2,1)S(1)}, u32[]{:S(2)}, u32[]{:S(2)}) collective-permute-start(bf16[1,256,384]{2,1,0:T(8,128)(2,1)S(1)} %fusion.4), channel_id=1, source_target_pairs={{0,2},{1,3},{2,0},{3,1},{4,6},{5,7},{6,4},{7,5},{8,10},{9,11},{10,... | collective-permute-start | bytes 589832 | tf_op jit(solution)/shard_map/ppermute | solution.py:67
  83.7 6.8 %collective-permute-start.43 = (bf16[1,256,384]{2,1,0:T(8,128)(2,1)S(1)}, bf16[1,256,384]{2,1,0:T(8,128)(2,1)S(1)}, u32[]{:S(2)}, u32[]{:S(2)}) collective-permute-start(bf16[1,256,384]{2,1,0:T(8,128)(2,1)S(1)} %slice.197), channel_id=1, source_target_pairs={{0,16},{1,17},{2,18},{3,19},{4,20},{5,21},{6,22},{7,23},{8,24},{9,... | collective-permute-start | bytes 589832 | tf_op jit(solution)/shard_map/ppermute | solution.py:67
  84.3 7.1 %collective-permute-start.44 = (bf16[1,256,384]{2,1,0:T(8,128)(2,1)S(1)}, bf16[1,256,384]{2,1,0:T(8,128)(2,1)S(1)}, u32[]{:S(2)}, u32[]{:S(2)}) collective-permute-start(bf16[1,256,384]{2,1,0:T(8,128)(2,1)S(1)} %slice.198), channel_id=1, source_target_pairs={{0,1},{1,0},{2,3},{3,2},{4,5},{5,4},{6,7},{7,6},{8,9},{9,8},{10,11... | collective-permute-start | bytes 589832 | tf_op jit(solution)/shard_map/ppermute | solution.py:67
  91.5 10.4 %collective-permute-start.48 = (bf16[1,256,384]{2,1,0:T(8,128)(2,1)S(1)}, bf16[1,256,384]{2,1,0:T(8,128)(2,1)S(1)}, u32[]{:S(2)}, u32[]{:S(2)}) collective-permute-start(bf16[1,256,384]{2,1,0:T(8,128)(2,1)S(1)} %fusion.8), channel_id=1, source_target_pairs={{0,4},{1,5},{2,6},{3,7},{4,0},{5,1},{6,2},{7,3},{8,12},{9,13},{10,... | collective-permute-start | bytes 589832 | tf_op jit(solution)/shard_map/ppermute | solution.py:67
  95.3 6.7 %collective-permute-start.46 = (bf16[1,256,384]{2,1,0:T(8,128)(2,1)S(1)}, bf16[1,256,384]{2,1,0:T(8,128)(2,1)S(1)}, u32[]{:S(2)}, u32[]{:S(2)}) collective-permute-start(bf16[1,256,384]{2,1,0:T(8,128)(2,1)S(1)} %fusion.10), channel_id=1, source_target_pairs={{0,16},{1,17},{2,18},{3,19},{4,20},{5,21},{6,22},{7,23},{8,24},{9,... | collective-permute-start | bytes 589832 | tf_op jit(solution)/shard_map/ppermute | solution.py:67
  96.0 5.9 %collective-permute-start.47 = (bf16[1,256,384]{2,1,0:T(8,128)(2,1)S(1)}, bf16[1,256,384]{2,1,0:T(8,128)(2,1)S(1)}, u32[]{:S(2)}, u32[]{:S(2)}) collective-permute-start(bf16[1,256,384]{2,1,0:T(8,128)(2,1)S(1)} %fusion.9), channel_id=1, source_target_pairs={{0,1},{1,0},{2,3},{3,2},{4,5},{5,4},{6,7},{7,6},{8,9},{9,8},{10,11... | collective-permute-start | bytes 589832 | tf_op jit(solution)/shard_map/ppermute | solution.py:67
  (18 other events, 78.5 us)

commit v7 on v6

--- a/solution.py
+++ b/solution.py
@@ -110,7 +110,7 @@
 
 def pieces(x, pair):
     blocks, over_x, over_y, first, last = pair
-    size = blocks[0][0][0].shape[1]
+    size = blocks[1][0][0].shape[1]
     arrays, found = [], []
     for z in range(2):
         for c in range(2):
@@ -295,7 +295,7 @@
 
 def first_part(place, x, pair, z_places, weights, following, later):
     arrays, found = pieces(x, pair)
-    size, narrow = pair[0][0][0][0].shape[1:]
+    size, narrow = pair[0][1][0][0].shape[1:]
     depth, width = weights[0].shape
     rows = 2 * size
     sums = pltpu.VMEM((width // HIDDEN_TILE, rows, HIDDEN_TILE), jnp.float32)
@@ -321,7 +321,7 @@
 
 def second_part(place, x, pair, z_places, weights, sums, shares, w_down, pairs):
     arrays, found = pieces(x, pair)
-    size, narrow = pair[0][0][0][0].shape[1:]
+    size, narrow = pair[0][1][0][0].shape[1:]
     depth, width = weights[0].shape
     rows, tail = 2 * size, shares[0].shape[1] - size
     part = pltpu.VMEM((2, 2, size, narrow), jnp.bfloat16)
@@ -393,13 +393,13 @@
     z0 = tokens[None]
     z1 = send(z0, z=1)
     own = shares_of(expert_ids, pair_logits)
+    block = jnp.concatenate([tokens, share_rows(own, narrow)])[None]
     sent = after(z0, own)
-    x0, y0, z2 = send(sent, x=1), send(sent, y=1), send(sent, z=2)
-    tail = share_rows(own, narrow)[None]
+    x0, y0, z2 = send(block, x=1), send(sent, y=1), send(sent, z=2)
     x1, y1 = send(z1, x=1), send(z1, y=1)
-    sz0, sz1, sx0, sx1, sy0, sy1 = swapped(z0, z1, x0, x1, y0, y1)
+    sz0, sz1, sx0, sx1, sy0, sy1 = swapped(block, z1, x0, x1, y0, y1)
     near_weights = pair_weights(place, 0, w_gate, w_up, narrow, x0)
-    (x1_, y1_), z2, near_weights, tail = after(((x1, y1), z2, near_weights, tail))
+    (x1_, y1_), z2, near_weights = after(((x1, y1), z2, near_weights))
     first, last = relayed([x0, x1_], [y0, y1_])
     z3 = send(z2, z=1)
     x2, y2 = send(z2, x=1), send(z2, y=1)
@@ -408,11 +408,10 @@
 
     z3, sums_0 = after((z3, sums_0))
     (first, last, x2, y2), sums_0 = after(((first, last, x2, y2), sums_0))
-    block = jnp.concatenate([z3, tail], axis=1)
-    x3, y3 = send(block, x=1), send(z3, y=1)
+    x3, y3 = send(z3, x=1), send(z3, y=1)
     both_of = lambda v: [(v, 0), (v, 1)]
     near[3:] = [both_of(v) for v in swapped(first, last)]
-    sz2, sz3, sx2, sy2 = swapped(z2, block, x2, y2)
+    sz2, sz3, sx2, sy2 = swapped(z2, z3, x2, y2)
     *sums_1, far_up = first_part(place, 1, near, (0, 1), near_weights, 2, w_up)
     far_weights = far_gate, far_up
     (x3, y3), sums_1 = after(((x3, y3), sums_1))
@@ -421,7 +420,7 @@
     far = [[(sz2, 0), (sz3, 0)], [(sx2, 0), (sx3, 0)], [(sy2, 0), (sy3, 0)], None, None]
     pairs = (3, 2), (1, 0)
     *parts_0, hidden, tile = second_part(
-        place, 0, far, (2, 3), far_weights, sums_0, sz3, w_down, pairs
+        place, 0, far, (2, 3), far_weights, sums_0, sz0, w_down, pairs
     )
     (first, last, sx2, sx3), parts_0 = after(((first, last, sx2, sx3), parts_0))
     far[1] = [(sx2, 0), (sx3, 0)]
@@ -432,7 +431,7 @@
     far_0 = parts_0[0], send(parts_0[1], c=1)
     near_0 = last_0[0], send(last_0[1], c=1)
     *parts_1, hidden = second_part(
-        place, 1, far, (2, 3), far_weights, sums_1, sx3, w_down, pairs
+        place, 1, far, (2, 3), far_weights, sums_1, sx0, w_down, pairs
     )
     far_0, near_0, parts_1 = after((far_0, near_0, parts_1))
     to_z = total(*[v[:, :1] for v in near_0]).astype(jnp.bfloat16)

time: 103 us -> 100 us (0.971)
  waiting for transfers between devices: 30.9 us -> 23.7 us
  starting transfers between devices: 37 us -> 40.4 us
    ppermute x49, waiting for transfers between devices: 30.9 us -> 23.7 us  [send(): return lax.ppermute(value, BOTH, pairs)]
    ppermute x49, starting transfers between devices: 37 us -> 40.4 us  [send(): return lax.ppermute(value, BOTH, pairs)]
  transfers between devices with their start and end apart: 49 -> 49, of which waited for: 12 -> 11; matrix products, arithmetic and copies ran while one was open for 3% -> 4% of each run, Pallas kernels for 30% -> 31%
where the time goes in v7:
time: 100 us; the launch traced here: 99.9 us
  starting transfers between devices  40.4 us (40%)
  Pallas kernels  30.7 us (31%)
  waiting for transfers between devices  23.7 us (24%)
  other arithmetic  4.49 us (4%)
    ppermute x49, starting transfers between devices, send(): return lax.ppermute(value, BOTH, pairs)  40.4 us
    ppermute x49, waiting for transfers between devices, send(): return lax.ppermute(value, BOTH, pairs)  23.7 us
    pallas_call x2, Pallas kernels, second_part(): pl.pallas_call(lambda *refs: second_kernel(*refs, x=x, found=found, z_pla...  13.8 us
    pallas_call x2, Pallas kernels, first_part(): pl.pallas_call(lambda *refs: first_kernel(*refs, found=found, z_places=z_...  8.7 us
    pallas_call x2, Pallas kernels, third_part(): pl.pallas_call(lambda *refs: third_kernel(*refs, pair=pair), in_specs=[SC...  4.73 us
    pallas_call x1, Pallas kernels, pair_weights(): pl.pallas_call(lambda *refs: weights_kernel(*refs, z=z), in_specs=[SCALAR...  3.41 us
  transfers between devices with their start and end apart: 49, of which 11 were waited for; matrix products, arithmetic and copies ran while one was open for 4% of the time, Pallas kernels for 31%

profile of v7, /device:TPU:0, one launch (start us, length us, event | category | flops | bytes accessed | tf_op | source)
XLA Modules:
  0.0 99.9 jit_solution(12732816997040214216)
XLA Ops:
  0.0 3.0 %collective-permute-start.1 = (bf16[1,256,384]{2,1,0:T(8,128)(2,1)}, bf16[1,256,384]{2,1,0:T(8,128)(2,1)S(1)}, u32[]{:S(2)}, u32[]{:S(2)}) collective-permute-start(bf16[1,256,384]{2,1,0:T(8,128)(2,1)} %bitcast.72), channel_id=1, source_target_pairs={{0,2},{1,3},{2,0},{3,1},{4,6},{5,7},{6,4},{7,5},{8,10},{9,11},{10,... | collective-permute-start | bytes 589832 | tf_op jit(solution)/shard_map/ppermute | solution.py:67
  5.5 1.6 %collective-permute-start.5 = (bf16[1,272,384]{2,1,0:T(8,128)(2,1)S(1)}, bf16[1,272,384]{2,1,0:T(8,128)(2,1)S(1)}, u32[]{:S(2)}, u32[]{:S(2)}) collective-permute-start(bf16[1,272,384]{2,1,0:T(8,128)(2,1)S(1)} %maximum_bitcast_fusion.refs_1_.refs_14_), channel_id=1, source_target_pairs={{0,16},{1,17},{2,18},{3,19},{4,20},{5,21},{6,22},{7,23},{8,24},{9,... | collective-permute-start | bytes 626696 | tf_op jit(solution)/shard_map/ppermute | solution.py:67
  7.0 1.5 %collective-permute-start = (bf16[1,256,384]{2,1,0:T(8,128)(2,1)}, bf16[1,256,384]{2,1,0:T(8,128)(2,1)S(1)}, u32[]{:S(2)}, u32[]{:S(2)}) collective-permute-start(bf16[1,256,384]{2,1,0:T(8,128)(2,1)} %bitcast.73), channel_id=1, source_target_pairs={{0,1},{1,0},{2,3},{3,2},{4,5},{5,4},{6,7},{7,6},{8,9},{9,8},{10,11... | collective-permute-start | bytes 589832 | tf_op jit(solution)/shard_map/ppermute | solution.py:67
  8.6 2.6 %collective-permute-start.4 = (bf16[1,256,384]{2,1,0:T(8,128)(2,1)}, bf16[1,256,384]{2,1,0:T(8,128)(2,1)S(1)}, u32[]{:S(2)}, u32[]{:S(2)}) collective-permute-start(bf16[1,256,384]{2,1,0:T(8,128)(2,1)} %bitcast.74), channel_id=1, source_target_pairs={{0,4},{1,5},{2,6},{3,7},{4,0},{5,1},{6,2},{7,3},{8,12},{9,13},{10,... | collective-permute-start | bytes 589832 | tf_op jit(solution)/shard_map/ppermute | solution.py:67
  12.3 1.8 %collective-permute-done.refs_2_ = bf16[1,256,384]{2,1,0:T(8,128)(2,1)S(1)} collective-permute-done((bf16[1,256,384]{2,1,0:T(8,128)(2,1)}, bf16[1,256,384]{2,1,0:T(8,128)(2,1)S(1)}, u32[]{:S(2)}, u32[]{:S(2)}) %collective-permute-start) | collective-permute-done | bytes 196640 | tf_op jit(solution)/shard_map/ppermute | solution.py:67
  14.7 3.4 %pair_weights.1 = (bf16[1536,1024]{1,0:T(8,128)(2,1)S(1)}, bf16[1536,1024]{1,0:T(8,128)(2,1)S(1)}) custom-call(s32[7]{0:T(128)S(1)} %stack.33.refs_0_, bf16[1,272,384]{2,1,0:T(8,128)(2,1)S(1)} %collective-permute-done.5.refs_1_.refs_14_, bf16[3072,1024]{1,0:T(8,128)(2,1)} %bitcast.66, bf16[3072,1024]{1,0:T(8,128)(2,1)} %bitcast.68), custom_call_target="tpu_custom_call" | custom-call | bytes 3145728 | tf_op jit(solution)/shard_map/pair_weights/pallas_call | solution.py:284
  18.2 1.4 %collective-permute-done.4.refs_1_ = bf16[1,256,384]{2,1,0:T(8,128)(2,1)S(1)} collective-permute-done((bf16[1,256,384]{2,1,0:T(8,128)(2,1)}, bf16[1,256,384]{2,1,0:T(8,128)(2,1)S(1)}, u32[]{:S(2)}, u32[]{:S(2)}) %collective-permute-start.4) | collective-permute-done | bytes 196640 | tf_op jit(solution)/shard_map/ppermute | solution.py:67
  21.5 1.9 %collective-permute-start.6 = (bf16[2,128,384]{2,1,0:T(8,128)(2,1)S(1)}, bf16[2,128,384]{2,1,0:T(8,128)(2,1)S(1)}, u32[]{:S(2)}, u32[]{:S(2)}) collective-permute-start(bf16[2,128,384]{2,1,0:T(8,128)(2,1)S(1)} %pad_maximum_fusion), channel_id=1, source_target_pairs={{0,16},{1,17},{2,18},{3,19},{4,20},{5,21},{6,22},{7,23},{8,24},{9,... | collective-permute-start | bytes 589832 | tf_op jit(solution)/shard_map/ppermute | solution.py:67
  24.4 2.5 %collective-permute-done.10.refs_5_ = bf16[1,256,384]{2,1,0:T(8,128)(2,1)S(1)} collective-permute-done((bf16[1,256,384]{2,1,0:T(8,128)(2,1)S(1)}, bf16[1,256,384]{2,1,0:T(8,128)(2,1)S(1)}, u32[]{:S(2)}, u32[]{:S(2)}) %collective-permute-start.10) | collective-permute-done | bytes 196640 | tf_op jit(solution)/shard_map/ppermute | solution.py:67
  26.9 4.3 %first_part.2 = (f32[2,512,512]{2,1,0:T(8,128)S(1)}, f32[2,512,512]{2,1,0:T(8,128)S(1)}, bf16[1536,1024]{1,0:T(8,128)(2,1)S(1)}) custom-call(s32[7]{0:T(128)S(1)} %stack.33.refs_0_, bf16[1,272,384]{2,1,0:T(8,128)(2,1)S(1)} %maximum_bitcast_fusion.refs_1_.refs_14_, bf16[1,256,384]{2,1,0:T(8,128)(2,1)S(1)} %collective-permute-done.refs_2_, ...), custom_call_target="tpu_custom_call" | custom-call | flops 805306368 | bytes 3014656 | tf_op jit(solution)/shard_map/first_part/pallas_call | solution.py:302
  32.4 1.3 %collective-permute-start.15 = (bf16[1,256,384]{2,1,0:T(8,128)(2,1)S(1)}, bf16[1,256,384]{2,1,0:T(8,128)(2,1)S(1)}, u32[]{:S(2)}, u32[]{:S(2)}) collective-permute-start(bf16[1,256,384]{2,1,0:T(8,128)(2,1)S(1)} %collective-permute-done.10.refs_5_), channel_id=1, source_target_pairs={{0,16},{1,17},{2,18},{3,19},{4,20},{5,21},{6,22},{7,23},{8,24},{9,... | collective-permute-start | bytes 589832 | tf_op jit(solution)/shard_map/ppermute | solution.py:67
  35.5 4.4 %first_part.3 = (f32[2,512,512]{2,1,0:T(8,128)S(1)}, f32[2,512,512]{2,1,0:T(8,128)S(1)}, bf16[1536,1024]{1,0:T(8,128)(2,1)S(1)}) custom-call(s32[7]{0:T(128)S(1)} %stack.33.refs_0_, bf16[1,272,384]{2,1,0:T(8,128)(2,1)S(1)} %collective-permute-done.5.refs_1_.refs_14_, bf16[2,128,384]{2,1,0:T(8,128)(2,1)S(1)} %collective-permute-done.6.refs_2_, ...), custom_call_target="tpu_custom_call" | custom-call | flops 805306368 | bytes 3014656 | tf_op jit(solution)/shard_map/first_part/pallas_call | solution.py:302
  40.6 1.1 %collective-permute-start.22 = (bf16[2,128,384]{2,1,0:T(8,128)(2,1)S(1)}, bf16[2,128,384]{2,1,0:T(8,128)(2,1)S(1)}, u32[]{:S(2)}, u32[]{:S(2)}) collective-permute-start(bf16[2,128,384]{2,1,0:T(8,128)(2,1)S(1)} %pad_maximum_fusion.3), channel_id=1, source_target_pairs={{0,1},{1,0},{2,3},{3,2},{4,5},{5,4},{6,7},{7,6},{8,9},{9,8},{10,11... | collective-permute-start | bytes 589832 | tf_op jit(solution)/shard_map/ppermute | solution.py:67
  42.4 6.8 %second_part.2 = (bf16[2,2,256,384]{3,2,1,0:T(8,128)(2,1)S(1)}, bf16[2,2,256,384]{3,2,1,0:T(8,128)(2,1)S(1)}, bf16[512,1024]{1,0:T(8,128)(2,1)S(1)}, bf16[1024,1536]{1,0:T(8,128)(2,1)S(1)}) custom-call(s32[7]{0:T(128)S(1)} %stack.33.refs_0_, bf16[1,256,384]{2,1,0:T(8,128)(2,1)S(1)} %collective-permute-done.4.refs_1_, ...), custom_call_target="tpu_custom_call" | custom-call | flops 1610612736 | bytes 5373952 | tf_op jit(solution)/shard_map/second_part/pallas_call | solution.py:329
  50.3 2.4 %third_part.2 = (bf16[2,2,256,384]{3,2,1,0:T(8,128)(2,1)S(1)}, bf16[2,2,256,384]{3,2,1,0:T(8,128)(2,1)S(1)}) custom-call(s32[7]{0:T(128)S(1)} %stack.33.refs_0_, bf16[512,1024]{1,0:T(8,128)(2,1)S(1)} %get-tuple-element.104.refs_1_, bf16[1024,1536]{1,0:T(8,128)(2,1)S(1)} %get-tuple-element.105.refs_2_), custom_call_target="tpu_custom_call" | custom-call | flops 402653184 | bytes 1441792 | tf_op jit(solution)/shard_map/third_part/pallas_call | solution.py:357
  52.8 7.0 %second_part.3 = (bf16[2,2,256,384]{3,2,1,0:T(8,128)(2,1)S(1)}, bf16[2,2,256,384]{3,2,1,0:T(8,128)(2,1)S(1)}, bf16[512,1024]{1,0:T(8,128)(2,1)S(1)}) custom-call(s32[7]{0:T(128)S(1)} %stack.33.refs_0_, bf16[1,256,384]{2,1,0:T(8,128)(2,1)S(1)} %collective-permute-done.8.refs_1_, bf16[2,128,384]{2,1,0:T(8,128)(2,1)S(1)} %collective-permute-done.21.refs_2_, ...), custom_call_target="tpu_custom_call" | custom-call | flops 1610612736 | bytes 5373952 | tf_op jit(solution)/shard_map/second_part/pallas_call | solution.py:329
  60.4 2.4 %third_part.3 = (bf16[2,2,256,384]{3,2,1,0:T(8,128)(2,1)S(1)}, bf16[2,2,256,384]{3,2,1,0:T(8,128)(2,1)S(1)}) custom-call(s32[7]{0:T(128)S(1)} %stack.33.refs_0_, bf16[512,1024]{1,0:T(8,128)(2,1)S(1)} %get-tuple-element.128.refs_1_, bf16[1024,1536]{1,0:T(8,128)(2,1)S(1)} %get-tuple-element.105.refs_2_), custom_call_target="tpu_custom_call" | custom-call | flops 402653184 | bytes 1441792 | tf_op jit(solution)/shard_map/third_part/pallas_call | solution.py:357
  63.0 2.0 %collective-permute-start.33 = (bf16[2,1,256,384]{3,2,1,0:T(8,128)(2,1)S(1)}, bf16[2,1,256,384]{3,2,1,0:T(8,128)(2,1)S(1)}, u32[]{:S(2)}, u32[]{:S(2)}) collective-permute-start(bf16[2,1,256,384]{3,2,1,0:T(8,128)(2,1)S(1)} %add_convert_fusion.1), channel_id=1, source_target_pairs={{0,2},{1,3},{2,0},{3,1},{4,6},{5,7},{6,4},{7,5},{8,10},{9,11},{10,... | collective-permute-start | bytes 1179656 | tf_op jit(solution)/shard_map/ppermute | solution.py:67
  65.1 1.4 %collective-permute-start.39 = (bf16[2,128,384]{2,1,0:T(8,128)(2,1)S(1)}, bf16[2,128,384]{2,1,0:T(8,128)(2,1)S(1)}, u32[]{:S(2)}, u32[]{:S(2)}) collective-permute-start(bf16[2,128,384]{2,1,0:T(8,128)(2,1)S(1)} %get-tuple-element.146), channel_id=1, source_target_pairs={{0,16},{1,17},{2,18},{3,19},{4,20},{5,21},{6,22},{7,23},{8,24},{9,... | collective-permute-start | bytes 589832 | tf_op jit(solution)/shard_map/ppermute | solution.py:67
  67.8 4.4 %collective-permute-done.39 = bf16[2,128,384]{2,1,0:T(8,128)(2,1)S(1)} collective-permute-done((bf16[2,128,384]{2,1,0:T(8,128)(2,1)S(1)}, bf16[2,128,384]{2,1,0:T(8,128)(2,1)S(1)}, u32[]{:S(2)}, u32[]{:S(2)}) %collective-permute-start.39) | collective-permute-done | bytes 196640 | tf_op jit(solution)/shard_map/ppermute | solution.py:67
  72.2 1.1 %collective-permute-done.40 = bf16[2,128,384]{2,1,0:T(8,128)(2,1)S(1)} collective-permute-done((bf16[2,128,384]{2,1,0:T(8,128)(2,1)S(1)}, bf16[2,128,384]{2,1,0:T(8,128)(2,1)S(1)}, u32[]{:S(2)}, u32[]{:S(2)}) %collective-permute-start.40) | collective-permute-done | bytes 196640 | tf_op jit(solution)/shard_map/ppermute | solution.py:67
  74.3 1.1 %collective-permute-start.42 = (bf16[1,256,384]{2,1,0:T(8,128)(2,1)S(1)}, bf16[1,256,384]{2,1,0:T(8,128)(2,1)S(1)}, u32[]{:S(2)}, u32[]{:S(2)}) collective-permute-start(bf16[1,256,384]{2,1,0:T(8,128)(2,1)S(1)} %slice.215), channel_id=1, source_target_pairs={{0,1},{1,0},{2,3},{3,2},{4,5},{5,4},{6,7},{7,6},{8,9},{9,8},{10,11... | collective-permute-start | bytes 589832 | tf_op jit(solution)/shard_map/ppermute | solution.py:67
  75.5 3.9 %collective-permute-done.41 = bf16[1,256,384]{2,1,0:T(8,128)(2,1)S(1)} collective-permute-done((bf16[1,256,384]{2,1,0:T(8,128)(2,1)S(1)}, bf16[1,256,384]{2,1,0:T(8,128)(2,1)S(1)}, u32[]{:S(2)}, u32[]{:S(2)}) %collective-permute-start.41) | collective-permute-done | bytes 196640 | tf_op jit(solution)/shard_map/ppermute | solution.py:67
  80.6 1.5 %collective-permute-start.43 = (bf16[1,256,384]{2,1,0:T(8,128)(2,1)S(1)}, bf16[1,256,384]{2,1,0:T(8,128)(2,1)S(1)}, u32[]{:S(2)}, u32[]{:S(2)}) collective-permute-start(bf16[1,256,384]{2,1,0:T(8,128)(2,1)S(1)} %slice.197), channel_id=1, source_target_pairs={{0,16},{1,17},{2,18},{3,19},{4,20},{5,21},{6,22},{7,23},{8,24},{9,... | collective-permute-start | bytes 589832 | tf_op jit(solution)/shard_map/ppermute | solution.py:67
  82.1 1.1 %collective-permute-start.44 = (bf16[1,256,384]{2,1,0:T(8,128)(2,1)S(1)}, bf16[1,256,384]{2,1,0:T(8,128)(2,1)S(1)}, u32[]{:S(2)}, u32[]{:S(2)}) collective-permute-start(bf16[1,256,384]{2,1,0:T(8,128)(2,1)S(1)} %slice.198), channel_id=1, source_target_pairs={{0,1},{1,0},{2,3},{3,2},{4,5},{5,4},{6,7},{7,6},{8,9},{9,8},{10,11... | collective-permute-start | bytes 589832 | tf_op jit(solution)/shard_map/ppermute | solution.py:67
  83.5 1.4 %collective-permute-start.37 = (bf16[1,128,384]{2,1,0:T(8,128)(2,1)S(1)}, bf16[1,128,384]{2,1,0:T(8,128)(2,1)S(1)}, u32[]{:S(2)}, u32[]{:S(2)}) collective-permute-start(bf16[1,128,384]{2,1,0:T(8,128)(2,1)S(1)} %get-tuple-element.144), channel_id=1, source_target_pairs={{0,16},{1,17},{2,18},{3,19},{4,20},{5,21},{6,22},{7,23},{8,24},{9,... | collective-permute-start | bytes 294920 | tf_op jit(solution)/shard_map/ppermute | solution.py:67
  84.9 2.0 %collective-permute-done.43 = bf16[1,256,384]{2,1,0:T(8,128)(2,1)S(1)} collective-permute-done((bf16[1,256,384]{2,1,0:T(8,128)(2,1)S(1)}, bf16[1,256,384]{2,1,0:T(8,128)(2,1)S(1)}, u32[]{:S(2)}, u32[]{:S(2)}) %collective-permute-start.43) | collective-permute-done | bytes 196640 | tf_op jit(solution)/shard_map/ppermute | solution.py:67
  86.9 1.1 %collective-permute-start.38 = (bf16[1,128,384]{2,1,0:T(8,128)(2,1)S(1)}, bf16[1,128,384]{2,1,0:T(8,128)(2,1)S(1)}, u32[]{:S(2)}, u32[]{:S(2)}) collective-permute-start(bf16[1,128,384]{2,1,0:T(8,128)(2,1)S(1)} %get-tuple-element.143), channel_id=1, source_target_pairs={{0,1},{1,0},{2,3},{3,2},{4,5},{5,4},{6,7},{7,6},{8,9},{9,8},{10,11... | collective-permute-start | bytes 294920 | tf_op jit(solution)/shard_map/ppermute | solution.py:67
  89.0 2.7 %collective-permute-start.48 = (bf16[1,256,384]{2,1,0:T(8,128)(2,1)S(1)}, bf16[1,256,384]{2,1,0:T(8,128)(2,1)S(1)}, u32[]{:S(2)}, u32[]{:S(2)}) collective-permute-start(bf16[1,256,384]{2,1,0:T(8,128)(2,1)S(1)} %fusion.8), channel_id=1, source_target_pairs={{0,4},{1,5},{2,6},{3,7},{4,0},{5,1},{6,2},{7,3},{8,12},{9,13},{10,... | collective-permute-start | bytes 589832 | tf_op jit(solution)/shard_map/ppermute | solution.py:67
  91.8 1.3 %collective-permute-start.46 = (bf16[1,256,384]{2,1,0:T(8,128)(2,1)S(1)}, bf16[1,256,384]{2,1,0:T(8,128)(2,1)S(1)}, u32[]{:S(2)}, u32[]{:S(2)}) collective-permute-start(bf16[1,256,384]{2,1,0:T(8,128)(2,1)S(1)} %fusion.10), channel_id=1, source_target_pairs={{0,16},{1,17},{2,18},{3,19},{4,20},{5,21},{6,22},{7,23},{8,24},{9,... | collective-permute-start | bytes 589832 | tf_op jit(solution)/shard_map/ppermute | solution.py:67
  93.3 1.1 %collective-permute-start.47 = (bf16[1,256,384]{2,1,0:T(8,128)(2,1)S(1)}, bf16[1,256,384]{2,1,0:T(8,128)(2,1)S(1)}, u32[]{:S(2)}, u32[]{:S(2)}) collective-permute-start(bf16[1,256,384]{2,1,0:T(8,128)(2,1)S(1)} %fusion.9), channel_id=1, source_target_pairs={{0,1},{1,0},{2,3},{3,2},{4,5},{5,4},{6,7},{7,6},{8,9},{9,8},{10,11... | collective-permute-start | bytes 589832 | tf_op jit(solution)/shard_map/ppermute | solution.py:67
  94.4 4.7 %collective-permute-done.48 = bf16[1,256,384]{2,1,0:T(8,128)(2,1)S(1)} collective-permute-done((bf16[1,256,384]{2,1,0:T(8,128)(2,1)S(1)}, bf16[1,256,384]{2,1,0:T(8,128)(2,1)S(1)}, u32[]{:S(2)}, u32[]{:S(2)}) %collective-permute-start.48) | collective-permute-done | bytes 196640 | tf_op jit(solution)/shard_map/ppermute | solution.py:67
  (108 shorter events, 19.3 us)
Async XLA Ops:
  0.0 11.2 %collective-permute-start.1 = (bf16[1,256,384]{2,1,0:T(8,128)(2,1)}, bf16[1,256,384]{2,1,0:T(8,128)(2,1)S(1)}, u32[]{:S(2)}, u32[]{:S(2)}) collective-permute-start(bf16[1,256,384]{2,1,0:T(8,128)(2,1)} %bitcast.72), channel_id=1, source_target_pairs={{0,2},{1,3},{2,0},{3,1},{4,6},{5,7},{6,4},{7,5},{8,10},{9,11},{10,... | collective-permute-start | bytes 589832 | tf_op jit(solution)/shard_map/ppermute | solution.py:67
  5.5 8.7 %collective-permute-start.5 = (bf16[1,272,384]{2,1,0:T(8,128)(2,1)S(1)}, bf16[1,272,384]{2,1,0:T(8,128)(2,1)S(1)}, u32[]{:S(2)}, u32[]{:S(2)}) collective-permute-start(bf16[1,272,384]{2,1,0:T(8,128)(2,1)S(1)} %maximum_bitcast_fusion.refs_1_.refs_14_), channel_id=1, source_target_pairs={{0,16},{1,17},{2,18},{3,19},{4,20},{5,21},{6,22},{7,23},{8,24},{9,... | collective-permute-start | bytes 626696 | tf_op jit(solution)/shard_map/ppermute | solution.py:67
  7.0 7.1 %collective-permute-start = (bf16[1,256,384]{2,1,0:T(8,128)(2,1)}, bf16[1,256,384]{2,1,0:T(8,128)(2,1)S(1)}, u32[]{:S(2)}, u32[]{:S(2)}) collective-permute-start(bf16[1,256,384]{2,1,0:T(8,128)(2,1)} %bitcast.73), channel_id=1, source_target_pairs={{0,1},{1,0},{2,3},{3,2},{4,5},{5,4},{6,7},{7,6},{8,9},{9,8},{10,11... | collective-permute-start | bytes 589832 | tf_op jit(solution)/shard_map/ppermute | solution.py:67
  8.6 11.0 %collective-permute-start.4 = (bf16[1,256,384]{2,1,0:T(8,128)(2,1)}, bf16[1,256,384]{2,1,0:T(8,128)(2,1)S(1)}, u32[]{:S(2)}, u32[]{:S(2)}) collective-permute-start(bf16[1,256,384]{2,1,0:T(8,128)(2,1)} %bitcast.74), channel_id=1, source_target_pairs={{0,4},{1,5},{2,6},{3,7},{4,0},{5,1},{6,2},{7,3},{8,12},{9,13},{10,... | collective-permute-start | bytes 589832 | tf_op jit(solution)/shard_map/ppermute | solution.py:67
  11.2 8.5 %collective-permute-start.2 = (bf16[1,256,384]{2,1,0:T(8,128)(2,1)S(1)}, bf16[1,256,384]{2,1,0:T(8,128)(2,1)S(1)}, u32[]{:S(2)}, u32[]{:S(2)}) collective-permute-start(bf16[1,256,384]{2,1,0:T(8,128)(2,1)S(1)} %collective-permute-done.1.refs_5_), channel_id=1, source_target_pairs={{0,16},{1,17},{2,18},{3,19},{4,20},{5,21},{6,22},{7,23},{8,24},{9,... | collective-permute-start | bytes 589832 | tf_op jit(solution)/shard_map/ppermute | solution.py:67
  11.7 7.9 %collective-permute-start.3 = (bf16[1,256,384]{2,1,0:T(8,128)(2,1)S(1)}, bf16[1,256,384]{2,1,0:T(8,128)(2,1)S(1)}, u32[]{:S(2)}, u32[]{:S(2)}) collective-permute-start(bf16[1,256,384]{2,1,0:T(8,128)(2,1)S(1)} %collective-permute-done.1.refs_5_), channel_id=1, source_target_pairs={{0,1},{1,0},{2,3},{3,2},{4,5},{5,4},{6,7},{7,6},{8,9},{9,8},{10,11... | collective-permute-start | bytes 589832 | tf_op jit(solution)/shard_map/ppermute | solution.py:67
  14.1 6.8 %collective-permute-start.12 = (bf16[1,256,384]{2,1,0:T(8,128)(2,1)S(1)}, bf16[1,256,384]{2,1,0:T(8,128)(2,1)S(1)}, u32[]{:S(2)}, u32[]{:S(2)}) collective-permute-start(bf16[1,256,384]{2,1,0:T(8,128)(2,1)S(1)} %collective-permute-done.refs_2_), channel_id=1, source_target_pairs={{0,8},{1,9},{2,10},{3,11},{4,12},{5,13},{6,14},{7,15},{8,0},{9,1},... | collective-permute-start | bytes 589832 | tf_op jit(solution)/shard_map/ppermute | solution.py:67
  19.6 7.3 %collective-permute-start.10 = (bf16[1,256,384]{2,1,0:T(8,128)(2,1)S(1)}, bf16[1,256,384]{2,1,0:T(8,128)(2,1)S(1)}, u32[]{:S(2)}, u32[]{:S(2)}) collective-permute-start(bf16[1,256,384]{2,1,0:T(8,128)(2,1)S(1)} %collective-permute-done.4.refs_1_), channel_id=1, source_target_pairs={{0,2},{1,3},{2,0},{3,1},{4,6},{5,7},{6,4},{7,5},{8,10},{9,11},{10,... | collective-permute-start | bytes 589832 | tf_op jit(solution)/shard_map/ppermute | solution.py:67
  20.3 11.5 %collective-permute-start.8 = (bf16[1,256,384]{2,1,0:T(8,128)(2,1)S(1)}, bf16[1,256,384]{2,1,0:T(8,128)(2,1)S(1)}, u32[]{:S(2)}, u32[]{:S(2)}) collective-permute-start(bf16[1,256,384]{2,1,0:T(8,128)(2,1)S(1)} %collective-permute-done.4.refs_1_), channel_id=1, source_target_pairs={{0,16},{1,17},{2,18},{3,19},{4,20},{5,21},{6,22},{7,23},{8,24},{9,... | collective-permute-start | bytes 589832 | tf_op jit(solution)/shard_map/ppermute | solution.py:67
  21.0 10.3 %collective-permute-start.7 = (bf16[2,128,384]{2,1,0:T(8,128)(2,1)S(1)}, bf16[2,128,384]{2,1,0:T(8,128)(2,1)S(1)}, u32[]{:S(2)}, u32[]{:S(2)}) collective-permute-start(bf16[2,128,384]{2,1,0:T(8,128)(2,1)S(1)} %pad_maximum_fusion.1), channel_id=1, source_target_pairs={{0,1},{1,0},{2,3},{3,2},{4,5},{5,4},{6,7},{7,6},{8,9},{9,8},{10,11... | collective-permute-start | bytes 589832 | tf_op jit(solution)/shard_map/ppermute | solution.py:67
  21.5 10.4 %collective-permute-start.6 = (bf16[2,128,384]{2,1,0:T(8,128)(2,1)S(1)}, bf16[2,128,384]{2,1,0:T(8,128)(2,1)S(1)}, u32[]{:S(2)}, u32[]{:S(2)}) collective-permute-start(bf16[2,128,384]{2,1,0:T(8,128)(2,1)S(1)} %pad_maximum_fusion), channel_id=1, source_target_pairs={{0,16},{1,17},{2,18},{3,19},{4,20},{5,21},{6,22},{7,23},{8,24},{9,... | collective-permute-start | bytes 589832 | tf_op jit(solution)/shard_map/ppermute | solution.py:67
  23.4 8.4 %collective-permute-start.9 = (bf16[1,256,384]{2,1,0:T(8,128)(2,1)S(1)}, bf16[1,256,384]{2,1,0:T(8,128)(2,1)S(1)}, u32[]{:S(2)}, u32[]{:S(2)}) collective-permute-start(bf16[1,256,384]{2,1,0:T(8,128)(2,1)S(1)} %collective-permute-done.4.refs_1_), channel_id=1, source_target_pairs={{0,1},{1,0},{2,3},{3,2},{4,5},{5,4},{6,7},{7,6},{8,9},{9,8},{10,11... | collective-permute-start | bytes 589832 | tf_op jit(solution)/shard_map/ppermute | solution.py:67
  26.9 6.8 %collective-permute-start.17 = (bf16[1,272,384]{2,1,0:T(8,128)(2,1)S(1)}, bf16[1,272,384]{2,1,0:T(8,128)(2,1)S(1)}, u32[]{:S(2)}, u32[]{:S(2)}) collective-permute-start(bf16[1,272,384]{2,1,0:T(8,128)(2,1)S(1)} %collective-permute-done.5.refs_1_.refs_14_), channel_id=1, source_target_pairs={{0,8},{1,9},{2,10},{3,11},{4,12},{5,13},{6,14},{7,15},{8,0},{9,1},... | collective-permute-start | bytes 626696 | tf_op jit(solution)/shard_map/ppermute | solution.py:67
  32.4 7.4 %collective-permute-start.15 = (bf16[1,256,384]{2,1,0:T(8,128)(2,1)S(1)}, bf16[1,256,384]{2,1,0:T(8,128)(2,1)S(1)}, u32[]{:S(2)}, u32[]{:S(2)}) collective-permute-start(bf16[1,256,384]{2,1,0:T(8,128)(2,1)S(1)} %collective-permute-done.10.refs_5_), channel_id=1, source_target_pairs={{0,16},{1,17},{2,18},{3,19},{4,20},{5,21},{6,22},{7,23},{8,24},{9,... | collective-permute-start | bytes 589832 | tf_op jit(solution)/shard_map/ppermute | solution.py:67
  33.7 6.6 %collective-permute-start.16 = (bf16[1,256,384]{2,1,0:T(8,128)(2,1)S(1)}, bf16[1,256,384]{2,1,0:T(8,128)(2,1)S(1)}, u32[]{:S(2)}, u32[]{:S(2)}) collective-permute-start(bf16[1,256,384]{2,1,0:T(8,128)(2,1)S(1)} %collective-permute-done.10.refs_5_), channel_id=1, source_target_pairs={{0,1},{1,0},{2,3},{3,2},{4,5},{5,4},{6,7},{7,6},{8,9},{9,8},{10,11... | collective-permute-start | bytes 589832 | tf_op jit(solution)/shard_map/ppermute | solution.py:67
  34.9 6.7 %collective-permute-start.26 = (bf16[1,256,384]{2,1,0:T(8,128)(2,1)S(1)}, bf16[1,256,384]{2,1,0:T(8,128)(2,1)S(1)}, u32[]{:S(2)}, u32[]{:S(2)}) collective-permute-start(bf16[1,256,384]{2,1,0:T(8,128)(2,1)S(1)} %collective-permute-done.9.refs_2_), channel_id=1, source_target_pairs={{0,8},{1,9},{2,10},{3,11},{4,12},{5,13},{6,14},{7,15},{8,0},{9,1},... | collective-permute-start | bytes 589832 | tf_op jit(solution)/shard_map/ppermute | solution.py:67
  35.4 7.0 %collective-permute-start.27 = (bf16[1,256,384]{2,1,0:T(8,128)(2,1)S(1)}, bf16[1,256,384]{2,1,0:T(8,128)(2,1)S(1)}, u32[]{:S(2)}, u32[]{:S(2)}) collective-permute-start(bf16[1,256,384]{2,1,0:T(8,128)(2,1)S(1)} %collective-permute-done.10.refs_5_), channel_id=1, source_target_pairs={{0,8},{1,9},{2,10},{3,11},{4,12},{5,13},{6,14},{7,15},{8,0},{9,1},... | collective-permute-start | bytes 589832 | tf_op jit(solution)/shard_map/ppermute | solution.py:67
  39.9 9.3 %collective-permute-start.23 = (bf16[1,256,384]{2,1,0:T(8,128)(2,1)S(1)}, bf16[1,256,384]{2,1,0:T(8,128)(2,1)S(1)}, u32[]{:S(2)}, u32[]{:S(2)}) collective-permute-start(bf16[1,256,384]{2,1,0:T(8,128)(2,1)S(1)} %collective-permute-done.8.refs_1_), channel_id=1, source_target_pairs={{0,8},{1,9},{2,10},{3,11},{4,12},{5,13},{6,14},{7,15},{8,0},{9,1},... | collective-permute-start | bytes 589832 | tf_op jit(solution)/shard_map/ppermute | solution.py:67
  40.6 8.6 %collective-permute-start.22 = (bf16[2,128,384]{2,1,0:T(8,128)(2,1)S(1)}, bf16[2,128,384]{2,1,0:T(8,128)(2,1)S(1)}, u32[]{:S(2)}, u32[]{:S(2)}) collective-permute-start(bf16[2,128,384]{2,1,0:T(8,128)(2,1)S(1)} %pad_maximum_fusion.3), channel_id=1, source_target_pairs={{0,1},{1,0},{2,3},{3,2},{4,5},{5,4},{6,7},{7,6},{8,9},{9,8},{10,11... | collective-permute-start | bytes 589832 | tf_op jit(solution)/shard_map/ppermute | solution.py:67
  41.6 7.6 %collective-permute-start.21 = (bf16[2,128,384]{2,1,0:T(8,128)(2,1)S(1)}, bf16[2,128,384]{2,1,0:T(8,128)(2,1)S(1)}, u32[]{:S(2)}, u32[]{:S(2)}) collective-permute-start(bf16[2,128,384]{2,1,0:T(8,128)(2,1)S(1)} %pad_maximum_fusion.2), channel_id=1, source_target_pairs={{0,16},{1,17},{2,18},{3,19},{4,20},{5,21},{6,22},{7,23},{8,24},{9,... | collective-permute-start | bytes 589832 | tf_op jit(solution)/shard_map/ppermute | solution.py:67
  42.3 6.9 %collective-permute-start.24 = (bf16[1,256,384]{2,1,0:T(8,128)(2,1)S(1)}, bf16[1,256,384]{2,1,0:T(8,128)(2,1)S(1)}, u32[]{:S(2)}, u32[]{:S(2)}) collective-permute-start(bf16[1,256,384]{2,1,0:T(8,128)(2,1)S(1)} %collective-permute-done.15.refs_7_), channel_id=1, source_target_pairs={{0,8},{1,9},{2,10},{3,11},{4,12},{5,13},{6,14},{7,15},{8,0},{9,1},... | collective-permute-start | bytes 589832 | tf_op jit(solution)/shard_map/ppermute | solution.py:67
  49.9 10.0 %collective-permute-start.29 = (bf16[2,2,256,384]{3,2,1,0:T(8,128)(2,1)S(1)}, bf16[2,2,256,384]{3,2,1,0:T(8,128)(2,1)S(1)}, u32[]{:S(2)}, u32[]{:S(2)}) collective-permute-start(bf16[2,2,256,384]{3,2,1,0:T(8,128)(2,1)S(1)} %get-tuple-element.101), channel_id=1, source_target_pairs={{0,8},{1,9},{2,10},{3,11},{4,12},{5,13},{6,14},{7,15},{8,0},{9,1},... | collective-permute-start | bytes 2359304 | tf_op jit(solution)/shard_map/ppermute | solution.py:67
  52.7 7.2 %collective-permute-start.32 = (bf16[2,2,256,384]{3,2,1,0:T(8,128)(2,1)S(1)}, bf16[2,2,256,384]{3,2,1,0:T(8,128)(2,1)S(1)}, u32[]{:S(2)}, u32[]{:S(2)}) collective-permute-start(bf16[2,2,256,384]{3,2,1,0:T(8,128)(2,1)S(1)} %get-tuple-element.109), channel_id=1, source_target_pairs={{0,8},{1,9},{2,10},{3,11},{4,12},{5,13},{6,14},{7,15},{8,0},{9,1},... | collective-permute-start | bytes 2359304 | tf_op jit(solution)/shard_map/ppermute | solution.py:67
  63.0 30.1 %collective-permute-start.33 = (bf16[2,1,256,384]{3,2,1,0:T(8,128)(2,1)S(1)}, bf16[2,1,256,384]{3,2,1,0:T(8,128)(2,1)S(1)}, u32[]{:S(2)}, u32[]{:S(2)}) collective-permute-start(bf16[2,1,256,384]{3,2,1,0:T(8,128)(2,1)S(1)} %add_convert_fusion.1), channel_id=1, source_target_pairs={{0,2},{1,3},{2,0},{3,1},{4,6},{5,7},{6,4},{7,5},{8,10},{9,11},{10,... | collective-permute-start | bytes 1179656 | tf_op jit(solution)/shard_map/ppermute | solution.py:67
  65.1 7.0 %collective-permute-start.39 = (bf16[2,128,384]{2,1,0:T(8,128)(2,1)S(1)}, bf16[2,128,384]{2,1,0:T(8,128)(2,1)S(1)}, u32[]{:S(2)}, u32[]{:S(2)}) collective-permute-start(bf16[2,128,384]{2,1,0:T(8,128)(2,1)S(1)} %get-tuple-element.146), channel_id=1, source_target_pairs={{0,16},{1,17},{2,18},{3,19},{4,20},{5,21},{6,22},{7,23},{8,24},{9,... | collective-permute-start | bytes 589832 | tf_op jit(solution)/shard_map/ppermute | solution.py:67
  66.6 6.7 %collective-permute-start.40 = (bf16[2,128,384]{2,1,0:T(8,128)(2,1)S(1)}, bf16[2,128,384]{2,1,0:T(8,128)(2,1)S(1)}, u32[]{:S(2)}, u32[]{:S(2)}) collective-permute-start(bf16[2,128,384]{2,1,0:T(8,128)(2,1)S(1)} %get-tuple-element.145), channel_id=1, source_target_pairs={{0,1},{1,0},{2,3},{3,2},{4,5},{5,4},{6,7},{7,6},{8,9},{9,8},{10,11... | collective-permute-start | bytes 589832 | tf_op jit(solution)/shard_map/ppermute | solution.py:67
  67.7 15.7 %collective-permute-start.36 = (bf16[2,1,256,384]{3,2,1,0:T(8,128)(2,1)S(1)}, bf16[2,1,256,384]{3,2,1,0:T(8,128)(2,1)S(1)}, u32[]{:S(2)}, u32[]{:S(2)}) collective-permute-start(bf16[2,1,256,384]{3,2,1,0:T(8,128)(2,1)S(1)} %add_convert_fusion), channel_id=1, source_target_pairs={{0,2},{1,3},{2,0},{3,1},{4,6},{5,7},{6,4},{7,5},{8,10},{9,11},{10,... | collective-permute-start | bytes 1179656 | tf_op jit(solution)/shard_map/ppermute | solution.py:67
  80.1 8.8 %collective-permute-start.45 = (bf16[1,256,384]{2,1,0:T(8,128)(2,1)S(1)}, bf16[1,256,384]{2,1,0:T(8,128)(2,1)S(1)}, u32[]{:S(2)}, u32[]{:S(2)}) collective-permute-start(bf16[1,256,384]{2,1,0:T(8,128)(2,1)S(1)} %fusion.4), channel_id=1, source_target_pairs={{0,2},{1,3},{2,0},{3,1},{4,6},{5,7},{6,4},{7,5},{8,10},{9,11},{10,... | collective-permute-start | bytes 589832 | tf_op jit(solution)/shard_map/ppermute | solution.py:67
  82.1 6.7 %collective-permute-start.44 = (bf16[1,256,384]{2,1,0:T(8,128)(2,1)S(1)}, bf16[1,256,384]{2,1,0:T(8,128)(2,1)S(1)}, u32[]{:S(2)}, u32[]{:S(2)}) collective-permute-start(bf16[1,256,384]{2,1,0:T(8,128)(2,1)S(1)} %slice.198), channel_id=1, source_target_pairs={{0,1},{1,0},{2,3},{3,2},{4,5},{5,4},{6,7},{7,6},{8,9},{9,8},{10,11... | collective-permute-start | bytes 589832 | tf_op jit(solution)/shard_map/ppermute | solution.py:67
  83.5 8.2 %collective-permute-start.37 = (bf16[1,128,384]{2,1,0:T(8,128)(2,1)S(1)}, bf16[1,128,384]{2,1,0:T(8,128)(2,1)S(1)}, u32[]{:S(2)}, u32[]{:S(2)}) collective-permute-start(bf16[1,128,384]{2,1,0:T(8,128)(2,1)S(1)} %get-tuple-element.144), channel_id=1, source_target_pairs={{0,16},{1,17},{2,18},{3,19},{4,20},{5,21},{6,22},{7,23},{8,24},{9,... | collective-permute-start | bytes 294920 | tf_op jit(solution)/shard_map/ppermute | solution.py:67
  89.0 10.1 %collective-permute-start.48 = (bf16[1,256,384]{2,1,0:T(8,128)(2,1)S(1)}, bf16[1,256,384]{2,1,0:T(8,128)(2,1)S(1)}, u32[]{:S(2)}, u32[]{:S(2)}) collective-permute-start(bf16[1,256,384]{2,1,0:T(8,128)(2,1)S(1)} %fusion.8), channel_id=1, source_target_pairs={{0,4},{1,5},{2,6},{3,7},{4,0},{5,1},{6,2},{7,3},{8,12},{9,13},{10,... | collective-permute-start | bytes 589832 | tf_op jit(solution)/shard_map/ppermute | solution.py:67
  91.8 7.3 %collective-permute-start.46 = (bf16[1,256,384]{2,1,0:T(8,128)(2,1)S(1)}, bf16[1,256,384]{2,1,0:T(8,128)(2,1)S(1)}, u32[]{:S(2)}, u32[]{:S(2)}) collective-permute-start(bf16[1,256,384]{2,1,0:T(8,128)(2,1)S(1)} %fusion.10), channel_id=1, source_target_pairs={{0,16},{1,17},{2,18},{3,19},{4,20},{5,21},{6,22},{7,23},{8,24},{9,... | collective-permute-start | bytes 589832 | tf_op jit(solution)/shard_map/ppermute | solution.py:67
  (17 other events, 72.1 us)

commit v8 on v7

--- a/solution.py
+++ b/solution.py
@@ -6,7 +6,7 @@
 from jax.sharding import PartitionSpec as P
 
 BOTH = ("expert", "split")
-HIDDEN_TILE = 512
+HIDDEN_TILE = 1024
 SCALE = 4
 
 

time: 100 us -> 99.6 us (level)
  transfers between devices with their start and end apart: 49 -> 49, of which waited for: 11 -> 11; matrix products, arithmetic and copies ran while one was open for 4% -> 4% of each run, Pallas kernels for 31% -> 30%
where the time goes in v8:
time: 99.6 us; the launch traced here: 99.4 us
  starting transfers between devices  40.5 us (41%)
  Pallas kernels  30.2 us (30%)
  waiting for transfers between devices  23.6 us (24%)
  other arithmetic  4.49 us (5%)
    ppermute x49, starting transfers between devices, send(): return lax.ppermute(value, BOTH, pairs)  40.5 us
    ppermute x49, waiting for transfers between devices, send(): return lax.ppermute(value, BOTH, pairs)  23.6 us
    pallas_call x2, Pallas kernels, second_part(): pl.pallas_call(lambda *refs: second_kernel(*refs, x=x, found=found, z_pla...  13.3 us
    pallas_call x2, Pallas kernels, first_part(): pl.pallas_call(lambda *refs: first_kernel(*refs, found=found, z_places=z_...  8.73 us
    pallas_call x2, Pallas kernels, third_part(): pl.pallas_call(lambda *refs: third_kernel(*refs, pair=pair), in_specs=[SC...  4.73 us
    pallas_call x1, Pallas kernels, pair_weights(): pl.pallas_call(lambda *refs: weights_kernel(*refs, z=z), in_specs=[SCALAR...  3.41 us
  transfers between devices with their start and end apart: 49, of which 11 were waited for; matrix products, arithmetic and copies ran while one was open for 4% of the time, Pallas kernels for 30%

profile of v8, /device:TPU:0, one launch (start us, length us, event | category | flops | bytes accessed | tf_op | source)
XLA Modules:
  0.0 99.4 jit_solution(9596815507861165927)
XLA Ops:
  0.0 3.0 %collective-permute-start.1 = (bf16[1,256,384]{2,1,0:T(8,128)(2,1)}, bf16[1,256,384]{2,1,0:T(8,128)(2,1)S(1)}, u32[]{:S(2)}, u32[]{:S(2)}) collective-permute-start(bf16[1,256,384]{2,1,0:T(8,128)(2,1)} %bitcast.72), channel_id=1, source_target_pairs={{0,2},{1,3},{2,0},{3,1},{4,6},{5,7},{6,4},{7,5},{8,10},{9,11},{10,... | collective-permute-start | bytes 589832 | tf_op jit(solution)/shard_map/ppermute | solution.py:67
  5.5 1.6 %collective-permute-start.5 = (bf16[1,272,384]{2,1,0:T(8,128)(2,1)S(1)}, bf16[1,272,384]{2,1,0:T(8,128)(2,1)S(1)}, u32[]{:S(2)}, u32[]{:S(2)}) collective-permute-start(bf16[1,272,384]{2,1,0:T(8,128)(2,1)S(1)} %maximum_bitcast_fusion.refs_1_.refs_14_), channel_id=1, source_target_pairs={{0,16},{1,17},{2,18},{3,19},{4,20},{5,21},{6,22},{7,23},{8,24},{9,... | collective-permute-start | bytes 626696 | tf_op jit(solution)/shard_map/ppermute | solution.py:67
  7.0 1.5 %collective-permute-start = (bf16[1,256,384]{2,1,0:T(8,128)(2,1)}, bf16[1,256,384]{2,1,0:T(8,128)(2,1)S(1)}, u32[]{:S(2)}, u32[]{:S(2)}) collective-permute-start(bf16[1,256,384]{2,1,0:T(8,128)(2,1)} %bitcast.73), channel_id=1, source_target_pairs={{0,1},{1,0},{2,3},{3,2},{4,5},{5,4},{6,7},{7,6},{8,9},{9,8},{10,11... | collective-permute-start | bytes 589832 | tf_op jit(solution)/shard_map/ppermute | solution.py:67
  8.6 2.6 %collective-permute-start.4 = (bf16[1,256,384]{2,1,0:T(8,128)(2,1)}, bf16[1,256,384]{2,1,0:T(8,128)(2,1)S(1)}, u32[]{:S(2)}, u32[]{:S(2)}) collective-permute-start(bf16[1,256,384]{2,1,0:T(8,128)(2,1)} %bitcast.74), channel_id=1, source_target_pairs={{0,4},{1,5},{2,6},{3,7},{4,0},{5,1},{6,2},{7,3},{8,12},{9,13},{10,... | collective-permute-start | bytes 589832 | tf_op jit(solution)/shard_map/ppermute | solution.py:67
  12.3 1.8 %collective-permute-done.refs_2_ = bf16[1,256,384]{2,1,0:T(8,128)(2,1)S(1)} collective-permute-done((bf16[1,256,384]{2,1,0:T(8,128)(2,1)}, bf16[1,256,384]{2,1,0:T(8,128)(2,1)S(1)}, u32[]{:S(2)}, u32[]{:S(2)}) %collective-permute-start) | collective-permute-done | bytes 196640 | tf_op jit(solution)/shard_map/ppermute | solution.py:67
  14.7 3.4 %pair_weights.1 = (bf16[1536,1024]{1,0:T(8,128)(2,1)S(1)}, bf16[1536,1024]{1,0:T(8,128)(2,1)S(1)}) custom-call(s32[7]{0:T(128)S(1)} %stack.33.refs_0_, bf16[1,272,384]{2,1,0:T(8,128)(2,1)S(1)} %collective-permute-done.5.refs_1_.refs_14_, bf16[3072,1024]{1,0:T(8,128)(2,1)} %bitcast.66, bf16[3072,1024]{1,0:T(8,128)(2,1)} %bitcast.68), custom_call_target="tpu_custom_call" | custom-call | bytes 3145728 | tf_op jit(solution)/shard_map/pair_weights/pallas_call | solution.py:284
  18.2 1.4 %collective-permute-done.4.refs_1_ = bf16[1,256,384]{2,1,0:T(8,128)(2,1)S(1)} collective-permute-done((bf16[1,256,384]{2,1,0:T(8,128)(2,1)}, bf16[1,256,384]{2,1,0:T(8,128)(2,1)S(1)}, u32[]{:S(2)}, u32[]{:S(2)}) %collective-permute-start.4) | collective-permute-done | bytes 196640 | tf_op jit(solution)/shard_map/ppermute | solution.py:67
  21.5 1.9 %collective-permute-start.6 = (bf16[2,128,384]{2,1,0:T(8,128)(2,1)S(1)}, bf16[2,128,384]{2,1,0:T(8,128)(2,1)S(1)}, u32[]{:S(2)}, u32[]{:S(2)}) collective-permute-start(bf16[2,128,384]{2,1,0:T(8,128)(2,1)S(1)} %pad_maximum_fusion), channel_id=1, source_target_pairs={{0,16},{1,17},{2,18},{3,19},{4,20},{5,21},{6,22},{7,23},{8,24},{9,... | collective-permute-start | bytes 589832 | tf_op jit(solution)/shard_map/ppermute | solution.py:67
  24.4 2.5 %collective-permute-done.10.refs_5_ = bf16[1,256,384]{2,1,0:T(8,128)(2,1)S(1)} collective-permute-done((bf16[1,256,384]{2,1,0:T(8,128)(2,1)S(1)}, bf16[1,256,384]{2,1,0:T(8,128)(2,1)S(1)}, u32[]{:S(2)}, u32[]{:S(2)}) %collective-permute-start.10) | collective-permute-done | bytes 196640 | tf_op jit(solution)/shard_map/ppermute | solution.py:67
  26.9 4.3 %first_part.2 = (f32[1,512,1024]{2,1,0:T(8,128)S(1)}, f32[1,512,1024]{2,1,0:T(8,128)S(1)}, bf16[1536,1024]{1,0:T(8,128)(2,1)S(1)}) custom-call(s32[7]{0:T(128)S(1)} %stack.33.refs_0_, bf16[1,272,384]{2,1,0:T(8,128)(2,1)S(1)} %maximum_bitcast_fusion.refs_1_.refs_14_, bf16[1,256,384]{2,1,0:T(8,128)(2,1)S(1)} %collective-permute-done.refs_2_, ...), custom_call_target="tpu_custom_call" | custom-call | flops 805306368 | bytes 3014656 | tf_op jit(solution)/shard_map/first_part/pallas_call | solution.py:302
  32.4 1.3 %collective-permute-start.15 = (bf16[1,256,384]{2,1,0:T(8,128)(2,1)S(1)}, bf16[1,256,384]{2,1,0:T(8,128)(2,1)S(1)}, u32[]{:S(2)}, u32[]{:S(2)}) collective-permute-start(bf16[1,256,384]{2,1,0:T(8,128)(2,1)S(1)} %collective-permute-done.10.refs_5_), channel_id=1, source_target_pairs={{0,16},{1,17},{2,18},{3,19},{4,20},{5,21},{6,22},{7,23},{8,24},{9,... | collective-permute-start | bytes 589832 | tf_op jit(solution)/shard_map/ppermute | solution.py:67
  35.5 4.4 %first_part.3 = (f32[1,512,1024]{2,1,0:T(8,128)S(1)}, f32[1,512,1024]{2,1,0:T(8,128)S(1)}, bf16[1536,1024]{1,0:T(8,128)(2,1)S(1)}) custom-call(s32[7]{0:T(128)S(1)} %stack.33.refs_0_, bf16[1,272,384]{2,1,0:T(8,128)(2,1)S(1)} %collective-permute-done.5.refs_1_.refs_14_, bf16[2,128,384]{2,1,0:T(8,128)(2,1)S(1)} %collective-permute-done.6.refs_2_, ...), custom_call_target="tpu_custom_call" | custom-call | flops 805306368 | bytes 3014656 | tf_op jit(solution)/shard_map/first_part/pallas_call | solution.py:302
  40.6 1.1 %collective-permute-start.22 = (bf16[2,128,384]{2,1,0:T(8,128)(2,1)S(1)}, bf16[2,128,384]{2,1,0:T(8,128)(2,1)S(1)}, u32[]{:S(2)}, u32[]{:S(2)}) collective-permute-start(bf16[2,128,384]{2,1,0:T(8,128)(2,1)S(1)} %pad_maximum_fusion.3), channel_id=1, source_target_pairs={{0,1},{1,0},{2,3},{3,2},{4,5},{5,4},{6,7},{7,6},{8,9},{9,8},{10,11... | collective-permute-start | bytes 589832 | tf_op jit(solution)/shard_map/ppermute | solution.py:67
  42.4 6.5 %second_part.2 = (bf16[2,2,256,384]{3,2,1,0:T(8,128)(2,1)S(1)}, bf16[2,2,256,384]{3,2,1,0:T(8,128)(2,1)S(1)}, bf16[512,1024]{1,0:T(8,128)(2,1)S(1)}, bf16[1024,1536]{1,0:T(8,128)(2,1)S(1)}) custom-call(s32[7]{0:T(128)S(1)} %stack.33.refs_0_, bf16[1,256,384]{2,1,0:T(8,128)(2,1)S(1)} %collective-permute-done.4.refs_1_, ...), custom_call_target="tpu_custom_call" | custom-call | flops 1610612736 | bytes 5373952 | tf_op jit(solution)/shard_map/second_part/pallas_call | solution.py:329
  50.0 2.4 %third_part.2 = (bf16[2,2,256,384]{3,2,1,0:T(8,128)(2,1)S(1)}, bf16[2,2,256,384]{3,2,1,0:T(8,128)(2,1)S(1)}) custom-call(s32[7]{0:T(128)S(1)} %stack.33.refs_0_, bf16[512,1024]{1,0:T(8,128)(2,1)S(1)} %get-tuple-element.104.refs_1_, bf16[1024,1536]{1,0:T(8,128)(2,1)S(1)} %get-tuple-element.105.refs_2_), custom_call_target="tpu_custom_call" | custom-call | flops 402653184 | bytes 1441792 | tf_op jit(solution)/shard_map/third_part/pallas_call | solution.py:357
  52.6 6.8 %second_part.3 = (bf16[2,2,256,384]{3,2,1,0:T(8,128)(2,1)S(1)}, bf16[2,2,256,384]{3,2,1,0:T(8,128)(2,1)S(1)}, bf16[512,1024]{1,0:T(8,128)(2,1)S(1)}) custom-call(s32[7]{0:T(128)S(1)} %stack.33.refs_0_, bf16[1,256,384]{2,1,0:T(8,128)(2,1)S(1)} %collective-permute-done.8.refs_1_, bf16[2,128,384]{2,1,0:T(8,128)(2,1)S(1)} %collective-permute-done.21.refs_2_, ...), custom_call_target="tpu_custom_call" | custom-call | flops 1610612736 | bytes 5373952 | tf_op jit(solution)/shard_map/second_part/pallas_call | solution.py:329
  59.9 2.4 %third_part.3 = (bf16[2,2,256,384]{3,2,1,0:T(8,128)(2,1)S(1)}, bf16[2,2,256,384]{3,2,1,0:T(8,128)(2,1)S(1)}) custom-call(s32[7]{0:T(128)S(1)} %stack.33.refs_0_, bf16[512,1024]{1,0:T(8,128)(2,1)S(1)} %get-tuple-element.128.refs_1_, bf16[1024,1536]{1,0:T(8,128)(2,1)S(1)} %get-tuple-element.105.refs_2_), custom_call_target="tpu_custom_call" | custom-call | flops 402653184 | bytes 1441792 | tf_op jit(solution)/shard_map/third_part/pallas_call | solution.py:357
  62.5 2.0 %collective-permute-start.33 = (bf16[2,1,256,384]{3,2,1,0:T(8,128)(2,1)S(1)}, bf16[2,1,256,384]{3,2,1,0:T(8,128)(2,1)S(1)}, u32[]{:S(2)}, u32[]{:S(2)}) collective-permute-start(bf16[2,1,256,384]{3,2,1,0:T(8,128)(2,1)S(1)} %add_convert_fusion.1), channel_id=1, source_target_pairs={{0,2},{1,3},{2,0},{3,1},{4,6},{5,7},{6,4},{7,5},{8,10},{9,11},{10,... | collective-permute-start | bytes 1179656 | tf_op jit(solution)/shard_map/ppermute | solution.py:67
  64.6 1.5 %collective-permute-start.39 = (bf16[2,128,384]{2,1,0:T(8,128)(2,1)S(1)}, bf16[2,128,384]{2,1,0:T(8,128)(2,1)S(1)}, u32[]{:S(2)}, u32[]{:S(2)}) collective-permute-start(bf16[2,128,384]{2,1,0:T(8,128)(2,1)S(1)} %get-tuple-element.146), channel_id=1, source_target_pairs={{0,16},{1,17},{2,18},{3,19},{4,20},{5,21},{6,22},{7,23},{8,24},{9,... | collective-permute-start | bytes 589832 | tf_op jit(solution)/shard_map/ppermute | solution.py:67
  67.2 4.3 %collective-permute-done.39 = bf16[2,128,384]{2,1,0:T(8,128)(2,1)S(1)} collective-permute-done((bf16[2,128,384]{2,1,0:T(8,128)(2,1)S(1)}, bf16[2,128,384]{2,1,0:T(8,128)(2,1)S(1)}, u32[]{:S(2)}, u32[]{:S(2)}) %collective-permute-start.39) | collective-permute-done | bytes 196640 | tf_op jit(solution)/shard_map/ppermute | solution.py:67
  71.6 1.1 %collective-permute-done.40 = bf16[2,128,384]{2,1,0:T(8,128)(2,1)S(1)} collective-permute-done((bf16[2,128,384]{2,1,0:T(8,128)(2,1)S(1)}, bf16[2,128,384]{2,1,0:T(8,128)(2,1)S(1)}, u32[]{:S(2)}, u32[]{:S(2)}) %collective-permute-start.40) | collective-permute-done | bytes 196640 | tf_op jit(solution)/shard_map/ppermute | solution.py:67
  73.7 1.1 %collective-permute-start.42 = (bf16[1,256,384]{2,1,0:T(8,128)(2,1)S(1)}, bf16[1,256,384]{2,1,0:T(8,128)(2,1)S(1)}, u32[]{:S(2)}, u32[]{:S(2)}) collective-permute-start(bf16[1,256,384]{2,1,0:T(8,128)(2,1)S(1)} %slice.215), channel_id=1, source_target_pairs={{0,1},{1,0},{2,3},{3,2},{4,5},{5,4},{6,7},{7,6},{8,9},{9,8},{10,11... | collective-permute-start | bytes 589832 | tf_op jit(solution)/shard_map/ppermute | solution.py:67
  74.9 3.8 %collective-permute-done.41 = bf16[1,256,384]{2,1,0:T(8,128)(2,1)S(1)} collective-permute-done((bf16[1,256,384]{2,1,0:T(8,128)(2,1)S(1)}, bf16[1,256,384]{2,1,0:T(8,128)(2,1)S(1)}, u32[]{:S(2)}, u32[]{:S(2)}) %collective-permute-start.41) | collective-permute-done | bytes 196640 | tf_op jit(solution)/shard_map/ppermute | solution.py:67
  80.1 1.5 %collective-permute-start.43 = (bf16[1,256,384]{2,1,0:T(8,128)(2,1)S(1)}, bf16[1,256,384]{2,1,0:T(8,128)(2,1)S(1)}, u32[]{:S(2)}, u32[]{:S(2)}) collective-permute-start(bf16[1,256,384]{2,1,0:T(8,128)(2,1)S(1)} %slice.197), channel_id=1, source_target_pairs={{0,16},{1,17},{2,18},{3,19},{4,20},{5,21},{6,22},{7,23},{8,24},{9,... | collective-permute-start | bytes 589832 | tf_op jit(solution)/shard_map/ppermute | solution.py:67
  81.6 1.1 %collective-permute-start.44 = (bf16[1,256,384]{2,1,0:T(8,128)(2,1)S(1)}, bf16[1,256,384]{2,1,0:T(8,128)(2,1)S(1)}, u32[]{:S(2)}, u32[]{:S(2)}) collective-permute-start(bf16[1,256,384]{2,1,0:T(8,128)(2,1)S(1)} %slice.198), channel_id=1, source_target_pairs={{0,1},{1,0},{2,3},{3,2},{4,5},{5,4},{6,7},{7,6},{8,9},{9,8},{10,11... | collective-permute-start | bytes 589832 | tf_op jit(solution)/shard_map/ppermute | solution.py:67
  83.0 1.4 %collective-permute-start.37 = (bf16[1,128,384]{2,1,0:T(8,128)(2,1)S(1)}, bf16[1,128,384]{2,1,0:T(8,128)(2,1)S(1)}, u32[]{:S(2)}, u32[]{:S(2)}) collective-permute-start(bf16[1,128,384]{2,1,0:T(8,128)(2,1)S(1)} %get-tuple-element.144), channel_id=1, source_target_pairs={{0,16},{1,17},{2,18},{3,19},{4,20},{5,21},{6,22},{7,23},{8,24},{9,... | collective-permute-start | bytes 294920 | tf_op jit(solution)/shard_map/ppermute | solution.py:67
  84.4 2.1 %collective-permute-done.43 = bf16[1,256,384]{2,1,0:T(8,128)(2,1)S(1)} collective-permute-done((bf16[1,256,384]{2,1,0:T(8,128)(2,1)S(1)}, bf16[1,256,384]{2,1,0:T(8,128)(2,1)S(1)}, u32[]{:S(2)}, u32[]{:S(2)}) %collective-permute-start.43) | collective-permute-done | bytes 196640 | tf_op jit(solution)/shard_map/ppermute | solution.py:67
  86.5 1.1 %collective-permute-start.38 = (bf16[1,128,384]{2,1,0:T(8,128)(2,1)S(1)}, bf16[1,128,384]{2,1,0:T(8,128)(2,1)S(1)}, u32[]{:S(2)}, u32[]{:S(2)}) collective-permute-start(bf16[1,128,384]{2,1,0:T(8,128)(2,1)S(1)} %get-tuple-element.143), channel_id=1, source_target_pairs={{0,1},{1,0},{2,3},{3,2},{4,5},{5,4},{6,7},{7,6},{8,9},{9,8},{10,11... | collective-permute-start | bytes 294920 | tf_op jit(solution)/shard_map/ppermute | solution.py:67
  88.5 2.7 %collective-permute-start.48 = (bf16[1,256,384]{2,1,0:T(8,128)(2,1)S(1)}, bf16[1,256,384]{2,1,0:T(8,128)(2,1)S(1)}, u32[]{:S(2)}, u32[]{:S(2)}) collective-permute-start(bf16[1,256,384]{2,1,0:T(8,128)(2,1)S(1)} %fusion.8), channel_id=1, source_target_pairs={{0,4},{1,5},{2,6},{3,7},{4,0},{5,1},{6,2},{7,3},{8,12},{9,13},{10,... | collective-permute-start | bytes 589832 | tf_op jit(solution)/shard_map/ppermute | solution.py:67
  91.3 1.4 %collective-permute-start.46 = (bf16[1,256,384]{2,1,0:T(8,128)(2,1)S(1)}, bf16[1,256,384]{2,1,0:T(8,128)(2,1)S(1)}, u32[]{:S(2)}, u32[]{:S(2)}) collective-permute-start(bf16[1,256,384]{2,1,0:T(8,128)(2,1)S(1)} %fusion.10), channel_id=1, source_target_pairs={{0,16},{1,17},{2,18},{3,19},{4,20},{5,21},{6,22},{7,23},{8,24},{9,... | collective-permute-start | bytes 589832 | tf_op jit(solution)/shard_map/ppermute | solution.py:67
  92.7 1.1 %collective-permute-start.47 = (bf16[1,256,384]{2,1,0:T(8,128)(2,1)S(1)}, bf16[1,256,384]{2,1,0:T(8,128)(2,1)S(1)}, u32[]{:S(2)}, u32[]{:S(2)}) collective-permute-start(bf16[1,256,384]{2,1,0:T(8,128)(2,1)S(1)} %fusion.9), channel_id=1, source_target_pairs={{0,1},{1,0},{2,3},{3,2},{4,5},{5,4},{6,7},{7,6},{8,9},{9,8},{10,11... | collective-permute-start | bytes 589832 | tf_op jit(solution)/shard_map/ppermute | solution.py:67
  93.9 4.7 %collective-permute-done.48 = bf16[1,256,384]{2,1,0:T(8,128)(2,1)S(1)} collective-permute-done((bf16[1,256,384]{2,1,0:T(8,128)(2,1)S(1)}, bf16[1,256,384]{2,1,0:T(8,128)(2,1)S(1)}, u32[]{:S(2)}, u32[]{:S(2)}) %collective-permute-start.48) | collective-permute-done | bytes 196640 | tf_op jit(solution)/shard_map/ppermute | solution.py:67
  (108 shorter events, 19.3 us)
Async XLA Ops:
  0.0 11.2 %collective-permute-start.1 = (bf16[1,256,384]{2,1,0:T(8,128)(2,1)}, bf16[1,256,384]{2,1,0:T(8,128)(2,1)S(1)}, u32[]{:S(2)}, u32[]{:S(2)}) collective-permute-start(bf16[1,256,384]{2,1,0:T(8,128)(2,1)} %bitcast.72), channel_id=1, source_target_pairs={{0,2},{1,3},{2,0},{3,1},{4,6},{5,7},{6,4},{7,5},{8,10},{9,11},{10,... | collective-permute-start | bytes 589832 | tf_op jit(solution)/shard_map/ppermute | solution.py:67
  5.5 8.7 %collective-permute-start.5 = (bf16[1,272,384]{2,1,0:T(8,128)(2,1)S(1)}, bf16[1,272,384]{2,1,0:T(8,128)(2,1)S(1)}, u32[]{:S(2)}, u32[]{:S(2)}) collective-permute-start(bf16[1,272,384]{2,1,0:T(8,128)(2,1)S(1)} %maximum_bitcast_fusion.refs_1_.refs_14_), channel_id=1, source_target_pairs={{0,16},{1,17},{2,18},{3,19},{4,20},{5,21},{6,22},{7,23},{8,24},{9,... | collective-permute-start | bytes 626696 | tf_op jit(solution)/shard_map/ppermute | solution.py:67
  7.0 7.1 %collective-permute-start = (bf16[1,256,384]{2,1,0:T(8,128)(2,1)}, bf16[1,256,384]{2,1,0:T(8,128)(2,1)S(1)}, u32[]{:S(2)}, u32[]{:S(2)}) collective-permute-start(bf16[1,256,384]{2,1,0:T(8,128)(2,1)} %bitcast.73), channel_id=1, source_target_pairs={{0,1},{1,0},{2,3},{3,2},{4,5},{5,4},{6,7},{7,6},{8,9},{9,8},{10,11... | collective-permute-start | bytes 589832 | tf_op jit(solution)/shard_map/ppermute | solution.py:67
  8.6 11.0 %collective-permute-start.4 = (bf16[1,256,384]{2,1,0:T(8,128)(2,1)}, bf16[1,256,384]{2,1,0:T(8,128)(2,1)S(1)}, u32[]{:S(2)}, u32[]{:S(2)}) collective-permute-start(bf16[1,256,384]{2,1,0:T(8,128)(2,1)} %bitcast.74), channel_id=1, source_target_pairs={{0,4},{1,5},{2,6},{3,7},{4,0},{5,1},{6,2},{7,3},{8,12},{9,13},{10,... | collective-permute-start | bytes 589832 | tf_op jit(solution)/shard_map/ppermute | solution.py:67
  11.2 8.5 %collective-permute-start.2 = (bf16[1,256,384]{2,1,0:T(8,128)(2,1)S(1)}, bf16[1,256,384]{2,1,0:T(8,128)(2,1)S(1)}, u32[]{:S(2)}, u32[]{:S(2)}) collective-permute-start(bf16[1,256,384]{2,1,0:T(8,128)(2,1)S(1)} %collective-permute-done.1.refs_5_), channel_id=1, source_target_pairs={{0,16},{1,17},{2,18},{3,19},{4,20},{5,21},{6,22},{7,23},{8,24},{9,... | collective-permute-start | bytes 589832 | tf_op jit(solution)/shard_map/ppermute | solution.py:67
  11.7 7.9 %collective-permute-start.3 = (bf16[1,256,384]{2,1,0:T(8,128)(2,1)S(1)}, bf16[1,256,384]{2,1,0:T(8,128)(2,1)S(1)}, u32[]{:S(2)}, u32[]{:S(2)}) collective-permute-start(bf16[1,256,384]{2,1,0:T(8,128)(2,1)S(1)} %collective-permute-done.1.refs_5_), channel_id=1, source_target_pairs={{0,1},{1,0},{2,3},{3,2},{4,5},{5,4},{6,7},{7,6},{8,9},{9,8},{10,11... | collective-permute-start | bytes 589832 | tf_op jit(solution)/shard_map/ppermute | solution.py:67
  14.1 6.8 %collective-permute-start.12 = (bf16[1,256,384]{2,1,0:T(8,128)(2,1)S(1)}, bf16[1,256,384]{2,1,0:T(8,128)(2,1)S(1)}, u32[]{:S(2)}, u32[]{:S(2)}) collective-permute-start(bf16[1,256,384]{2,1,0:T(8,128)(2,1)S(1)} %collective-permute-done.refs_2_), channel_id=1, source_target_pairs={{0,8},{1,9},{2,10},{3,11},{4,12},{5,13},{6,14},{7,15},{8,0},{9,1},... | collective-permute-start | bytes 589832 | tf_op jit(solution)/shard_map/ppermute | solution.py:67
  19.6 7.3 %collective-permute-start.10 = (bf16[1,256,384]{2,1,0:T(8,128)(2,1)S(1)}, bf16[1,256,384]{2,1,0:T(8,128)(2,1)S(1)}, u32[]{:S(2)}, u32[]{:S(2)}) collective-permute-start(bf16[1,256,384]{2,1,0:T(8,128)(2,1)S(1)} %collective-permute-done.4.refs_1_), channel_id=1, source_target_pairs={{0,2},{1,3},{2,0},{3,1},{4,6},{5,7},{6,4},{7,5},{8,10},{9,11},{10,... | collective-permute-start | bytes 589832 | tf_op jit(solution)/shard_map/ppermute | solution.py:67
  20.3 11.6 %collective-permute-start.8 = (bf16[1,256,384]{2,1,0:T(8,128)(2,1)S(1)}, bf16[1,256,384]{2,1,0:T(8,128)(2,1)S(1)}, u32[]{:S(2)}, u32[]{:S(2)}) collective-permute-start(bf16[1,256,384]{2,1,0:T(8,128)(2,1)S(1)} %collective-permute-done.4.refs_1_), channel_id=1, source_target_pairs={{0,16},{1,17},{2,18},{3,19},{4,20},{5,21},{6,22},{7,23},{8,24},{9,... | collective-permute-start | bytes 589832 | tf_op jit(solution)/shard_map/ppermute | solution.py:67
  21.0 10.3 %collective-permute-start.7 = (bf16[2,128,384]{2,1,0:T(8,128)(2,1)S(1)}, bf16[2,128,384]{2,1,0:T(8,128)(2,1)S(1)}, u32[]{:S(2)}, u32[]{:S(2)}) collective-permute-start(bf16[2,128,384]{2,1,0:T(8,128)(2,1)S(1)} %pad_maximum_fusion.1), channel_id=1, source_target_pairs={{0,1},{1,0},{2,3},{3,2},{4,5},{5,4},{6,7},{7,6},{8,9},{9,8},{10,11... | collective-permute-start | bytes 589832 | tf_op jit(solution)/shard_map/ppermute | solution.py:67
  21.5 10.4 %collective-permute-start.6 = (bf16[2,128,384]{2,1,0:T(8,128)(2,1)S(1)}, bf16[2,128,384]{2,1,0:T(8,128)(2,1)S(1)}, u32[]{:S(2)}, u32[]{:S(2)}) collective-permute-start(bf16[2,128,384]{2,1,0:T(8,128)(2,1)S(1)} %pad_maximum_fusion), channel_id=1, source_target_pairs={{0,16},{1,17},{2,18},{3,19},{4,20},{5,21},{6,22},{7,23},{8,24},{9,... | collective-permute-start | bytes 589832 | tf_op jit(solution)/shard_map/ppermute | solution.py:67
  23.4 8.4 %collective-permute-start.9 = (bf16[1,256,384]{2,1,0:T(8,128)(2,1)S(1)}, bf16[1,256,384]{2,1,0:T(8,128)(2,1)S(1)}, u32[]{:S(2)}, u32[]{:S(2)}) collective-permute-start(bf16[1,256,384]{2,1,0:T(8,128)(2,1)S(1)} %collective-permute-done.4.refs_1_), channel_id=1, source_target_pairs={{0,1},{1,0},{2,3},{3,2},{4,5},{5,4},{6,7},{7,6},{8,9},{9,8},{10,11... | collective-permute-start | bytes 589832 | tf_op jit(solution)/shard_map/ppermute | solution.py:67
  26.9 6.8 %collective-permute-start.17 = (bf16[1,272,384]{2,1,0:T(8,128)(2,1)S(1)}, bf16[1,272,384]{2,1,0:T(8,128)(2,1)S(1)}, u32[]{:S(2)}, u32[]{:S(2)}) collective-permute-start(bf16[1,272,384]{2,1,0:T(8,128)(2,1)S(1)} %collective-permute-done.5.refs_1_.refs_14_), channel_id=1, source_target_pairs={{0,8},{1,9},{2,10},{3,11},{4,12},{5,13},{6,14},{7,15},{8,0},{9,1},... | collective-permute-start | bytes 626696 | tf_op jit(solution)/shard_map/ppermute | solution.py:67
  32.4 7.4 %collective-permute-start.15 = (bf16[1,256,384]{2,1,0:T(8,128)(2,1)S(1)}, bf16[1,256,384]{2,1,0:T(8,128)(2,1)S(1)}, u32[]{:S(2)}, u32[]{:S(2)}) collective-permute-start(bf16[1,256,384]{2,1,0:T(8,128)(2,1)S(1)} %collective-permute-done.10.refs_5_), channel_id=1, source_target_pairs={{0,16},{1,17},{2,18},{3,19},{4,20},{5,21},{6,22},{7,23},{8,24},{9,... | collective-permute-start | bytes 589832 | tf_op jit(solution)/shard_map/ppermute | solution.py:67
  33.7 6.6 %collective-permute-start.16 = (bf16[1,256,384]{2,1,0:T(8,128)(2,1)S(1)}, bf16[1,256,384]{2,1,0:T(8,128)(2,1)S(1)}, u32[]{:S(2)}, u32[]{:S(2)}) collective-permute-start(bf16[1,256,384]{2,1,0:T(8,128)(2,1)S(1)} %collective-permute-done.10.refs_5_), channel_id=1, source_target_pairs={{0,1},{1,0},{2,3},{3,2},{4,5},{5,4},{6,7},{7,6},{8,9},{9,8},{10,11... | collective-permute-start | bytes 589832 | tf_op jit(solution)/shard_map/ppermute | solution.py:67
  34.9 6.7 %collective-permute-start.26 = (bf16[1,256,384]{2,1,0:T(8,128)(2,1)S(1)}, bf16[1,256,384]{2,1,0:T(8,128)(2,1)S(1)}, u32[]{:S(2)}, u32[]{:S(2)}) collective-permute-start(bf16[1,256,384]{2,1,0:T(8,128)(2,1)S(1)} %collective-permute-done.9.refs_2_), channel_id=1, source_target_pairs={{0,8},{1,9},{2,10},{3,11},{4,12},{5,13},{6,14},{7,15},{8,0},{9,1},... | collective-permute-start | bytes 589832 | tf_op jit(solution)/shard_map/ppermute | solution.py:67
  35.4 7.0 %collective-permute-start.27 = (bf16[1,256,384]{2,1,0:T(8,128)(2,1)S(1)}, bf16[1,256,384]{2,1,0:T(8,128)(2,1)S(1)}, u32[]{:S(2)}, u32[]{:S(2)}) collective-permute-start(bf16[1,256,384]{2,1,0:T(8,128)(2,1)S(1)} %collective-permute-done.10.refs_5_), channel_id=1, source_target_pairs={{0,8},{1,9},{2,10},{3,11},{4,12},{5,13},{6,14},{7,15},{8,0},{9,1},... | collective-permute-start | bytes 589832 | tf_op jit(solution)/shard_map/ppermute | solution.py:67
  39.9 9.1 %collective-permute-start.23 = (bf16[1,256,384]{2,1,0:T(8,128)(2,1)S(1)}, bf16[1,256,384]{2,1,0:T(8,128)(2,1)S(1)}, u32[]{:S(2)}, u32[]{:S(2)}) collective-permute-start(bf16[1,256,384]{2,1,0:T(8,128)(2,1)S(1)} %collective-permute-done.8.refs_1_), channel_id=1, source_target_pairs={{0,8},{1,9},{2,10},{3,11},{4,12},{5,13},{6,14},{7,15},{8,0},{9,1},... | collective-permute-start | bytes 589832 | tf_op jit(solution)/shard_map/ppermute | solution.py:67
  40.6 8.4 %collective-permute-start.22 = (bf16[2,128,384]{2,1,0:T(8,128)(2,1)S(1)}, bf16[2,128,384]{2,1,0:T(8,128)(2,1)S(1)}, u32[]{:S(2)}, u32[]{:S(2)}) collective-permute-start(bf16[2,128,384]{2,1,0:T(8,128)(2,1)S(1)} %pad_maximum_fusion.3), channel_id=1, source_target_pairs={{0,1},{1,0},{2,3},{3,2},{4,5},{5,4},{6,7},{7,6},{8,9},{9,8},{10,11... | collective-permute-start | bytes 589832 | tf_op jit(solution)/shard_map/ppermute | solution.py:67
  41.6 7.3 %collective-permute-start.21 = (bf16[2,128,384]{2,1,0:T(8,128)(2,1)S(1)}, bf16[2,128,384]{2,1,0:T(8,128)(2,1)S(1)}, u32[]{:S(2)}, u32[]{:S(2)}) collective-permute-start(bf16[2,128,384]{2,1,0:T(8,128)(2,1)S(1)} %pad_maximum_fusion.2), channel_id=1, source_target_pairs={{0,16},{1,17},{2,18},{3,19},{4,20},{5,21},{6,22},{7,23},{8,24},{9,... | collective-permute-start | bytes 589832 | tf_op jit(solution)/shard_map/ppermute | solution.py:67
  42.4 6.6 %collective-permute-start.24 = (bf16[1,256,384]{2,1,0:T(8,128)(2,1)S(1)}, bf16[1,256,384]{2,1,0:T(8,128)(2,1)S(1)}, u32[]{:S(2)}, u32[]{:S(2)}) collective-permute-start(bf16[1,256,384]{2,1,0:T(8,128)(2,1)S(1)} %collective-permute-done.15.refs_7_), channel_id=1, source_target_pairs={{0,8},{1,9},{2,10},{3,11},{4,12},{5,13},{6,14},{7,15},{8,0},{9,1},... | collective-permute-start | bytes 589832 | tf_op jit(solution)/shard_map/ppermute | solution.py:67
  49.6 9.7 %collective-permute-start.29 = (bf16[2,2,256,384]{3,2,1,0:T(8,128)(2,1)S(1)}, bf16[2,2,256,384]{3,2,1,0:T(8,128)(2,1)S(1)}, u32[]{:S(2)}, u32[]{:S(2)}) collective-permute-start(bf16[2,2,256,384]{3,2,1,0:T(8,128)(2,1)S(1)} %get-tuple-element.101), channel_id=1, source_target_pairs={{0,8},{1,9},{2,10},{3,11},{4,12},{5,13},{6,14},{7,15},{8,0},{9,1},... | collective-permute-start | bytes 2359304 | tf_op jit(solution)/shard_map/ppermute | solution.py:67
  52.4 6.9 %collective-permute-start.32 = (bf16[2,2,256,384]{3,2,1,0:T(8,128)(2,1)S(1)}, bf16[2,2,256,384]{3,2,1,0:T(8,128)(2,1)S(1)}, u32[]{:S(2)}, u32[]{:S(2)}) collective-permute-start(bf16[2,2,256,384]{3,2,1,0:T(8,128)(2,1)S(1)} %get-tuple-element.109), channel_id=1, source_target_pairs={{0,8},{1,9},{2,10},{3,11},{4,12},{5,13},{6,14},{7,15},{8,0},{9,1},... | collective-permute-start | bytes 2359304 | tf_op jit(solution)/shard_map/ppermute | solution.py:67
  62.5 30.2 %collective-permute-start.33 = (bf16[2,1,256,384]{3,2,1,0:T(8,128)(2,1)S(1)}, bf16[2,1,256,384]{3,2,1,0:T(8,128)(2,1)S(1)}, u32[]{:S(2)}, u32[]{:S(2)}) collective-permute-start(bf16[2,1,256,384]{3,2,1,0:T(8,128)(2,1)S(1)} %add_convert_fusion.1), channel_id=1, source_target_pairs={{0,2},{1,3},{2,0},{3,1},{4,6},{5,7},{6,4},{7,5},{8,10},{9,11},{10,... | collective-permute-start | bytes 1179656 | tf_op jit(solution)/shard_map/ppermute | solution.py:67
  64.6 7.0 %collective-permute-start.39 = (bf16[2,128,384]{2,1,0:T(8,128)(2,1)S(1)}, bf16[2,128,384]{2,1,0:T(8,128)(2,1)S(1)}, u32[]{:S(2)}, u32[]{:S(2)}) collective-permute-start(bf16[2,128,384]{2,1,0:T(8,128)(2,1)S(1)} %get-tuple-element.146), channel_id=1, source_target_pairs={{0,16},{1,17},{2,18},{3,19},{4,20},{5,21},{6,22},{7,23},{8,24},{9,... | collective-permute-start | bytes 589832 | tf_op jit(solution)/shard_map/ppermute | solution.py:67
  66.0 6.7 %collective-permute-start.40 = (bf16[2,128,384]{2,1,0:T(8,128)(2,1)S(1)}, bf16[2,128,384]{2,1,0:T(8,128)(2,1)S(1)}, u32[]{:S(2)}, u32[]{:S(2)}) collective-permute-start(bf16[2,128,384]{2,1,0:T(8,128)(2,1)S(1)} %get-tuple-element.145), channel_id=1, source_target_pairs={{0,1},{1,0},{2,3},{3,2},{4,5},{5,4},{6,7},{7,6},{8,9},{9,8},{10,11... | collective-permute-start | bytes 589832 | tf_op jit(solution)/shard_map/ppermute | solution.py:67
  67.2 15.7 %collective-permute-start.36 = (bf16[2,1,256,384]{3,2,1,0:T(8,128)(2,1)S(1)}, bf16[2,1,256,384]{3,2,1,0:T(8,128)(2,1)S(1)}, u32[]{:S(2)}, u32[]{:S(2)}) collective-permute-start(bf16[2,1,256,384]{3,2,1,0:T(8,128)(2,1)S(1)} %add_convert_fusion), channel_id=1, source_target_pairs={{0,2},{1,3},{2,0},{3,1},{4,6},{5,7},{6,4},{7,5},{8,10},{9,11},{10,... | collective-permute-start | bytes 1179656 | tf_op jit(solution)/shard_map/ppermute | solution.py:67
  79.5 8.8 %collective-permute-start.45 = (bf16[1,256,384]{2,1,0:T(8,128)(2,1)S(1)}, bf16[1,256,384]{2,1,0:T(8,128)(2,1)S(1)}, u32[]{:S(2)}, u32[]{:S(2)}) collective-permute-start(bf16[1,256,384]{2,1,0:T(8,128)(2,1)S(1)} %fusion.4), channel_id=1, source_target_pairs={{0,2},{1,3},{2,0},{3,1},{4,6},{5,7},{6,4},{7,5},{8,10},{9,11},{10,... | collective-permute-start | bytes 589832 | tf_op jit(solution)/shard_map/ppermute | solution.py:67
  81.6 6.8 %collective-permute-start.44 = (bf16[1,256,384]{2,1,0:T(8,128)(2,1)S(1)}, bf16[1,256,384]{2,1,0:T(8,128)(2,1)S(1)}, u32[]{:S(2)}, u32[]{:S(2)}) collective-permute-start(bf16[1,256,384]{2,1,0:T(8,128)(2,1)S(1)} %slice.198), channel_id=1, source_target_pairs={{0,1},{1,0},{2,3},{3,2},{4,5},{5,4},{6,7},{7,6},{8,9},{9,8},{10,11... | collective-permute-start | bytes 589832 | tf_op jit(solution)/shard_map/ppermute | solution.py:67
  83.0 8.2 %collective-permute-start.37 = (bf16[1,128,384]{2,1,0:T(8,128)(2,1)S(1)}, bf16[1,128,384]{2,1,0:T(8,128)(2,1)S(1)}, u32[]{:S(2)}, u32[]{:S(2)}) collective-permute-start(bf16[1,128,384]{2,1,0:T(8,128)(2,1)S(1)} %get-tuple-element.144), channel_id=1, source_target_pairs={{0,16},{1,17},{2,18},{3,19},{4,20},{5,21},{6,22},{7,23},{8,24},{9,... | collective-permute-start | bytes 294920 | tf_op jit(solution)/shard_map/ppermute | solution.py:67
  88.5 10.1 %collective-permute-start.48 = (bf16[1,256,384]{2,1,0:T(8,128)(2,1)S(1)}, bf16[1,256,384]{2,1,0:T(8,128)(2,1)S(1)}, u32[]{:S(2)}, u32[]{:S(2)}) collective-permute-start(bf16[1,256,384]{2,1,0:T(8,128)(2,1)S(1)} %fusion.8), channel_id=1, source_target_pairs={{0,4},{1,5},{2,6},{3,7},{4,0},{5,1},{6,2},{7,3},{8,12},{9,13},{10,... | collective-permute-start | bytes 589832 | tf_op jit(solution)/shard_map/ppermute | solution.py:67
  91.3 7.3 %collective-permute-start.46 = (bf16[1,256,384]{2,1,0:T(8,128)(2,1)S(1)}, bf16[1,256,384]{2,1,0:T(8,128)(2,1)S(1)}, u32[]{:S(2)}, u32[]{:S(2)}) collective-permute-start(bf16[1,256,384]{2,1,0:T(8,128)(2,1)S(1)} %fusion.10), channel_id=1, source_target_pairs={{0,16},{1,17},{2,18},{3,19},{4,20},{5,21},{6,22},{7,23},{8,24},{9,... | collective-permute-start | bytes 589832 | tf_op jit(solution)/shard_map/ppermute | solution.py:67
  (17 other events, 72.0 us)

commit v9 on v8

--- a/solution.py
+++ b/solution.py
@@ -90,7 +90,11 @@
     half = terms[0][0].shape[2] // 2
     first = summed(terms, 1, 1, slice(0, half)).astype(jnp.bfloat16)
     last = summed(terms, 1, 1, slice(half, 2 * half)).astype(jnp.bfloat16)
-    return send(first, x=1), send(last, y=1)
+    return first, last
+
+
+def across(halves):
+    return send(halves[0], x=1), send(halves[1], y=1)
 
 
 def plane_sums(terms, first, last):
@@ -434,15 +438,16 @@
         place, 1, far, (2, 3), far_weights, sums_1, sx0, w_down, pairs
     )
     far_0, near_0, parts_1 = after((far_0, near_0, parts_1))
-    to_z = total(*[v[:, :1] for v in near_0]).astype(jnp.bfloat16)
-    passed_0 = send(to_z, z=1)
     other_1 = send(parts_1[1], c=1)
     last_1 = third_part(place, after(hidden, far_0), tile, pairs[1], size)
     other_1, last_1 = after((other_1, last_1))
     far_1, near_1 = (parts_1[0], other_1), (last_1[0], send(last_1[1], c=1))
 
     far = far_0, far_1
-    corner = diagonal(far)
+    halves = diagonal(far)
+    corner = across(halves)
+    to_z = total(*[v[:, :1] for v in near_0]).astype(jnp.bfloat16)
+    passed_0 = send(after(to_z, halves), z=1)
     to_z = total(*[v[:, :1] for v in near_1]).astype(jnp.bfloat16)
     passed_1 = send(to_z, z=1)
     to_x, to_y = plane_sums(far, *after(corner, to_z))
@@ -454,7 +459,7 @@
     from_2 = send(to_x[1:], x=1), send(to_y[1:], y=1)
     last_block = lambda terms, passed: [v[:, 1:] for v in terms] + [passed]
     near = last_block(near_0, passed_0), last_block(near_1, passed_1)
-    corner = diagonal(near)
+    corner = across(diagonal(near))
     to_0 = total(here[1:], *from_2, to_2).astype(jnp.bfloat16)
     to_x, to_y = plane_sums(near, *after(corner, to_0))
     to_0 = send(to_0, z=2)

time: 99.6 us -> 101 us (1.014)
  starting transfers between devices: 40.5 us -> 42.9 us
    ppermute x49, starting transfers between devices: 40.5 us -> 42.9 us  [send(): return lax.ppermute(value, BOTH, pairs)]
where the time goes in v9:
time: 101 us
  starting transfers between devices  42.9 us (42%)
  Pallas kernels  30.2 us (30%)
  waiting for transfers between devices  23 us (23%)
  other arithmetic  4.5 us (4%)
    ppermute x49, starting transfers between devices, send(): return lax.ppermute(value, BOTH, pairs)  42.9 us
    ppermute x49, waiting for transfers between devices, send(): return lax.ppermute(value, BOTH, pairs)  23 us
    pallas_call x2, Pallas kernels, second_part(): pl.pallas_call(lambda *refs: second_kernel(*refs, x=x, found=found, z_pla...  13.3 us
    pallas_call x2, Pallas kernels, first_part(): pl.pallas_call(lambda *refs: first_kernel(*refs, found=found, z_places=z_...  8.73 us
    pallas_call x2, Pallas kernels, third_part(): pl.pallas_call(lambda *refs: third_kernel(*refs, pair=pair), in_specs=[SC...  4.73 us
    pallas_call x1, Pallas kernels, pair_weights(): pl.pallas_call(lambda *refs: weights_kernel(*refs, z=z), in_specs=[SCALAR...  3.41 us
  transfers between devices with their start and end apart: 49, of which 11 were waited for; matrix products, arithmetic and copies ran while one was open for 4% of the time, Pallas kernels for 30%

profile of v9, /device:TPU:0, one launch (start us, length us, event | category | flops | bytes accessed | tf_op | source)
XLA Modules:
  0.0 101.2 jit_solution(12369303078141301306)
XLA Ops:
  0.0 3.0 %collective-permute-start.1 = (bf16[1,256,384]{2,1,0:T(8,128)(2,1)}, bf16[1,256,384]{2,1,0:T(8,128)(2,1)S(1)}, u32[]{:S(2)}, u32[]{:S(2)}) collective-permute-start(bf16[1,256,384]{2,1,0:T(8,128)(2,1)} %bitcast.72), channel_id=1, source_target_pairs={{0,2},{1,3},{2,0},{3,1},{4,6},{5,7},{6,4},{7,5},{8,10},{9,11},{10,... | collective-permute-start | bytes 589832 | tf_op jit(solution)/shard_map/ppermute | solution.py:67
  5.5 1.6 %collective-permute-start.5 = (bf16[1,272,384]{2,1,0:T(8,128)(2,1)S(1)}, bf16[1,272,384]{2,1,0:T(8,128)(2,1)S(1)}, u32[]{:S(2)}, u32[]{:S(2)}) collective-permute-start(bf16[1,272,384]{2,1,0:T(8,128)(2,1)S(1)} %maximum_bitcast_fusion.refs_1_.refs_14_), channel_id=1, source_target_pairs={{0,16},{1,17},{2,18},{3,19},{4,20},{5,21},{6,22},{7,23},{8,24},{9,... | collective-permute-start | bytes 626696 | tf_op jit(solution)/shard_map/ppermute | solution.py:67
  7.0 1.5 %collective-permute-start = (bf16[1,256,384]{2,1,0:T(8,128)(2,1)}, bf16[1,256,384]{2,1,0:T(8,128)(2,1)S(1)}, u32[]{:S(2)}, u32[]{:S(2)}) collective-permute-start(bf16[1,256,384]{2,1,0:T(8,128)(2,1)} %bitcast.73), channel_id=1, source_target_pairs={{0,1},{1,0},{2,3},{3,2},{4,5},{5,4},{6,7},{7,6},{8,9},{9,8},{10,11... | collective-permute-start | bytes 589832 | tf_op jit(solution)/shard_map/ppermute | solution.py:67
  8.6 2.6 %collective-permute-start.4 = (bf16[1,256,384]{2,1,0:T(8,128)(2,1)}, bf16[1,256,384]{2,1,0:T(8,128)(2,1)S(1)}, u32[]{:S(2)}, u32[]{:S(2)}) collective-permute-start(bf16[1,256,384]{2,1,0:T(8,128)(2,1)} %bitcast.74), channel_id=1, source_target_pairs={{0,4},{1,5},{2,6},{3,7},{4,0},{5,1},{6,2},{7,3},{8,12},{9,13},{10,... | collective-permute-start | bytes 589832 | tf_op jit(solution)/shard_map/ppermute | solution.py:67
  12.3 1.8 %collective-permute-done.refs_2_ = bf16[1,256,384]{2,1,0:T(8,128)(2,1)S(1)} collective-permute-done((bf16[1,256,384]{2,1,0:T(8,128)(2,1)}, bf16[1,256,384]{2,1,0:T(8,128)(2,1)S(1)}, u32[]{:S(2)}, u32[]{:S(2)}) %collective-permute-start) | collective-permute-done | bytes 196640 | tf_op jit(solution)/shard_map/ppermute | solution.py:67
  14.7 3.4 %pair_weights.1 = (bf16[1536,1024]{1,0:T(8,128)(2,1)S(1)}, bf16[1536,1024]{1,0:T(8,128)(2,1)S(1)}) custom-call(s32[7]{0:T(128)S(1)} %stack.33.refs_0_, bf16[1,272,384]{2,1,0:T(8,128)(2,1)S(1)} %collective-permute-done.5.refs_1_.refs_14_, bf16[3072,1024]{1,0:T(8,128)(2,1)} %bitcast.66, bf16[3072,1024]{1,0:T(8,128)(2,1)} %bitcast.68), custom_call_target="tpu_custom_call" | custom-call | bytes 3145728 | tf_op jit(solution)/shard_map/pair_weights/pallas_call | solution.py:288
  18.2 1.4 %collective-permute-done.4.refs_1_ = bf16[1,256,384]{2,1,0:T(8,128)(2,1)S(1)} collective-permute-done((bf16[1,256,384]{2,1,0:T(8,128)(2,1)}, bf16[1,256,384]{2,1,0:T(8,128)(2,1)S(1)}, u32[]{:S(2)}, u32[]{:S(2)}) %collective-permute-start.4) | collective-permute-done | bytes 196640 | tf_op jit(solution)/shard_map/ppermute | solution.py:67
  21.5 1.9 %collective-permute-start.6 = (bf16[2,128,384]{2,1,0:T(8,128)(2,1)S(1)}, bf16[2,128,384]{2,1,0:T(8,128)(2,1)S(1)}, u32[]{:S(2)}, u32[]{:S(2)}) collective-permute-start(bf16[2,128,384]{2,1,0:T(8,128)(2,1)S(1)} %pad_maximum_fusion), channel_id=1, source_target_pairs={{0,16},{1,17},{2,18},{3,19},{4,20},{5,21},{6,22},{7,23},{8,24},{9,... | collective-permute-start | bytes 589832 | tf_op jit(solution)/shard_map/ppermute | solution.py:67
  24.4 2.5 %collective-permute-done.10.refs_5_ = bf16[1,256,384]{2,1,0:T(8,128)(2,1)S(1)} collective-permute-done((bf16[1,256,384]{2,1,0:T(8,128)(2,1)S(1)}, bf16[1,256,384]{2,1,0:T(8,128)(2,1)S(1)}, u32[]{:S(2)}, u32[]{:S(2)}) %collective-permute-start.10) | collective-permute-done | bytes 196640 | tf_op jit(solution)/shard_map/ppermute | solution.py:67
  26.9 4.3 %first_part.2 = (f32[1,512,1024]{2,1,0:T(8,128)S(1)}, f32[1,512,1024]{2,1,0:T(8,128)S(1)}, bf16[1536,1024]{1,0:T(8,128)(2,1)S(1)}) custom-call(s32[7]{0:T(128)S(1)} %stack.33.refs_0_, bf16[1,272,384]{2,1,0:T(8,128)(2,1)S(1)} %maximum_bitcast_fusion.refs_1_.refs_14_, bf16[1,256,384]{2,1,0:T(8,128)(2,1)S(1)} %collective-permute-done.refs_2_, ...), custom_call_target="tpu_custom_call" | custom-call | flops 805306368 | bytes 3014656 | tf_op jit(solution)/shard_map/first_part/pallas_call | solution.py:306
  32.4 1.3 %collective-permute-start.15 = (bf16[1,256,384]{2,1,0:T(8,128)(2,1)S(1)}, bf16[1,256,384]{2,1,0:T(8,128)(2,1)S(1)}, u32[]{:S(2)}, u32[]{:S(2)}) collective-permute-start(bf16[1,256,384]{2,1,0:T(8,128)(2,1)S(1)} %collective-permute-done.10.refs_5_), channel_id=1, source_target_pairs={{0,16},{1,17},{2,18},{3,19},{4,20},{5,21},{6,22},{7,23},{8,24},{9,... | collective-permute-start | bytes 589832 | tf_op jit(solution)/shard_map/ppermute | solution.py:67
  35.5 4.4 %first_part.3 = (f32[1,512,1024]{2,1,0:T(8,128)S(1)}, f32[1,512,1024]{2,1,0:T(8,128)S(1)}, bf16[1536,1024]{1,0:T(8,128)(2,1)S(1)}) custom-call(s32[7]{0:T(128)S(1)} %stack.33.refs_0_, bf16[1,272,384]{2,1,0:T(8,128)(2,1)S(1)} %collective-permute-done.5.refs_1_.refs_14_, bf16[2,128,384]{2,1,0:T(8,128)(2,1)S(1)} %collective-permute-done.6.refs_2_, ...), custom_call_target="tpu_custom_call" | custom-call | flops 805306368 | bytes 3014656 | tf_op jit(solution)/shard_map/first_part/pallas_call | solution.py:306
  40.6 1.1 %collective-permute-start.22 = (bf16[2,128,384]{2,1,0:T(8,128)(2,1)S(1)}, bf16[2,128,384]{2,1,0:T(8,128)(2,1)S(1)}, u32[]{:S(2)}, u32[]{:S(2)}) collective-permute-start(bf16[2,128,384]{2,1,0:T(8,128)(2,1)S(1)} %pad_maximum_fusion.3), channel_id=1, source_target_pairs={{0,1},{1,0},{2,3},{3,2},{4,5},{5,4},{6,7},{7,6},{8,9},{9,8},{10,11... | collective-permute-start | bytes 589832 | tf_op jit(solution)/shard_map/ppermute | solution.py:67
  42.4 6.5 %second_part.2 = (bf16[2,2,256,384]{3,2,1,0:T(8,128)(2,1)S(1)}, bf16[2,2,256,384]{3,2,1,0:T(8,128)(2,1)S(1)}, bf16[512,1024]{1,0:T(8,128)(2,1)S(1)}, bf16[1024,1536]{1,0:T(8,128)(2,1)S(1)}) custom-call(s32[7]{0:T(128)S(1)} %stack.33.refs_0_, bf16[1,256,384]{2,1,0:T(8,128)(2,1)S(1)} %collective-permute-done.4.refs_1_, ...), custom_call_target="tpu_custom_call" | custom-call | flops 1610612736 | bytes 5373952 | tf_op jit(solution)/shard_map/second_part/pallas_call | solution.py:333
  50.0 2.4 %third_part.2 = (bf16[2,2,256,384]{3,2,1,0:T(8,128)(2,1)S(1)}, bf16[2,2,256,384]{3,2,1,0:T(8,128)(2,1)S(1)}) custom-call(s32[7]{0:T(128)S(1)} %stack.33.refs_0_, bf16[512,1024]{1,0:T(8,128)(2,1)S(1)} %get-tuple-element.105.refs_1_, bf16[1024,1536]{1,0:T(8,128)(2,1)S(1)} %get-tuple-element.106.refs_2_), custom_call_target="tpu_custom_call" | custom-call | flops 402653184 | bytes 1441792 | tf_op jit(solution)/shard_map/third_part/pallas_call | solution.py:361
  52.6 6.8 %second_part.3 = (bf16[2,2,256,384]{3,2,1,0:T(8,128)(2,1)S(1)}, bf16[2,2,256,384]{3,2,1,0:T(8,128)(2,1)S(1)}, bf16[512,1024]{1,0:T(8,128)(2,1)S(1)}) custom-call(s32[7]{0:T(128)S(1)} %stack.33.refs_0_, bf16[1,256,384]{2,1,0:T(8,128)(2,1)S(1)} %collective-permute-done.8.refs_1_, bf16[2,128,384]{2,1,0:T(8,128)(2,1)S(1)} %collective-permute-done.21.refs_2_, ...), custom_call_target="tpu_custom_call" | custom-call | flops 1610612736 | bytes 5373952 | tf_op jit(solution)/shard_map/second_part/pallas_call | solution.py:333
  59.9 2.4 %third_part.3 = (bf16[2,2,256,384]{3,2,1,0:T(8,128)(2,1)S(1)}, bf16[2,2,256,384]{3,2,1,0:T(8,128)(2,1)S(1)}) custom-call(s32[7]{0:T(128)S(1)} %stack.33.refs_0_, bf16[512,1024]{1,0:T(8,128)(2,1)S(1)} %get-tuple-element.130.refs_1_, bf16[1024,1536]{1,0:T(8,128)(2,1)S(1)} %get-tuple-element.106.refs_2_), custom_call_target="tpu_custom_call" | custom-call | flops 402653184 | bytes 1441792 | tf_op jit(solution)/shard_map/third_part/pallas_call | solution.py:361
  62.6 1.3 %collective-permute-start.39 = (bf16[2,128,384]{2,1,0:T(8,128)(2,1)S(1)}, bf16[2,128,384]{2,1,0:T(8,128)(2,1)S(1)}, u32[]{:S(2)}, u32[]{:S(2)}) collective-permute-start(bf16[2,128,384]{2,1,0:T(8,128)(2,1)S(1)} %get-tuple-element.148), channel_id=1, source_target_pairs={{0,16},{1,17},{2,18},{3,19},{4,20},{5,21},{6,22},{7,23},{8,24},{9,... | collective-permute-start | bytes 589832 | tf_op jit(solution)/shard_map/ppermute | solution.py:67
  63.9 1.0 %collective-permute-start.40 = (bf16[2,128,384]{2,1,0:T(8,128)(2,1)S(1)}, bf16[2,128,384]{2,1,0:T(8,128)(2,1)S(1)}, u32[]{:S(2)}, u32[]{:S(2)}) collective-permute-start(bf16[2,128,384]{2,1,0:T(8,128)(2,1)S(1)} %get-tuple-element.147), channel_id=1, source_target_pairs={{0,1},{1,0},{2,3},{3,2},{4,5},{5,4},{6,7},{7,6},{8,9},{9,8},{10,11... | collective-permute-start | bytes 589832 | tf_op jit(solution)/shard_map/ppermute | solution.py:67
  65.1 2.1 %collective-permute-start.36 = (bf16[2,1,256,384]{3,2,1,0:T(8,128)(2,1)S(1)}, bf16[2,1,256,384]{3,2,1,0:T(8,128)(2,1)S(1)}, u32[]{:S(2)}, u32[]{:S(2)}) collective-permute-start(bf16[2,1,256,384]{3,2,1,0:T(8,128)(2,1)S(1)} %add_convert_fusion), channel_id=1, source_target_pairs={{0,2},{1,3},{2,0},{3,1},{4,6},{5,7},{6,4},{7,5},{8,10},{9,11},{10,... | collective-permute-start | bytes 1179656 | tf_op jit(solution)/shard_map/ppermute | solution.py:67
  67.2 2.8 %collective-permute-done.39 = bf16[2,128,384]{2,1,0:T(8,128)(2,1)S(1)} collective-permute-done((bf16[2,128,384]{2,1,0:T(8,128)(2,1)S(1)}, bf16[2,128,384]{2,1,0:T(8,128)(2,1)S(1)}, u32[]{:S(2)}, u32[]{:S(2)}) %collective-permute-start.39) | collective-permute-done | bytes 196640 | tf_op jit(solution)/shard_map/ppermute | solution.py:67
  72.0 1.1 %collective-permute-start.42 = (bf16[1,256,384]{2,1,0:T(8,128)(2,1)S(1)}, bf16[1,256,384]{2,1,0:T(8,128)(2,1)S(1)}, u32[]{:S(2)}, u32[]{:S(2)}) collective-permute-start(bf16[1,256,384]{2,1,0:T(8,128)(2,1)S(1)} %slice.215), channel_id=1, source_target_pairs={{0,1},{1,0},{2,3},{3,2},{4,5},{5,4},{6,7},{7,6},{8,9},{9,8},{10,11... | collective-permute-start | bytes 589832 | tf_op jit(solution)/shard_map/ppermute | solution.py:67
  73.2 1.9 %collective-permute-start.34 = (bf16[2,1,256,384]{3,2,1,0:T(8,128)(2,1)S(1)}, bf16[2,1,256,384]{3,2,1,0:T(8,128)(2,1)S(1)}, u32[]{:S(2)}, u32[]{:S(2)}) collective-permute-start(bf16[2,1,256,384]{3,2,1,0:T(8,128)(2,1)S(1)} %add_convert_fusion.1), channel_id=1, source_target_pairs={{0,2},{1,3},{2,0},{3,1},{4,6},{5,7},{6,4},{7,5},{8,10},{9,11},{10,... | collective-permute-start | bytes 1179656 | tf_op jit(solution)/shard_map/ppermute | solution.py:67
  75.2 2.1 %collective-permute-done.41 = bf16[1,256,384]{2,1,0:T(8,128)(2,1)S(1)} collective-permute-done((bf16[1,256,384]{2,1,0:T(8,128)(2,1)S(1)}, bf16[1,256,384]{2,1,0:T(8,128)(2,1)S(1)}, u32[]{:S(2)}, u32[]{:S(2)}) %collective-permute-start.41) | collective-permute-done | bytes 196640 | tf_op jit(solution)/shard_map/ppermute | solution.py:67
  78.1 2.0 %collective-permute-start.45 = (bf16[1,256,384]{2,1,0:T(8,128)(2,1)S(1)}, bf16[1,256,384]{2,1,0:T(8,128)(2,1)S(1)}, u32[]{:S(2)}, u32[]{:S(2)}) collective-permute-start(bf16[1,256,384]{2,1,0:T(8,128)(2,1)S(1)} %fusion.4), channel_id=1, source_target_pairs={{0,2},{1,3},{2,0},{3,1},{4,6},{5,7},{6,4},{7,5},{8,10},{9,11},{10,... | collective-permute-start | bytes 589832 | tf_op jit(solution)/shard_map/ppermute | solution.py:67
  80.0 1.4 %collective-permute-start.43 = (bf16[1,256,384]{2,1,0:T(8,128)(2,1)S(1)}, bf16[1,256,384]{2,1,0:T(8,128)(2,1)S(1)}, u32[]{:S(2)}, u32[]{:S(2)}) collective-permute-start(bf16[1,256,384]{2,1,0:T(8,128)(2,1)S(1)} %slice.197), channel_id=1, source_target_pairs={{0,16},{1,17},{2,18},{3,19},{4,20},{5,21},{6,22},{7,23},{8,24},{9,... | collective-permute-start | bytes 589832 | tf_op jit(solution)/shard_map/ppermute | solution.py:67
  81.5 1.1 %collective-permute-start.44 = (bf16[1,256,384]{2,1,0:T(8,128)(2,1)S(1)}, bf16[1,256,384]{2,1,0:T(8,128)(2,1)S(1)}, u32[]{:S(2)}, u32[]{:S(2)}) collective-permute-start(bf16[1,256,384]{2,1,0:T(8,128)(2,1)S(1)} %slice.198), channel_id=1, source_target_pairs={{0,1},{1,0},{2,3},{3,2},{4,5},{5,4},{6,7},{7,6},{8,9},{9,8},{10,11... | collective-permute-start | bytes 589832 | tf_op jit(solution)/shard_map/ppermute | solution.py:67
  83.4 2.4 %collective-permute-done.43 = bf16[1,256,384]{2,1,0:T(8,128)(2,1)S(1)} collective-permute-done((bf16[1,256,384]{2,1,0:T(8,128)(2,1)S(1)}, bf16[1,256,384]{2,1,0:T(8,128)(2,1)S(1)}, u32[]{:S(2)}, u32[]{:S(2)}) %collective-permute-start.43) | collective-permute-done | bytes 196640 | tf_op jit(solution)/shard_map/ppermute | solution.py:67
  86.9 1.4 %collective-permute-done.44 = bf16[1,256,384]{2,1,0:T(8,128)(2,1)S(1)} collective-permute-done((bf16[1,256,384]{2,1,0:T(8,128)(2,1)S(1)}, bf16[1,256,384]{2,1,0:T(8,128)(2,1)S(1)}, u32[]{:S(2)}, u32[]{:S(2)}) %collective-permute-start.44) | collective-permute-done | bytes 196640 | tf_op jit(solution)/shard_map/ppermute | solution.py:67
  89.1 2.8 %collective-permute-start.48 = (bf16[1,256,384]{2,1,0:T(8,128)(2,1)S(1)}, bf16[1,256,384]{2,1,0:T(8,128)(2,1)S(1)}, u32[]{:S(2)}, u32[]{:S(2)}) collective-permute-start(bf16[1,256,384]{2,1,0:T(8,128)(2,1)S(1)} %fusion.8), channel_id=1, source_target_pairs={{0,4},{1,5},{2,6},{3,7},{4,0},{5,1},{6,2},{7,3},{8,12},{9,13},{10,... | collective-permute-start | bytes 589832 | tf_op jit(solution)/shard_map/ppermute | solution.py:67
  91.9 1.3 %collective-permute-start.46 = (bf16[1,256,384]{2,1,0:T(8,128)(2,1)S(1)}, bf16[1,256,384]{2,1,0:T(8,128)(2,1)S(1)}, u32[]{:S(2)}, u32[]{:S(2)}) collective-permute-start(bf16[1,256,384]{2,1,0:T(8,128)(2,1)S(1)} %fusion.10), channel_id=1, source_target_pairs={{0,16},{1,17},{2,18},{3,19},{4,20},{5,21},{6,22},{7,23},{8,24},{9,... | collective-permute-start | bytes 589832 | tf_op jit(solution)/shard_map/ppermute | solution.py:67
  94.4 6.0 %collective-permute-done.48 = bf16[1,256,384]{2,1,0:T(8,128)(2,1)S(1)} collective-permute-done((bf16[1,256,384]{2,1,0:T(8,128)(2,1)S(1)}, bf16[1,256,384]{2,1,0:T(8,128)(2,1)S(1)}, u32[]{:S(2)}, u32[]{:S(2)}) %collective-permute-start.48) | collective-permute-done | bytes 196640 | tf_op jit(solution)/shard_map/ppermute | solution.py:67
  (108 shorter events, 21.1 us)
Async XLA Ops:
  0.0 11.2 %collective-permute-start.1 = (bf16[1,256,384]{2,1,0:T(8,128)(2,1)}, bf16[1,256,384]{2,1,0:T(8,128)(2,1)S(1)}, u32[]{:S(2)}, u32[]{:S(2)}) collective-permute-start(bf16[1,256,384]{2,1,0:T(8,128)(2,1)} %bitcast.72), channel_id=1, source_target_pairs={{0,2},{1,3},{2,0},{3,1},{4,6},{5,7},{6,4},{7,5},{8,10},{9,11},{10,... | collective-permute-start | bytes 589832 | tf_op jit(solution)/shard_map/ppermute | solution.py:67
  5.5 8.7 %collective-permute-start.5 = (bf16[1,272,384]{2,1,0:T(8,128)(2,1)S(1)}, bf16[1,272,384]{2,1,0:T(8,128)(2,1)S(1)}, u32[]{:S(2)}, u32[]{:S(2)}) collective-permute-start(bf16[1,272,384]{2,1,0:T(8,128)(2,1)S(1)} %maximum_bitcast_fusion.refs_1_.refs_14_), channel_id=1, source_target_pairs={{0,16},{1,17},{2,18},{3,19},{4,20},{5,21},{6,22},{7,23},{8,24},{9,... | collective-permute-start | bytes 626696 | tf_op jit(solution)/shard_map/ppermute | solution.py:67
  7.0 7.1 %collective-permute-start = (bf16[1,256,384]{2,1,0:T(8,128)(2,1)}, bf16[1,256,384]{2,1,0:T(8,128)(2,1)S(1)}, u32[]{:S(2)}, u32[]{:S(2)}) collective-permute-start(bf16[1,256,384]{2,1,0:T(8,128)(2,1)} %bitcast.73), channel_id=1, source_target_pairs={{0,1},{1,0},{2,3},{3,2},{4,5},{5,4},{6,7},{7,6},{8,9},{9,8},{10,11... | collective-permute-start | bytes 589832 | tf_op jit(solution)/shard_map/ppermute | solution.py:67
  8.6 11.0 %collective-permute-start.4 = (bf16[1,256,384]{2,1,0:T(8,128)(2,1)}, bf16[1,256,384]{2,1,0:T(8,128)(2,1)S(1)}, u32[]{:S(2)}, u32[]{:S(2)}) collective-permute-start(bf16[1,256,384]{2,1,0:T(8,128)(2,1)} %bitcast.74), channel_id=1, source_target_pairs={{0,4},{1,5},{2,6},{3,7},{4,0},{5,1},{6,2},{7,3},{8,12},{9,13},{10,... | collective-permute-start | bytes 589832 | tf_op jit(solution)/shard_map/ppermute | solution.py:67
  11.2 8.5 %collective-permute-start.2 = (bf16[1,256,384]{2,1,0:T(8,128)(2,1)S(1)}, bf16[1,256,384]{2,1,0:T(8,128)(2,1)S(1)}, u32[]{:S(2)}, u32[]{:S(2)}) collective-permute-start(bf16[1,256,384]{2,1,0:T(8,128)(2,1)S(1)} %collective-permute-done.1.refs_5_), channel_id=1, source_target_pairs={{0,16},{1,17},{2,18},{3,19},{4,20},{5,21},{6,22},{7,23},{8,24},{9,... | collective-permute-start | bytes 589832 | tf_op jit(solution)/shard_map/ppermute | solution.py:67
  11.7 7.9 %collective-permute-start.3 = (bf16[1,256,384]{2,1,0:T(8,128)(2,1)S(1)}, bf16[1,256,384]{2,1,0:T(8,128)(2,1)S(1)}, u32[]{:S(2)}, u32[]{:S(2)}) collective-permute-start(bf16[1,256,384]{2,1,0:T(8,128)(2,1)S(1)} %collective-permute-done.1.refs_5_), channel_id=1, source_target_pairs={{0,1},{1,0},{2,3},{3,2},{4,5},{5,4},{6,7},{7,6},{8,9},{9,8},{10,11... | collective-permute-start | bytes 589832 | tf_op jit(solution)/shard_map/ppermute | solution.py:67
  14.1 6.8 %collective-permute-start.12 = (bf16[1,256,384]{2,1,0:T(8,128)(2,1)S(1)}, bf16[1,256,384]{2,1,0:T(8,128)(2,1)S(1)}, u32[]{:S(2)}, u32[]{:S(2)}) collective-permute-start(bf16[1,256,384]{2,1,0:T(8,128)(2,1)S(1)} %collective-permute-done.refs_2_), channel_id=1, source_target_pairs={{0,8},{1,9},{2,10},{3,11},{4,12},{5,13},{6,14},{7,15},{8,0},{9,1},... | collective-permute-start | bytes 589832 | tf_op jit(solution)/shard_map/ppermute | solution.py:67
  19.6 7.3 %collective-permute-start.10 = (bf16[1,256,384]{2,1,0:T(8,128)(2,1)S(1)}, bf16[1,256,384]{2,1,0:T(8,128)(2,1)S(1)}, u32[]{:S(2)}, u32[]{:S(2)}) collective-permute-start(bf16[1,256,384]{2,1,0:T(8,128)(2,1)S(1)} %collective-permute-done.4.refs_1_), channel_id=1, source_target_pairs={{0,2},{1,3},{2,0},{3,1},{4,6},{5,7},{6,4},{7,5},{8,10},{9,11},{10,... | collective-permute-start | bytes 589832 | tf_op jit(solution)/shard_map/ppermute | solution.py:67
  20.3 11.6 %collective-permute-start.8 = (bf16[1,256,384]{2,1,0:T(8,128)(2,1)S(1)}, bf16[1,256,384]{2,1,0:T(8,128)(2,1)S(1)}, u32[]{:S(2)}, u32[]{:S(2)}) collective-permute-start(bf16[1,256,384]{2,1,0:T(8,128)(2,1)S(1)} %collective-permute-done.4.refs_1_), channel_id=1, source_target_pairs={{0,16},{1,17},{2,18},{3,19},{4,20},{5,21},{6,22},{7,23},{8,24},{9,... | collective-permute-start | bytes 589832 | tf_op jit(solution)/shard_map/ppermute | solution.py:67
  21.0 10.3 %collective-permute-start.7 = (bf16[2,128,384]{2,1,0:T(8,128)(2,1)S(1)}, bf16[2,128,384]{2,1,0:T(8,128)(2,1)S(1)}, u32[]{:S(2)}, u32[]{:S(2)}) collective-permute-start(bf16[2,128,384]{2,1,0:T(8,128)(2,1)S(1)} %pad_maximum_fusion.1), channel_id=1, source_target_pairs={{0,1},{1,0},{2,3},{3,2},{4,5},{5,4},{6,7},{7,6},{8,9},{9,8},{10,11... | collective-permute-start | bytes 589832 | tf_op jit(solution)/shard_map/ppermute | solution.py:67
  21.5 10.4 %collective-permute-start.6 = (bf16[2,128,384]{2,1,0:T(8,128)(2,1)S(1)}, bf16[2,128,384]{2,1,0:T(8,128)(2,1)S(1)}, u32[]{:S(2)}, u32[]{:S(2)}) collective-permute-start(bf16[2,128,384]{2,1,0:T(8,128)(2,1)S(1)} %pad_maximum_fusion), channel_id=1, source_target_pairs={{0,16},{1,17},{2,18},{3,19},{4,20},{5,21},{6,22},{7,23},{8,24},{9,... | collective-permute-start | bytes 589832 | tf_op jit(solution)/shard_map/ppermute | solution.py:67
  23.4 8.4 %collective-permute-start.9 = (bf16[1,256,384]{2,1,0:T(8,128)(2,1)S(1)}, bf16[1,256,384]{2,1,0:T(8,128)(2,1)S(1)}, u32[]{:S(2)}, u32[]{:S(2)}) collective-permute-start(bf16[1,256,384]{2,1,0:T(8,128)(2,1)S(1)} %collective-permute-done.4.refs_1_), channel_id=1, source_target_pairs={{0,1},{1,0},{2,3},{3,2},{4,5},{5,4},{6,7},{7,6},{8,9},{9,8},{10,11... | collective-permute-start | bytes 589832 | tf_op jit(solution)/shard_map/ppermute | solution.py:67
  26.9 6.8 %collective-permute-start.17 = (bf16[1,272,384]{2,1,0:T(8,128)(2,1)S(1)}, bf16[1,272,384]{2,1,0:T(8,128)(2,1)S(1)}, u32[]{:S(2)}, u32[]{:S(2)}) collective-permute-start(bf16[1,272,384]{2,1,0:T(8,128)(2,1)S(1)} %collective-permute-done.5.refs_1_.refs_14_), channel_id=1, source_target_pairs={{0,8},{1,9},{2,10},{3,11},{4,12},{5,13},{6,14},{7,15},{8,0},{9,1},... | collective-permute-start | bytes 626696 | tf_op jit(solution)/shard_map/ppermute | solution.py:67
  32.4 7.4 %collective-permute-start.15 = (bf16[1,256,384]{2,1,0:T(8,128)(2,1)S(1)}, bf16[1,256,384]{2,1,0:T(8,128)(2,1)S(1)}, u32[]{:S(2)}, u32[]{:S(2)}) collective-permute-start(bf16[1,256,384]{2,1,0:T(8,128)(2,1)S(1)} %collective-permute-done.10.refs_5_), channel_id=1, source_target_pairs={{0,16},{1,17},{2,18},{3,19},{4,20},{5,21},{6,22},{7,23},{8,24},{9,... | collective-permute-start | bytes 589832 | tf_op jit(solution)/shard_map/ppermute | solution.py:67
  33.7 6.6 %collective-permute-start.16 = (bf16[1,256,384]{2,1,0:T(8,128)(2,1)S(1)}, bf16[1,256,384]{2,1,0:T(8,128)(2,1)S(1)}, u32[]{:S(2)}, u32[]{:S(2)}) collective-permute-start(bf16[1,256,384]{2,1,0:T(8,128)(2,1)S(1)} %collective-permute-done.10.refs_5_), channel_id=1, source_target_pairs={{0,1},{1,0},{2,3},{3,2},{4,5},{5,4},{6,7},{7,6},{8,9},{9,8},{10,11... | collective-permute-start | bytes 589832 | tf_op jit(solution)/shard_map/ppermute | solution.py:67
  34.9 6.7 %collective-permute-start.26 = (bf16[1,256,384]{2,1,0:T(8,128)(2,1)S(1)}, bf16[1,256,384]{2,1,0:T(8,128)(2,1)S(1)}, u32[]{:S(2)}, u32[]{:S(2)}) collective-permute-start(bf16[1,256,384]{2,1,0:T(8,128)(2,1)S(1)} %collective-permute-done.9.refs_2_), channel_id=1, source_target_pairs={{0,8},{1,9},{2,10},{3,11},{4,12},{5,13},{6,14},{7,15},{8,0},{9,1},... | collective-permute-start | bytes 589832 | tf_op jit(solution)/shard_map/ppermute | solution.py:67
  35.4 7.0 %collective-permute-start.27 = (bf16[1,256,384]{2,1,0:T(8,128)(2,1)S(1)}, bf16[1,256,384]{2,1,0:T(8,128)(2,1)S(1)}, u32[]{:S(2)}, u32[]{:S(2)}) collective-permute-start(bf16[1,256,384]{2,1,0:T(8,128)(2,1)S(1)} %collective-permute-done.10.refs_5_), channel_id=1, source_target_pairs={{0,8},{1,9},{2,10},{3,11},{4,12},{5,13},{6,14},{7,15},{8,0},{9,1},... | collective-permute-start | bytes 589832 | tf_op jit(solution)/shard_map/ppermute | solution.py:67
  39.9 9.1 %collective-permute-start.23 = (bf16[1,256,384]{2,1,0:T(8,128)(2,1)S(1)}, bf16[1,256,384]{2,1,0:T(8,128)(2,1)S(1)}, u32[]{:S(2)}, u32[]{:S(2)}) collective-permute-start(bf16[1,256,384]{2,1,0:T(8,128)(2,1)S(1)} %collective-permute-done.8.refs_1_), channel_id=1, source_target_pairs={{0,8},{1,9},{2,10},{3,11},{4,12},{5,13},{6,14},{7,15},{8,0},{9,1},... | collective-permute-start | bytes 589832 | tf_op jit(solution)/shard_map/ppermute | solution.py:67
  40.6 8.4 %collective-permute-start.22 = (bf16[2,128,384]{2,1,0:T(8,128)(2,1)S(1)}, bf16[2,128,384]{2,1,0:T(8,128)(2,1)S(1)}, u32[]{:S(2)}, u32[]{:S(2)}) collective-permute-start(bf16[2,128,384]{2,1,0:T(8,128)(2,1)S(1)} %pad_maximum_fusion.3), channel_id=1, source_target_pairs={{0,1},{1,0},{2,3},{3,2},{4,5},{5,4},{6,7},{7,6},{8,9},{9,8},{10,11... | collective-permute-start | bytes 589832 | tf_op jit(solution)/shard_map/ppermute | solution.py:67
  41.6 7.3 %collective-permute-start.21 = (bf16[2,128,384]{2,1,0:T(8,128)(2,1)S(1)}, bf16[2,128,384]{2,1,0:T(8,128)(2,1)S(1)}, u32[]{:S(2)}, u32[]{:S(2)}) collective-permute-start(bf16[2,128,384]{2,1,0:T(8,128)(2,1)S(1)} %pad_maximum_fusion.2), channel_id=1, source_target_pairs={{0,16},{1,17},{2,18},{3,19},{4,20},{5,21},{6,22},{7,23},{8,24},{9,... | collective-permute-start | bytes 589832 | tf_op jit(solution)/shard_map/ppermute | solution.py:67
  49.6 9.7 %collective-permute-start.29 = (bf16[2,2,256,384]{3,2,1,0:T(8,128)(2,1)S(1)}, bf16[2,2,256,384]{3,2,1,0:T(8,128)(2,1)S(1)}, u32[]{:S(2)}, u32[]{:S(2)}) collective-permute-start(bf16[2,2,256,384]{3,2,1,0:T(8,128)(2,1)S(1)} %get-tuple-element.102), channel_id=1, source_target_pairs={{0,8},{1,9},{2,10},{3,11},{4,12},{5,13},{6,14},{7,15},{8,0},{9,1},... | collective-permute-start | bytes 2359304 | tf_op jit(solution)/shard_map/ppermute | solution.py:67
  52.4 6.9 %collective-permute-start.32 = (bf16[2,2,256,384]{3,2,1,0:T(8,128)(2,1)S(1)}, bf16[2,2,256,384]{3,2,1,0:T(8,128)(2,1)S(1)}, u32[]{:S(2)}, u32[]{:S(2)}) collective-permute-start(bf16[2,2,256,384]{3,2,1,0:T(8,128)(2,1)S(1)} %get-tuple-element.110), channel_id=1, source_target_pairs={{0,8},{1,9},{2,10},{3,11},{4,12},{5,13},{6,14},{7,15},{8,0},{9,1},... | collective-permute-start | bytes 2359304 | tf_op jit(solution)/shard_map/ppermute | solution.py:67
  62.6 7.3 %collective-permute-start.39 = (bf16[2,128,384]{2,1,0:T(8,128)(2,1)S(1)}, bf16[2,128,384]{2,1,0:T(8,128)(2,1)S(1)}, u32[]{:S(2)}, u32[]{:S(2)}) collective-permute-start(bf16[2,128,384]{2,1,0:T(8,128)(2,1)S(1)} %get-tuple-element.148), channel_id=1, source_target_pairs={{0,16},{1,17},{2,18},{3,19},{4,20},{5,21},{6,22},{7,23},{8,24},{9,... | collective-permute-start | bytes 589832 | tf_op jit(solution)/shard_map/ppermute | solution.py:67
  63.9 7.0 %collective-permute-start.40 = (bf16[2,128,384]{2,1,0:T(8,128)(2,1)S(1)}, bf16[2,128,384]{2,1,0:T(8,128)(2,1)S(1)}, u32[]{:S(2)}, u32[]{:S(2)}) collective-permute-start(bf16[2,128,384]{2,1,0:T(8,128)(2,1)S(1)} %get-tuple-element.147), channel_id=1, source_target_pairs={{0,1},{1,0},{2,3},{3,2},{4,5},{5,4},{6,7},{7,6},{8,9},{9,8},{10,11... | collective-permute-start | bytes 589832 | tf_op jit(solution)/shard_map/ppermute | solution.py:67
  65.1 17.6 %collective-permute-start.36 = (bf16[2,1,256,384]{3,2,1,0:T(8,128)(2,1)S(1)}, bf16[2,1,256,384]{3,2,1,0:T(8,128)(2,1)S(1)}, u32[]{:S(2)}, u32[]{:S(2)}) collective-permute-start(bf16[2,1,256,384]{3,2,1,0:T(8,128)(2,1)S(1)} %add_convert_fusion), channel_id=1, source_target_pairs={{0,2},{1,3},{2,0},{3,1},{4,6},{5,7},{6,4},{7,5},{8,10},{9,11},{10,... | collective-permute-start | bytes 1179656 | tf_op jit(solution)/shard_map/ppermute | solution.py:67
  73.2 20.0 %collective-permute-start.34 = (bf16[2,1,256,384]{3,2,1,0:T(8,128)(2,1)S(1)}, bf16[2,1,256,384]{3,2,1,0:T(8,128)(2,1)S(1)}, u32[]{:S(2)}, u32[]{:S(2)}) collective-permute-start(bf16[2,1,256,384]{3,2,1,0:T(8,128)(2,1)S(1)} %add_convert_fusion.1), channel_id=1, source_target_pairs={{0,2},{1,3},{2,0},{3,1},{4,6},{5,7},{6,4},{7,5},{8,10},{9,11},{10,... | collective-permute-start | bytes 1179656 | tf_op jit(solution)/shard_map/ppermute | solution.py:67
  78.1 10.9 %collective-permute-start.45 = (bf16[1,256,384]{2,1,0:T(8,128)(2,1)S(1)}, bf16[1,256,384]{2,1,0:T(8,128)(2,1)S(1)}, u32[]{:S(2)}, u32[]{:S(2)}) collective-permute-start(bf16[1,256,384]{2,1,0:T(8,128)(2,1)S(1)} %fusion.4), channel_id=1, source_target_pairs={{0,2},{1,3},{2,0},{3,1},{4,6},{5,7},{6,4},{7,5},{8,10},{9,11},{10,... | collective-permute-start | bytes 589832 | tf_op jit(solution)/shard_map/ppermute | solution.py:67
  81.5 6.8 %collective-permute-start.44 = (bf16[1,256,384]{2,1,0:T(8,128)(2,1)S(1)}, bf16[1,256,384]{2,1,0:T(8,128)(2,1)S(1)}, u32[]{:S(2)}, u32[]{:S(2)}) collective-permute-start(bf16[1,256,384]{2,1,0:T(8,128)(2,1)S(1)} %slice.198), channel_id=1, source_target_pairs={{0,1},{1,0},{2,3},{3,2},{4,5},{5,4},{6,7},{7,6},{8,9},{9,8},{10,11... | collective-permute-start | bytes 589832 | tf_op jit(solution)/shard_map/ppermute | solution.py:67
  82.7 9.1 %collective-permute-start.37 = (bf16[1,128,384]{2,1,0:T(8,128)(2,1)S(1)}, bf16[1,128,384]{2,1,0:T(8,128)(2,1)S(1)}, u32[]{:S(2)}, u32[]{:S(2)}) collective-permute-start(bf16[1,128,384]{2,1,0:T(8,128)(2,1)S(1)} %get-tuple-element.146), channel_id=1, source_target_pairs={{0,16},{1,17},{2,18},{3,19},{4,20},{5,21},{6,22},{7,23},{8,24},{9,... | collective-permute-start | bytes 294920 | tf_op jit(solution)/shard_map/ppermute | solution.py:67
  89.1 11.3 %collective-permute-start.48 = (bf16[1,256,384]{2,1,0:T(8,128)(2,1)S(1)}, bf16[1,256,384]{2,1,0:T(8,128)(2,1)S(1)}, u32[]{:S(2)}, u32[]{:S(2)}) collective-permute-start(bf16[1,256,384]{2,1,0:T(8,128)(2,1)S(1)} %fusion.8), channel_id=1, source_target_pairs={{0,4},{1,5},{2,6},{3,7},{4,0},{5,1},{6,2},{7,3},{8,12},{9,13},{10,... | collective-permute-start | bytes 589832 | tf_op jit(solution)/shard_map/ppermute | solution.py:67
  91.9 8.4 %collective-permute-start.46 = (bf16[1,256,384]{2,1,0:T(8,128)(2,1)S(1)}, bf16[1,256,384]{2,1,0:T(8,128)(2,1)S(1)}, u32[]{:S(2)}, u32[]{:S(2)}) collective-permute-start(bf16[1,256,384]{2,1,0:T(8,128)(2,1)S(1)} %fusion.10), channel_id=1, source_target_pairs={{0,16},{1,17},{2,18},{3,19},{4,20},{5,21},{6,22},{7,23},{8,24},{9,... | collective-permute-start | bytes 589832 | tf_op jit(solution)/shard_map/ppermute | solution.py:67
  93.4 7.0 %collective-permute-start.47 = (bf16[1,256,384]{2,1,0:T(8,128)(2,1)S(1)}, bf16[1,256,384]{2,1,0:T(8,128)(2,1)S(1)}, u32[]{:S(2)}, u32[]{:S(2)}) collective-permute-start(bf16[1,256,384]{2,1,0:T(8,128)(2,1)S(1)} %fusion.9), channel_id=1, source_target_pairs={{0,1},{1,0},{2,3},{3,2},{4,5},{5,4},{6,7},{7,6},{8,9},{9,8},{10,11... | collective-permute-start | bytes 589832 | tf_op jit(solution)/shard_map/ppermute | solution.py:67
  (17 other events, 72.0 us)

commit v10 on v8

--- a/solution.py
+++ b/solution.py
@@ -138,6 +138,15 @@
     return copies
 
 
+def store(place, arrays, found, z_places, rows):
+    my_y = place[place.shape[0] - 1]
+    for which, index, z, row, y, count in found:
+        narrow = arrays[which].shape[2]
+        column = ((place[z_places[z]] & 1) * 2 + (my_y ^ y)) * narrow
+        columns = pl.ds(pl.multiple_of(column, 128), narrow)
+        rows[row : row + count, columns] = arrays[which][index, :count]
+
+
 def all_of(copies):
     for copy in copies:
         copy.start()
@@ -223,20 +232,18 @@
 
 
 def second_kernel(place, *refs, x, found, z_places, pairs):
-    count = 16 if x else 17
+    count = 15 if x else 16
     arrays, refs = refs[:-count], refs[-count:]
     w_gate, w_up, gate, up, w_down = refs[:5]
     shares, results, hidden = refs[5:7], refs[7:9], refs[9]
-    rows, tails, sems, t_sems, d_sems, tile = refs[-6:]
-    copies = fill(place, arrays, found, z_places, rows, sems)
+    rows, tails, t_sems, d_sems, tile = refs[-5:]
     downs_in = [down_copy(place, pairs[0], w_down, tile, d_sems.at[0])]
     if x == 0:
         downs_in.append(down_copy(place, pairs[1], w_down, refs[10], d_sems.at[1]))
-    for copy in copies + downs_in:
+    for copy in downs_in:
         copy.start()
+    store(place, arrays, found, z_places, rows)
     share = 0.5 * share_column(place, shares, tails, t_sems, results[0].shape[2])
-    for copy in copies:
-        copy.wait()
     for t in range(gate.shape[0]):
         span = slice(t * HIDDEN_TILE, (t + 1) * HIDDEN_TILE)
         g = gate[t] + jnp.dot(rows[...], w_gate[:, span], preferred_element_type=jnp.float32)
@@ -330,12 +337,11 @@
         lambda *refs: second_kernel(
             *refs, x=x, found=found, z_places=z_places, pairs=pairs
         ),
-        in_specs=[SCALARS] + [ANY] * len(arrays) + [VMEM] * 4 + [ANY] * 3,
+        in_specs=[SCALARS] + [VMEM] * (len(arrays) + 4) + [ANY] * 3,
         out_specs=[VMEM] * (3 if x else 4),
         scratch_shapes=[
             pltpu.VMEM((rows, depth), jnp.bfloat16),
             pltpu.VMEM((2, tail, narrow), jnp.bfloat16),
-            SEMS((len(found),)),
             SEMS((2,)),
             SEMS((2,)),
             tile,
@@ -348,7 +354,7 @@
             transcendentals=rows * width,
         ),
         name="second_part",
-    )(place, *arrays, *[in_vmem(v) for v in (*weights, *sums)], w_down, *shares)
+    )(place, *[in_vmem(v) for v in (*arrays, *weights, *sums)], w_down, *shares)
 
 
 def third_part(place, hidden, tile, pair, size):

time: 99.6 us -> 98.9 us (level)
  no operation moved by 1% of the time
where the time goes in v10:
time: 98.9 us; the launch traced here: 98.7 us
  starting transfers between devices  40.4 us (41%)
  Pallas kernels  29.5 us (30%)
  waiting for transfers between devices  23.7 us (24%)
  other arithmetic  4.49 us (5%)
    ppermute x49, starting transfers between devices, send(): return lax.ppermute(value, BOTH, pairs)  40.4 us
    ppermute x49, waiting for transfers between devices, send(): return lax.ppermute(value, BOTH, pairs)  23.7 us
    pallas_call x2, Pallas kernels, second_part(): pl.pallas_call(lambda *refs: second_kernel(*refs, x=x, found=found, z_pla...  12.6 us
    pallas_call x2, Pallas kernels, first_part(): pl.pallas_call(lambda *refs: first_kernel(*refs, found=found, z_places=z_...  8.73 us
    pallas_call x2, Pallas kernels, third_part(): pl.pallas_call(lambda *refs: third_kernel(*refs, pair=pair), in_specs=[SC...  4.73 us
    pallas_call x1, Pallas kernels, pair_weights(): pl.pallas_call(lambda *refs: weights_kernel(*refs, z=z), in_specs=[SCALAR...  3.41 us
  transfers between devices with their start and end apart: 49, of which 11 were waited for; matrix products, arithmetic and copies ran while one was open for 4% of the time, Pallas kernels for 30%

profile of v10, /device:TPU:0, one launch (start us, length us, event | category | flops | bytes accessed | tf_op | source)
XLA Modules:
  0.0 98.7 jit_solution(13137081578636337809)
XLA Ops:
  0.0 3.0 %collective-permute-start.1 = (bf16[1,256,384]{2,1,0:T(8,128)(2,1)}, bf16[1,256,384]{2,1,0:T(8,128)(2,1)S(1)}, u32[]{:S(2)}, u32[]{:S(2)}) collective-permute-start(bf16[1,256,384]{2,1,0:T(8,128)(2,1)} %bitcast.72), channel_id=1, source_target_pairs={{0,2},{1,3},{2,0},{3,1},{4,6},{5,7},{6,4},{7,5},{8,10},{9,11},{10,... | collective-permute-start | bytes 589832 | tf_op jit(solution)/shard_map/ppermute | solution.py:67
  5.5 1.6 %collective-permute-start.5 = (bf16[1,272,384]{2,1,0:T(8,128)(2,1)S(1)}, bf16[1,272,384]{2,1,0:T(8,128)(2,1)S(1)}, u32[]{:S(2)}, u32[]{:S(2)}) collective-permute-start(bf16[1,272,384]{2,1,0:T(8,128)(2,1)S(1)} %maximum_bitcast_fusion.refs_1_.refs_14_), channel_id=1, source_target_pairs={{0,16},{1,17},{2,18},{3,19},{4,20},{5,21},{6,22},{7,23},{8,24},{9,... | collective-permute-start | bytes 626696 | tf_op jit(solution)/shard_map/ppermute | solution.py:67
  7.0 1.5 %collective-permute-start = (bf16[1,256,384]{2,1,0:T(8,128)(2,1)}, bf16[1,256,384]{2,1,0:T(8,128)(2,1)S(1)}, u32[]{:S(2)}, u32[]{:S(2)}) collective-permute-start(bf16[1,256,384]{2,1,0:T(8,128)(2,1)} %bitcast.73), channel_id=1, source_target_pairs={{0,1},{1,0},{2,3},{3,2},{4,5},{5,4},{6,7},{7,6},{8,9},{9,8},{10,11... | collective-permute-start | bytes 589832 | tf_op jit(solution)/shard_map/ppermute | solution.py:67
  8.6 2.6 %collective-permute-start.4 = (bf16[1,256,384]{2,1,0:T(8,128)(2,1)}, bf16[1,256,384]{2,1,0:T(8,128)(2,1)S(1)}, u32[]{:S(2)}, u32[]{:S(2)}) collective-permute-start(bf16[1,256,384]{2,1,0:T(8,128)(2,1)} %bitcast.74), channel_id=1, source_target_pairs={{0,4},{1,5},{2,6},{3,7},{4,0},{5,1},{6,2},{7,3},{8,12},{9,13},{10,... | collective-permute-start | bytes 589832 | tf_op jit(solution)/shard_map/ppermute | solution.py:67
  12.3 1.8 %collective-permute-done.refs_2_ = bf16[1,256,384]{2,1,0:T(8,128)(2,1)S(1)} collective-permute-done((bf16[1,256,384]{2,1,0:T(8,128)(2,1)}, bf16[1,256,384]{2,1,0:T(8,128)(2,1)S(1)}, u32[]{:S(2)}, u32[]{:S(2)}) %collective-permute-start) | collective-permute-done | bytes 196640 | tf_op jit(solution)/shard_map/ppermute | solution.py:67
  14.7 3.4 %pair_weights.1 = (bf16[1536,1024]{1,0:T(8,128)(2,1)S(1)}, bf16[1536,1024]{1,0:T(8,128)(2,1)S(1)}) custom-call(s32[7]{0:T(128)S(1)} %stack.33.refs_0_, bf16[1,272,384]{2,1,0:T(8,128)(2,1)S(1)} %collective-permute-done.5.refs_1_.refs_14_, bf16[3072,1024]{1,0:T(8,128)(2,1)} %bitcast.66, bf16[3072,1024]{1,0:T(8,128)(2,1)} %bitcast.68), custom_call_target="tpu_custom_call" | custom-call | bytes 3145728 | tf_op jit(solution)/shard_map/pair_weights/pallas_call | solution.py:291
  18.2 1.4 %collective-permute-done.4.refs_1_ = bf16[1,256,384]{2,1,0:T(8,128)(2,1)S(1)} collective-permute-done((bf16[1,256,384]{2,1,0:T(8,128)(2,1)}, bf16[1,256,384]{2,1,0:T(8,128)(2,1)S(1)}, u32[]{:S(2)}, u32[]{:S(2)}) %collective-permute-start.4) | collective-permute-done | bytes 196640 | tf_op jit(solution)/shard_map/ppermute | solution.py:67
  21.5 1.9 %collective-permute-start.6 = (bf16[2,128,384]{2,1,0:T(8,128)(2,1)S(1)}, bf16[2,128,384]{2,1,0:T(8,128)(2,1)S(1)}, u32[]{:S(2)}, u32[]{:S(2)}) collective-permute-start(bf16[2,128,384]{2,1,0:T(8,128)(2,1)S(1)} %pad_maximum_fusion), channel_id=1, source_target_pairs={{0,16},{1,17},{2,18},{3,19},{4,20},{5,21},{6,22},{7,23},{8,24},{9,... | collective-permute-start | bytes 589832 | tf_op jit(solution)/shard_map/ppermute | solution.py:67
  24.4 2.5 %collective-permute-done.10.refs_5_ = bf16[1,256,384]{2,1,0:T(8,128)(2,1)S(1)} collective-permute-done((bf16[1,256,384]{2,1,0:T(8,128)(2,1)S(1)}, bf16[1,256,384]{2,1,0:T(8,128)(2,1)S(1)}, u32[]{:S(2)}, u32[]{:S(2)}) %collective-permute-start.10) | collective-permute-done | bytes 196640 | tf_op jit(solution)/shard_map/ppermute | solution.py:67
  26.9 4.3 %first_part.2 = (f32[1,512,1024]{2,1,0:T(8,128)S(1)}, f32[1,512,1024]{2,1,0:T(8,128)S(1)}, bf16[1536,1024]{1,0:T(8,128)(2,1)S(1)}) custom-call(s32[7]{0:T(128)S(1)} %stack.33.refs_0_, bf16[1,272,384]{2,1,0:T(8,128)(2,1)S(1)} %maximum_bitcast_fusion.refs_1_.refs_14_, bf16[1,256,384]{2,1,0:T(8,128)(2,1)S(1)} %collective-permute-done.refs_2_, ...), custom_call_target="tpu_custom_call" | custom-call | flops 805306368 | bytes 3014656 | tf_op jit(solution)/shard_map/first_part/pallas_call | solution.py:309
  32.4 1.3 %collective-permute-start.15 = (bf16[1,256,384]{2,1,0:T(8,128)(2,1)S(1)}, bf16[1,256,384]{2,1,0:T(8,128)(2,1)S(1)}, u32[]{:S(2)}, u32[]{:S(2)}) collective-permute-start(bf16[1,256,384]{2,1,0:T(8,128)(2,1)S(1)} %collective-permute-done.10.refs_5_), channel_id=1, source_target_pairs={{0,16},{1,17},{2,18},{3,19},{4,20},{5,21},{6,22},{7,23},{8,24},{9,... | collective-permute-start | bytes 589832 | tf_op jit(solution)/shard_map/ppermute | solution.py:67
  35.5 4.4 %first_part.3 = (f32[1,512,1024]{2,1,0:T(8,128)S(1)}, f32[1,512,1024]{2,1,0:T(8,128)S(1)}, bf16[1536,1024]{1,0:T(8,128)(2,1)S(1)}) custom-call(s32[7]{0:T(128)S(1)} %stack.33.refs_0_, bf16[1,272,384]{2,1,0:T(8,128)(2,1)S(1)} %collective-permute-done.5.refs_1_.refs_14_, bf16[2,128,384]{2,1,0:T(8,128)(2,1)S(1)} %collective-permute-done.6.refs_2_, ...), custom_call_target="tpu_custom_call" | custom-call | flops 805306368 | bytes 3014656 | tf_op jit(solution)/shard_map/first_part/pallas_call | solution.py:309
  40.6 1.1 %collective-permute-start.22 = (bf16[2,128,384]{2,1,0:T(8,128)(2,1)S(1)}, bf16[2,128,384]{2,1,0:T(8,128)(2,1)S(1)}, u32[]{:S(2)}, u32[]{:S(2)}) collective-permute-start(bf16[2,128,384]{2,1,0:T(8,128)(2,1)S(1)} %pad_maximum_fusion.3), channel_id=1, source_target_pairs={{0,1},{1,0},{2,3},{3,2},{4,5},{5,4},{6,7},{7,6},{8,9},{9,8},{10,11... | collective-permute-start | bytes 589832 | tf_op jit(solution)/shard_map/ppermute | solution.py:67
  42.4 6.2 %second_part.2 = (bf16[2,2,256,384]{3,2,1,0:T(8,128)(2,1)S(1)}, bf16[2,2,256,384]{3,2,1,0:T(8,128)(2,1)S(1)}, bf16[512,1024]{1,0:T(8,128)(2,1)S(1)}, bf16[1024,1536]{1,0:T(8,128)(2,1)S(1)}) custom-call(s32[7]{0:T(128)S(1)} %stack.33.refs_0_, bf16[1,256,384]{2,1,0:T(8,128)(2,1)S(1)} %collective-permute-done.4.refs_1_, ...), custom_call_target="tpu_custom_call" | custom-call | flops 1610612736 | bytes 5373952 | tf_op jit(solution)/shard_map/second_part/pallas_call | solution.py:336
  49.7 2.4 %third_part.2 = (bf16[2,2,256,384]{3,2,1,0:T(8,128)(2,1)S(1)}, bf16[2,2,256,384]{3,2,1,0:T(8,128)(2,1)S(1)}) custom-call(s32[7]{0:T(128)S(1)} %stack.33.refs_0_, bf16[512,1024]{1,0:T(8,128)(2,1)S(1)} %get-tuple-element.104.refs_1_, bf16[1024,1536]{1,0:T(8,128)(2,1)S(1)} %get-tuple-element.105.refs_2_), custom_call_target="tpu_custom_call" | custom-call | flops 402653184 | bytes 1441792 | tf_op jit(solution)/shard_map/third_part/pallas_call | solution.py:363
  52.3 6.4 %second_part.3 = (bf16[2,2,256,384]{3,2,1,0:T(8,128)(2,1)S(1)}, bf16[2,2,256,384]{3,2,1,0:T(8,128)(2,1)S(1)}, bf16[512,1024]{1,0:T(8,128)(2,1)S(1)}) custom-call(s32[7]{0:T(128)S(1)} %stack.33.refs_0_, bf16[1,256,384]{2,1,0:T(8,128)(2,1)S(1)} %collective-permute-done.8.refs_1_, bf16[2,128,384]{2,1,0:T(8,128)(2,1)S(1)} %collective-permute-done.21.refs_2_, ...), custom_call_target="tpu_custom_call" | custom-call | flops 1610612736 | bytes 5373952 | tf_op jit(solution)/shard_map/second_part/pallas_call | solution.py:336
  59.2 2.4 %third_part.3 = (bf16[2,2,256,384]{3,2,1,0:T(8,128)(2,1)S(1)}, bf16[2,2,256,384]{3,2,1,0:T(8,128)(2,1)S(1)}) custom-call(s32[7]{0:T(128)S(1)} %stack.33.refs_0_, bf16[512,1024]{1,0:T(8,128)(2,1)S(1)} %get-tuple-element.128.refs_1_, bf16[1024,1536]{1,0:T(8,128)(2,1)S(1)} %get-tuple-element.105.refs_2_), custom_call_target="tpu_custom_call" | custom-call | flops 402653184 | bytes 1441792 | tf_op jit(solution)/shard_map/third_part/pallas_call | solution.py:363
  61.8 1.9 %collective-permute-start.33 = (bf16[2,1,256,384]{3,2,1,0:T(8,128)(2,1)S(1)}, bf16[2,1,256,384]{3,2,1,0:T(8,128)(2,1)S(1)}, u32[]{:S(2)}, u32[]{:S(2)}) collective-permute-start(bf16[2,1,256,384]{3,2,1,0:T(8,128)(2,1)S(1)} %add_convert_fusion.1), channel_id=1, source_target_pairs={{0,2},{1,3},{2,0},{3,1},{4,6},{5,7},{6,4},{7,5},{8,10},{9,11},{10,... | collective-permute-start | bytes 1179656 | tf_op jit(solution)/shard_map/ppermute | solution.py:67
  63.9 1.5 %collective-permute-start.39 = (bf16[2,128,384]{2,1,0:T(8,128)(2,1)S(1)}, bf16[2,128,384]{2,1,0:T(8,128)(2,1)S(1)}, u32[]{:S(2)}, u32[]{:S(2)}) collective-permute-start(bf16[2,128,384]{2,1,0:T(8,128)(2,1)S(1)} %get-tuple-element.146), channel_id=1, source_target_pairs={{0,16},{1,17},{2,18},{3,19},{4,20},{5,21},{6,22},{7,23},{8,24},{9,... | collective-permute-start | bytes 589832 | tf_op jit(solution)/shard_map/ppermute | solution.py:67
  66.6 4.3 %collective-permute-done.39 = bf16[2,128,384]{2,1,0:T(8,128)(2,1)S(1)} collective-permute-done((bf16[2,128,384]{2,1,0:T(8,128)(2,1)S(1)}, bf16[2,128,384]{2,1,0:T(8,128)(2,1)S(1)}, u32[]{:S(2)}, u32[]{:S(2)}) %collective-permute-start.39) | collective-permute-done | bytes 196640 | tf_op jit(solution)/shard_map/ppermute | solution.py:67
  70.9 1.1 %collective-permute-done.40 = bf16[2,128,384]{2,1,0:T(8,128)(2,1)S(1)} collective-permute-done((bf16[2,128,384]{2,1,0:T(8,128)(2,1)S(1)}, bf16[2,128,384]{2,1,0:T(8,128)(2,1)S(1)}, u32[]{:S(2)}, u32[]{:S(2)}) %collective-permute-start.40) | collective-permute-done | bytes 196640 | tf_op jit(solution)/shard_map/ppermute | solution.py:67
  73.1 1.1 %collective-permute-start.42 = (bf16[1,256,384]{2,1,0:T(8,128)(2,1)S(1)}, bf16[1,256,384]{2,1,0:T(8,128)(2,1)S(1)}, u32[]{:S(2)}, u32[]{:S(2)}) collective-permute-start(bf16[1,256,384]{2,1,0:T(8,128)(2,1)S(1)} %slice.215), channel_id=1, source_target_pairs={{0,1},{1,0},{2,3},{3,2},{4,5},{5,4},{6,7},{7,6},{8,9},{9,8},{10,11... | collective-permute-start | bytes 589832 | tf_op jit(solution)/shard_map/ppermute | solution.py:67
  74.2 3.9 %collective-permute-done.41 = bf16[1,256,384]{2,1,0:T(8,128)(2,1)S(1)} collective-permute-done((bf16[1,256,384]{2,1,0:T(8,128)(2,1)S(1)}, bf16[1,256,384]{2,1,0:T(8,128)(2,1)S(1)}, u32[]{:S(2)}, u32[]{:S(2)}) %collective-permute-start.41) | collective-permute-done | bytes 196640 | tf_op jit(solution)/shard_map/ppermute | solution.py:67
  79.4 1.5 %collective-permute-start.43 = (bf16[1,256,384]{2,1,0:T(8,128)(2,1)S(1)}, bf16[1,256,384]{2,1,0:T(8,128)(2,1)S(1)}, u32[]{:S(2)}, u32[]{:S(2)}) collective-permute-start(bf16[1,256,384]{2,1,0:T(8,128)(2,1)S(1)} %slice.197), channel_id=1, source_target_pairs={{0,16},{1,17},{2,18},{3,19},{4,20},{5,21},{6,22},{7,23},{8,24},{9,... | collective-permute-start | bytes 589832 | tf_op jit(solution)/shard_map/ppermute | solution.py:67
  80.9 1.1 %collective-permute-start.44 = (bf16[1,256,384]{2,1,0:T(8,128)(2,1)S(1)}, bf16[1,256,384]{2,1,0:T(8,128)(2,1)S(1)}, u32[]{:S(2)}, u32[]{:S(2)}) collective-permute-start(bf16[1,256,384]{2,1,0:T(8,128)(2,1)S(1)} %slice.198), channel_id=1, source_target_pairs={{0,1},{1,0},{2,3},{3,2},{4,5},{5,4},{6,7},{7,6},{8,9},{9,8},{10,11... | collective-permute-start | bytes 589832 | tf_op jit(solution)/shard_map/ppermute | solution.py:67
  82.3 1.4 %collective-permute-start.37 = (bf16[1,128,384]{2,1,0:T(8,128)(2,1)S(1)}, bf16[1,128,384]{2,1,0:T(8,128)(2,1)S(1)}, u32[]{:S(2)}, u32[]{:S(2)}) collective-permute-start(bf16[1,128,384]{2,1,0:T(8,128)(2,1)S(1)} %get-tuple-element.144), channel_id=1, source_target_pairs={{0,16},{1,17},{2,18},{3,19},{4,20},{5,21},{6,22},{7,23},{8,24},{9,... | collective-permute-start | bytes 294920 | tf_op jit(solution)/shard_map/ppermute | solution.py:67
  83.7 2.1 %collective-permute-done.43 = bf16[1,256,384]{2,1,0:T(8,128)(2,1)S(1)} collective-permute-done((bf16[1,256,384]{2,1,0:T(8,128)(2,1)S(1)}, bf16[1,256,384]{2,1,0:T(8,128)(2,1)S(1)}, u32[]{:S(2)}, u32[]{:S(2)}) %collective-permute-start.43) | collective-permute-done | bytes 196640 | tf_op jit(solution)/shard_map/ppermute | solution.py:67
  85.8 1.1 %collective-permute-start.38 = (bf16[1,128,384]{2,1,0:T(8,128)(2,1)S(1)}, bf16[1,128,384]{2,1,0:T(8,128)(2,1)S(1)}, u32[]{:S(2)}, u32[]{:S(2)}) collective-permute-start(bf16[1,128,384]{2,1,0:T(8,128)(2,1)S(1)} %get-tuple-element.143), channel_id=1, source_target_pairs={{0,1},{1,0},{2,3},{3,2},{4,5},{5,4},{6,7},{7,6},{8,9},{9,8},{10,11... | collective-permute-start | bytes 294920 | tf_op jit(solution)/shard_map/ppermute | solution.py:67
  87.8 2.7 %collective-permute-start.48 = (bf16[1,256,384]{2,1,0:T(8,128)(2,1)S(1)}, bf16[1,256,384]{2,1,0:T(8,128)(2,1)S(1)}, u32[]{:S(2)}, u32[]{:S(2)}) collective-permute-start(bf16[1,256,384]{2,1,0:T(8,128)(2,1)S(1)} %fusion.8), channel_id=1, source_target_pairs={{0,4},{1,5},{2,6},{3,7},{4,0},{5,1},{6,2},{7,3},{8,12},{9,13},{10,... | collective-permute-start | bytes 589832 | tf_op jit(solution)/shard_map/ppermute | solution.py:67
  90.6 1.4 %collective-permute-start.46 = (bf16[1,256,384]{2,1,0:T(8,128)(2,1)S(1)}, bf16[1,256,384]{2,1,0:T(8,128)(2,1)S(1)}, u32[]{:S(2)}, u32[]{:S(2)}) collective-permute-start(bf16[1,256,384]{2,1,0:T(8,128)(2,1)S(1)} %fusion.10), channel_id=1, source_target_pairs={{0,16},{1,17},{2,18},{3,19},{4,20},{5,21},{6,22},{7,23},{8,24},{9,... | collective-permute-start | bytes 589832 | tf_op jit(solution)/shard_map/ppermute | solution.py:67
  92.1 1.1 %collective-permute-start.47 = (bf16[1,256,384]{2,1,0:T(8,128)(2,1)S(1)}, bf16[1,256,384]{2,1,0:T(8,128)(2,1)S(1)}, u32[]{:S(2)}, u32[]{:S(2)}) collective-permute-start(bf16[1,256,384]{2,1,0:T(8,128)(2,1)S(1)} %fusion.9), channel_id=1, source_target_pairs={{0,1},{1,0},{2,3},{3,2},{4,5},{5,4},{6,7},{7,6},{8,9},{9,8},{10,11... | collective-permute-start | bytes 589832 | tf_op jit(solution)/shard_map/ppermute | solution.py:67
  93.2 4.7 %collective-permute-done.48 = bf16[1,256,384]{2,1,0:T(8,128)(2,1)S(1)} collective-permute-done((bf16[1,256,384]{2,1,0:T(8,128)(2,1)S(1)}, bf16[1,256,384]{2,1,0:T(8,128)(2,1)S(1)}, u32[]{:S(2)}, u32[]{:S(2)}) %collective-permute-start.48) | collective-permute-done | bytes 196640 | tf_op jit(solution)/shard_map/ppermute | solution.py:67
  (108 shorter events, 19.3 us)
Async XLA Ops:
  0.0 11.2 %collective-permute-start.1 = (bf16[1,256,384]{2,1,0:T(8,128)(2,1)}, bf16[1,256,384]{2,1,0:T(8,128)(2,1)S(1)}, u32[]{:S(2)}, u32[]{:S(2)}) collective-permute-start(bf16[1,256,384]{2,1,0:T(8,128)(2,1)} %bitcast.72), channel_id=1, source_target_pairs={{0,2},{1,3},{2,0},{3,1},{4,6},{5,7},{6,4},{7,5},{8,10},{9,11},{10,... | collective-permute-start | bytes 589832 | tf_op jit(solution)/shard_map/ppermute | solution.py:67
  5.5 8.7 %collective-permute-start.5 = (bf16[1,272,384]{2,1,0:T(8,128)(2,1)S(1)}, bf16[1,272,384]{2,1,0:T(8,128)(2,1)S(1)}, u32[]{:S(2)}, u32[]{:S(2)}) collective-permute-start(bf16[1,272,384]{2,1,0:T(8,128)(2,1)S(1)} %maximum_bitcast_fusion.refs_1_.refs_14_), channel_id=1, source_target_pairs={{0,16},{1,17},{2,18},{3,19},{4,20},{5,21},{6,22},{7,23},{8,24},{9,... | collective-permute-start | bytes 626696 | tf_op jit(solution)/shard_map/ppermute | solution.py:67
  7.0 7.1 %collective-permute-start = (bf16[1,256,384]{2,1,0:T(8,128)(2,1)}, bf16[1,256,384]{2,1,0:T(8,128)(2,1)S(1)}, u32[]{:S(2)}, u32[]{:S(2)}) collective-permute-start(bf16[1,256,384]{2,1,0:T(8,128)(2,1)} %bitcast.73), channel_id=1, source_target_pairs={{0,1},{1,0},{2,3},{3,2},{4,5},{5,4},{6,7},{7,6},{8,9},{9,8},{10,11... | collective-permute-start | bytes 589832 | tf_op jit(solution)/shard_map/ppermute | solution.py:67
  8.6 11.0 %collective-permute-start.4 = (bf16[1,256,384]{2,1,0:T(8,128)(2,1)}, bf16[1,256,384]{2,1,0:T(8,128)(2,1)S(1)}, u32[]{:S(2)}, u32[]{:S(2)}) collective-permute-start(bf16[1,256,384]{2,1,0:T(8,128)(2,1)} %bitcast.74), channel_id=1, source_target_pairs={{0,4},{1,5},{2,6},{3,7},{4,0},{5,1},{6,2},{7,3},{8,12},{9,13},{10,... | collective-permute-start | bytes 589832 | tf_op jit(solution)/shard_map/ppermute | solution.py:67
  11.2 8.5 %collective-permute-start.2 = (bf16[1,256,384]{2,1,0:T(8,128)(2,1)S(1)}, bf16[1,256,384]{2,1,0:T(8,128)(2,1)S(1)}, u32[]{:S(2)}, u32[]{:S(2)}) collective-permute-start(bf16[1,256,384]{2,1,0:T(8,128)(2,1)S(1)} %collective-permute-done.1.refs_5_), channel_id=1, source_target_pairs={{0,16},{1,17},{2,18},{3,19},{4,20},{5,21},{6,22},{7,23},{8,24},{9,... | collective-permute-start | bytes 589832 | tf_op jit(solution)/shard_map/ppermute | solution.py:67
  11.7 7.9 %collective-permute-start.3 = (bf16[1,256,384]{2,1,0:T(8,128)(2,1)S(1)}, bf16[1,256,384]{2,1,0:T(8,128)(2,1)S(1)}, u32[]{:S(2)}, u32[]{:S(2)}) collective-permute-start(bf16[1,256,384]{2,1,0:T(8,128)(2,1)S(1)} %collective-permute-done.1.refs_5_), channel_id=1, source_target_pairs={{0,1},{1,0},{2,3},{3,2},{4,5},{5,4},{6,7},{7,6},{8,9},{9,8},{10,11... | collective-permute-start | bytes 589832 | tf_op jit(solution)/shard_map/ppermute | solution.py:67
  14.1 6.8 %collective-permute-start.12 = (bf16[1,256,384]{2,1,0:T(8,128)(2,1)S(1)}, bf16[1,256,384]{2,1,0:T(8,128)(2,1)S(1)}, u32[]{:S(2)}, u32[]{:S(2)}) collective-permute-start(bf16[1,256,384]{2,1,0:T(8,128)(2,1)S(1)} %collective-permute-done.refs_2_), channel_id=1, source_target_pairs={{0,8},{1,9},{2,10},{3,11},{4,12},{5,13},{6,14},{7,15},{8,0},{9,1},... | collective-permute-start | bytes 589832 | tf_op jit(solution)/shard_map/ppermute | solution.py:67
  19.6 7.3 %collective-permute-start.10 = (bf16[1,256,384]{2,1,0:T(8,128)(2,1)S(1)}, bf16[1,256,384]{2,1,0:T(8,128)(2,1)S(1)}, u32[]{:S(2)}, u32[]{:S(2)}) collective-permute-start(bf16[1,256,384]{2,1,0:T(8,128)(2,1)S(1)} %collective-permute-done.4.refs_1_), channel_id=1, source_target_pairs={{0,2},{1,3},{2,0},{3,1},{4,6},{5,7},{6,4},{7,5},{8,10},{9,11},{10,... | collective-permute-start | bytes 589832 | tf_op jit(solution)/shard_map/ppermute | solution.py:67
  20.3 11.6 %collective-permute-start.8 = (bf16[1,256,384]{2,1,0:T(8,128)(2,1)S(1)}, bf16[1,256,384]{2,1,0:T(8,128)(2,1)S(1)}, u32[]{:S(2)}, u32[]{:S(2)}) collective-permute-start(bf16[1,256,384]{2,1,0:T(8,128)(2,1)S(1)} %collective-permute-done.4.refs_1_), channel_id=1, source_target_pairs={{0,16},{1,17},{2,18},{3,19},{4,20},{5,21},{6,22},{7,23},{8,24},{9,... | collective-permute-start | bytes 589832 | tf_op jit(solution)/shard_map/ppermute | solution.py:67
  21.0 10.3 %collective-permute-start.7 = (bf16[2,128,384]{2,1,0:T(8,128)(2,1)S(1)}, bf16[2,128,384]{2,1,0:T(8,128)(2,1)S(1)}, u32[]{:S(2)}, u32[]{:S(2)}) collective-permute-start(bf16[2,128,384]{2,1,0:T(8,128)(2,1)S(1)} %pad_maximum_fusion.1), channel_id=1, source_target_pairs={{0,1},{1,0},{2,3},{3,2},{4,5},{5,4},{6,7},{7,6},{8,9},{9,8},{10,11... | collective-permute-start | bytes 589832 | tf_op jit(solution)/shard_map/ppermute | solution.py:67
  21.5 10.4 %collective-permute-start.6 = (bf16[2,128,384]{2,1,0:T(8,128)(2,1)S(1)}, bf16[2,128,384]{2,1,0:T(8,128)(2,1)S(1)}, u32[]{:S(2)}, u32[]{:S(2)}) collective-permute-start(bf16[2,128,384]{2,1,0:T(8,128)(2,1)S(1)} %pad_maximum_fusion), channel_id=1, source_target_pairs={{0,16},{1,17},{2,18},{3,19},{4,20},{5,21},{6,22},{7,23},{8,24},{9,... | collective-permute-start | bytes 589832 | tf_op jit(solution)/shard_map/ppermute | solution.py:67
  23.4 8.4 %collective-permute-start.9 = (bf16[1,256,384]{2,1,0:T(8,128)(2,1)S(1)}, bf16[1,256,384]{2,1,0:T(8,128)(2,1)S(1)}, u32[]{:S(2)}, u32[]{:S(2)}) collective-permute-start(bf16[1,256,384]{2,1,0:T(8,128)(2,1)S(1)} %collective-permute-done.4.refs_1_), channel_id=1, source_target_pairs={{0,1},{1,0},{2,3},{3,2},{4,5},{5,4},{6,7},{7,6},{8,9},{9,8},{10,11... | collective-permute-start | bytes 589832 | tf_op jit(solution)/shard_map/ppermute | solution.py:67
  26.9 6.8 %collective-permute-start.17 = (bf16[1,272,384]{2,1,0:T(8,128)(2,1)S(1)}, bf16[1,272,384]{2,1,0:T(8,128)(2,1)S(1)}, u32[]{:S(2)}, u32[]{:S(2)}) collective-permute-start(bf16[1,272,384]{2,1,0:T(8,128)(2,1)S(1)} %collective-permute-done.5.refs_1_.refs_14_), channel_id=1, source_target_pairs={{0,8},{1,9},{2,10},{3,11},{4,12},{5,13},{6,14},{7,15},{8,0},{9,1},... | collective-permute-start | bytes 626696 | tf_op jit(solution)/shard_map/ppermute | solution.py:67
  32.4 7.4 %collective-permute-start.15 = (bf16[1,256,384]{2,1,0:T(8,128)(2,1)S(1)}, bf16[1,256,384]{2,1,0:T(8,128)(2,1)S(1)}, u32[]{:S(2)}, u32[]{:S(2)}) collective-permute-start(bf16[1,256,384]{2,1,0:T(8,128)(2,1)S(1)} %collective-permute-done.10.refs_5_), channel_id=1, source_target_pairs={{0,16},{1,17},{2,18},{3,19},{4,20},{5,21},{6,22},{7,23},{8,24},{9,... | collective-permute-start | bytes 589832 | tf_op jit(solution)/shard_map/ppermute | solution.py:67
  33.7 6.6 %collective-permute-start.16 = (bf16[1,256,384]{2,1,0:T(8,128)(2,1)S(1)}, bf16[1,256,384]{2,1,0:T(8,128)(2,1)S(1)}, u32[]{:S(2)}, u32[]{:S(2)}) collective-permute-start(bf16[1,256,384]{2,1,0:T(8,128)(2,1)S(1)} %collective-permute-done.10.refs_5_), channel_id=1, source_target_pairs={{0,1},{1,0},{2,3},{3,2},{4,5},{5,4},{6,7},{7,6},{8,9},{9,8},{10,11... | collective-permute-start | bytes 589832 | tf_op jit(solution)/shard_map/ppermute | solution.py:67
  34.9 6.7 %collective-permute-start.26 = (bf16[1,256,384]{2,1,0:T(8,128)(2,1)S(1)}, bf16[1,256,384]{2,1,0:T(8,128)(2,1)S(1)}, u32[]{:S(2)}, u32[]{:S(2)}) collective-permute-start(bf16[1,256,384]{2,1,0:T(8,128)(2,1)S(1)} %collective-permute-done.9.refs_2_), channel_id=1, source_target_pairs={{0,8},{1,9},{2,10},{3,11},{4,12},{5,13},{6,14},{7,15},{8,0},{9,1},... | collective-permute-start | bytes 589832 | tf_op jit(solution)/shard_map/ppermute | solution.py:67
  35.4 7.0 %collective-permute-start.27 = (bf16[1,256,384]{2,1,0:T(8,128)(2,1)S(1)}, bf16[1,256,384]{2,1,0:T(8,128)(2,1)S(1)}, u32[]{:S(2)}, u32[]{:S(2)}) collective-permute-start(bf16[1,256,384]{2,1,0:T(8,128)(2,1)S(1)} %collective-permute-done.10.refs_5_), channel_id=1, source_target_pairs={{0,8},{1,9},{2,10},{3,11},{4,12},{5,13},{6,14},{7,15},{8,0},{9,1},... | collective-permute-start | bytes 589832 | tf_op jit(solution)/shard_map/ppermute | solution.py:67
  39.9 8.7 %collective-permute-start.23 = (bf16[1,256,384]{2,1,0:T(8,128)(2,1)S(1)}, bf16[1,256,384]{2,1,0:T(8,128)(2,1)S(1)}, u32[]{:S(2)}, u32[]{:S(2)}) collective-permute-start(bf16[1,256,384]{2,1,0:T(8,128)(2,1)S(1)} %collective-permute-done.8.refs_1_), channel_id=1, source_target_pairs={{0,8},{1,9},{2,10},{3,11},{4,12},{5,13},{6,14},{7,15},{8,0},{9,1},... | collective-permute-start | bytes 589832 | tf_op jit(solution)/shard_map/ppermute | solution.py:67
  40.6 8.1 %collective-permute-start.22 = (bf16[2,128,384]{2,1,0:T(8,128)(2,1)S(1)}, bf16[2,128,384]{2,1,0:T(8,128)(2,1)S(1)}, u32[]{:S(2)}, u32[]{:S(2)}) collective-permute-start(bf16[2,128,384]{2,1,0:T(8,128)(2,1)S(1)} %pad_maximum_fusion.3), channel_id=1, source_target_pairs={{0,1},{1,0},{2,3},{3,2},{4,5},{5,4},{6,7},{7,6},{8,9},{9,8},{10,11... | collective-permute-start | bytes 589832 | tf_op jit(solution)/shard_map/ppermute | solution.py:67
  41.6 7.0 %collective-permute-start.21 = (bf16[2,128,384]{2,1,0:T(8,128)(2,1)S(1)}, bf16[2,128,384]{2,1,0:T(8,128)(2,1)S(1)}, u32[]{:S(2)}, u32[]{:S(2)}) collective-permute-start(bf16[2,128,384]{2,1,0:T(8,128)(2,1)S(1)} %pad_maximum_fusion.2), channel_id=1, source_target_pairs={{0,16},{1,17},{2,18},{3,19},{4,20},{5,21},{6,22},{7,23},{8,24},{9,... | collective-permute-start | bytes 589832 | tf_op jit(solution)/shard_map/ppermute | solution.py:67
  49.3 9.4 %collective-permute-start.29 = (bf16[2,2,256,384]{3,2,1,0:T(8,128)(2,1)S(1)}, bf16[2,2,256,384]{3,2,1,0:T(8,128)(2,1)S(1)}, u32[]{:S(2)}, u32[]{:S(2)}) collective-permute-start(bf16[2,2,256,384]{3,2,1,0:T(8,128)(2,1)S(1)} %get-tuple-element.101), channel_id=1, source_target_pairs={{0,8},{1,9},{2,10},{3,11},{4,12},{5,13},{6,14},{7,15},{8,0},{9,1},... | collective-permute-start | bytes 2359304 | tf_op jit(solution)/shard_map/ppermute | solution.py:67
  52.1 6.6 %collective-permute-start.32 = (bf16[2,2,256,384]{3,2,1,0:T(8,128)(2,1)S(1)}, bf16[2,2,256,384]{3,2,1,0:T(8,128)(2,1)S(1)}, u32[]{:S(2)}, u32[]{:S(2)}) collective-permute-start(bf16[2,2,256,384]{3,2,1,0:T(8,128)(2,1)S(1)} %get-tuple-element.109), channel_id=1, source_target_pairs={{0,8},{1,9},{2,10},{3,11},{4,12},{5,13},{6,14},{7,15},{8,0},{9,1},... | collective-permute-start | bytes 2359304 | tf_op jit(solution)/shard_map/ppermute | solution.py:67
  61.8 30.2 %collective-permute-start.33 = (bf16[2,1,256,384]{3,2,1,0:T(8,128)(2,1)S(1)}, bf16[2,1,256,384]{3,2,1,0:T(8,128)(2,1)S(1)}, u32[]{:S(2)}, u32[]{:S(2)}) collective-permute-start(bf16[2,1,256,384]{3,2,1,0:T(8,128)(2,1)S(1)} %add_convert_fusion.1), channel_id=1, source_target_pairs={{0,2},{1,3},{2,0},{3,1},{4,6},{5,7},{6,4},{7,5},{8,10},{9,11},{10,... | collective-permute-start | bytes 1179656 | tf_op jit(solution)/shard_map/ppermute | solution.py:67
  63.9 7.0 %collective-permute-start.39 = (bf16[2,128,384]{2,1,0:T(8,128)(2,1)S(1)}, bf16[2,128,384]{2,1,0:T(8,128)(2,1)S(1)}, u32[]{:S(2)}, u32[]{:S(2)}) collective-permute-start(bf16[2,128,384]{2,1,0:T(8,128)(2,1)S(1)} %get-tuple-element.146), channel_id=1, source_target_pairs={{0,16},{1,17},{2,18},{3,19},{4,20},{5,21},{6,22},{7,23},{8,24},{9,... | collective-permute-start | bytes 589832 | tf_op jit(solution)/shard_map/ppermute | solution.py:67
  65.3 6.7 %collective-permute-start.40 = (bf16[2,128,384]{2,1,0:T(8,128)(2,1)S(1)}, bf16[2,128,384]{2,1,0:T(8,128)(2,1)S(1)}, u32[]{:S(2)}, u32[]{:S(2)}) collective-permute-start(bf16[2,128,384]{2,1,0:T(8,128)(2,1)S(1)} %get-tuple-element.145), channel_id=1, source_target_pairs={{0,1},{1,0},{2,3},{3,2},{4,5},{5,4},{6,7},{7,6},{8,9},{9,8},{10,11... | collective-permute-start | bytes 589832 | tf_op jit(solution)/shard_map/ppermute | solution.py:67
  66.5 15.7 %collective-permute-start.36 = (bf16[2,1,256,384]{3,2,1,0:T(8,128)(2,1)S(1)}, bf16[2,1,256,384]{3,2,1,0:T(8,128)(2,1)S(1)}, u32[]{:S(2)}, u32[]{:S(2)}) collective-permute-start(bf16[2,1,256,384]{3,2,1,0:T(8,128)(2,1)S(1)} %add_convert_fusion), channel_id=1, source_target_pairs={{0,2},{1,3},{2,0},{3,1},{4,6},{5,7},{6,4},{7,5},{8,10},{9,11},{10,... | collective-permute-start | bytes 1179656 | tf_op jit(solution)/shard_map/ppermute | solution.py:67
  78.9 8.9 %collective-permute-start.45 = (bf16[1,256,384]{2,1,0:T(8,128)(2,1)S(1)}, bf16[1,256,384]{2,1,0:T(8,128)(2,1)S(1)}, u32[]{:S(2)}, u32[]{:S(2)}) collective-permute-start(bf16[1,256,384]{2,1,0:T(8,128)(2,1)S(1)} %fusion.4), channel_id=1, source_target_pairs={{0,2},{1,3},{2,0},{3,1},{4,6},{5,7},{6,4},{7,5},{8,10},{9,11},{10,... | collective-permute-start | bytes 589832 | tf_op jit(solution)/shard_map/ppermute | solution.py:67
  79.4 6.4 %collective-permute-start.43 = (bf16[1,256,384]{2,1,0:T(8,128)(2,1)S(1)}, bf16[1,256,384]{2,1,0:T(8,128)(2,1)S(1)}, u32[]{:S(2)}, u32[]{:S(2)}) collective-permute-start(bf16[1,256,384]{2,1,0:T(8,128)(2,1)S(1)} %slice.197), channel_id=1, source_target_pairs={{0,16},{1,17},{2,18},{3,19},{4,20},{5,21},{6,22},{7,23},{8,24},{9,... | collective-permute-start | bytes 589832 | tf_op jit(solution)/shard_map/ppermute | solution.py:67
  80.9 6.8 %collective-permute-start.44 = (bf16[1,256,384]{2,1,0:T(8,128)(2,1)S(1)}, bf16[1,256,384]{2,1,0:T(8,128)(2,1)S(1)}, u32[]{:S(2)}, u32[]{:S(2)}) collective-permute-start(bf16[1,256,384]{2,1,0:T(8,128)(2,1)S(1)} %slice.198), channel_id=1, source_target_pairs={{0,1},{1,0},{2,3},{3,2},{4,5},{5,4},{6,7},{7,6},{8,9},{9,8},{10,11... | collective-permute-start | bytes 589832 | tf_op jit(solution)/shard_map/ppermute | solution.py:67
  82.3 8.2 %collective-permute-start.37 = (bf16[1,128,384]{2,1,0:T(8,128)(2,1)S(1)}, bf16[1,128,384]{2,1,0:T(8,128)(2,1)S(1)}, u32[]{:S(2)}, u32[]{:S(2)}) collective-permute-start(bf16[1,128,384]{2,1,0:T(8,128)(2,1)S(1)} %get-tuple-element.144), channel_id=1, source_target_pairs={{0,16},{1,17},{2,18},{3,19},{4,20},{5,21},{6,22},{7,23},{8,24},{9,... | collective-permute-start | bytes 294920 | tf_op jit(solution)/shard_map/ppermute | solution.py:67
  87.8 10.1 %collective-permute-start.48 = (bf16[1,256,384]{2,1,0:T(8,128)(2,1)S(1)}, bf16[1,256,384]{2,1,0:T(8,128)(2,1)S(1)}, u32[]{:S(2)}, u32[]{:S(2)}) collective-permute-start(bf16[1,256,384]{2,1,0:T(8,128)(2,1)S(1)} %fusion.8), channel_id=1, source_target_pairs={{0,4},{1,5},{2,6},{3,7},{4,0},{5,1},{6,2},{7,3},{8,12},{9,13},{10,... | collective-permute-start | bytes 589832 | tf_op jit(solution)/shard_map/ppermute | solution.py:67
  90.6 7.3 %collective-permute-start.46 = (bf16[1,256,384]{2,1,0:T(8,128)(2,1)S(1)}, bf16[1,256,384]{2,1,0:T(8,128)(2,1)S(1)}, u32[]{:S(2)}, u32[]{:S(2)}) collective-permute-start(bf16[1,256,384]{2,1,0:T(8,128)(2,1)S(1)} %fusion.10), channel_id=1, source_target_pairs={{0,16},{1,17},{2,18},{3,19},{4,20},{5,21},{6,22},{7,23},{8,24},{9,... | collective-permute-start | bytes 589832 | tf_op jit(solution)/shard_map/ppermute | solution.py:67
  (17 other events, 72.0 us)

commit v11 on v10

--- a/solution.py
+++ b/solution.py
@@ -247,8 +247,9 @@
     for t in range(gate.shape[0]):
         span = slice(t * HIDDEN_TILE, (t + 1) * HIDDEN_TILE)
         g = gate[t] + jnp.dot(rows[...], w_gate[:, span], preferred_element_type=jnp.float32)
+        gated = (g + g * jnp.tanh(0.5 * g)) * share
         u = up[t] + jnp.dot(rows[...], w_up[:, span], preferred_element_type=jnp.float32)
-        value = (g + g * jnp.tanh(0.5 * g)) * u * share
+        value = gated * u
         hidden[:, span] = value.astype(jnp.bfloat16)
     downs_in[0].wait()
     down_products(place, pairs[0], hidden, tile, results)

time: 98.9 us -> 98.9 us (level)
  no operation moved by 1% of the time
where the time goes in v11:
time: 98.9 us; the launch traced here: 98.7 us
  starting transfers between devices  40.5 us (41%)
  Pallas kernels  29.5 us (30%)
  waiting for transfers between devices  23.6 us (24%)
  other arithmetic  4.49 us (5%)
    ppermute x49, starting transfers between devices, send(): return lax.ppermute(value, BOTH, pairs)  40.5 us
    ppermute x49, waiting for transfers between devices, send(): return lax.ppermute(value, BOTH, pairs)  23.6 us
    pallas_call x2, Pallas kernels, second_part(): pl.pallas_call(lambda *refs: second_kernel(*refs, x=x, found=found, z_pla...  12.6 us
    pallas_call x2, Pallas kernels, first_part(): pl.pallas_call(lambda *refs: first_kernel(*refs, found=found, z_places=z_...  8.73 us
    pallas_call x2, Pallas kernels, third_part(): pl.pallas_call(lambda *refs: third_kernel(*refs, pair=pair), in_specs=[SC...  4.73 us
    pallas_call x1, Pallas kernels, pair_weights(): pl.pallas_call(lambda *refs: weights_kernel(*refs, z=z), in_specs=[SCALAR...  3.41 us
  transfers between devices with their start and end apart: 49, of which 11 were waited for; matrix products, arithmetic and copies ran while one was open for 4% of the time, Pallas kernels for 30%

profile of v11, /device:TPU:0, one launch (start us, length us, event | category | flops | bytes accessed | tf_op | source)
XLA Modules:
  0.0 98.7 jit_solution(1550388666564458363)
XLA Ops:
  0.0 3.0 %collective-permute-start.1 = (bf16[1,256,384]{2,1,0:T(8,128)(2,1)}, bf16[1,256,384]{2,1,0:T(8,128)(2,1)S(1)}, u32[]{:S(2)}, u32[]{:S(2)}) collective-permute-start(bf16[1,256,384]{2,1,0:T(8,128)(2,1)} %bitcast.72), channel_id=1, source_target_pairs={{0,2},{1,3},{2,0},{3,1},{4,6},{5,7},{6,4},{7,5},{8,10},{9,11},{10,... | collective-permute-start | bytes 589832 | tf_op jit(solution)/shard_map/ppermute | solution.py:67
  5.5 1.6 %collective-permute-start.5 = (bf16[1,272,384]{2,1,0:T(8,128)(2,1)S(1)}, bf16[1,272,384]{2,1,0:T(8,128)(2,1)S(1)}, u32[]{:S(2)}, u32[]{:S(2)}) collective-permute-start(bf16[1,272,384]{2,1,0:T(8,128)(2,1)S(1)} %maximum_bitcast_fusion.refs_1_.refs_14_), channel_id=1, source_target_pairs={{0,16},{1,17},{2,18},{3,19},{4,20},{5,21},{6,22},{7,23},{8,24},{9,... | collective-permute-start | bytes 626696 | tf_op jit(solution)/shard_map/ppermute | solution.py:67
  7.0 1.5 %collective-permute-start = (bf16[1,256,384]{2,1,0:T(8,128)(2,1)}, bf16[1,256,384]{2,1,0:T(8,128)(2,1)S(1)}, u32[]{:S(2)}, u32[]{:S(2)}) collective-permute-start(bf16[1,256,384]{2,1,0:T(8,128)(2,1)} %bitcast.73), channel_id=1, source_target_pairs={{0,1},{1,0},{2,3},{3,2},{4,5},{5,4},{6,7},{7,6},{8,9},{9,8},{10,11... | collective-permute-start | bytes 589832 | tf_op jit(solution)/shard_map/ppermute | solution.py:67
  8.6 2.6 %collective-permute-start.4 = (bf16[1,256,384]{2,1,0:T(8,128)(2,1)}, bf16[1,256,384]{2,1,0:T(8,128)(2,1)S(1)}, u32[]{:S(2)}, u32[]{:S(2)}) collective-permute-start(bf16[1,256,384]{2,1,0:T(8,128)(2,1)} %bitcast.74), channel_id=1, source_target_pairs={{0,4},{1,5},{2,6},{3,7},{4,0},{5,1},{6,2},{7,3},{8,12},{9,13},{10,... | collective-permute-start | bytes 589832 | tf_op jit(solution)/shard_map/ppermute | solution.py:67
  12.3 1.8 %collective-permute-done.refs_2_ = bf16[1,256,384]{2,1,0:T(8,128)(2,1)S(1)} collective-permute-done((bf16[1,256,384]{2,1,0:T(8,128)(2,1)}, bf16[1,256,384]{2,1,0:T(8,128)(2,1)S(1)}, u32[]{:S(2)}, u32[]{:S(2)}) %collective-permute-start) | collective-permute-done | bytes 196640 | tf_op jit(solution)/shard_map/ppermute | solution.py:67
  14.7 3.4 %pair_weights.1 = (bf16[1536,1024]{1,0:T(8,128)(2,1)S(1)}, bf16[1536,1024]{1,0:T(8,128)(2,1)S(1)}) custom-call(s32[7]{0:T(128)S(1)} %stack.33.refs_0_, bf16[1,272,384]{2,1,0:T(8,128)(2,1)S(1)} %collective-permute-done.5.refs_1_.refs_14_, bf16[3072,1024]{1,0:T(8,128)(2,1)} %bitcast.66, bf16[3072,1024]{1,0:T(8,128)(2,1)} %bitcast.68), custom_call_target="tpu_custom_call" | custom-call | bytes 3145728 | tf_op jit(solution)/shard_map/pair_weights/pallas_call | solution.py:292
  18.2 1.4 %collective-permute-done.4.refs_1_ = bf16[1,256,384]{2,1,0:T(8,128)(2,1)S(1)} collective-permute-done((bf16[1,256,384]{2,1,0:T(8,128)(2,1)}, bf16[1,256,384]{2,1,0:T(8,128)(2,1)S(1)}, u32[]{:S(2)}, u32[]{:S(2)}) %collective-permute-start.4) | collective-permute-done | bytes 196640 | tf_op jit(solution)/shard_map/ppermute | solution.py:67
  21.5 1.9 %collective-permute-start.6 = (bf16[2,128,384]{2,1,0:T(8,128)(2,1)S(1)}, bf16[2,128,384]{2,1,0:T(8,128)(2,1)S(1)}, u32[]{:S(2)}, u32[]{:S(2)}) collective-permute-start(bf16[2,128,384]{2,1,0:T(8,128)(2,1)S(1)} %pad_maximum_fusion), channel_id=1, source_target_pairs={{0,16},{1,17},{2,18},{3,19},{4,20},{5,21},{6,22},{7,23},{8,24},{9,... | collective-permute-start | bytes 589832 | tf_op jit(solution)/shard_map/ppermute | solution.py:67
  24.4 2.5 %collective-permute-done.10.refs_5_ = bf16[1,256,384]{2,1,0:T(8,128)(2,1)S(1)} collective-permute-done((bf16[1,256,384]{2,1,0:T(8,128)(2,1)S(1)}, bf16[1,256,384]{2,1,0:T(8,128)(2,1)S(1)}, u32[]{:S(2)}, u32[]{:S(2)}) %collective-permute-start.10) | collective-permute-done | bytes 196640 | tf_op jit(solution)/shard_map/ppermute | solution.py:67
  26.9 4.3 %first_part.2 = (f32[1,512,1024]{2,1,0:T(8,128)S(1)}, f32[1,512,1024]{2,1,0:T(8,128)S(1)}, bf16[1536,1024]{1,0:T(8,128)(2,1)S(1)}) custom-call(s32[7]{0:T(128)S(1)} %stack.33.refs_0_, bf16[1,272,384]{2,1,0:T(8,128)(2,1)S(1)} %maximum_bitcast_fusion.refs_1_.refs_14_, bf16[1,256,384]{2,1,0:T(8,128)(2,1)S(1)} %collective-permute-done.refs_2_, ...), custom_call_target="tpu_custom_call" | custom-call | flops 805306368 | bytes 3014656 | tf_op jit(solution)/shard_map/first_part/pallas_call | solution.py:310
  32.4 1.3 %collective-permute-start.15 = (bf16[1,256,384]{2,1,0:T(8,128)(2,1)S(1)}, bf16[1,256,384]{2,1,0:T(8,128)(2,1)S(1)}, u32[]{:S(2)}, u32[]{:S(2)}) collective-permute-start(bf16[1,256,384]{2,1,0:T(8,128)(2,1)S(1)} %collective-permute-done.10.refs_5_), channel_id=1, source_target_pairs={{0,16},{1,17},{2,18},{3,19},{4,20},{5,21},{6,22},{7,23},{8,24},{9,... | collective-permute-start | bytes 589832 | tf_op jit(solution)/shard_map/ppermute | solution.py:67
  35.5 4.4 %first_part.3 = (f32[1,512,1024]{2,1,0:T(8,128)S(1)}, f32[1,512,1024]{2,1,0:T(8,128)S(1)}, bf16[1536,1024]{1,0:T(8,128)(2,1)S(1)}) custom-call(s32[7]{0:T(128)S(1)} %stack.33.refs_0_, bf16[1,272,384]{2,1,0:T(8,128)(2,1)S(1)} %collective-permute-done.5.refs_1_.refs_14_, bf16[2,128,384]{2,1,0:T(8,128)(2,1)S(1)} %collective-permute-done.6.refs_2_, ...), custom_call_target="tpu_custom_call" | custom-call | flops 805306368 | bytes 3014656 | tf_op jit(solution)/shard_map/first_part/pallas_call | solution.py:310
  40.6 1.1 %collective-permute-start.22 = (bf16[2,128,384]{2,1,0:T(8,128)(2,1)S(1)}, bf16[2,128,384]{2,1,0:T(8,128)(2,1)S(1)}, u32[]{:S(2)}, u32[]{:S(2)}) collective-permute-start(bf16[2,128,384]{2,1,0:T(8,128)(2,1)S(1)} %pad_maximum_fusion.3), channel_id=1, source_target_pairs={{0,1},{1,0},{2,3},{3,2},{4,5},{5,4},{6,7},{7,6},{8,9},{9,8},{10,11... | collective-permute-start | bytes 589832 | tf_op jit(solution)/shard_map/ppermute | solution.py:67
  42.4 6.2 %second_part.2 = (bf16[2,2,256,384]{3,2,1,0:T(8,128)(2,1)S(1)}, bf16[2,2,256,384]{3,2,1,0:T(8,128)(2,1)S(1)}, bf16[512,1024]{1,0:T(8,128)(2,1)S(1)}, bf16[1024,1536]{1,0:T(8,128)(2,1)S(1)}) custom-call(s32[7]{0:T(128)S(1)} %stack.33.refs_0_, bf16[1,256,384]{2,1,0:T(8,128)(2,1)S(1)} %collective-permute-done.4.refs_1_, ...), custom_call_target="tpu_custom_call" | custom-call | flops 1610612736 | bytes 5373952 | tf_op jit(solution)/shard_map/second_part/pallas_call | solution.py:337
  49.7 2.4 %third_part.2 = (bf16[2,2,256,384]{3,2,1,0:T(8,128)(2,1)S(1)}, bf16[2,2,256,384]{3,2,1,0:T(8,128)(2,1)S(1)}) custom-call(s32[7]{0:T(128)S(1)} %stack.33.refs_0_, bf16[512,1024]{1,0:T(8,128)(2,1)S(1)} %get-tuple-element.104.refs_1_, bf16[1024,1536]{1,0:T(8,128)(2,1)S(1)} %get-tuple-element.105.refs_2_), custom_call_target="tpu_custom_call" | custom-call | flops 402653184 | bytes 1441792 | tf_op jit(solution)/shard_map/third_part/pallas_call | solution.py:364
  52.3 6.4 %second_part.3 = (bf16[2,2,256,384]{3,2,1,0:T(8,128)(2,1)S(1)}, bf16[2,2,256,384]{3,2,1,0:T(8,128)(2,1)S(1)}, bf16[512,1024]{1,0:T(8,128)(2,1)S(1)}) custom-call(s32[7]{0:T(128)S(1)} %stack.33.refs_0_, bf16[1,256,384]{2,1,0:T(8,128)(2,1)S(1)} %collective-permute-done.8.refs_1_, bf16[2,128,384]{2,1,0:T(8,128)(2,1)S(1)} %collective-permute-done.21.refs_2_, ...), custom_call_target="tpu_custom_call" | custom-call | flops 1610612736 | bytes 5373952 | tf_op jit(solution)/shard_map/second_part/pallas_call | solution.py:337
  59.2 2.4 %third_part.3 = (bf16[2,2,256,384]{3,2,1,0:T(8,128)(2,1)S(1)}, bf16[2,2,256,384]{3,2,1,0:T(8,128)(2,1)S(1)}) custom-call(s32[7]{0:T(128)S(1)} %stack.33.refs_0_, bf16[512,1024]{1,0:T(8,128)(2,1)S(1)} %get-tuple-element.128.refs_1_, bf16[1024,1536]{1,0:T(8,128)(2,1)S(1)} %get-tuple-element.105.refs_2_), custom_call_target="tpu_custom_call" | custom-call | flops 402653184 | bytes 1441792 | tf_op jit(solution)/shard_map/third_part/pallas_call | solution.py:364
  61.8 2.0 %collective-permute-start.33 = (bf16[2,1,256,384]{3,2,1,0:T(8,128)(2,1)S(1)}, bf16[2,1,256,384]{3,2,1,0:T(8,128)(2,1)S(1)}, u32[]{:S(2)}, u32[]{:S(2)}) collective-permute-start(bf16[2,1,256,384]{3,2,1,0:T(8,128)(2,1)S(1)} %add_convert_fusion.1), channel_id=1, source_target_pairs={{0,2},{1,3},{2,0},{3,1},{4,6},{5,7},{6,4},{7,5},{8,10},{9,11},{10,... | collective-permute-start | bytes 1179656 | tf_op jit(solution)/shard_map/ppermute | solution.py:67
  63.9 1.5 %collective-permute-start.39 = (bf16[2,128,384]{2,1,0:T(8,128)(2,1)S(1)}, bf16[2,128,384]{2,1,0:T(8,128)(2,1)S(1)}, u32[]{:S(2)}, u32[]{:S(2)}) collective-permute-start(bf16[2,128,384]{2,1,0:T(8,128)(2,1)S(1)} %get-tuple-element.146), channel_id=1, source_target_pairs={{0,16},{1,17},{2,18},{3,19},{4,20},{5,21},{6,22},{7,23},{8,24},{9,... | collective-permute-start | bytes 589832 | tf_op jit(solution)/shard_map/ppermute | solution.py:67
  66.6 4.3 %collective-permute-done.39 = bf16[2,128,384]{2,1,0:T(8,128)(2,1)S(1)} collective-permute-done((bf16[2,128,384]{2,1,0:T(8,128)(2,1)S(1)}, bf16[2,128,384]{2,1,0:T(8,128)(2,1)S(1)}, u32[]{:S(2)}, u32[]{:S(2)}) %collective-permute-start.39) | collective-permute-done | bytes 196640 | tf_op jit(solution)/shard_map/ppermute | solution.py:67
  70.9 1.1 %collective-permute-done.40 = bf16[2,128,384]{2,1,0:T(8,128)(2,1)S(1)} collective-permute-done((bf16[2,128,384]{2,1,0:T(8,128)(2,1)S(1)}, bf16[2,128,384]{2,1,0:T(8,128)(2,1)S(1)}, u32[]{:S(2)}, u32[]{:S(2)}) %collective-permute-start.40) | collective-permute-done | bytes 196640 | tf_op jit(solution)/shard_map/ppermute | solution.py:67
  73.0 1.1 %collective-permute-start.42 = (bf16[1,256,384]{2,1,0:T(8,128)(2,1)S(1)}, bf16[1,256,384]{2,1,0:T(8,128)(2,1)S(1)}, u32[]{:S(2)}, u32[]{:S(2)}) collective-permute-start(bf16[1,256,384]{2,1,0:T(8,128)(2,1)S(1)} %slice.215), channel_id=1, source_target_pairs={{0,1},{1,0},{2,3},{3,2},{4,5},{5,4},{6,7},{7,6},{8,9},{9,8},{10,11... | collective-permute-start | bytes 589832 | tf_op jit(solution)/shard_map/ppermute | solution.py:67
  74.2 3.9 %collective-permute-done.41 = bf16[1,256,384]{2,1,0:T(8,128)(2,1)S(1)} collective-permute-done((bf16[1,256,384]{2,1,0:T(8,128)(2,1)S(1)}, bf16[1,256,384]{2,1,0:T(8,128)(2,1)S(1)}, u32[]{:S(2)}, u32[]{:S(2)}) %collective-permute-start.41) | collective-permute-done | bytes 196640 | tf_op jit(solution)/shard_map/ppermute | solution.py:67
  79.4 1.5 %collective-permute-start.43 = (bf16[1,256,384]{2,1,0:T(8,128)(2,1)S(1)}, bf16[1,256,384]{2,1,0:T(8,128)(2,1)S(1)}, u32[]{:S(2)}, u32[]{:S(2)}) collective-permute-start(bf16[1,256,384]{2,1,0:T(8,128)(2,1)S(1)} %slice.197), channel_id=1, source_target_pairs={{0,16},{1,17},{2,18},{3,19},{4,20},{5,21},{6,22},{7,23},{8,24},{9,... | collective-permute-start | bytes 589832 | tf_op jit(solution)/shard_map/ppermute | solution.py:67
  80.9 1.1 %collective-permute-start.44 = (bf16[1,256,384]{2,1,0:T(8,128)(2,1)S(1)}, bf16[1,256,384]{2,1,0:T(8,128)(2,1)S(1)}, u32[]{:S(2)}, u32[]{:S(2)}) collective-permute-start(bf16[1,256,384]{2,1,0:T(8,128)(2,1)S(1)} %slice.198), channel_id=1, source_target_pairs={{0,1},{1,0},{2,3},{3,2},{4,5},{5,4},{6,7},{7,6},{8,9},{9,8},{10,11... | collective-permute-start | bytes 589832 | tf_op jit(solution)/shard_map/ppermute | solution.py:67
  82.3 1.4 %collective-permute-start.37 = (bf16[1,128,384]{2,1,0:T(8,128)(2,1)S(1)}, bf16[1,128,384]{2,1,0:T(8,128)(2,1)S(1)}, u32[]{:S(2)}, u32[]{:S(2)}) collective-permute-start(bf16[1,128,384]{2,1,0:T(8,128)(2,1)S(1)} %get-tuple-element.144), channel_id=1, source_target_pairs={{0,16},{1,17},{2,18},{3,19},{4,20},{5,21},{6,22},{7,23},{8,24},{9,... | collective-permute-start | bytes 294920 | tf_op jit(solution)/shard_map/ppermute | solution.py:67
  83.7 2.0 %collective-permute-done.43 = bf16[1,256,384]{2,1,0:T(8,128)(2,1)S(1)} collective-permute-done((bf16[1,256,384]{2,1,0:T(8,128)(2,1)S(1)}, bf16[1,256,384]{2,1,0:T(8,128)(2,1)S(1)}, u32[]{:S(2)}, u32[]{:S(2)}) %collective-permute-start.43) | collective-permute-done | bytes 196640 | tf_op jit(solution)/shard_map/ppermute | solution.py:67
  85.7 1.2 %collective-permute-start.38 = (bf16[1,128,384]{2,1,0:T(8,128)(2,1)S(1)}, bf16[1,128,384]{2,1,0:T(8,128)(2,1)S(1)}, u32[]{:S(2)}, u32[]{:S(2)}) collective-permute-start(bf16[1,128,384]{2,1,0:T(8,128)(2,1)S(1)} %get-tuple-element.143), channel_id=1, source_target_pairs={{0,1},{1,0},{2,3},{3,2},{4,5},{5,4},{6,7},{7,6},{8,9},{9,8},{10,11... | collective-permute-start | bytes 294920 | tf_op jit(solution)/shard_map/ppermute | solution.py:67
  87.8 2.7 %collective-permute-start.48 = (bf16[1,256,384]{2,1,0:T(8,128)(2,1)S(1)}, bf16[1,256,384]{2,1,0:T(8,128)(2,1)S(1)}, u32[]{:S(2)}, u32[]{:S(2)}) collective-permute-start(bf16[1,256,384]{2,1,0:T(8,128)(2,1)S(1)} %fusion.8), channel_id=1, source_target_pairs={{0,4},{1,5},{2,6},{3,7},{4,0},{5,1},{6,2},{7,3},{8,12},{9,13},{10,... | collective-permute-start | bytes 589832 | tf_op jit(solution)/shard_map/ppermute | solution.py:67
  90.6 1.4 %collective-permute-start.46 = (bf16[1,256,384]{2,1,0:T(8,128)(2,1)S(1)}, bf16[1,256,384]{2,1,0:T(8,128)(2,1)S(1)}, u32[]{:S(2)}, u32[]{:S(2)}) collective-permute-start(bf16[1,256,384]{2,1,0:T(8,128)(2,1)S(1)} %fusion.10), channel_id=1, source_target_pairs={{0,16},{1,17},{2,18},{3,19},{4,20},{5,21},{6,22},{7,23},{8,24},{9,... | collective-permute-start | bytes 589832 | tf_op jit(solution)/shard_map/ppermute | solution.py:67
  92.1 1.1 %collective-permute-start.47 = (bf16[1,256,384]{2,1,0:T(8,128)(2,1)S(1)}, bf16[1,256,384]{2,1,0:T(8,128)(2,1)S(1)}, u32[]{:S(2)}, u32[]{:S(2)}) collective-permute-start(bf16[1,256,384]{2,1,0:T(8,128)(2,1)S(1)} %fusion.9), channel_id=1, source_target_pairs={{0,1},{1,0},{2,3},{3,2},{4,5},{5,4},{6,7},{7,6},{8,9},{9,8},{10,11... | collective-permute-start | bytes 589832 | tf_op jit(solution)/shard_map/ppermute | solution.py:67
  93.2 4.7 %collective-permute-done.48 = bf16[1,256,384]{2,1,0:T(8,128)(2,1)S(1)} collective-permute-done((bf16[1,256,384]{2,1,0:T(8,128)(2,1)S(1)}, bf16[1,256,384]{2,1,0:T(8,128)(2,1)S(1)}, u32[]{:S(2)}, u32[]{:S(2)}) %collective-permute-start.48) | collective-permute-done | bytes 196640 | tf_op jit(solution)/shard_map/ppermute | solution.py:67
  (108 shorter events, 19.2 us)
Async XLA Ops:
  0.0 11.2 %collective-permute-start.1 = (bf16[1,256,384]{2,1,0:T(8,128)(2,1)}, bf16[1,256,384]{2,1,0:T(8,128)(2,1)S(1)}, u32[]{:S(2)}, u32[]{:S(2)}) collective-permute-start(bf16[1,256,384]{2,1,0:T(8,128)(2,1)} %bitcast.72), channel_id=1, source_target_pairs={{0,2},{1,3},{2,0},{3,1},{4,6},{5,7},{6,4},{7,5},{8,10},{9,11},{10,... | collective-permute-start | bytes 589832 | tf_op jit(solution)/shard_map/ppermute | solution.py:67
  5.5 8.7 %collective-permute-start.5 = (bf16[1,272,384]{2,1,0:T(8,128)(2,1)S(1)}, bf16[1,272,384]{2,1,0:T(8,128)(2,1)S(1)}, u32[]{:S(2)}, u32[]{:S(2)}) collective-permute-start(bf16[1,272,384]{2,1,0:T(8,128)(2,1)S(1)} %maximum_bitcast_fusion.refs_1_.refs_14_), channel_id=1, source_target_pairs={{0,16},{1,17},{2,18},{3,19},{4,20},{5,21},{6,22},{7,23},{8,24},{9,... | collective-permute-start | bytes 626696 | tf_op jit(solution)/shard_map/ppermute | solution.py:67
  7.0 7.1 %collective-permute-start = (bf16[1,256,384]{2,1,0:T(8,128)(2,1)}, bf16[1,256,384]{2,1,0:T(8,128)(2,1)S(1)}, u32[]{:S(2)}, u32[]{:S(2)}) collective-permute-start(bf16[1,256,384]{2,1,0:T(8,128)(2,1)} %bitcast.73), channel_id=1, source_target_pairs={{0,1},{1,0},{2,3},{3,2},{4,5},{5,4},{6,7},{7,6},{8,9},{9,8},{10,11... | collective-permute-start | bytes 589832 | tf_op jit(solution)/shard_map/ppermute | solution.py:67
  8.6 11.0 %collective-permute-start.4 = (bf16[1,256,384]{2,1,0:T(8,128)(2,1)}, bf16[1,256,384]{2,1,0:T(8,128)(2,1)S(1)}, u32[]{:S(2)}, u32[]{:S(2)}) collective-permute-start(bf16[1,256,384]{2,1,0:T(8,128)(2,1)} %bitcast.74), channel_id=1, source_target_pairs={{0,4},{1,5},{2,6},{3,7},{4,0},{5,1},{6,2},{7,3},{8,12},{9,13},{10,... | collective-permute-start | bytes 589832 | tf_op jit(solution)/shard_map/ppermute | solution.py:67
  11.2 8.5 %collective-permute-start.2 = (bf16[1,256,384]{2,1,0:T(8,128)(2,1)S(1)}, bf16[1,256,384]{2,1,0:T(8,128)(2,1)S(1)}, u32[]{:S(2)}, u32[]{:S(2)}) collective-permute-start(bf16[1,256,384]{2,1,0:T(8,128)(2,1)S(1)} %collective-permute-done.1.refs_5_), channel_id=1, source_target_pairs={{0,16},{1,17},{2,18},{3,19},{4,20},{5,21},{6,22},{7,23},{8,24},{9,... | collective-permute-start | bytes 589832 | tf_op jit(solution)/shard_map/ppermute | solution.py:67
  11.7 7.9 %collective-permute-start.3 = (bf16[1,256,384]{2,1,0:T(8,128)(2,1)S(1)}, bf16[1,256,384]{2,1,0:T(8,128)(2,1)S(1)}, u32[]{:S(2)}, u32[]{:S(2)}) collective-permute-start(bf16[1,256,384]{2,1,0:T(8,128)(2,1)S(1)} %collective-permute-done.1.refs_5_), channel_id=1, source_target_pairs={{0,1},{1,0},{2,3},{3,2},{4,5},{5,4},{6,7},{7,6},{8,9},{9,8},{10,11... | collective-permute-start | bytes 589832 | tf_op jit(solution)/shard_map/ppermute | solution.py:67
  14.1 6.8 %collective-permute-start.12 = (bf16[1,256,384]{2,1,0:T(8,128)(2,1)S(1)}, bf16[1,256,384]{2,1,0:T(8,128)(2,1)S(1)}, u32[]{:S(2)}, u32[]{:S(2)}) collective-permute-start(bf16[1,256,384]{2,1,0:T(8,128)(2,1)S(1)} %collective-permute-done.refs_2_), channel_id=1, source_target_pairs={{0,8},{1,9},{2,10},{3,11},{4,12},{5,13},{6,14},{7,15},{8,0},{9,1},... | collective-permute-start | bytes 589832 | tf_op jit(solution)/shard_map/ppermute | solution.py:67
  19.6 7.3 %collective-permute-start.10 = (bf16[1,256,384]{2,1,0:T(8,128)(2,1)S(1)}, bf16[1,256,384]{2,1,0:T(8,128)(2,1)S(1)}, u32[]{:S(2)}, u32[]{:S(2)}) collective-permute-start(bf16[1,256,384]{2,1,0:T(8,128)(2,1)S(1)} %collective-permute-done.4.refs_1_), channel_id=1, source_target_pairs={{0,2},{1,3},{2,0},{3,1},{4,6},{5,7},{6,4},{7,5},{8,10},{9,11},{10,... | collective-permute-start | bytes 589832 | tf_op jit(solution)/shard_map/ppermute | solution.py:67
  20.3 11.6 %collective-permute-start.8 = (bf16[1,256,384]{2,1,0:T(8,128)(2,1)S(1)}, bf16[1,256,384]{2,1,0:T(8,128)(2,1)S(1)}, u32[]{:S(2)}, u32[]{:S(2)}) collective-permute-start(bf16[1,256,384]{2,1,0:T(8,128)(2,1)S(1)} %collective-permute-done.4.refs_1_), channel_id=1, source_target_pairs={{0,16},{1,17},{2,18},{3,19},{4,20},{5,21},{6,22},{7,23},{8,24},{9,... | collective-permute-start | bytes 589832 | tf_op jit(solution)/shard_map/ppermute | solution.py:67
  21.0 10.3 %collective-permute-start.7 = (bf16[2,128,384]{2,1,0:T(8,128)(2,1)S(1)}, bf16[2,128,384]{2,1,0:T(8,128)(2,1)S(1)}, u32[]{:S(2)}, u32[]{:S(2)}) collective-permute-start(bf16[2,128,384]{2,1,0:T(8,128)(2,1)S(1)} %pad_maximum_fusion.1), channel_id=1, source_target_pairs={{0,1},{1,0},{2,3},{3,2},{4,5},{5,4},{6,7},{7,6},{8,9},{9,8},{10,11... | collective-permute-start | bytes 589832 | tf_op jit(solution)/shard_map/ppermute | solution.py:67
  21.5 10.4 %collective-permute-start.6 = (bf16[2,128,384]{2,1,0:T(8,128)(2,1)S(1)}, bf16[2,128,384]{2,1,0:T(8,128)(2,1)S(1)}, u32[]{:S(2)}, u32[]{:S(2)}) collective-permute-start(bf16[2,128,384]{2,1,0:T(8,128)(2,1)S(1)} %pad_maximum_fusion), channel_id=1, source_target_pairs={{0,16},{1,17},{2,18},{3,19},{4,20},{5,21},{6,22},{7,23},{8,24},{9,... | collective-permute-start | bytes 589832 | tf_op jit(solution)/shard_map/ppermute | solution.py:67
  23.4 8.4 %collective-permute-start.9 = (bf16[1,256,384]{2,1,0:T(8,128)(2,1)S(1)}, bf16[1,256,384]{2,1,0:T(8,128)(2,1)S(1)}, u32[]{:S(2)}, u32[]{:S(2)}) collective-permute-start(bf16[1,256,384]{2,1,0:T(8,128)(2,1)S(1)} %collective-permute-done.4.refs_1_), channel_id=1, source_target_pairs={{0,1},{1,0},{2,3},{3,2},{4,5},{5,4},{6,7},{7,6},{8,9},{9,8},{10,11... | collective-permute-start | bytes 589832 | tf_op jit(solution)/shard_map/ppermute | solution.py:67
  26.9 6.8 %collective-permute-start.17 = (bf16[1,272,384]{2,1,0:T(8,128)(2,1)S(1)}, bf16[1,272,384]{2,1,0:T(8,128)(2,1)S(1)}, u32[]{:S(2)}, u32[]{:S(2)}) collective-permute-start(bf16[1,272,384]{2,1,0:T(8,128)(2,1)S(1)} %collective-permute-done.5.refs_1_.refs_14_), channel_id=1, source_target_pairs={{0,8},{1,9},{2,10},{3,11},{4,12},{5,13},{6,14},{7,15},{8,0},{9,1},... | collective-permute-start | bytes 626696 | tf_op jit(solution)/shard_map/ppermute | solution.py:67
  32.4 7.4 %collective-permute-start.15 = (bf16[1,256,384]{2,1,0:T(8,128)(2,1)S(1)}, bf16[1,256,384]{2,1,0:T(8,128)(2,1)S(1)}, u32[]{:S(2)}, u32[]{:S(2)}) collective-permute-start(bf16[1,256,384]{2,1,0:T(8,128)(2,1)S(1)} %collective-permute-done.10.refs_5_), channel_id=1, source_target_pairs={{0,16},{1,17},{2,18},{3,19},{4,20},{5,21},{6,22},{7,23},{8,24},{9,... | collective-permute-start | bytes 589832 | tf_op jit(solution)/shard_map/ppermute | solution.py:67
  33.7 6.6 %collective-permute-start.16 = (bf16[1,256,384]{2,1,0:T(8,128)(2,1)S(1)}, bf16[1,256,384]{2,1,0:T(8,128)(2,1)S(1)}, u32[]{:S(2)}, u32[]{:S(2)}) collective-permute-start(bf16[1,256,384]{2,1,0:T(8,128)(2,1)S(1)} %collective-permute-done.10.refs_5_), channel_id=1, source_target_pairs={{0,1},{1,0},{2,3},{3,2},{4,5},{5,4},{6,7},{7,6},{8,9},{9,8},{10,11... | collective-permute-start | bytes 589832 | tf_op jit(solution)/shard_map/ppermute | solution.py:67
  34.9 6.7 %collective-permute-start.26 = (bf16[1,256,384]{2,1,0:T(8,128)(2,1)S(1)}, bf16[1,256,384]{2,1,0:T(8,128)(2,1)S(1)}, u32[]{:S(2)}, u32[]{:S(2)}) collective-permute-start(bf16[1,256,384]{2,1,0:T(8,128)(2,1)S(1)} %collective-permute-done.9.refs_2_), channel_id=1, source_target_pairs={{0,8},{1,9},{2,10},{3,11},{4,12},{5,13},{6,14},{7,15},{8,0},{9,1},... | collective-permute-start | bytes 589832 | tf_op jit(solution)/shard_map/ppermute | solution.py:67
  35.4 7.0 %collective-permute-start.27 = (bf16[1,256,384]{2,1,0:T(8,128)(2,1)S(1)}, bf16[1,256,384]{2,1,0:T(8,128)(2,1)S(1)}, u32[]{:S(2)}, u32[]{:S(2)}) collective-permute-start(bf16[1,256,384]{2,1,0:T(8,128)(2,1)S(1)} %collective-permute-done.10.refs_5_), channel_id=1, source_target_pairs={{0,8},{1,9},{2,10},{3,11},{4,12},{5,13},{6,14},{7,15},{8,0},{9,1},... | collective-permute-start | bytes 589832 | tf_op jit(solution)/shard_map/ppermute | solution.py:67
  39.9 8.7 %collective-permute-start.23 = (bf16[1,256,384]{2,1,0:T(8,128)(2,1)S(1)}, bf16[1,256,384]{2,1,0:T(8,128)(2,1)S(1)}, u32[]{:S(2)}, u32[]{:S(2)}) collective-permute-start(bf16[1,256,384]{2,1,0:T(8,128)(2,1)S(1)} %collective-permute-done.8.refs_1_), channel_id=1, source_target_pairs={{0,8},{1,9},{2,10},{3,11},{4,12},{5,13},{6,14},{7,15},{8,0},{9,1},... | collective-permute-start | bytes 589832 | tf_op jit(solution)/shard_map/ppermute | solution.py:67
  40.6 8.1 %collective-permute-start.22 = (bf16[2,128,384]{2,1,0:T(8,128)(2,1)S(1)}, bf16[2,128,384]{2,1,0:T(8,128)(2,1)S(1)}, u32[]{:S(2)}, u32[]{:S(2)}) collective-permute-start(bf16[2,128,384]{2,1,0:T(8,128)(2,1)S(1)} %pad_maximum_fusion.3), channel_id=1, source_target_pairs={{0,1},{1,0},{2,3},{3,2},{4,5},{5,4},{6,7},{7,6},{8,9},{9,8},{10,11... | collective-permute-start | bytes 589832 | tf_op jit(solution)/shard_map/ppermute | solution.py:67
  41.6 7.0 %collective-permute-start.21 = (bf16[2,128,384]{2,1,0:T(8,128)(2,1)S(1)}, bf16[2,128,384]{2,1,0:T(8,128)(2,1)S(1)}, u32[]{:S(2)}, u32[]{:S(2)}) collective-permute-start(bf16[2,128,384]{2,1,0:T(8,128)(2,1)S(1)} %pad_maximum_fusion.2), channel_id=1, source_target_pairs={{0,16},{1,17},{2,18},{3,19},{4,20},{5,21},{6,22},{7,23},{8,24},{9,... | collective-permute-start | bytes 589832 | tf_op jit(solution)/shard_map/ppermute | solution.py:67
  49.3 9.4 %collective-permute-start.29 = (bf16[2,2,256,384]{3,2,1,0:T(8,128)(2,1)S(1)}, bf16[2,2,256,384]{3,2,1,0:T(8,128)(2,1)S(1)}, u32[]{:S(2)}, u32[]{:S(2)}) collective-permute-start(bf16[2,2,256,384]{3,2,1,0:T(8,128)(2,1)S(1)} %get-tuple-element.101), channel_id=1, source_target_pairs={{0,8},{1,9},{2,10},{3,11},{4,12},{5,13},{6,14},{7,15},{8,0},{9,1},... | collective-permute-start | bytes 2359304 | tf_op jit(solution)/shard_map/ppermute | solution.py:67
  52.1 6.6 %collective-permute-start.32 = (bf16[2,2,256,384]{3,2,1,0:T(8,128)(2,1)S(1)}, bf16[2,2,256,384]{3,2,1,0:T(8,128)(2,1)S(1)}, u32[]{:S(2)}, u32[]{:S(2)}) collective-permute-start(bf16[2,2,256,384]{3,2,1,0:T(8,128)(2,1)S(1)} %get-tuple-element.109), channel_id=1, source_target_pairs={{0,8},{1,9},{2,10},{3,11},{4,12},{5,13},{6,14},{7,15},{8,0},{9,1},... | collective-permute-start | bytes 2359304 | tf_op jit(solution)/shard_map/ppermute | solution.py:67
  61.8 30.1 %collective-permute-start.33 = (bf16[2,1,256,384]{3,2,1,0:T(8,128)(2,1)S(1)}, bf16[2,1,256,384]{3,2,1,0:T(8,128)(2,1)S(1)}, u32[]{:S(2)}, u32[]{:S(2)}) collective-permute-start(bf16[2,1,256,384]{3,2,1,0:T(8,128)(2,1)S(1)} %add_convert_fusion.1), channel_id=1, source_target_pairs={{0,2},{1,3},{2,0},{3,1},{4,6},{5,7},{6,4},{7,5},{8,10},{9,11},{10,... | collective-permute-start | bytes 1179656 | tf_op jit(solution)/shard_map/ppermute | solution.py:67
  63.9 7.0 %collective-permute-start.39 = (bf16[2,128,384]{2,1,0:T(8,128)(2,1)S(1)}, bf16[2,128,384]{2,1,0:T(8,128)(2,1)S(1)}, u32[]{:S(2)}, u32[]{:S(2)}) collective-permute-start(bf16[2,128,384]{2,1,0:T(8,128)(2,1)S(1)} %get-tuple-element.146), channel_id=1, source_target_pairs={{0,16},{1,17},{2,18},{3,19},{4,20},{5,21},{6,22},{7,23},{8,24},{9,... | collective-permute-start | bytes 589832 | tf_op jit(solution)/shard_map/ppermute | solution.py:67
  65.4 6.7 %collective-permute-start.40 = (bf16[2,128,384]{2,1,0:T(8,128)(2,1)S(1)}, bf16[2,128,384]{2,1,0:T(8,128)(2,1)S(1)}, u32[]{:S(2)}, u32[]{:S(2)}) collective-permute-start(bf16[2,128,384]{2,1,0:T(8,128)(2,1)S(1)} %get-tuple-element.145), channel_id=1, source_target_pairs={{0,1},{1,0},{2,3},{3,2},{4,5},{5,4},{6,7},{7,6},{8,9},{9,8},{10,11... | collective-permute-start | bytes 589832 | tf_op jit(solution)/shard_map/ppermute | solution.py:67
  66.5 15.7 %collective-permute-start.36 = (bf16[2,1,256,384]{3,2,1,0:T(8,128)(2,1)S(1)}, bf16[2,1,256,384]{3,2,1,0:T(8,128)(2,1)S(1)}, u32[]{:S(2)}, u32[]{:S(2)}) collective-permute-start(bf16[2,1,256,384]{3,2,1,0:T(8,128)(2,1)S(1)} %add_convert_fusion), channel_id=1, source_target_pairs={{0,2},{1,3},{2,0},{3,1},{4,6},{5,7},{6,4},{7,5},{8,10},{9,11},{10,... | collective-permute-start | bytes 1179656 | tf_op jit(solution)/shard_map/ppermute | solution.py:67
  78.9 8.8 %collective-permute-start.45 = (bf16[1,256,384]{2,1,0:T(8,128)(2,1)S(1)}, bf16[1,256,384]{2,1,0:T(8,128)(2,1)S(1)}, u32[]{:S(2)}, u32[]{:S(2)}) collective-permute-start(bf16[1,256,384]{2,1,0:T(8,128)(2,1)S(1)} %fusion.4), channel_id=1, source_target_pairs={{0,2},{1,3},{2,0},{3,1},{4,6},{5,7},{6,4},{7,5},{8,10},{9,11},{10,... | collective-permute-start | bytes 589832 | tf_op jit(solution)/shard_map/ppermute | solution.py:67
  79.4 6.3 %collective-permute-start.43 = (bf16[1,256,384]{2,1,0:T(8,128)(2,1)S(1)}, bf16[1,256,384]{2,1,0:T(8,128)(2,1)S(1)}, u32[]{:S(2)}, u32[]{:S(2)}) collective-permute-start(bf16[1,256,384]{2,1,0:T(8,128)(2,1)S(1)} %slice.197), channel_id=1, source_target_pairs={{0,16},{1,17},{2,18},{3,19},{4,20},{5,21},{6,22},{7,23},{8,24},{9,... | collective-permute-start | bytes 589832 | tf_op jit(solution)/shard_map/ppermute | solution.py:67
  80.9 6.8 %collective-permute-start.44 = (bf16[1,256,384]{2,1,0:T(8,128)(2,1)S(1)}, bf16[1,256,384]{2,1,0:T(8,128)(2,1)S(1)}, u32[]{:S(2)}, u32[]{:S(2)}) collective-permute-start(bf16[1,256,384]{2,1,0:T(8,128)(2,1)S(1)} %slice.198), channel_id=1, source_target_pairs={{0,1},{1,0},{2,3},{3,2},{4,5},{5,4},{6,7},{7,6},{8,9},{9,8},{10,11... | collective-permute-start | bytes 589832 | tf_op jit(solution)/shard_map/ppermute | solution.py:67
  82.3 8.2 %collective-permute-start.37 = (bf16[1,128,384]{2,1,0:T(8,128)(2,1)S(1)}, bf16[1,128,384]{2,1,0:T(8,128)(2,1)S(1)}, u32[]{:S(2)}, u32[]{:S(2)}) collective-permute-start(bf16[1,128,384]{2,1,0:T(8,128)(2,1)S(1)} %get-tuple-element.144), channel_id=1, source_target_pairs={{0,16},{1,17},{2,18},{3,19},{4,20},{5,21},{6,22},{7,23},{8,24},{9,... | collective-permute-start | bytes 294920 | tf_op jit(solution)/shard_map/ppermute | solution.py:67
  87.8 10.1 %collective-permute-start.48 = (bf16[1,256,384]{2,1,0:T(8,128)(2,1)S(1)}, bf16[1,256,384]{2,1,0:T(8,128)(2,1)S(1)}, u32[]{:S(2)}, u32[]{:S(2)}) collective-permute-start(bf16[1,256,384]{2,1,0:T(8,128)(2,1)S(1)} %fusion.8), channel_id=1, source_target_pairs={{0,4},{1,5},{2,6},{3,7},{4,0},{5,1},{6,2},{7,3},{8,12},{9,13},{10,... | collective-permute-start | bytes 589832 | tf_op jit(solution)/shard_map/ppermute | solution.py:67
  90.6 7.3 %collective-permute-start.46 = (bf16[1,256,384]{2,1,0:T(8,128)(2,1)S(1)}, bf16[1,256,384]{2,1,0:T(8,128)(2,1)S(1)}, u32[]{:S(2)}, u32[]{:S(2)}) collective-permute-start(bf16[1,256,384]{2,1,0:T(8,128)(2,1)S(1)} %fusion.10), channel_id=1, source_target_pairs={{0,16},{1,17},{2,18},{3,19},{4,20},{5,21},{6,22},{7,23},{8,24},{9,... | collective-permute-start | bytes 589832 | tf_op jit(solution)/shard_map/ppermute | solution.py:67
  (17 other events, 72.0 us)
